TPU v7x, 128 devices: a whole 4x4x4 slice. The times are simulated.
128 devices in a mesh: dp: 8 (over y, z_hi), px: 8 (over x, z_lo), py: 2 (over core).
Axes of the slice: x: 4, y: 4, z: 4 (z_hi: 2, z_lo: 2; z = z_hi * 2 + z_lo), core: 2. Of those that a mesh axis runs over, the one named last changes fastest.
Arguments:
- fields: bfloat16 [8, 32, 16, 32, 256], P('dp', 'px', 'py'), may hold values from -6 to 6
- cotangent: bfloat16 [8, 32, 16, 32, 256], P('dp', 'px', 'py'), may hold values from -6 to 6
- first_weight: bfloat16 [6912, 256], replicated, may hold values from -0.078125 to 0.078125
- second_weight: bfloat16 [6912, 256], replicated, may hold values from -0.078125 to 0.078125
Outputs:
- output: bfloat16 [8, 32, 16, 32, 256], P('dp', 'px', 'py')
- field_grad: bfloat16 [8, 32, 16, 32, 256], P('dp', 'px', 'py')
- first_grad: float32 [6912, 256], P('dp', ('px', 'py'))
- second_grad: float32 [6912, 256], P('dp', ('px', 'py'))
All inputs are finite; a program needn't handle non-finite values.
Results may differ from a plain program's by a relative error of at most 0.0033.
Values may be sent and summed in bfloat16 or wider, within the bound.
No kernel may reach another device: no remote copies, remote signals or barrier semaphores. Data moves between devices by JAX's collectives and lax.ppermute only.
A program may use at most 128 MiB of HBM per device.

v0:
```python
import jax
import jax.numpy as jnp
from jax import lax
from jax.sharding import PartitionSpec as P


def with_halo(block, sides, width):
    for axis, dim in sides:
        count = lax.axis_size(axis)
        forward = [(i, i + 1) for i in range(count - 1)]
        backward = [(target, source) for source, target in forward]
        low = lax.ppermute(
            lax.slice_in_dim(block, block.shape[dim] - width, None, axis=dim), axis, forward
        )
        high = lax.ppermute(lax.slice_in_dim(block, 0, width, axis=dim), axis, backward)
        block = jnp.concatenate([low, block, high], axis=dim)
    return block


def gelu_tanh(v):
    return jax.nn.gelu(v, approximate=True)


def pad_faces(field):
    padded = with_halo(field, (("px", 1), ("py", 2)), 1)
    return jnp.pad(padded, ((0, 0), (0, 0), (0, 0), (1, 1), (0, 0)))


def window(padded, start_x, start_y, start_z):
    batch, size_x, size_y, size_z, width = padded.shape
    block = padded[
        :,
        start_x : start_x + size_x - 2,
        start_y : start_y + size_y - 2,
        start_z : start_z + size_z - 2,
        :,
    ]
    return block.reshape(-1, width)


def conv(padded, weight, flipped):
    width = padded.shape[-1]
    total = None
    for offset in range(27):
        first, second, third = (offset // 9, offset // 3 % 3, offset % 3)
        block = weight[offset * width : (offset + 1) * width]
        if flipped:
            rows = window(padded, 2 - first, 2 - second, 2 - third)
            term = lax.dot_general(
                rows, block, (((1,), (1,)), ((), ())), preferred_element_type=jnp.float32
            )
        else:
            rows = window(padded, first, second, third)
            term = jnp.dot(rows, block, preferred_element_type=jnp.float32)
        total = term if total is None else total + term
    return total


def weight_terms(padded, grads):
    blocks = []
    for offset in range(27):
        first, second, third = (offset // 9, offset // 3 % 3, offset % 3)
        rows = window(padded, first, second, third)
        blocks.append(
            lax.dot_general(
                rows, grads, (((0,), (0,)), ((), ())), preferred_element_type=jnp.float32
            )
        )
    return jnp.concatenate(blocks, axis=0)


def body(fields, cotangent, first_weight, second_weight):
    shape = fields.shape
    width = shape[-1]
    rollouts = shape[0] * lax.axis_size("dp")
    fields_padded = pad_faces(fields)
    pre = conv(fields_padded, first_weight, False)
    hidden = gelu_tanh(pre).astype(jnp.bfloat16)
    hidden_padded = pad_faces(hidden.reshape(shape))
    second_out = conv(hidden_padded, second_weight, False)
    output = (
        (fields.reshape(-1, width).astype(jnp.float32) + second_out)
        .astype(jnp.bfloat16)
        .reshape(shape)
    )
    cot_flat = cotangent.reshape(-1, width)
    cot_padded = pad_faces(cotangent)
    hidden_grad = conv(cot_padded, second_weight, True)
    second_terms = weight_terms(hidden_padded, cot_flat) / rollouts
    gelu_back = jax.vjp(gelu_tanh, pre)[1]
    pre_grad = gelu_back(hidden_grad)[0].astype(jnp.bfloat16)
    pre_padded = pad_faces(pre_grad.reshape(shape))
    field_term = conv(pre_padded, first_weight, True)
    field_grad = (cot_flat.astype(jnp.float32) + field_term).astype(jnp.bfloat16).reshape(shape)
    first_terms = weight_terms(fields_padded, pre_grad) / rollouts
    partial_sums = (
        lax.psum_scatter(first_terms, "dp", scatter_dimension=0, tiled=True),
        lax.psum_scatter(second_terms, "dp", scatter_dimension=0, tiled=True),
    )
    first_grad, second_grad = (
        lax.psum_scatter(partial_sums[0], ("px", "py"), scatter_dimension=1, tiled=True),
        lax.psum_scatter(partial_sums[1], ("px", "py"), scatter_dimension=1, tiled=True),
    )
    return (output, field_grad, first_grad, second_grad)


def solution(mesh):
    placed = (P("dp", "px", "py", None, None), P("dp", "px", "py", None, None), P(), P())
    return jax.shard_map(
        body,
        mesh=mesh,
        in_specs=placed,
        out_specs=(
            P("dp", "px", "py", None, None),
            P("dp", "px", "py", None, None),
            P("dp", ("px", "py")),
            P("dp", ("px", "py")),
        ),
        check_vma=False,
    )
```

profile of v0, /device:TPU:0, one launch (start us, length us, event | category | flops | bytes accessed | tf_op | source)
XLA Modules:
  0.0 430.0 jit_solution(1453633113811331594)
XLA Ops:
  7.2 1.0 fusion.284
  8.3 3.9 collective-permute-start
  12.2 1.3 collective-permute-start.1
  13.5 1.0 fusion.282
  14.5 4.6 %collective-permute-start.8 = (bf16[1,1,8,32,256]{4,3,2,1,0:T(8,128)(2,1)S(1)}, bf16[1,1,8,32,256]{4,3,2,1,0:T(8,128)(2,1)S(1)}, u32[]{:S(2)}, u32[]{:S(2)}) collective-permute-start(bf16[1,1,8,32,256]{4,3,2,1,0:T(8,128)(2,1)S(1)} %get-tuple-element.134), channel_id=1, source_target_pairs={{0,2},{2,4},{4,6},{6,8},{8,10},{10,12},{12,14},{1,3},{3,5},{5,7},{... | collective-permute-start | bytes 393224 | tf_op jit(solution)/shard_map/ppermute | solution.py:12
  19.0 1.3 collective-permute-start.9
  20.4 1.7 pad_maximum_fusion.11
  22.1 1.3 collective-permute-start.2
  23.4 1.3 collective-permute-start.3
  24.8 1.1 collective-permute-done.9
  25.9 1.1 pad_maximum_fusion.5
  27.0 1.9 collective-permute-start.10
  29.0 1.3 collective-permute-start.11
  30.3 0.7 fusion.24
  31.0 3.0 fusion.274
  35.5 0.7 select_maximum_fusion.4
  36.2 3.3 fusion.272
  40.9 1.4 fusion.123
  56.8 0.6 multiply_convert_fusion
  57.7 0.9 fusion.61
  59.7 0.6 convolution_dynamic-update-slice_fusion.22
  68.5 3.4 broadcast_multiply_fusion.1
  72.0 4.5 %collective-permute-start.4 = (bf16[1,1,8,32,256]{4,3,2,1,0:T(8,128)(2,1)S(1)}, bf16[1,1,8,32,256]{4,3,2,1,0:T(8,128)(2,1)S(1)}, u32[]{:S(2)}, u32[]{:S(2)}) collective-permute-start(bf16[1,1,8,32,256]{4,3,2,1,0:T(8,128)(2,1)S(1)} %get-tuple-element.137), channel_id=1, source_target_pairs={{0,2},{2,4},{4,6},{6,8},{8,10},{10,12},{12,14},{1,3},{3,5},{5,7},{... | collective-permute-start | bytes 393224 | tf_op jit(solution)/shard_map/ppermute | solution.py:12
  76.6 1.3 collective-permute-start.5
  77.9 0.7 fusion.281
  78.6 5.4 %collective-permute-start.12 = (bf16[1,1,8,32,256]{4,3,2,1,0:T(8,128)(2,1)}, bf16[1,1,8,32,256]{4,3,2,1,0:T(8,128)(2,1)S(1)}, u32[]{:S(2)}, u32[]{:S(2)}) collective-permute-start(bf16[1,1,8,32,256]{4,3,2,1,0:T(8,128)(2,1)} %get-tuple-element.128), channel_id=1, source_target_pairs={{0,2},{2,4},{4,6},{6,8},{8,10},{10,12},{12,14},{1,3},{3,5},{5,7},{... | collective-permute-start | bytes 393224 | tf_op jit(solution)/shard_map/ppermute | solution.py:12
  83.9 1.3 collective-permute-start.13
  85.6 2.2 collective-permute-start.6
  87.8 1.8 collective-permute-start.7
  89.6 1.3 collective-permute-done.7
  91.1 0.7 select_maximum_fusion.6
  93.6 0.4 fusion.48
  101.4 3.3 broadcast_multiply_fusion
  104.8 0.8 pad_maximum_fusion.16
  105.6 2.1 collective-permute-start.14
  107.6 1.3 collective-permute-start.15
  108.9 1.0 pad_maximum_fusion.2
  109.9 0.9 collective-permute-done.15
  110.8 1.1 maximum_maximum_fusion.1
  112.0 1.6 select_maximum_fusion
  113.6 3.7 fusion.271
  118.4 4.2 fusion.273
  124.5 0.4 fusion.3
  128.0 1.2 fusion.277
  136.7 53.0 %reduce-scatter.9.cloned.1.call-done = f32[864,256]{1,0:T(8,128)} async-done(((f32[6912,256]{1,0:T(8,128)}), f32[864,256]{1,0:T(8,128)}) %reduce-scatter.9.cloned.1.call-update) | async-done | bytes 884752 | tf_op jit(solution)/shard_map/reduce_scatter | solution.py:97
  189.7 2.5 copy.39
  192.5 2.3 fusion.16
  194.7 1.4 convolution_add_fusion.57
  196.2 1.3 convolution_add_fusion.56
  197.4 1.3 convolution_add_fusion.55
  198.7 1.2 convolution_add_fusion.54
  199.9 1.2 convolution_add_fusion.53
  201.2 1.3 convolution_add_fusion.52
  202.5 95.8 %reduce-scatter.11.cloned.1.call-done = f32[864,256]{1,0:T(8,128)} async-done(((f32[6912,256]{1,0:T(8,128)}), f32[864,256]{1,0:T(8,128)}) %reduce-scatter.11.cloned.1.call-update) | async-done | bytes 884752 | tf_op jit(solution)/shard_map/reduce_scatter | solution.py:98
  298.3 2.5 copy.41
  300.8 1.4 convolution_add_fusion.51
  302.2 1.2 fusion.132
  303.4 1.4 convolution_add_fusion.50
  304.8 1.3 fusion.9
  306.1 1.2 convolution_add_fusion.48
  307.4 1.2 convolution_add_fusion.47
  308.6 2.0 fusion.15
  310.6 49.8 %reduce-scatter.13.cloned.1.call-done = f32[16,864]{1,0:T(8,128)} async-done(((f32[256,864]{1,0:T(8,128)}), f32[16,864]{1,0:T(8,128)}) %reduce-scatter.13.cloned.1.call-update) | async-done | bytes 55312
  360.4 62.8 %reduce-scatter.15.cloned.1.call-done = f32[16,864]{1,0:T(8,128)} async-done(((f32[256,864]{1,0:T(8,128)}), f32[16,864]{1,0:T(8,128)}) %reduce-scatter.15.cloned.1.call-update) | async-done | bytes 55312
  (240 shorter events, 49.8 us)
Async XLA Ops:
  7.2 18.7 %copy-start.9 = (bf16[1,4,8,32,256]{4,3,2,1,0:T(8,128)(2,1)S(1)}, bf16[1,4,8,32,256]{4,3,2,1,0:T(8,128)(2,1)}, u32[]{:S(2)}) copy-start(bf16[1,4,8,32,256]{4,3,2,1,0:T(8,128)(2,1)} %param.5) | copy-start | bytes 1572868
  7.2 182.5 %reduce-scatter.9.cloned.1.call-start = ((), (), s32[]{:S(2)}) async-start(), calls=%async_computation.4 | async-start | bytes 7962624 | tf_op jit(solution)/shard_map/reduce_scatter | solution.py:97
  8.3 12.1 %collective-permute-start = (bf16[1,1,8,32,256]{4,3,2,1,0:T(8,128)(2,1)S(1)}, bf16[1,1,8,32,256]{4,3,2,1,0:T(8,128)(2,1)S(1)}, u32[]{:S(2)}, u32[]{:S(2)}) collective-permute-start(bf16[1,1,8,32,256]{4,3,2,1,0:T(8,128)(2,1)S(1)} %get-tuple-element.143), channel_id=1, source_target_pairs={{0,2},{2,4},{4,6},{6,8},{8,10},{10,12},{12,14},{1,3},{3,5},{5,7},{... | collective-permute-start | bytes 393224 | tf_op jit(solution)/shard_map/ppermute | solution.py:12
  12.2 8.2 %collective-permute-start.1 = (bf16[1,1,8,32,256]{4,3,2,1,0:T(8,128)(2,1)S(1)}, bf16[1,1,8,32,256]{4,3,2,1,0:T(8,128)(2,1)S(1)}, u32[]{:S(2)}, u32[]{:S(2)}) collective-permute-start(bf16[1,1,8,32,256]{4,3,2,1,0:T(8,128)(2,1)S(1)} %get-tuple-element.142), channel_id=1, source_target_pairs={{2,0},{4,2},{6,4},{8,6},{10,8},{12,10},{14,12},{3,1},{5,3},{7,5},{... | collective-permute-start | bytes 393224 | tf_op jit(solution)/shard_map/ppermute | solution.py:15
  14.5 10.3 %collective-permute-start.8 = (bf16[1,1,8,32,256]{4,3,2,1,0:T(8,128)(2,1)S(1)}, bf16[1,1,8,32,256]{4,3,2,1,0:T(8,128)(2,1)S(1)}, u32[]{:S(2)}, u32[]{:S(2)}) collective-permute-start(bf16[1,1,8,32,256]{4,3,2,1,0:T(8,128)(2,1)S(1)} %get-tuple-element.134), channel_id=1, source_target_pairs={{0,2},{2,4},{4,6},{6,8},{8,10},{10,12},{12,14},{1,3},{3,5},{5,7},{... | collective-permute-start | bytes 393224 | tf_op jit(solution)/shard_map/ppermute | solution.py:12
  19.0 6.9 %collective-permute-start.9 = (bf16[1,1,8,32,256]{4,3,2,1,0:T(8,128)(2,1)S(1)}, bf16[1,1,8,32,256]{4,3,2,1,0:T(8,128)(2,1)S(1)}, u32[]{:S(2)}, u32[]{:S(2)}) collective-permute-start(bf16[1,1,8,32,256]{4,3,2,1,0:T(8,128)(2,1)S(1)} %get-tuple-element.133), channel_id=1, source_target_pairs={{2,0},{4,2},{6,4},{8,6},{10,8},{12,10},{14,12},{3,1},{5,3},{7,5},{... | collective-permute-start | bytes 393224 | tf_op jit(solution)/shard_map/ppermute | solution.py:15
  22.1 21.4 %copy-start.25 = (bf16[1,4,8,32,256]{4,3,2,1,0:T(8,128)(2,1)}, bf16[1,4,8,32,256]{4,3,2,1,0:T(8,128)(2,1)S(1)}, u32[]{:S(2)}) copy-start(bf16[1,4,8,32,256]{4,3,2,1,0:T(8,128)(2,1)S(1)} %get-tuple-element.141) | copy-start | bytes 1572868
  22.1 26.4 %copy-start.23 = (bf16[1,4,8,32,256]{4,3,2,1,0:T(8,128)(2,1)}, bf16[1,4,8,32,256]{4,3,2,1,0:T(8,128)(2,1)S(1)}, u32[]{:S(2)}) copy-start(bf16[1,4,8,32,256]{4,3,2,1,0:T(8,128)(2,1)S(1)} %get-tuple-element.139) | copy-start | bytes 1572868
  22.1 8.2 %collective-permute-start.2 = (bf16[1,6,1,32,256]{4,3,2,1,0:T(8,128)(2,1)S(1)}, bf16[1,6,1,32,256]{4,3,2,1,0:T(8,128)(2,1)S(1)}, u32[]{:S(2)}, u32[]{:S(2)}) collective-permute-start(bf16[1,6,1,32,256]{4,3,2,1,0:T(8,128)(2,1)S(1)} %get-tuple-element.124), channel_id=1, source_target_pairs={{0,1},{2,3},{4,5},{6,7},{8,9},{10,11},{12,13},{14,15},{16,17},{18,... | collective-permute-start | bytes 294920 | tf_op jit(solution)/shard_map/ppermute | solution.py:12
  23.4 6.9 %collective-permute-start.3 = (bf16[1,6,1,32,256]{4,3,2,1,0:T(8,128)(2,1)S(1)}, bf16[1,6,1,32,256]{4,3,2,1,0:T(8,128)(2,1)S(1)}, u32[]{:S(2)}, u32[]{:S(2)}) collective-permute-start(bf16[1,6,1,32,256]{4,3,2,1,0:T(8,128)(2,1)S(1)} %get-tuple-element.125), channel_id=1, source_target_pairs={{1,0},{3,2},{5,4},{7,6},{9,8},{11,10},{13,12},{15,14},{17,16},{19,... | collective-permute-start | bytes 294920 | tf_op jit(solution)/shard_map/ppermute | solution.py:15
  27.0 8.5 %collective-permute-start.10 = (bf16[1,6,1,32,256]{4,3,2,1,0:T(8,128)(2,1)S(1)}, bf16[1,6,1,32,256]{4,3,2,1,0:T(8,128)(2,1)S(1)}, u32[]{:S(2)}, u32[]{:S(2)}) collective-permute-start(bf16[1,6,1,32,256]{4,3,2,1,0:T(8,128)(2,1)S(1)} %get-tuple-element.115), channel_id=1, source_target_pairs={{0,1},{2,3},{4,5},{6,7},{8,9},{10,11},{12,13},{14,15},{16,17},{18,... | collective-permute-start | bytes 294920 | tf_op jit(solution)/shard_map/ppermute | solution.py:12
  29.0 6.5 %collective-permute-start.11 = (bf16[1,6,1,32,256]{4,3,2,1,0:T(8,128)(2,1)S(1)}, bf16[1,6,1,32,256]{4,3,2,1,0:T(8,128)(2,1)S(1)}, u32[]{:S(2)}, u32[]{:S(2)}) collective-permute-start(bf16[1,6,1,32,256]{4,3,2,1,0:T(8,128)(2,1)S(1)} %get-tuple-element.116), channel_id=1, source_target_pairs={{1,0},{3,2},{5,4},{7,6},{9,8},{11,10},{13,12},{15,14},{17,16},{19,... | collective-permute-start | bytes 294920 | tf_op jit(solution)/shard_map/ppermute | solution.py:15
  31.0 3.0 copy-start
  36.2 3.4 copy-start.2
  42.5 5.3 %copy-start.29 = (bf16[1,4,8,32,256]{4,3,2,1,0:T(8,128)(2,1)}, bf16[1,4,8,32,256]{4,3,2,1,0:T(8,128)(2,1)S(1)}, u32[]{:S(2)}) copy-start(bf16[1,4,8,32,256]{4,3,2,1,0:T(8,128)(2,1)S(1)} %get-tuple-element.123) | copy-start | bytes 1572868
  45.0 1.0 copy-start.4
  49.4 1.0 copy-start.28
  55.1 1.0 copy-start.27
  56.5 1.2 copy-start.31
  58.7 1.7 copy-start.26
  63.9 1.8 copy-start.30
  65.0 1.8 copy-start.24
  71.9 226.3 %reduce-scatter.11.cloned.1.call-start = ((), (), s32[]{:S(2)}) async-start(), calls=%async_computation.5 | async-start | bytes 7962624 | tf_op jit(solution)/shard_map/reduce_scatter | solution.py:98
  72.0 13.2 %collective-permute-start.4 = (bf16[1,1,8,32,256]{4,3,2,1,0:T(8,128)(2,1)S(1)}, bf16[1,1,8,32,256]{4,3,2,1,0:T(8,128)(2,1)S(1)}, u32[]{:S(2)}, u32[]{:S(2)}) collective-permute-start(bf16[1,1,8,32,256]{4,3,2,1,0:T(8,128)(2,1)S(1)} %get-tuple-element.137), channel_id=1, source_target_pairs={{0,2},{2,4},{4,6},{6,8},{8,10},{10,12},{12,14},{1,3},{3,5},{5,7},{... | collective-permute-start | bytes 393224 | tf_op jit(solution)/shard_map/ppermute | solution.py:12
  76.6 9.0 %collective-permute-start.5 = (bf16[1,1,8,32,256]{4,3,2,1,0:T(8,128)(2,1)S(1)}, bf16[1,1,8,32,256]{4,3,2,1,0:T(8,128)(2,1)S(1)}, u32[]{:S(2)}, u32[]{:S(2)}) collective-permute-start(bf16[1,1,8,32,256]{4,3,2,1,0:T(8,128)(2,1)S(1)} %get-tuple-element.138), channel_id=1, source_target_pairs={{2,0},{4,2},{6,4},{8,6},{10,8},{12,10},{14,12},{3,1},{5,3},{7,5},{... | collective-permute-start | bytes 393224 | tf_op jit(solution)/shard_map/ppermute | solution.py:15
  78.6 26.2 %collective-permute-start.12 = (bf16[1,1,8,32,256]{4,3,2,1,0:T(8,128)(2,1)}, bf16[1,1,8,32,256]{4,3,2,1,0:T(8,128)(2,1)S(1)}, u32[]{:S(2)}, u32[]{:S(2)}) collective-permute-start(bf16[1,1,8,32,256]{4,3,2,1,0:T(8,128)(2,1)} %get-tuple-element.128), channel_id=1, source_target_pairs={{0,2},{2,4},{4,6},{6,8},{8,10},{10,12},{12,14},{1,3},{3,5},{5,7},{... | collective-permute-start | bytes 393224 | tf_op jit(solution)/shard_map/ppermute | solution.py:12
  83.9 20.8 %collective-permute-start.13 = (bf16[1,1,8,32,256]{4,3,2,1,0:T(8,128)(2,1)}, bf16[1,1,8,32,256]{4,3,2,1,0:T(8,128)(2,1)}, u32[]{:S(2)}, u32[]{:S(2)}) collective-permute-start(bf16[1,1,8,32,256]{4,3,2,1,0:T(8,128)(2,1)} %get-tuple-element.129), channel_id=1, source_target_pairs={{2,0},{4,2},{6,4},{8,6},{10,8},{12,10},{14,12},{3,1},{5,3},{7,5},{... | collective-permute-start | bytes 393224 | tf_op jit(solution)/shard_map/ppermute | solution.py:15
  85.6 4.1 collective-permute-start.6
  87.8 3.2 collective-permute-start.7
  89.6 3.6 copy-start.21
  89.6 10.0 %copy-start.19 = (bf16[1,4,8,32,256]{4,3,2,1,0:T(8,128)(2,1)}, bf16[1,4,8,32,256]{4,3,2,1,0:T(8,128)(2,1)S(1)}, u32[]{:S(2)}) copy-start(bf16[1,4,8,32,256]{4,3,2,1,0:T(8,128)(2,1)S(1)} %get-tuple-element.135) | copy-start | bytes 1572868
  91.1 7.5 %copy-start.7 = (bf16[1,6,9,32,256]{4,3,2,1,0:T(8,128)(2,1)}, bf16[1,6,9,32,256]{4,3,2,1,0:T(8,128)(2,1)S(1)}, u32[]{:S(2)}) copy-start(bf16[1,6,9,32,256]{4,3,2,1,0:T(8,128)(2,1)S(1)} %get-tuple-element.118) | copy-start | bytes 2654212
  91.1 9.6 %copy-start.5 = (bf16[1,6,9,32,256]{4,3,2,1,0:T(8,128)(2,1)}, bf16[1,6,9,32,256]{4,3,2,1,0:T(8,128)(2,1)S(1)}, u32[]{:S(2)}) copy-start(bf16[1,6,9,32,256]{4,3,2,1,0:T(8,128)(2,1)S(1)} %get-tuple-element.117) | copy-start | bytes 2654212
  104.7 255.7 %reduce-scatter.13.cloned.1.call-start = ((), (), s32[]{:S(2)}) async-start(), calls=%async_computation.6 | async-start | bytes 974848
  105.6 4.4 %collective-permute-start.14 = (bf16[1,6,1,32,256]{4,3,2,1,0:T(8,128)(2,1)S(1)}, bf16[1,6,1,32,256]{4,3,2,1,0:T(8,128)(2,1)S(1)}, u32[]{:S(2)}, u32[]{:S(2)}) collective-permute-start(bf16[1,6,1,32,256]{4,3,2,1,0:T(8,128)(2,1)S(1)} %get-tuple-element.110), channel_id=1, source_target_pairs={{0,1},{2,3},{4,5},{6,7},{8,9},{10,11},{12,13},{14,15},{16,17},{18,... | collective-permute-start | bytes 294920 | tf_op jit(solution)/shard_map/ppermute | solution.py:12
  107.6 3.2 collective-permute-start.15
  113.6 3.8 copy-start.1
  118.3 4.3 copy-start.3
  126.5 1.2 copy-start.6
  126.5 1.4 copy-start.8
  129.2 1.1 copy-start.22
  192.2 231.1 %reduce-scatter.15.cloned.1.call-start = ((), (), s32[]{:S(2)}) async-start(), calls=%async_computation.7 | async-start | bytes 974848
  192.4 3.7 copy-start.15
  192.4 5.0 %copy-start.18 = (bf16[1,4,8,32,256]{4,3,2,1,0:T(8,128)(2,1)S(1)}, bf16[1,4,8,32,256]{4,3,2,1,0:T(8,128)(2,1)}, u32[]{:S(2)}) copy-start(bf16[1,4,8,32,256]{4,3,2,1,0:T(8,128)(2,1)} %get-tuple-element.97) | copy-start | bytes 1572868
  194.7 4.0 copy-start.14
  196.2 3.8 copy-start.13
  197.4 3.7 copy-start.17
  201.1 101.0 %copy-start.10 = (bf16[1,4,8,32,256]{4,3,2,1,0:T(8,128)(2,1)S(1)}, bf16[1,4,8,32,256]{4,3,2,1,0:T(8,128)(2,1)}, u32[]{:S(2)}) copy-start(bf16[1,4,8,32,256]{4,3,2,1,0:T(8,128)(2,1)} %get-tuple-element.50) | copy-start | bytes 1572868
  300.8 4.1 copy-start.20
  303.4 2.7 copy-start.12
  304.8 2.6 copy-start.16
  306.1 2.5 copy-start.11
Sparse Core Ops, SparseCore 0:
  72.1 117.5 reduce-scatter.8
  194.2 103.9 reduce-scatter.10
  301.2 59.1 reduce-scatter.12
  363.3 59.8 reduce-scatter.14
where the time goes:
time: 436 us; the launch traced here: 430 us
  waiting for transfers between devices  265 us (61%)
  matrix products  70.3 us (16%)
  starting transfers between devices  37 us (8%)
  local copies, waits for them, and re-layouts  25 us (6%)
  other arithmetic  16.8 us (4%)
  between operations  15.8 us (4%)
    unnamed x6, waiting for transfers between devices  113 us
    reduce_scatter x1, waiting for transfers between devices, body(): lax.psum_scatter(second_terms, 'dp', scatter_dimension=0, tiled=True)  95.8 us
    reduce_scatter x1, waiting for transfers between devices, body(): lax.psum_scatter(first_terms, 'dp', scatter_dimension=0, tiled=True)  53 us
    dot_general x54, matrix products, conv(): term = jnp.dot(rows, block, preferred_element_type=jnp.float32)  29.9 us
    ppermute x8, starting transfers between devices, with_halo(): lax.ppermute(lax.slice_in_dim(block, block.shape[dim] - width, None, axis...  25.8 us
    dot_general x54, matrix products, conv(): lax.dot_general(rows, block, (((1,), (1,)), ((), ())), preferred_element_...  21.4 us
    dot_general x54, matrix products, weight_terms(): lax.dot_general(rows, grads, (((0,), (0,)), ((), ())), preferred_element_...  18.9 us
    slice x6, local copies, waits for them, and re-layouts, window(): padded[:, start_x:start_x + size_x - 2, start_y:start_y + size_y - 2, sta...  15.8 us
  transfers between devices with their start and end apart: 20, of which 8 were waited for; matrix products, arithmetic and copies ran while one was open for 17% of the time, Pallas kernels for 0%

commit v1 on v0

v1 whole, which is shorter than its diff:
```python
import functools

import jax
import jax.numpy as jnp
from jax import lax
from jax.experimental import pallas as pl
from jax.experimental.pallas import tpu as pltpu
from jax.sharding import PartitionSpec as P

BF = jnp.bfloat16
F32 = jnp.float32
ALL = ("dp", "px", "py")
X, Y, Z = 0, 1, 2
ORDER = ((X, Y, Z), (Y, Z, X))
LANES = 896


def device(x, y, z, core):
    x, y, z = x % 4, y % 4, z % 4
    return (y * 2 + z // 2) * 16 + (x * 2 + z % 2) * 2 + core


def hop_pairs(stage, distance):
    pairs = []
    for core in range(2):
        step = [0, 0, 0]
        step[ORDER[core][stage]] = distance
        for x in range(4):
            for y in range(4):
                for z in range(4):
                    pairs.append(
                        (
                            device(x, y, z, core),
                            device(x + step[0], y + step[1], z + step[2], core),
                        )
                    )
    return pairs


def shifted(block):
    wide = block.astype(F32)
    place = lax.broadcasted_iota(jnp.int32, wide.shape, 1)
    low = jnp.where(place == 0, 0.0, pltpu.roll(wide, 1, 1)).astype(BF)
    high = jnp.where(place == 31, 0.0, pltpu.roll(wide, 31, 1)).astype(BF)
    return low, high


def put(stack, row, start, block, flip):
    low, high = shifted(block)
    if flip:
        low, high = high, low
    rows = pl.ds(start, block.shape[0])
    stack[row, rows, :, 0:256] = low
    stack[row, rows, :, 256:512] = block
    stack[row, rows, :, 512:768] = high


def put_grid(stack, own, low, high, which, first, flip):
    put(stack, 0, first, low[which], flip)
    put(stack, 5, first, high[which], flip)

    def step(i, _):
        put(stack, i + 1, first, own[i], flip)
        return 0

    lax.fori_loop(0, 4, step, 0)


def put_face(stack, core, other, place_first, place_second, flip):
    place = jnp.where(core == 0, place_first, place_second)
    row = jnp.where(core == 0, 9, 0)
    zeros = jnp.zeros((1, 32, 768), BF)

    def step(i, _):
        put(stack, i, row, other[i, pl.ds(place, 1)], flip)
        stack[i, pl.ds(9 - row, 1)] = zeros
        return 0

    lax.fori_loop(0, 6, step, 0)


def conv_into(total, stack, weight):
    for k in range(9):
        a, b = k // 3, k % 3
        rows = stack[a : a + 4, b : b + 8].reshape(1024, 768)
        term = jnp.dot(rows, weight[k * 768 : (k + 1) * 768], preferred_element_type=F32)
        if k == 0:
            total[...] = term
        else:
            total[...] += term


def conv_back_into(total, stack, weight):
    for k in range(9):
        a, b = k // 3, k % 3
        term = None
        for c in range(3):
            rows = stack[2 - a : 6 - a, 2 - b : 10 - b, :, c * 256 : (c + 1) * 256]
            block = weight[(k * 3 + c) * 256 : (k * 3 + c + 1) * 256]
            part = lax.dot_general(
                rows.reshape(1024, 256),
                block,
                (((1,), (1,)), ((), ())),
                preferred_element_type=F32,
            )
            term = part if term is None else term + part
        if k == 0:
            total[...] = term
        else:
            total[...] += term


def gelu_and_slope(v):
    scale = 0.7978845608028654
    square = v * v
    t = jnp.tanh(scale * (v + 0.044715 * (square * v)))
    half = 0.5 * (1.0 + t)
    slope = half + 0.5 * v * (1.0 - t * t) * (scale * (1.0 + 3.0 * 0.044715 * square))
    return v * half, slope


def first_kernel(
    place, cot, field, low, high, other, first_w, second_w, hidden, pre_grad, stack, back, pre, grad
):
    core = place[0]
    put_grid(stack, field, low, high, 1, 1, False)
    put_face(stack, core, other, 0, 8, False)
    conv_into(pre, stack, first_w)
    put_grid(back, cot, low, high, 0, 1, True)
    put_face(back, core, other, 8, 7, True)
    conv_back_into(grad, back, second_w)

    def step(i, _):
        rows = pl.ds(pl.multiple_of(i * 256, 256), 256)
        value, slope = gelu_and_slope(pre[rows])
        hidden[i] = value.astype(BF).reshape(8, 32, 256)
        pre_grad[i] = (grad[rows] * slope).astype(BF).reshape(8, 32, 256)
        return 0

    lax.fori_loop(0, 4, step, 0)


def last_kernel(
    place, hid, pre_grad, low, high, other, field, cot, first_w, second_w, out, field_grad,
    stack, back, total, grad,
):
    core = place[0]
    put_grid(stack, hid, low, high, 0, 1, False)
    put_face(stack, core, other, 8, 7, False)
    conv_into(total, stack, second_w)
    put_grid(back, pre_grad, low, high, 1, 1, True)
    put_face(back, core, other, 0, 8, True)
    conv_back_into(grad, back, first_w)

    def step(i, _):
        rows = pl.ds(pl.multiple_of(i * 256, 256), 256)
        one = field[i].astype(F32).reshape(256, 256) + total[rows]
        out[i] = one.astype(BF).reshape(8, 32, 256)
        two = cot[i].astype(F32).reshape(256, 256) + grad[rows]
        field_grad[i] = two.astype(BF).reshape(8, 32, 256)
        return 0

    lax.fori_loop(0, 4, step, 0)


def weight_kernel(
    place, cot, field, low1, high1, other1, hid, pre_grad, low2, high2, other2,
    own, send1, send2, send3, stack, turned, flat, tiles,
):
    core = place[0]

    def fill(value, low, high, which, far, near_grad, far_grad, half):
        put_grid(stack, value, low, high, which, 1 + 8 * half, False)

        def step(i, _):
            put(stack, i, 1 + 8 * (1 - half), far[i, 0:8], False)
            edge = jnp.zeros((1, 32, 768), BF)
            stack[i, 0:1] = edge
            stack[i, 17:18] = edge
            return 0

        lax.fori_loop(0, 6, step, 0)
        for i in range(4):
            at = i * 512 + 256 * half
            turned[:, at : at + 256] = near_grad[i].reshape(256, 256).T
            at = i * 512 + 256 * (1 - half)
            turned[:, at : at + 256] = far_grad[i + 1, 0:8].reshape(256, 256).T

    @pl.when(core == 0)
    def _():
        fill(field, low1, high1, 1, other1, pre_grad, other2, 0)

    @pl.when(core == 1)
    def _():
        fill(hid, low2, high2, 0, other2, cot, other1, 1)

    flat[:, 6912:7040] = jnp.zeros((256, 128), BF)

    def block(k, _):
        a, b = k // 3, k % 3
        rows = stack[pl.ds(a, 4), pl.ds(b, 16)].reshape(2048, 768)
        term = jnp.dot(turned[...], rows, preferred_element_type=F32)
        flat[:, pl.ds(pl.multiple_of(k * 768, 768), 768)] = (term * 0.125).astype(BF)
        return 0

    lax.fori_loop(0, 9, block, 0)
    for k in range(8):
        tiles[k] = flat[:, k * 864 : k * 864 + LANES]
    x, y, z = place[1], place[2], place[3]
    zero = core == 0
    for first, ref in enumerate((own, send1, send2, send3)):

        def pick(i, _):
            second, third = i // 4, i % 4
            to_x = lax.rem(x + jnp.where(zero, first, third), 4)
            to_y = lax.rem(y + jnp.where(zero, second, first), 4)
            to_z = lax.rem(z + jnp.where(zero, third, second), 4)
            to_dp = to_y * 2 + to_z // 2
            to_px = to_x * 2 + lax.rem(to_z, 2)
            ref[i] = tiles[to_dp, pl.ds(pl.multiple_of(to_px * 32, 32), 32), :]
            return 0

        lax.fori_loop(0, 16, pick, 0)


def call(kernel, name, flops, args, outs, scratch):
    whole = pl.BlockSpec(memory_space=pltpu.VMEM)
    return pl.pallas_call(
        kernel,
        name=name,
        out_shape=outs,
        in_specs=[pl.BlockSpec(memory_space=pltpu.SMEM)] + [whole] * (len(args) - 1),
        out_specs=[whole] * len(outs),
        scratch_shapes=scratch,
        compiler_params=pltpu.CompilerParams(vmem_limit_bytes=56 * 2**20),
        cost_estimate=pl.CostEstimate(
            flops=flops, bytes_accessed=8 * 2**20, transcendentals=0
        ),
    )(*args)


def exchange(first, second, core):
    count = lax.axis_size("px")
    forward = [(i, i + 1) for i in range(count - 1)]
    backward = [(i + 1, i) for i in range(count - 1)]
    low = lax.ppermute(jnp.stack([first[3], second[3]]), "px", forward)
    high = lax.ppermute(jnp.stack([first[0], second[0]]), "px", backward)
    first = jnp.concatenate([low[0:1], first, high[0:1]], axis=0)
    second = jnp.concatenate([low[1:2], second, high[1:2]], axis=0)
    full = jnp.where(core == 0, first, second)
    face = jnp.where(core == 0, second[:, 7:8], first[:, 0:1])
    other = lax.ppermute(
        jnp.concatenate([full, face], axis=1), "py", [(0, 1), (1, 0)]
    )
    return low, high, other


def hop(parts, stage):
    return [
        lax.ppermute(part, ALL, hop_pairs(stage, distance))
        for part, distance in zip(parts, (1, 3, 2))
    ]


def reduce_tiles(own, plus, two, minus, core):
    got = hop((plus, minus, two), 0)
    total = own.astype(F32)
    for part in got:
        total = total + part.astype(F32)
    got = hop([total[4 * d : 4 * d + 4].astype(BF) for d in (1, 3, 2)], 1)
    total = total[0:4]
    for part in got:
        total = total + part.astype(F32)
    got = hop([total[d] for d in (1, 3, 2)], 2)
    total = total[0] + got[0] + got[1] + got[2]
    keep = jnp.where(core == 0, total[:16], total[16:])
    give = jnp.where(core == 0, total[16:], total[:16])
    other = lax.ppermute(give, "py", [(0, 1), (1, 0)])
    first = jnp.where(core == 0, keep, other)[:, :864]
    second = jnp.where(core == 0, other, keep)[:, :864]
    return first.T, second.T


def body(fields, cotangent, first_weight, second_weight):
    shape = jax.ShapeDtypeStruct
    core = lax.axis_index("py")
    dp, px = lax.axis_index("dp"), lax.axis_index("px")
    place = jnp.stack([core, px // 2, dp // 2, (dp % 2) * 2 + px % 2]).astype(jnp.int32)
    field, cot = fields[0], cotangent[0]
    grid = shape((4, 8, 32, 256), BF)
    conv_scratch = [
        pltpu.VMEM((6, 10, 32, 768), BF),
        pltpu.VMEM((6, 10, 32, 768), BF),
        pltpu.VMEM((1024, 256), F32),
        pltpu.VMEM((1024, 256), F32),
    ]
    low1, high1, other1 = exchange(cot, field, core)
    hidden, pre_grad = call(
        first_kernel,
        "hidden",
        2 * 2 * 1024 * 6912 * 256,
        (place, cot, field, low1, high1, other1, first_weight, second_weight),
        [grid, grid],
        conv_scratch,
    )
    low2, high2, other2 = exchange(hidden, pre_grad, core)
    own, send1, send2, send3 = call(
        weight_kernel,
        "weight_terms",
        2 * 2 * 1024 * 6912 * 256,
        (place, cot, field, low1, high1, other1, hidden, pre_grad, low2, high2, other2),
        [shape((16, 32, LANES), BF)] * 4,
        [
            pltpu.VMEM((6, 18, 32, 768), BF),
            pltpu.VMEM((256, 2048), BF),
            pltpu.VMEM((256, 7040), BF),
            pltpu.VMEM((8, 256, LANES), BF),
        ],
    )
    output, field_grad = call(
        last_kernel,
        "outputs",
        2 * 2 * 1024 * 6912 * 256,
        (place, hidden, pre_grad, low2, high2, other2, field, cot, first_weight, second_weight),
        [grid, grid],
        conv_scratch,
    )
    first_grad, second_grad = reduce_tiles(own, send1, send2, send3, core)
    return output[None], field_grad[None], first_grad, second_grad


def solution(mesh):
    placed = P("dp", "px", "py", None, None)
    return jax.shard_map(
        body,
        mesh=mesh,
        in_specs=(placed, placed, P(), P()),
        out_specs=(placed, placed, P("dp", ("px", "py")), P("dp", ("px", "py"))),
        check_vma=False,
    )
```

time: 436 us -> 157 us (0.36)
  waiting for transfers between devices: 265 us -> 56.2 us
  matrix products: 70.3 us -> 0 us
  Pallas kernels: 0 us -> 59.2 us
  local copies, waits for them, and re-layouts: 25 us -> 6.19 us
  between operations: 15.8 us -> 0.91 us
  other arithmetic: 16.8 us -> 3.84 us
  starting transfers between devices: 37 us -> 28.5 us
    reduce_scatter x2 -> x0, waiting for transfers between devices: 149 us -> none  [the longest x1 95.8 us: body(): lax.psum_scatter(second_terms, 'dp', scatter_dimension=0, tiled=True)]
    unnamed x6 -> x0, waiting for transfers between devices: 113 us -> none
    dot_general x162 -> x0, matrix products: 70.3 us -> none  [the longest x54 29.9 us: conv(): term = jnp.dot(rows, block, preferred_element_type=jnp.float32)]
    pallas_call x0 -> x3, Pallas kernels: none -> 59.2 us  [call(): pl.pallas_call(kernel, name=name, out_shape=outs, in_specs=[pl.BlockSpec(...]
    ppermute x16, waiting for transfers between devices: 3.62 us -> 56.2 us  [the longest x9 31.7 us: hop(): lax.ppermute(part, ALL, hop_pairs(stage, distance))]
    slice x12 -> x8, local copies, waits for them, and re-layouts: 18.6 us -> 3.41 us  [the longest x3 3.28 us: exchange(): high = lax.ppermute(jnp.stack([first[0], second[0]]), 'px', backward)]
    concatenate x12 -> x2, other arithmetic: 9.32 us -> 0.17 us  [exchange(): jnp.concatenate([full, face], axis=1)]
    ppermute x16, starting transfers between devices: 36.6 us -> 28.5 us  [the longest x9 16 us: hop(): lax.ppermute(part, ALL, hop_pairs(stage, distance))]
  transfers between devices with their start and end apart: 20 -> 16, of which waited for: 8 -> 15; matrix products, arithmetic and copies ran while one was open for 17% -> 0% of each run, Pallas kernels for 0% -> 14%
where the time goes in v1:
time: 157 us; the launch traced here: 155 us
  Pallas kernels  59.2 us (38%)
  waiting for transfers between devices  56.2 us (36%)
  starting transfers between devices  28.5 us (18%)
  local copies, waits for them, and re-layouts  6.19 us (4%)
  other arithmetic  3.84 us (2%)
    pallas_call x3, Pallas kernels, call(): pl.pallas_call(kernel, name=name, out_shape=outs, in_specs=[pl.BlockSpec(...  59.2 us
    ppermute x9, waiting for transfers between devices, hop(): lax.ppermute(part, ALL, hop_pairs(stage, distance))  31.7 us
    ppermute x9, starting transfers between devices, hop(): lax.ppermute(part, ALL, hop_pairs(stage, distance))  16 us
    ppermute x2, waiting for transfers between devices, exchange(): low = lax.ppermute(jnp.stack([first[3], second[3]]), 'px', forward)  11.5 us
    ppermute x2, starting transfers between devices, exchange(): low = lax.ppermute(jnp.stack([first[3], second[3]]), 'px', forward)  9.59 us
    ppermute x2, waiting for transfers between devices, exchange(): high = lax.ppermute(jnp.stack([first[0], second[0]]), 'px', backward)  8.91 us
    ppermute x2, waiting for transfers between devices, exchange(): lax.ppermute(jnp.concatenate([full, face], axis=1), 'py', [(0, 1), (1, 0)])  4.11 us
    slice x3, local copies, waits for them, and re-layouts, exchange(): high = lax.ppermute(jnp.stack([first[0], second[0]]), 'px', backward)  3.28 us
  transfers between devices with their start and end apart: 16, of which 15 were waited for; matrix products, arithmetic and copies ran while one was open for 0% of the time, Pallas kernels for 14%

profile of v1, /device:TPU:0, one launch (start us, length us, event | category | flops | bytes accessed | tf_op | source)
XLA Modules:
  0.0 154.9 jit_solution(15560591543341440048)
XLA Ops:
  0.6 0.0 copy-start.2
  0.6 0.0 copy-start.3
  0.7 1.2 slice_bitcast_fusion
  1.9 1.3 collective-permute-start.1
  3.2 4.6 %collective-permute-start = (bf16[2,8,32,256]{3,2,1,0:T(8,128)(2,1)S(1)}, bf16[2,8,32,256]{3,2,1,0:T(8,128)(2,1)S(1)}, u32[]{:S(2)}, u32[]{:S(2)}) collective-permute-start(bf16[2,8,32,256]{3,2,1,0:T(8,128)(2,1)S(1)} %pad_maximum_fusion.6), channel_id=1, source_target_pairs={{0,2},{2,4},{4,6},{6,8},{8,10},{10,12},{12,14},{1,3},{3,5},{5,7},{... | collective-permute-start | bytes 786440 | tf_op jit(solution)/shard_map/ppermute | solution.py:246
  7.8 4.3 %collective-permute-done.1.high.high1 = bf16[2,8,32,256]{3,2,1,0:T(8,128)(2,1)S(1)} collective-permute-done((bf16[2,8,32,256]{3,2,1,0:T(8,128)(2,1)S(1)}, bf16[2,8,32,256]{3,2,1,0:T(8,128)(2,1)S(1)}, u32[]{:S(2)}, u32[]{:S(2)}) %collective-permute-start.1) | collective-permute-done | bytes 262176 | tf_op jit(solution)/shard_map/ppermute | solution.py:247
  12.1 0.0 copy-start.4
  12.1 5.7 %collective-permute-done.low.low1 = bf16[2,8,32,256]{3,2,1,0:T(8,128)(2,1)S(1)} collective-permute-done((bf16[2,8,32,256]{3,2,1,0:T(8,128)(2,1)S(1)}, bf16[2,8,32,256]{3,2,1,0:T(8,128)(2,1)S(1)}, u32[]{:S(2)}, u32[]{:S(2)}) %collective-permute-start) | collective-permute-done | bytes 262176 | tf_op jit(solution)/shard_map/ppermute | solution.py:246
  17.9 0.0 copy-start.5
  17.9 0.0 copy-done.2
  17.9 0.0 copy-done.3
  17.9 0.2 broadcast_select_fusion.1
  18.1 0.0 copy-done.4
  18.2 0.4 copy-done.5
  18.6 0.1 pad_maximum_fusion
  18.7 0.1 collective-permute-start.2
  18.8 0.7 pad_add_fusion.place
  19.5 1.7 %collective-permute-done.2.other.other1 = bf16[6,9,32,256]{3,2,1,0:T(8,128)(2,1)S(1)} collective-permute-done((bf16[6,9,32,256]{3,2,1,0:T(8,128)(2,1)S(1)}, bf16[6,9,32,256]{3,2,1,0:T(8,128)(2,1)S(1)}, u32[]{:S(2)}, u32[]{:S(2)}) %collective-permute-start.2) | collective-permute-done | bytes 884768 | tf_op jit(solution)/shard_map/ppermute | solution.py:252
  21.2 0.0 copy-start.8
  21.2 0.9 copy-done.8
  22.1 21.2 %hidden.1 = (bf16[4,8,32,256]{3,2,1,0:T(8,128)(2,1)}, bf16[4,8,32,256]{3,2,1,0:T(8,128)(2,1)}) custom-call(s32[4]{0:T(128)} %pad_add_fusion.place, bf16[4,8,32,256]{3,2,1,0:T(8,128)(2,1)} %bitcast.34, bf16[4,8,32,256]{3,2,1,0:T(8,128)(2,1)} %bitcast.38, bf16[2,8,32,256]{3,2,1,0:T(8,128)(2,1)} %copy-done.5, bf16[2,8,32,256]{3,2,1,0:T(8,128)(2,1)} %copy-done.4, ...), custom_call_target="tpu_custom_call" | custom-call | flops 7247757312 | bytes 8388608 | tf_op jit(solution)/shard_map/hidden/pallas_call | solution.py:228
  43.4 0.0 copy-start
  43.4 0.0 copy-start.1
  43.4 1.1 fusion.8
  44.5 1.0 fusion.7
  45.5 1.3 collective-permute-start.4
  46.8 5.0 %collective-permute-start.3 = (bf16[2,8,32,256]{3,2,1,0:T(8,128)(2,1)S(1)}, bf16[2,8,32,256]{3,2,1,0:T(8,128)(2,1)S(1)}, u32[]{:S(2)}, u32[]{:S(2)}) collective-permute-start(bf16[2,8,32,256]{3,2,1,0:T(8,128)(2,1)S(1)} %pad_maximum_fusion.8), channel_id=1, source_target_pairs={{0,2},{2,4},{4,6},{6,8},{8,10},{10,12},{12,14},{1,3},{3,5},{5,7},{... | collective-permute-start | bytes 786440 | tf_op jit(solution)/shard_map/ppermute | solution.py:246
  51.9 4.6 %collective-permute-done.4.high.high2 = bf16[2,8,32,256]{3,2,1,0:T(8,128)(2,1)S(1)} collective-permute-done((bf16[2,8,32,256]{3,2,1,0:T(8,128)(2,1)S(1)}, bf16[2,8,32,256]{3,2,1,0:T(8,128)(2,1)S(1)}, u32[]{:S(2)}, u32[]{:S(2)}) %collective-permute-start.4) | collective-permute-done | bytes 262176 | tf_op jit(solution)/shard_map/ppermute | solution.py:247
  56.5 5.7 %collective-permute-done.3.low.low2 = bf16[2,8,32,256]{3,2,1,0:T(8,128)(2,1)S(1)} collective-permute-done((bf16[2,8,32,256]{3,2,1,0:T(8,128)(2,1)S(1)}, bf16[2,8,32,256]{3,2,1,0:T(8,128)(2,1)S(1)}, u32[]{:S(2)}, u32[]{:S(2)}) %collective-permute-start.3) | collective-permute-done | bytes 262176 | tf_op jit(solution)/shard_map/ppermute | solution.py:246
  62.3 0.0 copy-done
  62.3 0.0 copy-done.1
  62.3 0.2 broadcast_select_fusion
  62.5 0.0 copy-done.6
  62.5 0.4 copy-done.7
  63.0 0.1 pad_maximum_fusion.1
  63.1 0.1 collective-permute-start.5
  63.2 2.4 %collective-permute-done.5.other.other2 = bf16[6,9,32,256]{3,2,1,0:T(8,128)(2,1)S(1)} collective-permute-done((bf16[6,9,32,256]{3,2,1,0:T(8,128)(2,1)S(1)}, bf16[6,9,32,256]{3,2,1,0:T(8,128)(2,1)S(1)}, u32[]{:S(2)}, u32[]{:S(2)}) %collective-permute-start.5) | collective-permute-done | bytes 884768 | tf_op jit(solution)/shard_map/ppermute | solution.py:252
  65.6 0.9 copy-done.9
  66.5 16.9 %weight_terms.1 = (bf16[16,32,896]{2,1,0:T(8,128)(2,1)}, bf16[16,32,896]{2,1,0:T(8,128)(2,1)}, bf16[16,32,896]{2,1,0:T(8,128)(2,1)}, bf16[16,32,896]{2,1,0:T(8,128)(2,1)}) custom-call(s32[4]{0:T(128)} %pad_add_fusion.place, bf16[4,8,32,256]{3,2,1,0:T(8,128)(2,1)} %bitcast.35, bf16[4,8,32,256]{3,2,1,0:T(8,128)(2,1)} %bitcast.39, ...), custom_call_target="tpu_custom_call" | custom-call | flops 7247757312 | bytes 8388608 | tf_op jit(solution)/shard_map/weight_terms/pallas_call | solution.py:228
  83.4 3.0 %collective-permute-start.8 = (bf16[16,32,896]{2,1,0:T(8,128)(2,1)}, bf16[16,32,896]{2,1,0:T(8,128)(2,1)S(1)}, u32[]{:S(2)}, u32[]{:S(2)}) collective-permute-start(bf16[16,32,896]{2,1,0:T(8,128)(2,1)} %get-tuple-element.19), channel_id=1, source_target_pairs={{0,8},{2,10},{16,24},{18,26},{32,40},{34,42},{48,56},{50,58},{64,7... | collective-permute-start | bytes 2752520 | tf_op jit(solution)/shard_map/ppermute | solution.py:260
  86.5 1.1 collective-permute-start.7
  87.6 0.9 collective-permute-start.6
  88.5 10.2 %collective-permute-done.8 = bf16[16,32,896]{2,1,0:T(8,128)(2,1)S(1)} collective-permute-done((bf16[16,32,896]{2,1,0:T(8,128)(2,1)}, bf16[16,32,896]{2,1,0:T(8,128)(2,1)S(1)}, u32[]{:S(2)}, u32[]{:S(2)}) %collective-permute-start.8) | collective-permute-done | bytes 917536 | tf_op jit(solution)/shard_map/ppermute | solution.py:260
  98.6 8.7 %collective-permute-done.7 = bf16[16,32,896]{2,1,0:T(8,128)(2,1)S(1)} collective-permute-done((bf16[16,32,896]{2,1,0:T(8,128)(2,1)}, bf16[16,32,896]{2,1,0:T(8,128)(2,1)S(1)}, u32[]{:S(2)}, u32[]{:S(2)}) %collective-permute-start.7) | collective-permute-done | bytes 917536 | tf_op jit(solution)/shard_map/ppermute | solution.py:260
  107.4 1.0 collective-permute-done.6
  108.4 1.6 %fusion.5 = (bf16[16,32,896]{2,1,0:T(8,128)(2,1)S(1)}, f32[16,32,896]{2,1,0:T(8,128)S(1)}) fusion(bf16[16,32,896]{2,1,0:T(8,128)(2,1)S(1)} %collective-permute-done.8, bf16[16,32,896]{2,1,0:T(8,128)(2,1)S(1)} %collective-permute-done.7, bf16[16,32,896]{2,1,0:T(8,128)(2,1)S(1)} %collective-permute-done.6, bf16[16,32,896]{2,1,0:T(8,128)(2,1)} %get-tuple-element.16), kind=kLoop, calls=%fused_computation.34 | loop fusion | flops 3670016 | bytes 6422528 | tf_op jit(solution)/shard_map/convert.2
  110.0 0.1 fusion.6
  110.1 3.3 %collective-permute-start.11 = (bf16[4,32,896]{2,1,0:T(8,128)(2,1)S(1)}, bf16[4,32,896]{2,1,0:T(8,128)(2,1)S(1)}, u32[]{:S(2)}, u32[]{:S(2)}) collective-permute-start(bf16[4,32,896]{2,1,0:T(8,128)(2,1)S(1)} %get-tuple-element.23), channel_id=1, source_target_pairs={{0,64},{2,66},{16,80},{18,82},{32,96},{34,98},{48,112},{50,114},{6... | collective-permute-start | bytes 688136 | tf_op jit(solution)/shard_map/ppermute | solution.py:260
  113.4 1.1 collective-permute-start.10
  114.4 1.0 collective-permute-start.9
  115.4 2.3 %collective-permute-done.11 = bf16[4,32,896]{2,1,0:T(8,128)(2,1)S(1)} collective-permute-done((bf16[4,32,896]{2,1,0:T(8,128)(2,1)S(1)}, bf16[4,32,896]{2,1,0:T(8,128)(2,1)S(1)}, u32[]{:S(2)}, u32[]{:S(2)}) %collective-permute-start.11) | collective-permute-done | bytes 229408 | tf_op jit(solution)/shard_map/ppermute | solution.py:260
  117.7 2.8 %collective-permute-done.10 = bf16[4,32,896]{2,1,0:T(8,128)(2,1)S(1)} collective-permute-done((bf16[4,32,896]{2,1,0:T(8,128)(2,1)S(1)}, bf16[4,32,896]{2,1,0:T(8,128)(2,1)S(1)}, u32[]{:S(2)}, u32[]{:S(2)}) %collective-permute-start.10) | collective-permute-done | bytes 229408 | tf_op jit(solution)/shard_map/ppermute | solution.py:260
  120.5 1.2 collective-permute-done.9
  121.7 0.1 fusion.1
  121.8 3.7 %collective-permute-start.14 = (f32[32,896]{1,0:T(8,128)S(1)}, f32[32,896]{1,0:T(8,128)S(1)}, u32[]{:S(2)}, u32[]{:S(2)}) collective-permute-start(f32[32,896]{1,0:T(8,128)S(1)} %get-tuple-element.40), channel_id=1, source_target_pairs={{0,16},{2,18},{16,0},{18,2},{32,48},{34,50},{48,32},{50,34},{64,80... | collective-permute-start | bytes 344072 | tf_op jit(solution)/shard_map/ppermute | solution.py:260
  125.5 1.6 %collective-permute-start.13 = (f32[32,896]{1,0:T(8,128)S(1)}, f32[32,896]{1,0:T(8,128)S(1)}, u32[]{:S(2)}, u32[]{:S(2)}) collective-permute-start(f32[32,896]{1,0:T(8,128)S(1)} %get-tuple-element.41), channel_id=1, source_target_pairs={{0,18},{2,0},{16,2},{18,16},{32,50},{34,32},{48,34},{50,48},{64,82... | collective-permute-start | bytes 344072 | tf_op jit(solution)/shard_map/ppermute | solution.py:260
  127.0 0.5 collective-permute-start.12
  127.5 0.7 collective-permute-done.14
  128.2 3.1 %collective-permute-done.13 = f32[32,896]{1,0:T(8,128)S(1)} collective-permute-done((f32[32,896]{1,0:T(8,128)S(1)}, f32[32,896]{1,0:T(8,128)S(1)}, u32[]{:S(2)}, u32[]{:S(2)}) %collective-permute-start.13) | collective-permute-done | bytes 114720 | tf_op jit(solution)/shard_map/ppermute | solution.py:260
  131.3 1.7 %collective-permute-done.12 = f32[32,896]{1,0:T(8,128)S(1)} collective-permute-done((f32[32,896]{1,0:T(8,128)S(1)}, f32[32,896]{1,0:T(8,128)S(1)}, u32[]{:S(2)}, u32[]{:S(2)}) %collective-permute-start.12) | collective-permute-done | bytes 114720 | tf_op jit(solution)/shard_map/ppermute | solution.py:260
  133.1 0.1 collective-permute-start.15
  133.2 21.1 %outputs.1 = (bf16[4,8,32,256]{3,2,1,0:T(8,128)(2,1)}, bf16[4,8,32,256]{3,2,1,0:T(8,128)(2,1)}) custom-call(s32[4]{0:T(128)} %pad_add_fusion.place, bf16[4,8,32,256]{3,2,1,0:T(8,128)(2,1)} %get-tuple-element.12.hid, bf16[4,8,32,256]{3,2,1,0:T(8,128)(2,1)} %get-tuple-element.13.pre_grad, bf16[2,8,32,256]{3,2,1,0:T(8,128)(2,1)} %copy-done.7, ...), custom_call_target="tpu_custom_call" | custom-call | flops 7247757312 | bytes 8388608 | tf_op jit(solution)/shard_map/outputs/pallas_call | solution.py:228
  154.3 0.0 collective-permute-done.15
  154.3 0.7 select_bitcast_fusion
  (16 shorter events, 0.3 us)
Async XLA Ops:
  0.6 17.3 %copy-start.2 = (bf16[1,4,8,32,256]{4,3,2,1,0:T(8,128)(2,1)S(1)}, bf16[1,4,8,32,256]{4,3,2,1,0:T(8,128)(2,1)}, u32[]{:S(2)}) copy-start(bf16[1,4,8,32,256]{4,3,2,1,0:T(8,128)(2,1)} %param.5) | copy-start | bytes 1572868
  0.6 17.3 %copy-start.3 = (bf16[1,4,8,32,256]{4,3,2,1,0:T(8,128)(2,1)S(1)}, bf16[1,4,8,32,256]{4,3,2,1,0:T(8,128)(2,1)}, u32[]{:S(2)}) copy-start(bf16[1,4,8,32,256]{4,3,2,1,0:T(8,128)(2,1)} %param.4) | copy-start | bytes 1572868
  1.9 10.2 %collective-permute-start.1 = (bf16[2,8,32,256]{3,2,1,0:T(8,128)(2,1)S(1)}, bf16[2,8,32,256]{3,2,1,0:T(8,128)(2,1)S(1)}, u32[]{:S(2)}, u32[]{:S(2)}) collective-permute-start(bf16[2,8,32,256]{3,2,1,0:T(8,128)(2,1)S(1)} %pad_maximum_fusion.7), channel_id=1, source_target_pairs={{2,0},{4,2},{6,4},{8,6},{10,8},{12,10},{14,12},{3,1},{5,3},{7,5},{... | collective-permute-start | bytes 786440 | tf_op jit(solution)/shard_map/ppermute | solution.py:247
  3.2 14.6 %collective-permute-start = (bf16[2,8,32,256]{3,2,1,0:T(8,128)(2,1)S(1)}, bf16[2,8,32,256]{3,2,1,0:T(8,128)(2,1)S(1)}, u32[]{:S(2)}, u32[]{:S(2)}) collective-permute-start(bf16[2,8,32,256]{3,2,1,0:T(8,128)(2,1)S(1)} %pad_maximum_fusion.6), channel_id=1, source_target_pairs={{0,2},{2,4},{4,6},{6,8},{8,10},{10,12},{12,14},{1,3},{3,5},{5,7},{... | collective-permute-start | bytes 786440 | tf_op jit(solution)/shard_map/ppermute | solution.py:246
  12.1 6.0 %copy-start.4 = (bf16[2,8,32,256]{3,2,1,0:T(8,128)(2,1)}, bf16[2,8,32,256]{3,2,1,0:T(8,128)(2,1)S(1)}, u32[]{:S(2)}) copy-start(bf16[2,8,32,256]{3,2,1,0:T(8,128)(2,1)S(1)} %collective-permute-done.1.high.high1) | copy-start | bytes 786436
  17.9 0.7 copy-start.5
  18.7 2.5 %collective-permute-start.2 = (bf16[6,9,32,256]{3,2,1,0:T(8,128)(2,1)S(1)}, bf16[6,9,32,256]{3,2,1,0:T(8,128)(2,1)S(1)}, u32[]{:S(2)}, u32[]{:S(2)}) collective-permute-start(bf16[6,9,32,256]{3,2,1,0:T(8,128)(2,1)S(1)} %pad_maximum_fusion), channel_id=1, source_target_pairs={{0,1},{1,0},{2,3},{3,2},{4,5},{5,4},{6,7},{7,6},{8,9},{9,8},{10,11... | collective-permute-start | bytes 2654216 | tf_op jit(solution)/shard_map/ppermute | solution.py:252
  21.2 0.9 copy-start.8
  43.4 18.9 %copy-start = (bf16[4,8,32,256]{3,2,1,0:T(8,128)(2,1)S(1)}, bf16[4,8,32,256]{3,2,1,0:T(8,128)(2,1)}, u32[]{:S(2)}) copy-start(bf16[4,8,32,256]{3,2,1,0:T(8,128)(2,1)} %get-tuple-element.12.hid) | copy-start | bytes 1572868
  43.4 18.9 %copy-start.1 = (bf16[4,8,32,256]{3,2,1,0:T(8,128)(2,1)S(1)}, bf16[4,8,32,256]{3,2,1,0:T(8,128)(2,1)}, u32[]{:S(2)}) copy-start(bf16[4,8,32,256]{3,2,1,0:T(8,128)(2,1)} %get-tuple-element.13.pre_grad) | copy-start | bytes 1572868
  45.5 11.0 %collective-permute-start.4 = (bf16[2,8,32,256]{3,2,1,0:T(8,128)(2,1)S(1)}, bf16[2,8,32,256]{3,2,1,0:T(8,128)(2,1)S(1)}, u32[]{:S(2)}, u32[]{:S(2)}) collective-permute-start(bf16[2,8,32,256]{3,2,1,0:T(8,128)(2,1)S(1)} %pad_maximum_fusion.9), channel_id=1, source_target_pairs={{2,0},{4,2},{6,4},{8,6},{10,8},{12,10},{14,12},{3,1},{5,3},{7,5},{... | collective-permute-start | bytes 786440 | tf_op jit(solution)/shard_map/ppermute | solution.py:247
  46.8 15.4 %collective-permute-start.3 = (bf16[2,8,32,256]{3,2,1,0:T(8,128)(2,1)S(1)}, bf16[2,8,32,256]{3,2,1,0:T(8,128)(2,1)S(1)}, u32[]{:S(2)}, u32[]{:S(2)}) collective-permute-start(bf16[2,8,32,256]{3,2,1,0:T(8,128)(2,1)S(1)} %pad_maximum_fusion.8), channel_id=1, source_target_pairs={{0,2},{2,4},{4,6},{6,8},{8,10},{10,12},{12,14},{1,3},{3,5},{5,7},{... | collective-permute-start | bytes 786440 | tf_op jit(solution)/shard_map/ppermute | solution.py:246
  56.5 6.0 %copy-start.6 = (bf16[2,8,32,256]{3,2,1,0:T(8,128)(2,1)}, bf16[2,8,32,256]{3,2,1,0:T(8,128)(2,1)S(1)}, u32[]{:S(2)}) copy-start(bf16[2,8,32,256]{3,2,1,0:T(8,128)(2,1)S(1)} %collective-permute-done.4.high.high2) | copy-start | bytes 786436
  62.3 0.7 copy-start.7
  63.1 2.5 %collective-permute-start.5 = (bf16[6,9,32,256]{3,2,1,0:T(8,128)(2,1)S(1)}, bf16[6,9,32,256]{3,2,1,0:T(8,128)(2,1)S(1)}, u32[]{:S(2)}, u32[]{:S(2)}) collective-permute-start(bf16[6,9,32,256]{3,2,1,0:T(8,128)(2,1)S(1)} %pad_maximum_fusion.1), channel_id=1, source_target_pairs={{0,1},{1,0},{2,3},{3,2},{4,5},{5,4},{6,7},{7,6},{8,9},{9,8},{10,11... | collective-permute-start | bytes 2654216 | tf_op jit(solution)/shard_map/ppermute | solution.py:252
  65.6 0.9 copy-start.9
  83.4 15.2 %collective-permute-start.8 = (bf16[16,32,896]{2,1,0:T(8,128)(2,1)}, bf16[16,32,896]{2,1,0:T(8,128)(2,1)S(1)}, u32[]{:S(2)}, u32[]{:S(2)}) collective-permute-start(bf16[16,32,896]{2,1,0:T(8,128)(2,1)} %get-tuple-element.19), channel_id=1, source_target_pairs={{0,8},{2,10},{16,24},{18,26},{32,40},{34,42},{48,56},{50,58},{64,7... | collective-permute-start | bytes 2752520 | tf_op jit(solution)/shard_map/ppermute | solution.py:260
  86.5 20.9 %collective-permute-start.7 = (bf16[16,32,896]{2,1,0:T(8,128)(2,1)}, bf16[16,32,896]{2,1,0:T(8,128)(2,1)S(1)}, u32[]{:S(2)}, u32[]{:S(2)}) collective-permute-start(bf16[16,32,896]{2,1,0:T(8,128)(2,1)} %get-tuple-element.18), channel_id=1, source_target_pairs={{0,12},{2,14},{16,28},{18,30},{32,44},{34,46},{48,60},{50,62},{64,... | collective-permute-start | bytes 2752520 | tf_op jit(solution)/shard_map/ppermute | solution.py:260
  87.6 20.8 %collective-permute-start.6 = (bf16[16,32,896]{2,1,0:T(8,128)(2,1)}, bf16[16,32,896]{2,1,0:T(8,128)(2,1)S(1)}, u32[]{:S(2)}, u32[]{:S(2)}) collective-permute-start(bf16[16,32,896]{2,1,0:T(8,128)(2,1)} %get-tuple-element.17), channel_id=1, source_target_pairs={{0,4},{2,6},{16,20},{18,22},{32,36},{34,38},{48,52},{50,54},{64,68... | collective-permute-start | bytes 2752520 | tf_op jit(solution)/shard_map/ppermute | solution.py:260
  110.1 7.6 %collective-permute-start.11 = (bf16[4,32,896]{2,1,0:T(8,128)(2,1)S(1)}, bf16[4,32,896]{2,1,0:T(8,128)(2,1)S(1)}, u32[]{:S(2)}, u32[]{:S(2)}) collective-permute-start(bf16[4,32,896]{2,1,0:T(8,128)(2,1)S(1)} %get-tuple-element.23), channel_id=1, source_target_pairs={{0,64},{2,66},{16,80},{18,82},{32,96},{34,98},{48,112},{50,114},{6... | collective-permute-start | bytes 688136 | tf_op jit(solution)/shard_map/ppermute | solution.py:260
  113.4 7.1 %collective-permute-start.10 = (bf16[4,32,896]{2,1,0:T(8,128)(2,1)S(1)}, bf16[4,32,896]{2,1,0:T(8,128)(2,1)S(1)}, u32[]{:S(2)}, u32[]{:S(2)}) collective-permute-start(bf16[4,32,896]{2,1,0:T(8,128)(2,1)S(1)} %get-tuple-element.24), channel_id=1, source_target_pairs={{0,96},{2,98},{16,112},{18,114},{32,0},{34,2},{48,16},{50,18},{64,... | collective-permute-start | bytes 688136 | tf_op jit(solution)/shard_map/ppermute | solution.py:260
  114.4 7.2 %collective-permute-start.9 = (bf16[4,32,896]{2,1,0:T(8,128)(2,1)S(1)}, bf16[4,32,896]{2,1,0:T(8,128)(2,1)S(1)}, u32[]{:S(2)}, u32[]{:S(2)}) collective-permute-start(bf16[4,32,896]{2,1,0:T(8,128)(2,1)S(1)} %get-tuple-element.22), channel_id=1, source_target_pairs={{0,32},{2,34},{16,48},{18,50},{32,64},{34,66},{48,80},{50,82},{64,... | collective-permute-start | bytes 688136 | tf_op jit(solution)/shard_map/ppermute | solution.py:260
  121.8 6.4 %collective-permute-start.14 = (f32[32,896]{1,0:T(8,128)S(1)}, f32[32,896]{1,0:T(8,128)S(1)}, u32[]{:S(2)}, u32[]{:S(2)}) collective-permute-start(f32[32,896]{1,0:T(8,128)S(1)} %get-tuple-element.40), channel_id=1, source_target_pairs={{0,16},{2,18},{16,0},{18,2},{32,48},{34,50},{48,32},{50,34},{64,80... | collective-permute-start | bytes 344072 | tf_op jit(solution)/shard_map/ppermute | solution.py:260
  125.5 5.9 %collective-permute-start.13 = (f32[32,896]{1,0:T(8,128)S(1)}, f32[32,896]{1,0:T(8,128)S(1)}, u32[]{:S(2)}, u32[]{:S(2)}) collective-permute-start(f32[32,896]{1,0:T(8,128)S(1)} %get-tuple-element.41), channel_id=1, source_target_pairs={{0,18},{2,0},{16,2},{18,16},{32,50},{34,32},{48,34},{50,48},{64,82... | collective-permute-start | bytes 344072 | tf_op jit(solution)/shard_map/ppermute | solution.py:260
  127.0 6.0 %collective-permute-start.12 = (f32[32,896]{1,0:T(8,128)S(1)}, f32[32,896]{1,0:T(8,128)S(1)}, u32[]{:S(2)}, u32[]{:S(2)}) collective-permute-start(f32[32,896]{1,0:T(8,128)S(1)} %get-tuple-element.39), channel_id=1, source_target_pairs={{0,2},{2,16},{16,18},{18,0},{32,34},{34,48},{48,50},{50,32},{64,66... | collective-permute-start | bytes 344072 | tf_op jit(solution)/shard_map/ppermute | solution.py:260
  133.1 21.2 %collective-permute-start.15 = (f32[16,896]{1,0:T(8,128)S(1)}, f32[16,896]{1,0:T(8,128)S(1)}, u32[]{:S(2)}, u32[]{:S(2)}) collective-permute-start(f32[16,896]{1,0:T(8,128)S(1)} %get-tuple-element.53), channel_id=1, source_target_pairs={{0,1},{1,0},{2,3},{3,2},{4,5},{5,4},{6,7},{7,6},{8,9},{9,8},{10,11... | collective-permute-start | bytes 172040 | tf_op jit(solution)/shard_map/ppermute | solution.py:278

commit v2 on v1

v2 whole, which is shorter than its diff:
```python
import jax
import jax.numpy as jnp
from jax import lax
from jax.experimental import pallas as pl
from jax.experimental.pallas import tpu as pltpu
from jax.sharding import PartitionSpec as P

BF = jnp.bfloat16
F32 = jnp.float32
ALL = ("dp", "px", "py")
X, Y, Z = 0, 1, 2
ORDER = ((X, Y, Z), (Y, Z, X))
LANES = 896


def device(x, y, z, core):
    x, y, z = x % 4, y % 4, z % 4
    return (y * 2 + z // 2) * 16 + (x * 2 + z % 2) * 2 + core


def hop_pairs(stage, distance):
    pairs = []
    for core in range(2):
        step = [0, 0, 0]
        step[ORDER[core][stage]] = distance
        for x in range(4):
            for y in range(4):
                for z in range(4):
                    pairs.append(
                        (
                            device(x, y, z, core),
                            device(x + step[0], y + step[1], z + step[2], core),
                        )
                    )
    return pairs


def shifted(block):
    wide = block.astype(F32)
    place = lax.broadcasted_iota(jnp.int32, wide.shape, 1)
    low = jnp.where(place == 0, 0.0, pltpu.roll(wide, 1, 1)).astype(BF)
    high = jnp.where(place == 31, 0.0, pltpu.roll(wide, 31, 1)).astype(BF)
    return low, high


def put(stack, row, start, block, flip):
    low, high = shifted(block)
    if flip:
        low, high = high, low
    rows = pl.ds(start, block.shape[0])
    stack[row, rows, :, 0:256] = low
    stack[row, rows, :, 256:512] = block
    stack[row, rows, :, 512:768] = high


def put_own(stack, slab, start, own, flip):
    def step(i, _):
        put(stack, i + slab, start, own[i], flip)
        return 0

    lax.fori_loop(0, own.shape[0], step, 0)


def put_faces(stack, core, slab, count, other, at_first, at_second, flip):
    at = jnp.where(core == 0, at_first, at_second)
    row = jnp.where(core == 0, 9, 0)

    def step(i, _):
        put(stack, i + slab, row, other[i, pl.ds(at, 1)], flip)
        stack[i + slab, pl.ds(9 - row, 1)] = jnp.zeros((1, 32, 768), BF)
        return 0

    lax.fori_loop(0, count, step, 0)


def put_halo(stack, core, slab, halo, which, flip):
    row = jnp.where(core == 0, 9, 0)
    put(stack, slab, 1, halo[which, 0:8], flip)
    put(stack, slab, row, halo[which, 8:9], flip)
    stack[slab, pl.ds(9 - row, 1)] = jnp.zeros((1, 32, 768), BF)


def conv_into(total, slabs, stack, weight):
    for k in range(9):
        a, b = k // 3, k % 3
        rows = [
            stack[x : x + n, b : b + 8].reshape(n * 256, 768) for x, n in slabs(a)
        ]
        rows = rows[0] if len(rows) == 1 else jnp.concatenate(rows, axis=0)
        term = jnp.dot(rows, weight[k * 768 : (k + 1) * 768], preferred_element_type=F32)
        if k == 0:
            total[...] = term
        else:
            total[...] += term


def conv_back_into(total, slabs, stack, weight):
    for k in range(9):
        a, b = k // 3, k % 3
        term = None
        for c in range(3):
            lanes = slice(c * 256, (c + 1) * 256)
            rows = [
                stack[x : x + n, 2 - b : 10 - b, :, lanes].reshape(n * 256, 256)
                for x, n in slabs(2 - a)
            ]
            rows = rows[0] if len(rows) == 1 else jnp.concatenate(rows, axis=0)
            block = weight[(k * 3 + c) * 256 : (k * 3 + c + 1) * 256]
            part = lax.dot_general(
                rows, block, (((1,), (1,)), ((), ())), preferred_element_type=F32
            )
            term = part if term is None else term + part
        if k == 0:
            total[...] = term
        else:
            total[...] += term


def gelu_and_slope(v):
    scale = 0.7978845608028654
    square = v * v
    t = jnp.tanh(scale * (v + 0.044715 * (square * v)))
    half = 0.5 * (1.0 + t)
    slope = half + 0.5 * v * (1.0 - t * t) * (scale * (1.0 + 3.0 * 0.044715 * square))
    return v * half, slope


def inner_kernel(
    place, cot, field, other, first_w, second_w, hidden, pre_grad, stack, back, pre, grad
):
    core = place[0]
    put_own(stack, 0, 1, field, False)
    put_faces(stack, core, 0, 4, other, 0, 8, False)
    put_own(back, 0, 1, cot, True)
    put_faces(back, core, 0, 4, other, 8, 7, True)
    conv_into(pre, lambda a: [(a, 2)], stack, first_w)
    conv_back_into(grad, lambda a: [(a, 2)], back, second_w)
    for i in range(2):
        rows = slice(i * 256, (i + 1) * 256)
        value, slope = gelu_and_slope(pre[rows])
        hidden[i] = value.astype(BF).reshape(8, 32, 256)
        pre_grad[i] = (grad[rows] * slope).astype(BF).reshape(8, 32, 256)


def outer_kernel(
    place, cot, field, other, low, high, inner_hidden, inner_grad, first_w, second_w,
    hidden, pre_grad, send, stack, back, pre, grad,
):
    core = place[0]
    put_own(stack, 1, 1, field, False)
    put_faces(stack, core, 1, 4, other, 0, 8, False)
    put_halo(stack, core, 0, low, 1, False)
    put_halo(stack, core, 5, high, 1, False)
    put_own(back, 1, 1, cot, True)
    put_faces(back, core, 1, 4, other, 8, 7, True)
    put_halo(back, core, 0, low, 0, True)
    put_halo(back, core, 5, high, 0, True)
    conv_into(pre, lambda a: [(a, 1), (a + 3, 1)], stack, first_w)
    conv_back_into(grad, lambda a: [(a, 1), (a + 3, 1)], back, second_w)
    for i in range(2):
        rows = slice(i * 256, (i + 1) * 256)
        value, slope = gelu_and_slope(pre[rows])
        hidden[3 * i] = value.astype(BF).reshape(8, 32, 256)
        pre_grad[3 * i] = (grad[rows] * slope).astype(BF).reshape(8, 32, 256)
        hidden[1 + i] = inner_hidden[i]
        pre_grad[1 + i] = inner_grad[i]

    @pl.when(core == 0)
    def _():
        send[:, 0:8] = hidden[...]
        send[:, 8:9] = pre_grad[:, 7:8]

    @pl.when(core == 1)
    def _():
        send[:, 0:8] = pre_grad[...]
        send[:, 8:9] = hidden[:, 0:1]


def last_kernel(
    place, hid, pre_grad, other, low, high, field, cot, first_w, second_w, out, field_grad,
    stack, back, total, grad,
):
    core = place[0]
    put_own(stack, 1, 1, hid, False)
    put_faces(stack, core, 1, 4, other, 8, 7, False)
    put_halo(stack, core, 0, low, 0, False)
    put_halo(stack, core, 5, high, 0, False)
    put_own(back, 1, 1, pre_grad, True)
    put_faces(back, core, 1, 4, other, 0, 8, True)
    put_halo(back, core, 0, low, 1, True)
    put_halo(back, core, 5, high, 1, True)
    conv_into(total, lambda a: [(a, 4)], stack, second_w)
    conv_back_into(grad, lambda a: [(a, 4)], back, first_w)
    for i in range(4):
        rows = slice(i * 256, (i + 1) * 256)
        one = field[i].astype(F32).reshape(256, 256) + total[rows]
        out[i] = one.astype(BF).reshape(8, 32, 256)
        two = cot[i].astype(F32).reshape(256, 256) + grad[rows]
        field_grad[i] = two.astype(BF).reshape(8, 32, 256)


def weight_kernel(
    place, cot, field, low1, high1, other1, edges, hid, pre_grad, other2,
    own, send1, send2, send3, stack, turned, local, flat, tiles,
):
    core = place[0]

    def fill(value, which, half, flip):
        near, far = 1 + 8 * half, 9 - 8 * half
        put_own(stack, 1, near, value, flip)
        put(stack, 0, near, low1[which, 0:8], flip)
        put(stack, 5, near, high1[which, 0:8], flip)
        put(stack, 0, far, edges[0], flip)
        put(stack, 5, far, edges[1], flip)

        def step(i, _):
            put(stack, i + 1, far, other1[i, 0:8], flip)
            return 0

        lax.fori_loop(0, 4, step, 0)
        for i in range(6):
            stack[i, 0:1] = jnp.zeros((1, 32, 768), BF)
            stack[i, 17:18] = jnp.zeros((1, 32, 768), BF)

    flat[:, 6912:7040] = jnp.zeros((256, 128), BF)

    @pl.when(core == 0)
    def _():
        fill(field, 1, 0, False)
        for i in range(4):
            turned[:, i * 512 : i * 512 + 256] = pre_grad[i].reshape(256, 256).T
            turned[:, i * 512 + 256 : i * 512 + 512] = other2[i, 0:8].reshape(256, 256).T

        def block(k, _):
            a, b = k // 3, k % 3
            rows = stack[pl.ds(a, 4), pl.ds(b, 16)].reshape(2048, 768)
            term = jnp.dot(turned[...], rows, preferred_element_type=F32)
            flat[:, pl.ds(pl.multiple_of(k * 768, 768), 768)] = (term * 0.125).astype(BF)
            return 0

        lax.fori_loop(0, 9, block, 0)

    @pl.when(core == 1)
    def _():
        fill(cot, 0, 1, True)
        for i in range(4):
            local[i * 512 : i * 512 + 256] = other2[i, 0:8].reshape(256, 256)
            local[i * 512 + 256 : i * 512 + 512] = hid[i].reshape(256, 256)

        def block(k, _):
            a, b = 2 - k // 3, 2 - k % 3
            rows = stack[pl.ds(a, 4), pl.ds(b, 16)].reshape(2048, 768)
            term = lax.dot_general(
                rows, local[...], (((0,), (0,)), ((), ())), preferred_element_type=F32
            )
            term = (term * 0.125).astype(BF)
            for c in range(3):
                lanes = pl.ds(pl.multiple_of((k * 3 + c) * 256, 256), 256)
                flat[:, lanes] = term[c * 256 : (c + 1) * 256]
            return 0

        lax.fori_loop(0, 9, block, 0)

    for k in range(8):
        tiles[k] = flat[:, k * 864 : k * 864 + LANES]
    x, y, z = place[1], place[2], place[3]
    zero = core == 0
    for first, ref in enumerate((own, send1, send2, send3)):

        def pick(i, _):
            second, third = i // 4, i % 4
            to_x = lax.rem(x + jnp.where(zero, first, third), 4)
            to_y = lax.rem(y + jnp.where(zero, second, first), 4)
            to_z = lax.rem(z + jnp.where(zero, third, second), 4)
            to_dp = to_y * 2 + to_z // 2
            to_px = to_x * 2 + lax.rem(to_z, 2)
            ref[i] = tiles[to_dp, pl.ds(pl.multiple_of(to_px * 32, 32), 32), :]
            return 0

        lax.fori_loop(0, 16, pick, 0)


def call(kernel, name, flops, args, outs, scratch, limit):
    whole = pl.BlockSpec(memory_space=pltpu.VMEM)
    return pl.pallas_call(
        kernel,
        name=name,
        out_shape=outs,
        in_specs=[pl.BlockSpec(memory_space=pltpu.SMEM)] + [whole] * (len(args) - 1),
        out_specs=[whole] * len(outs),
        scratch_shapes=scratch,
        compiler_params=pltpu.CompilerParams(vmem_limit_bytes=limit * 2**20),
        cost_estimate=pl.CostEstimate(
            flops=flops, bytes_accessed=8 * 2**20, transcendentals=0
        ),
    )(*args)


def swap_cores(value):
    return lax.ppermute(value, "py", [(0, 1), (1, 0)])


def swap_slabs(first, second, first_face, second_face):
    count = lax.axis_size("px")
    forward = [(i, i + 1) for i in range(count - 1)]
    backward = [(i + 1, i) for i in range(count - 1)]

    def slab(i):
        return jnp.stack(
            [
                jnp.concatenate([first[i], first_face[i]], axis=0),
                jnp.concatenate([second[i], second_face[i]], axis=0),
            ]
        )

    return lax.ppermute(slab(3), "px", forward), lax.ppermute(slab(0), "px", backward)


def hop(parts, stage):
    return [
        lax.ppermute(part, ALL, hop_pairs(stage, distance))
        for part, distance in zip(parts, (1, 3, 2))
    ]


def reduce_tiles(own, got, core):
    total = own.astype(F32)
    for part in got:
        total = total + part.astype(F32)
    got = hop([total[4 * d : 4 * d + 4].astype(BF) for d in (1, 3, 2)], 1)
    total = total[0:4]
    for part in got:
        total = total + part.astype(F32)
    got = hop([total[d] for d in (1, 3, 2)], 2)
    total = total[0] + got[0] + got[1] + got[2]
    keep = jnp.where(core == 0, total[:16], total[16:])
    give = jnp.where(core == 0, total[16:], total[:16])
    other = swap_cores(give)
    first = jnp.where(core == 0, keep, other)[:, :864]
    second = jnp.where(core == 0, other, keep)[:, :864]
    return first.T, second.T


def body(fields, cotangent, first_weight, second_weight):
    shape = jax.ShapeDtypeStruct
    core = lax.axis_index("py")
    dp, px = lax.axis_index("dp"), lax.axis_index("px")
    zero = core == 0
    two = jnp.int32(2)
    place = jnp.stack(
        [core, lax.div(px, two), lax.div(dp, two), lax.rem(dp, two) * 2 + lax.rem(px, two)]
    )
    field, cot = fields[0], cotangent[0]
    grid, half = shape((4, 8, 32, 256), BF), shape((2, 8, 32, 256), BF)

    def conv_scratch(slabs, rows):
        return [pltpu.VMEM((slabs, 10, 32, 768), BF)] * 2 + [pltpu.VMEM((rows, 256), F32)] * 2

    flops = 2 * 2 * 1024 * 6912 * 256
    other1 = swap_cores(
        jnp.where(
            zero,
            jnp.concatenate([cot, field[:, 7:8]], axis=1),
            jnp.concatenate([field, cot[:, 0:1]], axis=1),
        )
    )
    low1, high1 = swap_slabs(
        cot,
        field,
        jnp.where(zero, other1[:, 8:9], other1[:, 7:8]),
        jnp.where(zero, other1[:, 0:1], other1[:, 8:9]),
    )
    inner_hidden, inner_grad = call(
        inner_kernel,
        "inner",
        flops // 2,
        (place, cot, field, other1, first_weight, second_weight),
        [half, half],
        conv_scratch(4, 512),
        24,
    )
    hidden, pre_grad, send = call(
        outer_kernel,
        "outer",
        flops // 2,
        (
            place, cot, field, other1, low1, high1, inner_hidden, inner_grad,
            first_weight, second_weight,
        ),
        [grid, grid, shape((4, 9, 32, 256), BF)],
        conv_scratch(6, 512),
        26,
    )
    edges = swap_cores(
        jnp.where(
            zero,
            jnp.stack([low1[0, 0:8], high1[0, 0:8]]),
            jnp.stack([low1[1, 0:8], high1[1, 0:8]]),
        )
    )
    other2 = swap_cores(send)
    low2, high2 = swap_slabs(
        hidden,
        pre_grad,
        jnp.where(zero, other2[:, 8:9], other2[:, 7:8]),
        jnp.where(zero, other2[:, 0:1], other2[:, 8:9]),
    )
    own, send1, send2, send3 = call(
        weight_kernel,
        "weight_terms",
        flops,
        (place, cot, field, low1, high1, other1, edges, hidden, pre_grad, other2),
        [shape((16, 32, LANES), BF)] * 4,
        [
            pltpu.VMEM((6, 18, 32, 768), BF),
            pltpu.VMEM((256, 2048), BF),
            pltpu.VMEM((2048, 256), BF),
            pltpu.VMEM((256, 7040), BF),
            pltpu.VMEM((8, 256, LANES), BF),
        ],
        34,
    )
    got = hop((send1, send3, send2), 0)
    hidden, pre_grad, send1 = lax.optimization_barrier((hidden, pre_grad, send1))
    output, field_grad = call(
        last_kernel,
        "outputs",
        flops,
        (
            place, hidden, pre_grad, other2, low2, high2, field, cot,
            first_weight, second_weight,
        ),
        [grid, grid],
        conv_scratch(6, 1024),
        28,
    )
    own, output, field_grad = lax.optimization_barrier((own, output, field_grad))
    first_grad, second_grad = reduce_tiles(own, got, core)
    return output[None], field_grad[None], first_grad, second_grad


def solution(mesh):
    placed = P("dp", "px", "py", None, None)
    return jax.shard_map(
        body,
        mesh=mesh,
        in_specs=(placed, placed, P(), P()),
        out_specs=(placed, placed, P("dp", ("px", "py")), P("dp", ("px", "py"))),
        check_vma=False,
    )
```

time: 157 us -> 103 us (0.66)
  waiting for transfers between devices: 56.2 us -> 29.4 us
  Pallas kernels: 59.2 us -> 33.6 us
  local copies, waits for them, and re-layouts: 6.19 us -> 4.01 us
  starting transfers between devices: 28.5 us -> 30.4 us
    pallas_call x3 -> x4, Pallas kernels: 59.2 us -> 33.6 us  [call(): pl.pallas_call(kernel, name=name, out_shape=outs, in_specs=[pl.BlockSpec(...]
    ppermute x7 -> x8, waiting for transfers between devices: 24.5 us -> 8.83 us  [the longest x2 4.5 us: swap_slabs(): lax.ppermute(slab(3), 'px', forward)]
    ppermute x9, waiting for transfers between devices: 31.7 us -> 20.6 us  [hop(): lax.ppermute(part, ALL, hop_pairs(stage, distance))]
    ppermute x9, starting transfers between devices: 16 us -> 18 us  [hop(): lax.ppermute(part, ALL, hop_pairs(stage, distance))]
    another operation x6 -> x14, other arithmetic: 2.41 us -> 0.83 us
    slice x7 -> x4, local copies, waits for them, and re-layouts: 3.35 us -> 1.82 us  [the longest x1 0.94 us: body(): field[:, 7:8]]
    ppermute x7 -> x8, starting transfers between devices: 12.5 us -> 12.4 us  [the longest x2 8.97 us: swap_slabs(): lax.ppermute(slab(3), 'px', forward)]
  transfers between devices with their start and end apart: 16 -> 17, of which waited for: 15 -> 10; matrix products, arithmetic and copies ran while one was open for 0% -> 0% of each run, Pallas kernels for 14% -> 28%
where the time goes in v2:
time: 103 us; the launch traced here: 101 us
  Pallas kernels  33.6 us (33%)
  starting transfers between devices  30.4 us (30%)
  waiting for transfers between devices  29.4 us (29%)
  local copies, waits for them, and re-layouts  4.01 us (4%)
  other arithmetic  3.01 us (3%)
    pallas_call x4, Pallas kernels, call(): pl.pallas_call(kernel, name=name, out_shape=outs, in_specs=[pl.BlockSpec(...  33.6 us
    ppermute x9, waiting for transfers between devices, hop(): lax.ppermute(part, ALL, hop_pairs(stage, distance))  20.6 us
    ppermute x9, starting transfers between devices, hop(): lax.ppermute(part, ALL, hop_pairs(stage, distance))  18 us
    ppermute x2, starting transfers between devices, swap_slabs(): lax.ppermute(slab(3), 'px', forward)  8.97 us
    ppermute x2, waiting for transfers between devices, swap_slabs(): lax.ppermute(slab(3), 'px', forward)  4.5 us
    ppermute x4, waiting for transfers between devices, swap_cores(): return lax.ppermute(value, 'py', [(0, 1), (1, 0)])  4.33 us
    ppermute x2, starting transfers between devices, swap_slabs(): lax.ppermute(slab(0), 'px', backward)  2.58 us
  transfers between devices with their start and end apart: 17, of which 10 were waited for; matrix products, arithmetic and copies ran while one was open for 0% of the time, Pallas kernels for 28%

profile of v2, /device:TPU:0, one launch (start us, length us, event | category | flops | bytes accessed | tf_op | source)
XLA Modules:
  0.0 101.5 jit_solution(811205366183072416)
XLA Ops:
  0.6 0.0 copy-start.1
  0.6 0.0 copy-start
  0.7 0.9 slice.171
  1.6 0.8 slice.172
  2.4 1.3 %maximum_select_fusion = bf16[4,9,32,256]{3,2,1,0:T(8,128)(2,1)S(1)} fusion(bf16[4,1,32,256]{3,2,1,0:T(8,128)(2,1)S(1)} %slice.171, bf16[4,8,32,256]{3,2,1,0:T(8,128)(2,1)} %bitcast.75, bf16[4,1,32,256]{3,2,1,0:T(8,128)(2,1)S(1)} %slice.172, bf16[4,8,32,256]{3,2,1,0:T(8,128)(2,1)} %bitcast.81, pred[]{:T(512)S(6)} %eq.2), kind=kLoop, calls=%fused_computation.1 | loop fusion | flops 884736 | bytes 1769473 | tf_op jit(solution)/shard_map/jit(_where)/select_n | solution.py:361
  3.7 0.1 collective-permute-start
  3.8 0.1 pad_add_fusion.place
  3.9 0.0 copy-done.1
  3.9 0.0 copy-start.2
  3.9 0.0 copy-done
  4.0 1.8 %collective-permute-done.other.other1 = bf16[4,9,32,256]{3,2,1,0:T(8,128)(2,1)S(1)} collective-permute-done((bf16[4,9,32,256]{3,2,1,0:T(8,128)(2,1)S(1)}, bf16[4,9,32,256]{3,2,1,0:T(8,128)(2,1)S(1)}, u32[]{:S(2)}, u32[]{:S(2)}) %collective-permute-start) | collective-permute-done | bytes 589856 | tf_op jit(solution)/shard_map/ppermute | solution.py:300
  5.9 1.3 %collective-permute-start.2 = (bf16[2,9,32,256]{3,2,1,0:T(8,128)(2,1)S(1)}, bf16[2,9,32,256]{3,2,1,0:T(8,128)(2,1)S(1)}, u32[]{:S(2)}, u32[]{:S(2)}) collective-permute-start(bf16[2,9,32,256]{3,2,1,0:T(8,128)(2,1)S(1)} %pad_maximum_fusion.1), channel_id=1, source_target_pairs={{2,0},{4,2},{6,4},{8,6},{10,8},{12,10},{14,12},{3,1},{5,3},{7,5},{... | collective-permute-start | bytes 884744 | tf_op jit(solution)/shard_map/ppermute | solution.py:316
  7.3 4.6 %collective-permute-start.1 = (bf16[2,9,32,256]{3,2,1,0:T(8,128)(2,1)S(1)}, bf16[2,9,32,256]{3,2,1,0:T(8,128)(2,1)S(1)}, u32[]{:S(2)}, u32[]{:S(2)}) collective-permute-start(bf16[2,9,32,256]{3,2,1,0:T(8,128)(2,1)S(1)} %pad_maximum_fusion), channel_id=1, source_target_pairs={{0,2},{2,4},{4,6},{6,8},{8,10},{10,12},{12,14},{1,3},{3,5},{5,7},{... | collective-permute-start | bytes 884744 | tf_op jit(solution)/shard_map/ppermute | solution.py:316
  11.9 0.0 copy-done.2
  11.9 0.0 copy-start.3
  11.9 2.0 %copy-done.3 = bf16[6912,256]{1,0:T(8,128)(2,1)S(1)} copy-done((bf16[6912,256]{1,0:T(8,128)(2,1)S(1)}, bf16[6912,256]{1,0:T(8,128)(2,1)}, u32[]{:S(2)}) %copy-start.3) | copy-done | bytes 3538968
  13.9 0.0 copy-start.4
  13.9 5.2 %inner.1 = (bf16[2,8,32,256]{3,2,1,0:T(8,128)(2,1)S(1)}, bf16[2,8,32,256]{3,2,1,0:T(8,128)(2,1)S(1)}) custom-call(s32[4]{0:T(128)S(1)} %pad_add_fusion.place, bf16[4,8,32,256]{3,2,1,0:T(8,128)(2,1)S(1)} %bitcast.76, bf16[4,8,32,256]{3,2,1,0:T(8,128)(2,1)S(1)} %bitcast.82, bf16[4,9,32,256]{3,2,1,0:T(8,128)(2,1)S(1)} %collective-permute-done.other.other1, ...), custom_call_target="tpu_custom_call" | custom-call | flops 3623878656 | bytes 8388608 | tf_op jit(solution)/shard_map/inner/pallas_call | solution.py:285
  19.1 0.0 collective-permute-done.2.high.high1
  19.1 4.5 %collective-permute-done.1.low.low1 = bf16[2,9,32,256]{3,2,1,0:T(8,128)(2,1)S(1)} collective-permute-done((bf16[2,9,32,256]{3,2,1,0:T(8,128)(2,1)S(1)}, bf16[2,9,32,256]{3,2,1,0:T(8,128)(2,1)S(1)}, u32[]{:S(2)}, u32[]{:S(2)}) %collective-permute-start.1) | collective-permute-done | bytes 294944 | tf_op jit(solution)/shard_map/ppermute | solution.py:316
  23.6 0.0 copy-done.4
  23.6 5.4 %outer.1 = (bf16[4,8,32,256]{3,2,1,0:T(8,128)(2,1)S(1)}, bf16[4,8,32,256]{3,2,1,0:T(8,128)(2,1)S(1)}, bf16[4,9,32,256]{3,2,1,0:T(8,128)(2,1)S(1)}) custom-call(s32[4]{0:T(128)S(1)} %pad_add_fusion.place, bf16[4,8,32,256]{3,2,1,0:T(8,128)(2,1)S(1)} %bitcast.77, bf16[4,8,32,256]{3,2,1,0:T(8,128)(2,1)S(1)} %bitcast.83, ...), custom_call_target="tpu_custom_call" | custom-call | flops 3623878656 | bytes 8388608 | tf_op jit(solution)/shard_map/outer/pallas_call | solution.py:285
  29.1 0.1 collective-permute-start.4
  29.3 0.6 collective-permute-start.3
  29.9 1.3 %collective-permute-done.4.other2.other = bf16[4,9,32,256]{3,2,1,0:T(8,128)(2,1)S(1)} collective-permute-done((bf16[4,9,32,256]{3,2,1,0:T(8,128)(2,1)S(1)}, bf16[4,9,32,256]{3,2,1,0:T(8,128)(2,1)S(1)}, u32[]{:S(2)}, u32[]{:S(2)}) %collective-permute-start.4) | collective-permute-done | bytes 589856 | tf_op jit(solution)/shard_map/ppermute | solution.py:300
  31.3 4.4 %collective-permute-start.5 = (bf16[2,9,32,256]{3,2,1,0:T(8,128)(2,1)S(1)}, bf16[2,9,32,256]{3,2,1,0:T(8,128)(2,1)S(1)}, u32[]{:S(2)}, u32[]{:S(2)}) collective-permute-start(bf16[2,9,32,256]{3,2,1,0:T(8,128)(2,1)S(1)} %pad_maximum_fusion.2), channel_id=1, source_target_pairs={{0,2},{2,4},{4,6},{6,8},{8,10},{10,12},{12,14},{1,3},{3,5},{5,7},{... | collective-permute-start | bytes 884744 | tf_op jit(solution)/shard_map/ppermute | solution.py:316
  35.8 1.3 %collective-permute-start.6 = (bf16[2,9,32,256]{3,2,1,0:T(8,128)(2,1)S(1)}, bf16[2,9,32,256]{3,2,1,0:T(8,128)(2,1)S(1)}, u32[]{:S(2)}, u32[]{:S(2)}) collective-permute-start(bf16[2,9,32,256]{3,2,1,0:T(8,128)(2,1)S(1)} %pad_maximum_fusion.3), channel_id=1, source_target_pairs={{2,0},{4,2},{6,4},{8,6},{10,8},{12,10},{14,12},{3,1},{5,3},{7,5},{... | collective-permute-start | bytes 884744 | tf_op jit(solution)/shard_map/ppermute | solution.py:316
  37.1 0.0 collective-permute-done.3.edges
  37.1 13.2 %weight_terms.1 = (bf16[16,32,896]{2,1,0:T(8,128)(2,1)S(1)}, bf16[16,32,896]{2,1,0:T(8,128)(2,1)S(1)}, bf16[16,32,896]{2,1,0:T(8,128)(2,1)S(1)}, bf16[16,32,896]{2,1,0:T(8,128)(2,1)S(1)}) custom-call(s32[4]{0:T(128)S(1)} %pad_add_fusion.place, bf16[4,8,32,256]{3,2,1,0:T(8,128)(2,1)S(1)} %bitcast.78, bf16[4,8,32,256]{3,2,1,0:T(8,128)(2,1)S(1)} %bitcast.84, ...), custom_call_target="tpu_custom_call" | custom-call | flops 7247757312 | bytes 8388608 | tf_op jit(solution)/shard_map/weight_terms/pallas_call | solution.py:285
  50.3 3.9 %collective-permute-start.8 = (bf16[16,32,896]{2,1,0:T(8,128)(2,1)S(1)}, bf16[16,32,896]{2,1,0:T(8,128)(2,1)S(1)}, u32[]{:S(2)}, u32[]{:S(2)}) collective-permute-start(bf16[16,32,896]{2,1,0:T(8,128)(2,1)S(1)} %get-tuple-element.34), channel_id=1, source_target_pairs={{0,12},{2,14},{16,28},{18,30},{32,44},{34,46},{48,60},{50,62},{64,... | collective-permute-start | bytes 2752520 | tf_op jit(solution)/shard_map/ppermute | solution.py:321
  54.2 1.0 collective-permute-start.9
  55.2 0.9 collective-permute-start.7
  56.1 0.0 collective-permute-done.5.low
  56.1 0.0 collective-permute-done.6.high
  56.1 9.8 %outputs.1 = (bf16[4,8,32,256]{3,2,1,0:T(8,128)(2,1)}, bf16[4,8,32,256]{3,2,1,0:T(8,128)(2,1)}) custom-call(s32[4]{0:T(128)S(1)} %pad_add_fusion.place, bf16[4,8,32,256]{3,2,1,0:T(8,128)(2,1)S(1)} %get-tuple-element.27.hid, bf16[4,8,32,256]{3,2,1,0:T(8,128)(2,1)S(1)} %get-tuple-element.28.pre_grad, ...), custom_call_target="tpu_custom_call" | custom-call | flops 7247757312 | bytes 8388608 | tf_op jit(solution)/shard_map/outputs/pallas_call | solution.py:285
  65.8 9.1 %collective-permute-done.8 = bf16[16,32,896]{2,1,0:T(8,128)(2,1)S(1)} collective-permute-done((bf16[16,32,896]{2,1,0:T(8,128)(2,1)S(1)}, bf16[16,32,896]{2,1,0:T(8,128)(2,1)S(1)}, u32[]{:S(2)}, u32[]{:S(2)}) %collective-permute-start.8) | collective-permute-done | bytes 917536 | tf_op jit(solution)/shard_map/ppermute | solution.py:321
  75.0 0.0 collective-permute-done.9
  75.0 4.0 %collective-permute-done.7 = bf16[16,32,896]{2,1,0:T(8,128)(2,1)S(1)} collective-permute-done((bf16[16,32,896]{2,1,0:T(8,128)(2,1)S(1)}, bf16[16,32,896]{2,1,0:T(8,128)(2,1)S(1)}, u32[]{:S(2)}, u32[]{:S(2)}) %collective-permute-start.7) | collective-permute-done | bytes 917536 | tf_op jit(solution)/shard_map/ppermute | solution.py:321
  78.9 0.5 fusion.5
  79.4 0.1 fusion.6
  79.5 1.6 %collective-permute-start.10 = (bf16[4,32,896]{2,1,0:T(8,128)(2,1)S(1)}, bf16[4,32,896]{2,1,0:T(8,128)(2,1)S(1)}, u32[]{:S(2)}, u32[]{:S(2)}) collective-permute-start(bf16[4,32,896]{2,1,0:T(8,128)(2,1)S(1)} %get-tuple-element.38), channel_id=1, source_target_pairs={{0,32},{2,34},{16,48},{18,50},{32,64},{34,66},{48,80},{50,82},{64,... | collective-permute-start | bytes 688136 | tf_op jit(solution)/shard_map/ppermute | solution.py:321
  81.2 2.9 %collective-permute-start.12 = (bf16[4,32,896]{2,1,0:T(8,128)(2,1)S(1)}, bf16[4,32,896]{2,1,0:T(8,128)(2,1)S(1)}, u32[]{:S(2)}, u32[]{:S(2)}) collective-permute-start(bf16[4,32,896]{2,1,0:T(8,128)(2,1)S(1)} %get-tuple-element.39), channel_id=1, source_target_pairs={{0,64},{2,66},{16,80},{18,82},{32,96},{34,98},{48,112},{50,114},{6... | collective-permute-start | bytes 688136 | tf_op jit(solution)/shard_map/ppermute | solution.py:321
  84.1 1.3 %collective-permute-start.11 = (bf16[4,32,896]{2,1,0:T(8,128)(2,1)S(1)}, bf16[4,32,896]{2,1,0:T(8,128)(2,1)S(1)}, u32[]{:S(2)}, u32[]{:S(2)}) collective-permute-start(bf16[4,32,896]{2,1,0:T(8,128)(2,1)S(1)} %get-tuple-element.40), channel_id=1, source_target_pairs={{0,96},{2,98},{16,112},{18,114},{32,0},{34,2},{48,16},{50,18},{64,... | collective-permute-start | bytes 688136 | tf_op jit(solution)/shard_map/ppermute | solution.py:321
  85.4 1.4 %collective-permute-done.10 = bf16[4,32,896]{2,1,0:T(8,128)(2,1)S(1)} collective-permute-done((bf16[4,32,896]{2,1,0:T(8,128)(2,1)S(1)}, bf16[4,32,896]{2,1,0:T(8,128)(2,1)S(1)}, u32[]{:S(2)}, u32[]{:S(2)}) %collective-permute-start.10) | collective-permute-done | bytes 229408 | tf_op jit(solution)/shard_map/ppermute | solution.py:321
  86.8 3.7 %collective-permute-done.12 = bf16[4,32,896]{2,1,0:T(8,128)(2,1)S(1)} collective-permute-done((bf16[4,32,896]{2,1,0:T(8,128)(2,1)S(1)}, bf16[4,32,896]{2,1,0:T(8,128)(2,1)S(1)}, u32[]{:S(2)}, u32[]{:S(2)}) %collective-permute-start.12) | collective-permute-done | bytes 229408 | tf_op jit(solution)/shard_map/ppermute | solution.py:321
  90.5 0.0 collective-permute-done.11
  90.5 0.1 fusion.1
  90.7 0.1 collective-permute-start.13
  90.7 3.8 %collective-permute-start.15 = (f32[32,896]{1,0:T(8,128)S(1)}, f32[32,896]{1,0:T(8,128)S(1)}, u32[]{:S(2)}, u32[]{:S(2)}) collective-permute-start(f32[32,896]{1,0:T(8,128)S(1)} %get-tuple-element.54), channel_id=1, source_target_pairs={{0,16},{2,18},{16,0},{18,2},{32,48},{34,50},{48,32},{50,34},{64,80... | collective-permute-start | bytes 344072 | tf_op jit(solution)/shard_map/ppermute | solution.py:321
  94.5 2.5 %collective-permute-start.14 = (f32[32,896]{1,0:T(8,128)S(1)}, f32[32,896]{1,0:T(8,128)S(1)}, u32[]{:S(2)}, u32[]{:S(2)}) collective-permute-start(f32[32,896]{1,0:T(8,128)S(1)} %get-tuple-element.55), channel_id=1, source_target_pairs={{0,18},{2,0},{16,2},{18,16},{32,50},{34,32},{48,34},{50,48},{64,82... | collective-permute-start | bytes 344072 | tf_op jit(solution)/shard_map/ppermute | solution.py:321
  97.1 0.0 collective-permute-done.13
  97.1 1.4 %collective-permute-done.15 = f32[32,896]{1,0:T(8,128)S(1)} collective-permute-done((f32[32,896]{1,0:T(8,128)S(1)}, f32[32,896]{1,0:T(8,128)S(1)}, u32[]{:S(2)}, u32[]{:S(2)}) %collective-permute-start.15) | collective-permute-done | bytes 114720 | tf_op jit(solution)/shard_map/ppermute | solution.py:321
  98.4 1.0 collective-permute-done.14
  99.5 0.1 collective-permute-start.16
  99.6 1.2 %collective-permute-done.16 = f32[16,896]{1,0:T(8,128)S(1)} collective-permute-done((f32[16,896]{1,0:T(8,128)S(1)}, f32[16,896]{1,0:T(8,128)S(1)}, u32[]{:S(2)}, u32[]{:S(2)}) %collective-permute-start.16) | collective-permute-done | bytes 57376 | tf_op jit(solution)/shard_map/ppermute | solution.py:300
  100.8 0.7 select_bitcast_fusion
  (27 shorter events, 0.5 us)
Async XLA Ops:
  0.6 3.3 %copy-start.1 = (bf16[1,4,8,32,256]{4,3,2,1,0:T(8,128)(2,1)S(1)}, bf16[1,4,8,32,256]{4,3,2,1,0:T(8,128)(2,1)}, u32[]{:S(2)}) copy-start(bf16[1,4,8,32,256]{4,3,2,1,0:T(8,128)(2,1)} %param.4) | copy-start | bytes 1572868
  0.6 3.3 %copy-start = (bf16[1,4,8,32,256]{4,3,2,1,0:T(8,128)(2,1)S(1)}, bf16[1,4,8,32,256]{4,3,2,1,0:T(8,128)(2,1)}, u32[]{:S(2)}) copy-start(bf16[1,4,8,32,256]{4,3,2,1,0:T(8,128)(2,1)} %param.5) | copy-start | bytes 1572868
  3.7 2.1 %collective-permute-start = (bf16[4,9,32,256]{3,2,1,0:T(8,128)(2,1)S(1)}, bf16[4,9,32,256]{3,2,1,0:T(8,128)(2,1)S(1)}, u32[]{:S(2)}, u32[]{:S(2)}) collective-permute-start(bf16[4,9,32,256]{3,2,1,0:T(8,128)(2,1)S(1)} %maximum_select_fusion), channel_id=1, source_target_pairs={{0,1},{1,0},{2,3},{3,2},{4,5},{5,4},{6,7},{7,6},{8,9},{9,8},{10,11... | collective-permute-start | bytes 1769480 | tf_op jit(solution)/shard_map/ppermute | solution.py:300
  3.9 8.0 %copy-start.2 = (bf16[6912,256]{1,0:T(8,128)(2,1)S(1)}, bf16[6912,256]{1,0:T(8,128)(2,1)}, u32[]{:S(2)}) copy-start(bf16[6912,256]{1,0:T(8,128)(2,1)} %first_w.5) | copy-start | bytes 10616836
  5.9 13.2 %collective-permute-start.2 = (bf16[2,9,32,256]{3,2,1,0:T(8,128)(2,1)S(1)}, bf16[2,9,32,256]{3,2,1,0:T(8,128)(2,1)S(1)}, u32[]{:S(2)}, u32[]{:S(2)}) collective-permute-start(bf16[2,9,32,256]{3,2,1,0:T(8,128)(2,1)S(1)} %pad_maximum_fusion.1), channel_id=1, source_target_pairs={{2,0},{4,2},{6,4},{8,6},{10,8},{12,10},{14,12},{3,1},{5,3},{7,5},{... | collective-permute-start | bytes 884744 | tf_op jit(solution)/shard_map/ppermute | solution.py:316
  7.3 16.3 %collective-permute-start.1 = (bf16[2,9,32,256]{3,2,1,0:T(8,128)(2,1)S(1)}, bf16[2,9,32,256]{3,2,1,0:T(8,128)(2,1)S(1)}, u32[]{:S(2)}, u32[]{:S(2)}) collective-permute-start(bf16[2,9,32,256]{3,2,1,0:T(8,128)(2,1)S(1)} %pad_maximum_fusion), channel_id=1, source_target_pairs={{0,2},{2,4},{4,6},{6,8},{8,10},{10,12},{12,14},{1,3},{3,5},{5,7},{... | collective-permute-start | bytes 884744 | tf_op jit(solution)/shard_map/ppermute | solution.py:316
  11.9 2.0 %copy-start.3 = (bf16[6912,256]{1,0:T(8,128)(2,1)S(1)}, bf16[6912,256]{1,0:T(8,128)(2,1)}, u32[]{:S(2)}) copy-start(bf16[6912,256]{1,0:T(8,128)(2,1)} %second_w.5) | copy-start | bytes 10616836
  13.9 9.7 %copy-start.4 = (bf16[6912,256]{1,0:T(8,128)(2,1)S(1)}, bf16[6912,256]{1,0:T(8,128)(2,1)}, u32[]{:S(2)}) copy-start(bf16[6912,256]{1,0:T(8,128)(2,1)} %second_w.5) | copy-start | bytes 10616836
  29.1 2.1 %collective-permute-start.4 = (bf16[4,9,32,256]{3,2,1,0:T(8,128)(2,1)S(1)}, bf16[4,9,32,256]{3,2,1,0:T(8,128)(2,1)S(1)}, u32[]{:S(2)}, u32[]{:S(2)}) collective-permute-start(bf16[4,9,32,256]{3,2,1,0:T(8,128)(2,1)S(1)} %get-tuple-element.24), channel_id=1, source_target_pairs={{0,1},{1,0},{2,3},{3,2},{4,5},{5,4},{6,7},{7,6},{8,9},{9,8},{10,11... | collective-permute-start | bytes 1769480 | tf_op jit(solution)/shard_map/ppermute | solution.py:300
  29.3 7.8 %collective-permute-start.3 = (bf16[2,8,32,256]{3,2,1,0:T(8,128)(2,1)S(1)}, bf16[2,8,32,256]{3,2,1,0:T(8,128)(2,1)S(1)}, u32[]{:S(2)}, u32[]{:S(2)}) collective-permute-start(bf16[2,8,32,256]{3,2,1,0:T(8,128)(2,1)S(1)} %maximum_select_fusion.1), channel_id=1, source_target_pairs={{0,1},{1,0},{2,3},{3,2},{4,5},{5,4},{6,7},{7,6},{8,9},{9,8},{10,11... | collective-permute-start | bytes 786440 | tf_op jit(solution)/shard_map/ppermute | solution.py:300
  31.3 24.8 %collective-permute-start.5 = (bf16[2,9,32,256]{3,2,1,0:T(8,128)(2,1)S(1)}, bf16[2,9,32,256]{3,2,1,0:T(8,128)(2,1)S(1)}, u32[]{:S(2)}, u32[]{:S(2)}) collective-permute-start(bf16[2,9,32,256]{3,2,1,0:T(8,128)(2,1)S(1)} %pad_maximum_fusion.2), channel_id=1, source_target_pairs={{0,2},{2,4},{4,6},{6,8},{8,10},{10,12},{12,14},{1,3},{3,5},{5,7},{... | collective-permute-start | bytes 884744 | tf_op jit(solution)/shard_map/ppermute | solution.py:316
  35.8 20.3 %collective-permute-start.6 = (bf16[2,9,32,256]{3,2,1,0:T(8,128)(2,1)S(1)}, bf16[2,9,32,256]{3,2,1,0:T(8,128)(2,1)S(1)}, u32[]{:S(2)}, u32[]{:S(2)}) collective-permute-start(bf16[2,9,32,256]{3,2,1,0:T(8,128)(2,1)S(1)} %pad_maximum_fusion.3), channel_id=1, source_target_pairs={{2,0},{4,2},{6,4},{8,6},{10,8},{12,10},{14,12},{3,1},{5,3},{7,5},{... | collective-permute-start | bytes 884744 | tf_op jit(solution)/shard_map/ppermute | solution.py:316
  50.3 24.6 %collective-permute-start.8 = (bf16[16,32,896]{2,1,0:T(8,128)(2,1)S(1)}, bf16[16,32,896]{2,1,0:T(8,128)(2,1)S(1)}, u32[]{:S(2)}, u32[]{:S(2)}) collective-permute-start(bf16[16,32,896]{2,1,0:T(8,128)(2,1)S(1)} %get-tuple-element.34), channel_id=1, source_target_pairs={{0,12},{2,14},{16,28},{18,30},{32,44},{34,46},{48,60},{50,62},{64,... | collective-permute-start | bytes 2752520 | tf_op jit(solution)/shard_map/ppermute | solution.py:321
  54.2 20.7 %collective-permute-start.9 = (bf16[16,32,896]{2,1,0:T(8,128)(2,1)S(1)}, bf16[16,32,896]{2,1,0:T(8,128)(2,1)S(1)}, u32[]{:S(2)}, u32[]{:S(2)}) collective-permute-start(bf16[16,32,896]{2,1,0:T(8,128)(2,1)S(1)} %get-tuple-element.35), channel_id=1, source_target_pairs={{0,8},{2,10},{16,24},{18,26},{32,40},{34,42},{48,56},{50,58},{64,7... | collective-permute-start | bytes 2752520 | tf_op jit(solution)/shard_map/ppermute | solution.py:321
  55.2 23.8 %collective-permute-start.7 = (bf16[16,32,896]{2,1,0:T(8,128)(2,1)S(1)}, bf16[16,32,896]{2,1,0:T(8,128)(2,1)S(1)}, u32[]{:S(2)}, u32[]{:S(2)}) collective-permute-start(bf16[16,32,896]{2,1,0:T(8,128)(2,1)S(1)} %get-tuple-element.26), channel_id=1, source_target_pairs={{0,4},{2,6},{16,20},{18,22},{32,36},{34,38},{48,52},{50,54},{64,68... | collective-permute-start | bytes 2752520 | tf_op jit(solution)/shard_map/ppermute | solution.py:321
  79.5 7.3 %collective-permute-start.10 = (bf16[4,32,896]{2,1,0:T(8,128)(2,1)S(1)}, bf16[4,32,896]{2,1,0:T(8,128)(2,1)S(1)}, u32[]{:S(2)}, u32[]{:S(2)}) collective-permute-start(bf16[4,32,896]{2,1,0:T(8,128)(2,1)S(1)} %get-tuple-element.38), channel_id=1, source_target_pairs={{0,32},{2,34},{16,48},{18,50},{32,64},{34,66},{48,80},{50,82},{64,... | collective-permute-start | bytes 688136 | tf_op jit(solution)/shard_map/ppermute | solution.py:321
  81.2 9.4 %collective-permute-start.12 = (bf16[4,32,896]{2,1,0:T(8,128)(2,1)S(1)}, bf16[4,32,896]{2,1,0:T(8,128)(2,1)S(1)}, u32[]{:S(2)}, u32[]{:S(2)}) collective-permute-start(bf16[4,32,896]{2,1,0:T(8,128)(2,1)S(1)} %get-tuple-element.39), channel_id=1, source_target_pairs={{0,64},{2,66},{16,80},{18,82},{32,96},{34,98},{48,112},{50,114},{6... | collective-permute-start | bytes 688136 | tf_op jit(solution)/shard_map/ppermute | solution.py:321
  84.1 6.5 %collective-permute-start.11 = (bf16[4,32,896]{2,1,0:T(8,128)(2,1)S(1)}, bf16[4,32,896]{2,1,0:T(8,128)(2,1)S(1)}, u32[]{:S(2)}, u32[]{:S(2)}) collective-permute-start(bf16[4,32,896]{2,1,0:T(8,128)(2,1)S(1)} %get-tuple-element.40), channel_id=1, source_target_pairs={{0,96},{2,98},{16,112},{18,114},{32,0},{34,2},{48,16},{50,18},{64,... | collective-permute-start | bytes 688136 | tf_op jit(solution)/shard_map/ppermute | solution.py:321
  90.7 6.4 %collective-permute-start.13 = (f32[32,896]{1,0:T(8,128)S(1)}, f32[32,896]{1,0:T(8,128)S(1)}, u32[]{:S(2)}, u32[]{:S(2)}) collective-permute-start(f32[32,896]{1,0:T(8,128)S(1)} %get-tuple-element.53), channel_id=1, source_target_pairs={{0,2},{2,16},{16,18},{18,0},{32,34},{34,48},{48,50},{50,32},{64,66... | collective-permute-start | bytes 344072 | tf_op jit(solution)/shard_map/ppermute | solution.py:321
  90.7 7.7 %collective-permute-start.15 = (f32[32,896]{1,0:T(8,128)S(1)}, f32[32,896]{1,0:T(8,128)S(1)}, u32[]{:S(2)}, u32[]{:S(2)}) collective-permute-start(f32[32,896]{1,0:T(8,128)S(1)} %get-tuple-element.54), channel_id=1, source_target_pairs={{0,16},{2,18},{16,0},{18,2},{32,48},{34,50},{48,32},{50,34},{64,80... | collective-permute-start | bytes 344072 | tf_op jit(solution)/shard_map/ppermute | solution.py:321
  94.5 4.9 %collective-permute-start.14 = (f32[32,896]{1,0:T(8,128)S(1)}, f32[32,896]{1,0:T(8,128)S(1)}, u32[]{:S(2)}, u32[]{:S(2)}) collective-permute-start(f32[32,896]{1,0:T(8,128)S(1)} %get-tuple-element.55), channel_id=1, source_target_pairs={{0,18},{2,0},{16,2},{18,16},{32,50},{34,32},{48,34},{50,48},{64,82... | collective-permute-start | bytes 344072 | tf_op jit(solution)/shard_map/ppermute | solution.py:321
  99.5 1.3 %collective-permute-start.16 = (f32[16,896]{1,0:T(8,128)S(1)}, f32[16,896]{1,0:T(8,128)S(1)}, u32[]{:S(2)}, u32[]{:S(2)}) collective-permute-start(f32[16,896]{1,0:T(8,128)S(1)} %get-tuple-element.63), channel_id=1, source_target_pairs={{0,1},{1,0},{2,3},{3,2},{4,5},{5,4},{6,7},{7,6},{8,9},{9,8},{10,11... | collective-permute-start | bytes 172040 | tf_op jit(solution)/shard_map/ppermute | solution.py:300

commit v3 on v2

--- a/solution.py
+++ b/solution.py
@@ -80,40 +80,48 @@
     stack[slab, pl.ds(9 - row, 1)] = jnp.zeros((1, 32, 768), BF)
 
 
-def conv_into(total, slabs, stack, weight):
-    for k in range(9):
-        a, b = k // 3, k % 3
-        rows = [
-            stack[x : x + n, b : b + 8].reshape(n * 256, 768) for x, n in slabs(a)
-        ]
-        rows = rows[0] if len(rows) == 1 else jnp.concatenate(rows, axis=0)
-        term = jnp.dot(rows, weight[k * 768 : (k + 1) * 768], preferred_element_type=F32)
-        if k == 0:
-            total[...] = term
-        else:
-            total[...] += term
-
-
-def conv_back_into(total, slabs, stack, weight):
-    for k in range(9):
-        a, b = k // 3, k % 3
-        term = None
-        for c in range(3):
-            lanes = slice(c * 256, (c + 1) * 256)
-            rows = [
-                stack[x : x + n, 2 - b : 10 - b, :, lanes].reshape(n * 256, 256)
-                for x, n in slabs(2 - a)
-            ]
-            rows = rows[0] if len(rows) == 1 else jnp.concatenate(rows, axis=0)
-            block = weight[(k * 3 + c) * 256 : (k * 3 + c + 1) * 256]
-            part = lax.dot_general(
-                rows, block, (((1,), (1,)), ((), ())), preferred_element_type=F32
-            )
-            term = part if term is None else term + part
-        if k == 0:
-            total[...] = term
-        else:
-            total[...] += term
+def term_of(rows, weight, k, back):
+    if not back:
+        return jnp.dot(rows, weight[k * 768 : (k + 1) * 768], preferred_element_type=F32)
+    term = None
+    for c in range(3):
+        part = lax.dot_general(
+            rows[:, c * 256 : (c + 1) * 256],
+            weight[(k * 3 + c) * 256 : (k * 3 + c + 1) * 256],
+            (((1,), (1,)), ((), ())),
+            preferred_element_type=F32,
+        )
+        term = part if term is None else term + part
+    return term
+
+
+def conv_own(total, stack, weight, back):
+    for a in (1, 0, 2):
+        step = 1 - a if back else a - 1
+        count = 4 - abs(step)
+        to = max(0, -step)
+        for b in range(3):
+            at = 2 - b if back else b
+            rows = stack[to + step : to + step + count, at : at + 8].reshape(count * 256, 768)
+            term = term_of(rows, weight, a * 3 + b, back)
+            span = slice(to * 256, (to + count) * 256)
+            if a == 1 and b == 0:
+                total[span] = term
+            else:
+                total[span] += term
+
+
+def conv_edges(part, stack, weight, back):
+    sums = []
+    for side in range(2):
+        a = 2 * side if not back else 2 - 2 * side
+        total = part[side]
+        for b in range(3):
+            at = 2 - b if back else b
+            rows = stack[side, at : at + 8].reshape(256, 768)
+            total = total + term_of(rows, weight, a * 3 + b, back)
+        sums.append(total)
+    return sums
 
 
 def gelu_and_slope(v):
@@ -125,43 +133,77 @@
     return v * half, slope
 
 
+def near_side(place):
+    return 1 - lax.rem(place[3], 2)
+
+
+def pack_kernel(place, cot, field, send, arrived):
+    core = place[0]
+
+    def pack(whole, row):
+        copies = [
+            pltpu.make_async_copy(whole, send.at[:, 0:8], arrived.at[0]),
+            pltpu.make_async_copy(row, send.at[:, 8:9], arrived.at[1]),
+        ]
+        for copy in copies:
+            copy.start()
+        for copy in copies:
+            copy.wait()
+
+    @pl.when(core == 0)
+    def _():
+        pack(cot, field.at[:, 7:8])
+
+    @pl.when(core == 1)
+    def _():
+        pack(field, cot.at[:, 0:1])
+
+
 def inner_kernel(
-    place, cot, field, other, first_w, second_w, hidden, pre_grad, stack, back, pre, grad
+    place, cot, field, other, first_hbm, second_hbm, hidden, pre_grad, part_pre, part_grad,
+    first_w, second_w, stack, back, pre, grad, arrived,
 ):
     core = place[0]
+    copies = [
+        pltpu.make_async_copy(first_hbm, first_w, arrived.at[0]),
+        pltpu.make_async_copy(second_hbm, second_w, arrived.at[1]),
+    ]
+    for copy in copies:
+        copy.start()
     put_own(stack, 0, 1, field, False)
     put_faces(stack, core, 0, 4, other, 0, 8, False)
     put_own(back, 0, 1, cot, True)
     put_faces(back, core, 0, 4, other, 8, 7, True)
-    conv_into(pre, lambda a: [(a, 2)], stack, first_w)
-    conv_back_into(grad, lambda a: [(a, 2)], back, second_w)
+    copies[0].wait()
+    conv_own(pre, stack, first_w, False)
+    copies[1].wait()
+    conv_own(grad, back, second_w, True)
     for i in range(2):
-        rows = slice(i * 256, (i + 1) * 256)
+        rows = slice((i + 1) * 256, (i + 2) * 256)
         value, slope = gelu_and_slope(pre[rows])
         hidden[i] = value.astype(BF).reshape(8, 32, 256)
         pre_grad[i] = (grad[rows] * slope).astype(BF).reshape(8, 32, 256)
+        rows = slice(i * 768, i * 768 + 256)
+        part_pre[i] = pre[rows]
+        part_grad[i] = grad[rows]
 
 
 def outer_kernel(
-    place, cot, field, other, low, high, inner_hidden, inner_grad, first_w, second_w,
-    hidden, pre_grad, send, stack, back, pre, grad,
+    place, near, far, inner_hidden, inner_grad, part_pre, part_grad, first_w, second_w,
+    hidden, pre_grad, send, stack, back,
 ):
     core = place[0]
-    put_own(stack, 1, 1, field, False)
-    put_faces(stack, core, 1, 4, other, 0, 8, False)
-    put_halo(stack, core, 0, low, 1, False)
-    put_halo(stack, core, 5, high, 1, False)
-    put_own(back, 1, 1, cot, True)
-    put_faces(back, core, 1, 4, other, 8, 7, True)
-    put_halo(back, core, 0, low, 0, True)
-    put_halo(back, core, 5, high, 0, True)
-    conv_into(pre, lambda a: [(a, 1), (a + 3, 1)], stack, first_w)
-    conv_back_into(grad, lambda a: [(a, 1), (a + 3, 1)], back, second_w)
+    side = near_side(place)
+    put_halo(stack, core, side, near, 1, False)
+    put_halo(stack, core, 1 - side, far, 1, False)
+    put_halo(back, core, side, near, 0, True)
+    put_halo(back, core, 1 - side, far, 0, True)
+    pre = conv_edges(part_pre, stack, first_w, False)
+    grad = conv_edges(part_grad, back, second_w, True)
     for i in range(2):
-        rows = slice(i * 256, (i + 1) * 256)
-        value, slope = gelu_and_slope(pre[rows])
+        value, slope = gelu_and_slope(pre[i])
         hidden[3 * i] = value.astype(BF).reshape(8, 32, 256)
-        pre_grad[3 * i] = (grad[rows] * slope).astype(BF).reshape(8, 32, 256)
+        pre_grad[3 * i] = (grad[i] * slope).astype(BF).reshape(8, 32, 256)
         hidden[1 + i] = inner_hidden[i]
         pre_grad[1 + i] = inner_grad[i]
 
@@ -176,45 +218,66 @@
         send[:, 8:9] = hidden[:, 0:1]
 
 
-def last_kernel(
-    place, hid, pre_grad, other, low, high, field, cot, first_w, second_w, out, field_grad,
-    stack, back, total, grad,
+def last_inner_kernel(
+    place, hid, pre_grad, other, field, cot, first_w, second_w,
+    out, field_grad, part_out, part_grad, stack, back, total, grad,
 ):
     core = place[0]
-    put_own(stack, 1, 1, hid, False)
-    put_faces(stack, core, 1, 4, other, 8, 7, False)
-    put_halo(stack, core, 0, low, 0, False)
-    put_halo(stack, core, 5, high, 0, False)
-    put_own(back, 1, 1, pre_grad, True)
-    put_faces(back, core, 1, 4, other, 0, 8, True)
-    put_halo(back, core, 0, low, 1, True)
-    put_halo(back, core, 5, high, 1, True)
-    conv_into(total, lambda a: [(a, 4)], stack, second_w)
-    conv_back_into(grad, lambda a: [(a, 4)], back, first_w)
-    for i in range(4):
-        rows = slice(i * 256, (i + 1) * 256)
-        one = field[i].astype(F32).reshape(256, 256) + total[rows]
+    put_own(stack, 0, 1, hid, False)
+    put_faces(stack, core, 0, 4, other, 8, 7, False)
+    put_own(back, 0, 1, pre_grad, True)
+    put_faces(back, core, 0, 4, other, 0, 8, True)
+    conv_own(total, stack, second_w, False)
+    conv_own(grad, back, first_w, True)
+    for i in range(2):
+        rows = slice((i + 1) * 256, (i + 2) * 256)
+        one = field[i + 1].astype(F32).reshape(256, 256) + total[rows]
         out[i] = one.astype(BF).reshape(8, 32, 256)
-        two = cot[i].astype(F32).reshape(256, 256) + grad[rows]
+        two = cot[i + 1].astype(F32).reshape(256, 256) + grad[rows]
         field_grad[i] = two.astype(BF).reshape(8, 32, 256)
+        rows = slice(i * 768, i * 768 + 256)
+        part_out[i] = total[rows]
+        part_grad[i] = grad[rows]
+
+
+def last_outer_kernel(
+    place, near, far, inner_out, inner_grad, part_out, part_grad, field, cot, first_w, second_w,
+    out, field_grad, stack, back,
+):
+    core = place[0]
+    side = near_side(place)
+    put_halo(stack, core, side, near, 0, False)
+    put_halo(stack, core, 1 - side, far, 0, False)
+    put_halo(back, core, side, near, 1, True)
+    put_halo(back, core, 1 - side, far, 1, True)
+    total = conv_edges(part_out, stack, second_w, False)
+    grad = conv_edges(part_grad, back, first_w, True)
+    for i in range(2):
+        one = field[3 * i].astype(F32).reshape(256, 256) + total[i]
+        out[3 * i] = one.astype(BF).reshape(8, 32, 256)
+        two = cot[3 * i].astype(F32).reshape(256, 256) + grad[i]
+        field_grad[3 * i] = two.astype(BF).reshape(8, 32, 256)
+        out[1 + i] = inner_out[i]
+        field_grad[1 + i] = inner_grad[i]
 
 
 def weight_kernel(
-    place, cot, field, low1, high1, other1, edges, hid, pre_grad, other2,
+    place, cot, field, near1, far1, other1, edges, hid, pre_grad, other2,
     own, send1, send2, send3, stack, turned, local, flat, tiles,
 ):
     core = place[0]
 
     def fill(value, which, half, flip):
-        near, far = 1 + 8 * half, 9 - 8 * half
-        put_own(stack, 1, near, value, flip)
-        put(stack, 0, near, low1[which, 0:8], flip)
-        put(stack, 5, near, high1[which, 0:8], flip)
-        put(stack, 0, far, edges[0], flip)
-        put(stack, 5, far, edges[1], flip)
+        mine, others = 1 + 8 * half, 9 - 8 * half
+        near = 5 * near_side(place)
+        put_own(stack, 1, mine, value, flip)
+        put(stack, near, mine, near1[which, 0:8], flip)
+        put(stack, 5 - near, mine, far1[which, 0:8], flip)
+        put(stack, near, others, edges[0], flip)
+        put(stack, 5 - near, others, edges[1], flip)
 
         def step(i, _):
-            put(stack, i + 1, far, other1[i, 0:8], flip)
+            put(stack, i + 1, others, other1[i, 0:8], flip)
             return 0
 
         lax.fori_loop(0, 4, step, 0)
@@ -238,7 +301,7 @@
             flat[:, pl.ds(pl.multiple_of(k * 768, 768), 768)] = (term * 0.125).astype(BF)
             return 0
 
-        lax.fori_loop(0, 9, block, 0)
+        lax.fori_loop(0, 9, block, 0, unroll=True)
 
     @pl.when(core == 1)
     def _():
@@ -259,7 +322,7 @@
                 flat[:, lanes] = term[c * 256 : (c + 1) * 256]
             return 0
 
-        lax.fori_loop(0, 9, block, 0)
+        lax.fori_loop(0, 9, block, 0, unroll=True)
 
     for k in range(8):
         tiles[k] = flat[:, k * 864 : k * 864 + LANES]
@@ -277,16 +340,20 @@
             ref[i] = tiles[to_dp, pl.ds(pl.multiple_of(to_px * 32, 32), 32), :]
             return 0
 
-        lax.fori_loop(0, 16, pick, 0)
-
-
-def call(kernel, name, flops, args, outs, scratch, limit):
+        lax.fori_loop(0, 16, pick, 0, unroll=8)
+
+
+def call(kernel, name, flops, args, outs, scratch, limit, far=()):
     whole = pl.BlockSpec(memory_space=pltpu.VMEM)
     return pl.pallas_call(
         kernel,
         name=name,
         out_shape=outs,
-        in_specs=[pl.BlockSpec(memory_space=pltpu.SMEM)] + [whole] * (len(args) - 1),
+        in_specs=[pl.BlockSpec(memory_space=pltpu.SMEM)]
+        + [
+            pl.BlockSpec(memory_space=pltpu.HBM) if i in far else whole
+            for i in range(1, len(args))
+        ],
         out_specs=[whole] * len(outs),
         scratch_shapes=scratch,
         compiler_params=pltpu.CompilerParams(vmem_limit_bytes=limit * 2**20),
@@ -300,10 +367,10 @@
     return lax.ppermute(value, "py", [(0, 1), (1, 0)])
 
 
-def swap_slabs(first, second, first_face, second_face):
+def swap_slabs(first, second, first_face, second_face, low_half):
     count = lax.axis_size("px")
-    forward = [(i, i + 1) for i in range(count - 1)]
-    backward = [(i + 1, i) for i in range(count - 1)]
+    near = [(i, i ^ 1) for i in range(count)]
+    far = [(i, i + 1 if i % 2 else i - 1) for i in range(1, count - 1)]
 
     def slab(i):
         return jnp.stack(
@@ -313,7 +380,10 @@
             ]
         )
 
-    return lax.ppermute(slab(3), "px", forward), lax.ppermute(slab(0), "px", backward)
+    low, high = slab(0), slab(3)
+    got_far = lax.ppermute(jnp.where(low_half, low, high), "px", far)
+    got_near = lax.ppermute(jnp.where(low_half, high, low), "px", near)
+    return got_near, got_far
 
 
 def hop(parts, stage):
@@ -353,63 +423,63 @@
     field, cot = fields[0], cotangent[0]
     grid, half = shape((4, 8, 32, 256), BF), shape((2, 8, 32, 256), BF)
 
-    def conv_scratch(slabs, rows):
-        return [pltpu.VMEM((slabs, 10, 32, 768), BF)] * 2 + [pltpu.VMEM((rows, 256), F32)] * 2
-
+    part = shape((2, 256, 256), F32)
+    low_half = lax.rem(px, two) == 0
+    own_scratch = [pltpu.VMEM((4, 10, 32, 768), BF)] * 2 + [pltpu.VMEM((1024, 256), F32)] * 2
+    edge_scratch = [pltpu.VMEM((2, 10, 32, 768), BF)] * 2
+    weights = (first_weight, second_weight)
     flops = 2 * 2 * 1024 * 6912 * 256
-    other1 = swap_cores(
-        jnp.where(
-            zero,
-            jnp.concatenate([cot, field[:, 7:8]], axis=1),
-            jnp.concatenate([field, cot[:, 0:1]], axis=1),
-        )
-    )
-    low1, high1 = swap_slabs(
+    (sent1,) = call(
+        pack_kernel,
+        "pack",
+        0,
+        (place, cot, field),
+        [shape((4, 9, 32, 256), BF)],
+        [pltpu.SemaphoreType.DMA((2,))],
+        56,
+        (1, 2),
+    )
+    other1 = swap_cores(sent1)
+    near1, far1 = swap_slabs(
         cot,
         field,
         jnp.where(zero, other1[:, 8:9], other1[:, 7:8]),
         jnp.where(zero, other1[:, 0:1], other1[:, 8:9]),
-    )
-    inner_hidden, inner_grad = call(
+        low_half,
+    )
+    inner = call(
         inner_kernel,
         "inner",
-        flops // 2,
-        (place, cot, field, other1, first_weight, second_weight),
-        [half, half],
-        conv_scratch(4, 512),
-        24,
-    )
-    hidden, pre_grad, send = call(
+        flops * 5 // 6,
+        (place, cot, field, other1, *weights),
+        [half, half, part, part, shape((6912, 256), BF), shape((6912, 256), BF)],
+        own_scratch + [pltpu.SemaphoreType.DMA((2,))],
+        42,
+        (4, 5),
+    )
+    inner, weights = inner[:4], inner[4:]
+    hidden, pre_grad, sent2 = call(
         outer_kernel,
         "outer",
-        flops // 2,
-        (
-            place, cot, field, other1, low1, high1, inner_hidden, inner_grad,
-            first_weight, second_weight,
-        ),
+        flops // 6,
+        (place, near1, far1, *inner, *weights),
         [grid, grid, shape((4, 9, 32, 256), BF)],
-        conv_scratch(6, 512),
-        26,
+        edge_scratch,
+        24,
     )
     edges = swap_cores(
         jnp.where(
             zero,
-            jnp.stack([low1[0, 0:8], high1[0, 0:8]]),
-            jnp.stack([low1[1, 0:8], high1[1, 0:8]]),
+            jnp.stack([near1[0, 0:8], far1[0, 0:8]]),
+            jnp.stack([near1[1, 0:8], far1[1, 0:8]]),
         )
     )
-    other2 = swap_cores(send)
-    low2, high2 = swap_slabs(
-        hidden,
-        pre_grad,
-        jnp.where(zero, other2[:, 8:9], other2[:, 7:8]),
-        jnp.where(zero, other2[:, 0:1], other2[:, 8:9]),
-    )
+    other2 = swap_cores(sent2)
     own, send1, send2, send3 = call(
         weight_kernel,
         "weight_terms",
         flops,
-        (place, cot, field, low1, high1, other1, edges, hidden, pre_grad, other2),
+        (place, cot, field, near1, far1, other1, edges, hidden, pre_grad, other2),
         [shape((16, 32, LANES), BF)] * 4,
         [
             pltpu.VMEM((6, 18, 32, 768), BF),
@@ -421,18 +491,31 @@
         34,
     )
     got = hop((send1, send3, send2), 0)
-    hidden, pre_grad, send1 = lax.optimization_barrier((hidden, pre_grad, send1))
+    hidden, pre_grad, other2, own = lax.optimization_barrier((hidden, pre_grad, other2, own))
+    near2, far2 = swap_slabs(
+        hidden,
+        pre_grad,
+        jnp.where(zero, other2[:, 8:9], other2[:, 7:8]),
+        jnp.where(zero, other2[:, 0:1], other2[:, 8:9]),
+        low_half,
+    )
+    last = call(
+        last_inner_kernel,
+        "outputs_inner",
+        flops * 5 // 6,
+        (place, hidden, pre_grad, other2, field, cot, *weights),
+        [half, half, part, part],
+        own_scratch,
+        26,
+    )
     output, field_grad = call(
-        last_kernel,
-        "outputs",
-        flops,
-        (
-            place, hidden, pre_grad, other2, low2, high2, field, cot,
-            first_weight, second_weight,
-        ),
+        last_outer_kernel,
+        "outputs_outer",
+        flops // 6,
+        (place, near2, far2, *last, field, cot, *weights),
         [grid, grid],
-        conv_scratch(6, 1024),
-        28,
+        edge_scratch,
+        24,
     )
     own, output, field_grad = lax.optimization_barrier((own, output, field_grad))
     first_grad, second_grad = reduce_tiles(own, got, core)

time: 103 us -> 102 us (level)
  Pallas kernels: 33.6 us -> 42 us
  waiting for transfers between devices: 29.4 us -> 22 us
  local copies, waits for them, and re-layouts: 4.01 us -> 0.24 us
  starting transfers between devices: 30.4 us -> 32.9 us
    pallas_call x4 -> x6, Pallas kernels: 33.6 us -> 42 us  [call(): pl.pallas_call(kernel, name=name, out_shape=outs, in_specs=[pl.BlockSpec(...]
    ppermute x9, starting transfers between devices: 18 us -> 25.7 us  [hop(): lax.ppermute(part, ALL, hop_pairs(stage, distance))]
    ppermute x4, starting transfers between devices: 11.6 us -> 6.33 us  [the longest x2 4.73 us: swap_slabs(): got_near = lax.ppermute(jnp.where(low_half, high, low), 'px', near)]
    ppermute x9, waiting for transfers between devices: 20.6 us -> 15.9 us  [hop(): lax.ppermute(part, ALL, hop_pairs(stage, distance))]
    ppermute x4, waiting for transfers between devices: 4.5 us -> 1.06 us  [the longest x2 1.05 us: swap_slabs(): got_near = lax.ppermute(jnp.where(low_half, high, low), 'px', near)]
    unnamed x10 -> x6, local copies, waits for them, and re-layouts: 2.02 us -> 0.02 us
    slice x4 -> x2, local copies, waits for them, and re-layouts: 1.82 us -> 0.04 us  [the longest x1 0.02 us: body(): near1[1, 0:8]]
    select_n x2 -> x3, other arithmetic: 1.34 us -> 0.16 us  [the longest x2 0.11 us: swap_slabs(): got_far = lax.ppermute(jnp.where(low_half, low, high), 'px', far)]
  transfers between devices with their start and end apart: 17 -> 17, of which waited for: 10 -> 10; matrix products, arithmetic and copies ran while one was open for 0% -> 0% of each run, Pallas kernels for 28% -> 26%
where the time goes in v3:
time: 102 us; the launch traced here: 100 us
  Pallas kernels  42 us (41%)
  starting transfers between devices  32.9 us (32%)
  waiting for transfers between devices  22 us (22%)
  other arithmetic  2.25 us (2%)
    pallas_call x6, Pallas kernels, call(): pl.pallas_call(kernel, name=name, out_shape=outs, in_specs=[pl.BlockSpec(...  42 us
    ppermute x9, starting transfers between devices, hop(): lax.ppermute(part, ALL, hop_pairs(stage, distance))  25.7 us
    ppermute x9, waiting for transfers between devices, hop(): lax.ppermute(part, ALL, hop_pairs(stage, distance))  15.9 us
    ppermute x4, waiting for transfers between devices, swap_cores(): return lax.ppermute(value, 'py', [(0, 1), (1, 0)])  5.02 us
    ppermute x2, starting transfers between devices, swap_slabs(): got_near = lax.ppermute(jnp.where(low_half, high, low), 'px', near)  4.73 us
  transfers between devices with their start and end apart: 17, of which 10 were waited for; matrix products, arithmetic and copies ran while one was open for 0% of the time, Pallas kernels for 26%

profile of v3, /device:TPU:0, one launch (start us, length us, event | category | flops | bytes accessed | tf_op | source)
XLA Modules:
  0.0 100.4 jit_solution(5817917910626418004)
XLA Ops:
  0.6 0.0 copy-start
  0.6 0.0 copy-start.1
  0.7 0.7 pad_add_fusion.place
  1.3 2.6 %pack.1 = bf16[4,9,32,256]{3,2,1,0:T(8,128)(2,1)} custom-call(s32[4]{0:T(128)} %pad_add_fusion.place, bf16[4,8,32,256]{3,2,1,0:T(8,128)(2,1)} %bitcast.74, bf16[4,8,32,256]{3,2,1,0:T(8,128)(2,1)} %bitcast.79), custom_call_target="tpu_custom_call" | custom-call | bytes 8388608 | tf_op jit(solution)/shard_map/pack/pallas_call | solution.py:348
  3.9 0.1 collective-permute-start
  4.0 0.0 copy-done
  4.0 0.0 copy-start.2
  4.0 0.0 copy-done.1
  4.1 2.1 %collective-permute-done.other.other1 = bf16[4,9,32,256]{3,2,1,0:T(8,128)(2,1)S(1)} collective-permute-done((bf16[4,9,32,256]{3,2,1,0:T(8,128)(2,1)}, bf16[4,9,32,256]{3,2,1,0:T(8,128)(2,1)S(1)}, u32[]{:S(2)}, u32[]{:S(2)}) %collective-permute-start) | collective-permute-done | bytes 589856 | tf_op jit(solution)/shard_map/ppermute | solution.py:367
  6.3 0.1 broadcast_select_fusion.2
  6.4 2.1 %collective-permute-start.1 = (bf16[2,9,32,256]{3,2,1,0:T(8,128)(2,1)S(1)}, bf16[2,9,32,256]{3,2,1,0:T(8,128)(2,1)S(1)}, u32[]{:S(2)}, u32[]{:S(2)}) collective-permute-start(bf16[2,9,32,256]{3,2,1,0:T(8,128)(2,1)S(1)} %get-tuple-element.66), channel_id=1, source_target_pairs={{0,2},{2,0},{4,6},{6,4},{8,10},{10,8},{12,14},{14,12},{1,3},{3,1},... | collective-permute-start | bytes 884744 | tf_op jit(solution)/shard_map/ppermute | solution.py:385
  8.5 0.7 collective-permute-start.2
  9.1 0.0 copy-done.2
  9.2 15.1 %inner.1 = (bf16[2,8,32,256]{3,2,1,0:T(8,128)(2,1)S(1)}, bf16[2,8,32,256]{3,2,1,0:T(8,128)(2,1)S(1)}, f32[2,256,256]{2,1,0:T(8,128)S(1)}, f32[2,256,256]{2,1,0:T...) custom-call(s32[4]{0:T(128)S(1)} %copy-done.2, bf16[4,8,32,256]{3,2,1,0:T(8,128)(2,1)S(1)} %bitcast.75, ...), custom_call_target="tpu_custom_call" | custom-call | flops 6039797760 | bytes 8388608 | tf_op jit(solution)/shard_map/inner/pallas_call | solution.py:348
  24.3 0.0 collective-permute-done.1.near.near1
  24.3 0.0 collective-permute-done.2.far.far1
  24.3 2.4 %outer.1 = (bf16[4,8,32,256]{3,2,1,0:T(8,128)(2,1)S(1)}, bf16[4,8,32,256]{3,2,1,0:T(8,128)(2,1)S(1)}, bf16[4,9,32,256]{3,2,1,0:T(8,128)(2,1)S(1)}) custom-call(s32[4]{0:T(128)S(1)} %copy-done.2, bf16[2,9,32,256]{3,2,1,0:T(8,128)(2,1)S(1)} %collective-permute-done.1.near.near1, bf16[2,9,32,256]{3,2,1,0:T(8,128)(2,1)S(1)} %collective-permute-done.2.far.far1, ...), custom_call_target="tpu_custom_call" | custom-call | flops 1207959552 | bytes 8388608 | tf_op jit(solution)/shard_map/outer/pallas_call | solution.py:348
  26.7 0.1 collective-permute-start.3
  26.9 0.6 collective-permute-start.4
  27.4 1.7 %collective-permute-done.4.edges = bf16[2,8,32,256]{3,2,1,0:T(8,128)(2,1)S(1)} collective-permute-done((bf16[2,8,32,256]{3,2,1,0:T(8,128)(2,1)S(1)}, bf16[2,8,32,256]{3,2,1,0:T(8,128)(2,1)S(1)}, u32[]{:S(2)}, u32[]{:S(2)}) %collective-permute-start.4) | collective-permute-done | bytes 262176 | tf_op jit(solution)/shard_map/ppermute | solution.py:367
  29.1 0.0 collective-permute-done.3.other2.other
  29.1 11.4 %weight_terms.1 = (bf16[16,32,896]{2,1,0:T(8,128)(2,1)S(1)}, bf16[16,32,896]{2,1,0:T(8,128)(2,1)S(1)}, bf16[16,32,896]{2,1,0:T(8,128)(2,1)S(1)}, bf16[16,32,896]{2,1,0:T(8,128)(2,1)S(1)}) custom-call(s32[4]{0:T(128)S(1)} %copy-done.2, bf16[4,8,32,256]{3,2,1,0:T(8,128)(2,1)S(1)} %bitcast.76, bf16[4,8,32,256]{3,2,1,0:T(8,128)(2,1)S(1)} %bitcast.81, ...), custom_call_target="tpu_custom_call" | custom-call | flops 7247757312 | bytes 8388608 | tf_op jit(solution)/shard_map/weight_terms/pallas_call | solution.py:348
  40.7 2.8 %collective-permute-start.7 = (bf16[16,32,896]{2,1,0:T(8,128)(2,1)S(1)}, bf16[16,32,896]{2,1,0:T(8,128)(2,1)S(1)}, u32[]{:S(2)}, u32[]{:S(2)}) collective-permute-start(bf16[16,32,896]{2,1,0:T(8,128)(2,1)S(1)} %get-tuple-element.53), channel_id=1, source_target_pairs={{0,4},{2,6},{16,20},{18,22},{32,36},{34,38},{48,52},{50,54},{64,68... | collective-permute-start | bytes 2752520 | tf_op jit(solution)/shard_map/ppermute | solution.py:391
  43.5 1.7 %collective-permute-start.8 = (bf16[16,32,896]{2,1,0:T(8,128)(2,1)S(1)}, bf16[16,32,896]{2,1,0:T(8,128)(2,1)S(1)}, u32[]{:S(2)}, u32[]{:S(2)}) collective-permute-start(bf16[16,32,896]{2,1,0:T(8,128)(2,1)S(1)} %get-tuple-element.54), channel_id=1, source_target_pairs={{0,12},{2,14},{16,28},{18,30},{32,44},{34,46},{48,60},{50,62},{64,... | collective-permute-start | bytes 2752520 | tf_op jit(solution)/shard_map/ppermute | solution.py:391
  45.2 1.9 %collective-permute-start.9 = (bf16[16,32,896]{2,1,0:T(8,128)(2,1)S(1)}, bf16[16,32,896]{2,1,0:T(8,128)(2,1)S(1)}, u32[]{:S(2)}, u32[]{:S(2)}) collective-permute-start(bf16[16,32,896]{2,1,0:T(8,128)(2,1)S(1)} %get-tuple-element.55), channel_id=1, source_target_pairs={{0,8},{2,10},{16,24},{18,26},{32,40},{34,42},{48,56},{50,58},{64,7... | collective-permute-start | bytes 2752520 | tf_op jit(solution)/shard_map/ppermute | solution.py:391
  47.2 0.1 broadcast_select_fusion
  47.2 2.7 %collective-permute-start.5 = (bf16[2,9,32,256]{3,2,1,0:T(8,128)(2,1)S(1)}, bf16[2,9,32,256]{3,2,1,0:T(8,128)(2,1)S(1)}, u32[]{:S(2)}, u32[]{:S(2)}) collective-permute-start(bf16[2,9,32,256]{3,2,1,0:T(8,128)(2,1)S(1)} %get-tuple-element.62), channel_id=1, source_target_pairs={{0,2},{2,0},{4,6},{6,4},{8,10},{10,8},{12,14},{14,12},{1,3},{3,1},... | collective-permute-start | bytes 884744 | tf_op jit(solution)/shard_map/ppermute | solution.py:385
  49.9 0.9 collective-permute-start.6
  50.8 7.4 %outputs_inner.1 = (bf16[2,8,32,256]{3,2,1,0:T(8,128)(2,1)S(1)}, bf16[2,8,32,256]{3,2,1,0:T(8,128)(2,1)S(1)}, f32[2,256,256]{2,1,0:T(8,128)S(1)}, f32[2,256,256]{2,1,0:T(8,128)S(1)}) custom-call(s32[4]{0:T(128)S(1)} %copy-done.2, bf16[4,8,32,256]{3,2,1,0:T(8,128)(2,1)S(1)} %get-tuple-element.41.hid, bf16[4,8,32,256]{3,2,1,0:T(8,128)(2,1)S(1)} %get-tuple-element.43.pre_grad, ...), custom_call_target="tpu_custom_call" | custom-call | flops 6039797760 | bytes 8388608 | tf_op jit(solution)/shard_map/outputs_inner/pallas_call | solution.py:348
  58.3 1.1 %collective-permute-done.5.near = bf16[2,9,32,256]{3,2,1,0:T(8,128)(2,1)S(1)} collective-permute-done((bf16[2,9,32,256]{3,2,1,0:T(8,128)(2,1)S(1)}, bf16[2,9,32,256]{3,2,1,0:T(8,128)(2,1)S(1)}, u32[]{:S(2)}, u32[]{:S(2)}) %collective-permute-start.5) | collective-permute-done | bytes 294944 | tf_op jit(solution)/shard_map/ppermute | solution.py:385
  59.3 0.0 collective-permute-done.6.far
  59.3 3.2 %outputs_outer.1 = (bf16[4,8,32,256]{3,2,1,0:T(8,128)(2,1)}, bf16[4,8,32,256]{3,2,1,0:T(8,128)(2,1)}) custom-call(s32[4]{0:T(128)S(1)} %copy-done.2, bf16[2,9,32,256]{3,2,1,0:T(8,128)(2,1)S(1)} %collective-permute-done.5.near, bf16[2,9,32,256]{3,2,1,0:T(8,128)(2,1)S(1)} %collective-permute-done.6.far, ...), custom_call_target="tpu_custom_call" | custom-call | flops 1207959552 | bytes 8388608 | tf_op jit(solution)/shard_map/outputs_outer/pallas_call | solution.py:348
  62.5 0.0 collective-permute-done.7
  62.5 0.0 collective-permute-done.8
  62.5 5.3 %collective-permute-done.9 = bf16[16,32,896]{2,1,0:T(8,128)(2,1)S(1)} collective-permute-done((bf16[16,32,896]{2,1,0:T(8,128)(2,1)S(1)}, bf16[16,32,896]{2,1,0:T(8,128)(2,1)S(1)}, u32[]{:S(2)}, u32[]{:S(2)}) %collective-permute-start.9) | collective-permute-done | bytes 917536 | tf_op jit(solution)/shard_map/ppermute | solution.py:391
  67.8 0.5 fusion.5
  68.2 0.1 fusion.6
  68.3 1.6 %collective-permute-start.10 = (bf16[4,32,896]{2,1,0:T(8,128)(2,1)S(1)}, bf16[4,32,896]{2,1,0:T(8,128)(2,1)S(1)}, u32[]{:S(2)}, u32[]{:S(2)}) collective-permute-start(bf16[4,32,896]{2,1,0:T(8,128)(2,1)S(1)} %get-tuple-element.58), channel_id=1, source_target_pairs={{0,32},{2,34},{16,48},{18,50},{32,64},{34,66},{48,80},{50,82},{64,... | collective-permute-start | bytes 688136 | tf_op jit(solution)/shard_map/ppermute | solution.py:391
  69.9 1.7 %collective-permute-start.11 = (bf16[4,32,896]{2,1,0:T(8,128)(2,1)S(1)}, bf16[4,32,896]{2,1,0:T(8,128)(2,1)S(1)}, u32[]{:S(2)}, u32[]{:S(2)}) collective-permute-start(bf16[4,32,896]{2,1,0:T(8,128)(2,1)S(1)} %get-tuple-element.60), channel_id=1, source_target_pairs={{0,96},{2,98},{16,112},{18,114},{32,0},{34,2},{48,16},{50,18},{64,... | collective-permute-start | bytes 688136 | tf_op jit(solution)/shard_map/ppermute | solution.py:391
  71.6 2.0 %collective-permute-start.12 = (bf16[4,32,896]{2,1,0:T(8,128)(2,1)S(1)}, bf16[4,32,896]{2,1,0:T(8,128)(2,1)S(1)}, u32[]{:S(2)}, u32[]{:S(2)}) collective-permute-start(bf16[4,32,896]{2,1,0:T(8,128)(2,1)S(1)} %get-tuple-element.59), channel_id=1, source_target_pairs={{0,64},{2,66},{16,80},{18,82},{32,96},{34,98},{48,112},{50,114},{6... | collective-permute-start | bytes 688136 | tf_op jit(solution)/shard_map/ppermute | solution.py:391
  73.6 2.0 %collective-permute-done.10 = bf16[4,32,896]{2,1,0:T(8,128)(2,1)S(1)} collective-permute-done((bf16[4,32,896]{2,1,0:T(8,128)(2,1)S(1)}, bf16[4,32,896]{2,1,0:T(8,128)(2,1)S(1)}, u32[]{:S(2)}, u32[]{:S(2)}) %collective-permute-start.10) | collective-permute-done | bytes 229408 | tf_op jit(solution)/shard_map/ppermute | solution.py:391
  75.6 0.4 collective-permute-done.11
  76.0 3.3 %collective-permute-done.12 = bf16[4,32,896]{2,1,0:T(8,128)(2,1)S(1)} collective-permute-done((bf16[4,32,896]{2,1,0:T(8,128)(2,1)S(1)}, bf16[4,32,896]{2,1,0:T(8,128)(2,1)S(1)}, u32[]{:S(2)}, u32[]{:S(2)}) %collective-permute-start.12) | collective-permute-done | bytes 229408 | tf_op jit(solution)/shard_map/ppermute | solution.py:391
  79.3 0.1 fusion.1
  79.4 10.1 %collective-permute-start.13 = (f32[32,896]{1,0:T(8,128)S(1)}, f32[32,896]{1,0:T(8,128)S(1)}, u32[]{:S(2)}, u32[]{:S(2)}) collective-permute-start(f32[32,896]{1,0:T(8,128)S(1)} %get-tuple-element.77), channel_id=1, source_target_pairs={{0,2},{2,16},{16,18},{18,0},{32,34},{34,48},{48,50},{50,32},{64,66... | collective-permute-start | bytes 344072 | tf_op jit(solution)/shard_map/ppermute | solution.py:391
  89.6 2.5 %collective-permute-start.14 = (f32[32,896]{1,0:T(8,128)S(1)}, f32[32,896]{1,0:T(8,128)S(1)}, u32[]{:S(2)}, u32[]{:S(2)}) collective-permute-start(f32[32,896]{1,0:T(8,128)S(1)} %get-tuple-element.79), channel_id=1, source_target_pairs={{0,18},{2,0},{16,2},{18,16},{32,50},{34,32},{48,34},{50,48},{64,82... | collective-permute-start | bytes 344072 | tf_op jit(solution)/shard_map/ppermute | solution.py:391
  92.1 1.4 %collective-permute-start.15 = (f32[32,896]{1,0:T(8,128)S(1)}, f32[32,896]{1,0:T(8,128)S(1)}, u32[]{:S(2)}, u32[]{:S(2)}) collective-permute-start(f32[32,896]{1,0:T(8,128)S(1)} %get-tuple-element.78), channel_id=1, source_target_pairs={{0,16},{2,18},{16,0},{18,2},{32,48},{34,50},{48,32},{50,34},{64,80... | collective-permute-start | bytes 344072 | tf_op jit(solution)/shard_map/ppermute | solution.py:391
  93.4 1.3 %collective-permute-done.13 = f32[32,896]{1,0:T(8,128)S(1)} collective-permute-done((f32[32,896]{1,0:T(8,128)S(1)}, f32[32,896]{1,0:T(8,128)S(1)}, u32[]{:S(2)}, u32[]{:S(2)}) %collective-permute-start.13) | collective-permute-done | bytes 114720 | tf_op jit(solution)/shard_map/ppermute | solution.py:391
  94.8 0.0 collective-permute-done.14
  94.8 3.6 %collective-permute-done.15 = f32[32,896]{1,0:T(8,128)S(1)} collective-permute-done((f32[32,896]{1,0:T(8,128)S(1)}, f32[32,896]{1,0:T(8,128)S(1)}, u32[]{:S(2)}, u32[]{:S(2)}) %collective-permute-start.15) | collective-permute-done | bytes 114720 | tf_op jit(solution)/shard_map/ppermute | solution.py:391
  98.4 0.1 collective-permute-start.16
  98.5 1.2 %collective-permute-done.16 = f32[16,896]{1,0:T(8,128)S(1)} collective-permute-done((f32[16,896]{1,0:T(8,128)S(1)}, f32[16,896]{1,0:T(8,128)S(1)}, u32[]{:S(2)}, u32[]{:S(2)}) %collective-permute-start.16) | collective-permute-done | bytes 57376 | tf_op jit(solution)/shard_map/ppermute | solution.py:367
  99.7 0.7 select_bitcast_fusion
  (23 shorter events, 0.4 us)
Async XLA Ops:
  0.6 3.4 %copy-start = (bf16[1,4,8,32,256]{4,3,2,1,0:T(8,128)(2,1)S(1)}, bf16[1,4,8,32,256]{4,3,2,1,0:T(8,128)(2,1)}, u32[]{:S(2)}) copy-start(bf16[1,4,8,32,256]{4,3,2,1,0:T(8,128)(2,1)} %param.5) | copy-start | bytes 1572868
  0.6 3.4 %copy-start.1 = (bf16[1,4,8,32,256]{4,3,2,1,0:T(8,128)(2,1)S(1)}, bf16[1,4,8,32,256]{4,3,2,1,0:T(8,128)(2,1)}, u32[]{:S(2)}) copy-start(bf16[1,4,8,32,256]{4,3,2,1,0:T(8,128)(2,1)} %param.4) | copy-start | bytes 1572868
  3.9 2.3 %collective-permute-start = (bf16[4,9,32,256]{3,2,1,0:T(8,128)(2,1)}, bf16[4,9,32,256]{3,2,1,0:T(8,128)(2,1)S(1)}, u32[]{:S(2)}, u32[]{:S(2)}) collective-permute-start(bf16[4,9,32,256]{3,2,1,0:T(8,128)(2,1)} %pack.1), channel_id=1, source_target_pairs={{0,1},{1,0},{2,3},{3,2},{4,5},{5,4},{6,7},{7,6},{8,9},{9,8},{10,11... | collective-permute-start | bytes 1769480 | tf_op jit(solution)/shard_map/ppermute | solution.py:367
  4.0 5.1 %copy-start.2 = (s32[4]{0:T(128)S(1)}, s32[4]{0:T(128)}, u32[]{:S(2)}) copy-start(s32[4]{0:T(128)} %pad_add_fusion.place) | copy-start | bytes 52
  6.4 17.9 %collective-permute-start.1 = (bf16[2,9,32,256]{3,2,1,0:T(8,128)(2,1)S(1)}, bf16[2,9,32,256]{3,2,1,0:T(8,128)(2,1)S(1)}, u32[]{:S(2)}, u32[]{:S(2)}) collective-permute-start(bf16[2,9,32,256]{3,2,1,0:T(8,128)(2,1)S(1)} %get-tuple-element.66), channel_id=1, source_target_pairs={{0,2},{2,0},{4,6},{6,4},{8,10},{10,8},{12,14},{14,12},{1,3},{3,1},... | collective-permute-start | bytes 884744 | tf_op jit(solution)/shard_map/ppermute | solution.py:385
  8.5 15.8 %collective-permute-start.2 = (bf16[2,9,32,256]{3,2,1,0:T(8,128)(2,1)S(1)}, bf16[2,9,32,256]{3,2,1,0:T(8,128)(2,1)S(1)}, u32[]{:S(2)}, u32[]{:S(2)}) collective-permute-start(bf16[2,9,32,256]{3,2,1,0:T(8,128)(2,1)S(1)} %get-tuple-element.65), channel_id=1, source_target_pairs={{2,4},{4,2},{6,8},{8,6},{10,12},{12,10},{3,5},{5,3},{7,9},{9,7},{1... | collective-permute-start | bytes 884744 | tf_op jit(solution)/shard_map/ppermute | solution.py:384
  26.7 2.5 %collective-permute-start.3 = (bf16[4,9,32,256]{3,2,1,0:T(8,128)(2,1)S(1)}, bf16[4,9,32,256]{3,2,1,0:T(8,128)(2,1)S(1)}, u32[]{:S(2)}, u32[]{:S(2)}) collective-permute-start(bf16[4,9,32,256]{3,2,1,0:T(8,128)(2,1)S(1)} %get-tuple-element.38), channel_id=1, source_target_pairs={{0,1},{1,0},{2,3},{3,2},{4,5},{5,4},{6,7},{7,6},{8,9},{9,8},{10,11... | collective-permute-start | bytes 1769480 | tf_op jit(solution)/shard_map/ppermute | solution.py:367
  26.9 2.3 %collective-permute-start.4 = (bf16[2,8,32,256]{3,2,1,0:T(8,128)(2,1)S(1)}, bf16[2,8,32,256]{3,2,1,0:T(8,128)(2,1)S(1)}, u32[]{:S(2)}, u32[]{:S(2)}) collective-permute-start(bf16[2,8,32,256]{3,2,1,0:T(8,128)(2,1)S(1)} %maximum_select_fusion), channel_id=1, source_target_pairs={{0,1},{1,0},{2,3},{3,2},{4,5},{5,4},{6,7},{7,6},{8,9},{9,8},{10,11... | collective-permute-start | bytes 786440 | tf_op jit(solution)/shard_map/ppermute | solution.py:367
  40.7 21.8 %collective-permute-start.7 = (bf16[16,32,896]{2,1,0:T(8,128)(2,1)S(1)}, bf16[16,32,896]{2,1,0:T(8,128)(2,1)S(1)}, u32[]{:S(2)}, u32[]{:S(2)}) collective-permute-start(bf16[16,32,896]{2,1,0:T(8,128)(2,1)S(1)} %get-tuple-element.53), channel_id=1, source_target_pairs={{0,4},{2,6},{16,20},{18,22},{32,36},{34,38},{48,52},{50,54},{64,68... | collective-permute-start | bytes 2752520 | tf_op jit(solution)/shard_map/ppermute | solution.py:391
  43.5 19.0 %collective-permute-start.8 = (bf16[16,32,896]{2,1,0:T(8,128)(2,1)S(1)}, bf16[16,32,896]{2,1,0:T(8,128)(2,1)S(1)}, u32[]{:S(2)}, u32[]{:S(2)}) collective-permute-start(bf16[16,32,896]{2,1,0:T(8,128)(2,1)S(1)} %get-tuple-element.54), channel_id=1, source_target_pairs={{0,12},{2,14},{16,28},{18,30},{32,44},{34,46},{48,60},{50,62},{64,... | collective-permute-start | bytes 2752520 | tf_op jit(solution)/shard_map/ppermute | solution.py:391
  45.2 22.6 %collective-permute-start.9 = (bf16[16,32,896]{2,1,0:T(8,128)(2,1)S(1)}, bf16[16,32,896]{2,1,0:T(8,128)(2,1)S(1)}, u32[]{:S(2)}, u32[]{:S(2)}) collective-permute-start(bf16[16,32,896]{2,1,0:T(8,128)(2,1)S(1)} %get-tuple-element.55), channel_id=1, source_target_pairs={{0,8},{2,10},{16,24},{18,26},{32,40},{34,42},{48,56},{50,58},{64,7... | collective-permute-start | bytes 2752520 | tf_op jit(solution)/shard_map/ppermute | solution.py:391
  47.2 12.1 %collective-permute-start.5 = (bf16[2,9,32,256]{3,2,1,0:T(8,128)(2,1)S(1)}, bf16[2,9,32,256]{3,2,1,0:T(8,128)(2,1)S(1)}, u32[]{:S(2)}, u32[]{:S(2)}) collective-permute-start(bf16[2,9,32,256]{3,2,1,0:T(8,128)(2,1)S(1)} %get-tuple-element.62), channel_id=1, source_target_pairs={{0,2},{2,0},{4,6},{6,4},{8,10},{10,8},{12,14},{14,12},{1,3},{3,1},... | collective-permute-start | bytes 884744 | tf_op jit(solution)/shard_map/ppermute | solution.py:385
  49.9 9.4 %collective-permute-start.6 = (bf16[2,9,32,256]{3,2,1,0:T(8,128)(2,1)S(1)}, bf16[2,9,32,256]{3,2,1,0:T(8,128)(2,1)S(1)}, u32[]{:S(2)}, u32[]{:S(2)}) collective-permute-start(bf16[2,9,32,256]{3,2,1,0:T(8,128)(2,1)S(1)} %get-tuple-element.61), channel_id=1, source_target_pairs={{2,4},{4,2},{6,8},{8,6},{10,12},{12,10},{3,5},{5,3},{7,9},{9,7},{1... | collective-permute-start | bytes 884744 | tf_op jit(solution)/shard_map/ppermute | solution.py:384
  68.3 7.3 %collective-permute-start.10 = (bf16[4,32,896]{2,1,0:T(8,128)(2,1)S(1)}, bf16[4,32,896]{2,1,0:T(8,128)(2,1)S(1)}, u32[]{:S(2)}, u32[]{:S(2)}) collective-permute-start(bf16[4,32,896]{2,1,0:T(8,128)(2,1)S(1)} %get-tuple-element.58), channel_id=1, source_target_pairs={{0,32},{2,34},{16,48},{18,50},{32,64},{34,66},{48,80},{50,82},{64,... | collective-permute-start | bytes 688136 | tf_op jit(solution)/shard_map/ppermute | solution.py:391
  69.9 6.0 %collective-permute-start.11 = (bf16[4,32,896]{2,1,0:T(8,128)(2,1)S(1)}, bf16[4,32,896]{2,1,0:T(8,128)(2,1)S(1)}, u32[]{:S(2)}, u32[]{:S(2)}) collective-permute-start(bf16[4,32,896]{2,1,0:T(8,128)(2,1)S(1)} %get-tuple-element.60), channel_id=1, source_target_pairs={{0,96},{2,98},{16,112},{18,114},{32,0},{34,2},{48,16},{50,18},{64,... | collective-permute-start | bytes 688136 | tf_op jit(solution)/shard_map/ppermute | solution.py:391
  71.6 7.7 %collective-permute-start.12 = (bf16[4,32,896]{2,1,0:T(8,128)(2,1)S(1)}, bf16[4,32,896]{2,1,0:T(8,128)(2,1)S(1)}, u32[]{:S(2)}, u32[]{:S(2)}) collective-permute-start(bf16[4,32,896]{2,1,0:T(8,128)(2,1)S(1)} %get-tuple-element.59), channel_id=1, source_target_pairs={{0,64},{2,66},{16,80},{18,82},{32,96},{34,98},{48,112},{50,114},{6... | collective-permute-start | bytes 688136 | tf_op jit(solution)/shard_map/ppermute | solution.py:391
  79.4 15.3 %collective-permute-start.13 = (f32[32,896]{1,0:T(8,128)S(1)}, f32[32,896]{1,0:T(8,128)S(1)}, u32[]{:S(2)}, u32[]{:S(2)}) collective-permute-start(f32[32,896]{1,0:T(8,128)S(1)} %get-tuple-element.77), channel_id=1, source_target_pairs={{0,2},{2,16},{16,18},{18,0},{32,34},{34,48},{48,50},{50,32},{64,66... | collective-permute-start | bytes 344072 | tf_op jit(solution)/shard_map/ppermute | solution.py:391
  89.6 5.2 %collective-permute-start.14 = (f32[32,896]{1,0:T(8,128)S(1)}, f32[32,896]{1,0:T(8,128)S(1)}, u32[]{:S(2)}, u32[]{:S(2)}) collective-permute-start(f32[32,896]{1,0:T(8,128)S(1)} %get-tuple-element.79), channel_id=1, source_target_pairs={{0,18},{2,0},{16,2},{18,16},{32,50},{34,32},{48,34},{50,48},{64,82... | collective-permute-start | bytes 344072 | tf_op jit(solution)/shard_map/ppermute | solution.py:391
  92.1 6.3 %collective-permute-start.15 = (f32[32,896]{1,0:T(8,128)S(1)}, f32[32,896]{1,0:T(8,128)S(1)}, u32[]{:S(2)}, u32[]{:S(2)}) collective-permute-start(f32[32,896]{1,0:T(8,128)S(1)} %get-tuple-element.78), channel_id=1, source_target_pairs={{0,16},{2,18},{16,0},{18,2},{32,48},{34,50},{48,32},{50,34},{64,80... | collective-permute-start | bytes 344072 | tf_op jit(solution)/shard_map/ppermute | solution.py:391
  98.4 1.3 %collective-permute-start.16 = (f32[16,896]{1,0:T(8,128)S(1)}, f32[16,896]{1,0:T(8,128)S(1)}, u32[]{:S(2)}, u32[]{:S(2)}) collective-permute-start(f32[16,896]{1,0:T(8,128)S(1)} %get-tuple-element.87), channel_id=1, source_target_pairs={{0,1},{1,0},{2,3},{3,2},{4,5},{5,4},{6,7},{7,6},{8,9},{9,8},{10,11... | collective-permute-start | bytes 172040 | tf_op jit(solution)/shard_map/ppermute | solution.py:367

commit v4 on v3

--- a/solution.py
+++ b/solution.py
@@ -174,9 +174,9 @@
     put_faces(stack, core, 0, 4, other, 0, 8, False)
     put_own(back, 0, 1, cot, True)
     put_faces(back, core, 0, 4, other, 8, 7, True)
-    copies[0].wait()
+    for copy in copies:
+        copy.wait()
     conv_own(pre, stack, first_w, False)
-    copies[1].wait()
     conv_own(grad, back, second_w, True)
     for i in range(2):
         rows = slice((i + 1) * 256, (i + 2) * 256)
@@ -475,6 +475,13 @@
         )
     )
     other2 = swap_cores(sent2)
+    near2, far2 = swap_slabs(
+        hidden,
+        pre_grad,
+        jnp.where(zero, other2[:, 8:9], other2[:, 7:8]),
+        jnp.where(zero, other2[:, 0:1], other2[:, 8:9]),
+        low_half,
+    )
     own, send1, send2, send3 = call(
         weight_kernel,
         "weight_terms",
@@ -490,15 +497,9 @@
         ],
         34,
     )
+    send1, near2, far2 = lax.optimization_barrier((send1, near2, far2))
     got = hop((send1, send3, send2), 0)
     hidden, pre_grad, other2, own = lax.optimization_barrier((hidden, pre_grad, other2, own))
-    near2, far2 = swap_slabs(
-        hidden,
-        pre_grad,
-        jnp.where(zero, other2[:, 8:9], other2[:, 7:8]),
-        jnp.where(zero, other2[:, 0:1], other2[:, 8:9]),
-        low_half,
-    )
     last = call(
         last_inner_kernel,
         "outputs_inner",

time: 102 us -> 94.6 us (0.927)
  starting transfers between devices: 32.9 us -> 23.9 us
  waiting for transfers between devices: 22 us -> 29 us
  Pallas kernels: 42 us -> 37 us
    ppermute x9, starting transfers between devices: 25.7 us -> 17.1 us  [hop(): lax.ppermute(part, ALL, hop_pairs(stage, distance))]
    ppermute x9, waiting for transfers between devices: 15.9 us -> 22.2 us  [hop(): lax.ppermute(part, ALL, hop_pairs(stage, distance))]
    pallas_call x6, Pallas kernels: 42 us -> 37 us  [call(): pl.pallas_call(kernel, name=name, out_shape=outs, in_specs=[pl.BlockSpec(...]
    ppermute x2, waiting for transfers between devices: 1.05 us -> 2.12 us  [swap_slabs(): got_near = lax.ppermute(jnp.where(low_half, high, low), 'px', near)]
  transfers between devices with their start and end apart: 17 -> 17, of which waited for: 10 -> 12; matrix products, arithmetic and copies ran while one was open for 0% -> 0% of each run, Pallas kernels for 26% -> 34%
where the time goes in v4:
time: 94.6 us; the launch traced here: 93.4 us
  Pallas kernels  37 us (39%)
  waiting for transfers between devices  29 us (31%)
  starting transfers between devices  23.9 us (25%)
  other arithmetic  2.25 us (2%)
  between operations  1 us (1%)
    pallas_call x6, Pallas kernels, call(): pl.pallas_call(kernel, name=name, out_shape=outs, in_specs=[pl.BlockSpec(...  37 us
    ppermute x9, waiting for transfers between devices, hop(): lax.ppermute(part, ALL, hop_pairs(stage, distance))  22.2 us
    ppermute x9, starting transfers between devices, hop(): lax.ppermute(part, ALL, hop_pairs(stage, distance))  17.1 us
    ppermute x2, starting transfers between devices, swap_slabs(): got_near = lax.ppermute(jnp.where(low_half, high, low), 'px', near)  4.64 us
    ppermute x4, waiting for transfers between devices, swap_cores(): return lax.ppermute(value, 'py', [(0, 1), (1, 0)])  4.6 us
    ppermute x2, waiting for transfers between devices, swap_slabs(): got_near = lax.ppermute(jnp.where(low_half, high, low), 'px', near)  2.12 us
  transfers between devices with their start and end apart: 17, of which 12 were waited for; matrix products, arithmetic and copies ran while one was open for 0% of the time, Pallas kernels for 34%

profile of v4, /device:TPU:0, one launch (start us, length us, event | category | flops | bytes accessed | tf_op | source)
XLA Modules:
  0.0 93.4 jit_solution(11218094017991453106)
XLA Ops:
  0.6 0.0 copy-start
  0.6 0.0 copy-start.1
  0.7 0.7 pad_add_fusion.place
  1.3 2.6 %pack.1 = bf16[4,9,32,256]{3,2,1,0:T(8,128)(2,1)} custom-call(s32[4]{0:T(128)} %pad_add_fusion.place, bf16[4,8,32,256]{3,2,1,0:T(8,128)(2,1)} %bitcast.74, bf16[4,8,32,256]{3,2,1,0:T(8,128)(2,1)} %bitcast.79), custom_call_target="tpu_custom_call" | custom-call | bytes 8388608 | tf_op jit(solution)/shard_map/pack/pallas_call | solution.py:348
  3.9 0.1 collective-permute-start
  4.0 0.0 copy-done
  4.0 0.0 copy-start.2
  4.0 0.0 copy-done.1
  4.1 2.1 %collective-permute-done.other.other1 = bf16[4,9,32,256]{3,2,1,0:T(8,128)(2,1)S(1)} collective-permute-done((bf16[4,9,32,256]{3,2,1,0:T(8,128)(2,1)}, bf16[4,9,32,256]{3,2,1,0:T(8,128)(2,1)S(1)}, u32[]{:S(2)}, u32[]{:S(2)}) %collective-permute-start) | collective-permute-done | bytes 589856 | tf_op jit(solution)/shard_map/ppermute | solution.py:367
  6.3 0.1 broadcast_select_fusion.2
  6.4 2.1 %collective-permute-start.1 = (bf16[2,9,32,256]{3,2,1,0:T(8,128)(2,1)S(1)}, bf16[2,9,32,256]{3,2,1,0:T(8,128)(2,1)S(1)}, u32[]{:S(2)}, u32[]{:S(2)}) collective-permute-start(bf16[2,9,32,256]{3,2,1,0:T(8,128)(2,1)S(1)} %get-tuple-element.72), channel_id=1, source_target_pairs={{0,2},{2,0},{4,6},{6,4},{8,10},{10,8},{12,14},{14,12},{1,3},{3,1},... | collective-permute-start | bytes 884744 | tf_op jit(solution)/shard_map/ppermute | solution.py:385
  8.5 0.7 collective-permute-start.2
  9.1 0.0 copy-done.2
  9.2 10.1 %inner.1 = (bf16[2,8,32,256]{3,2,1,0:T(8,128)(2,1)S(1)}, bf16[2,8,32,256]{3,2,1,0:T(8,128)(2,1)S(1)}, f32[2,256,256]{2,1,0:T(8,128)S(1)}, f32[2,256,256]{2,1,0:T...) custom-call(s32[4]{0:T(128)S(1)} %copy-done.2, bf16[4,8,32,256]{3,2,1,0:T(8,128)(2,1)S(1)} %bitcast.75, ...), custom_call_target="tpu_custom_call" | custom-call | flops 6039797760 | bytes 8388608 | tf_op jit(solution)/shard_map/inner/pallas_call | solution.py:348
  19.2 2.1 %collective-permute-done.1.near.near1 = bf16[2,9,32,256]{3,2,1,0:T(8,128)(2,1)S(1)} collective-permute-done((bf16[2,9,32,256]{3,2,1,0:T(8,128)(2,1)S(1)}, bf16[2,9,32,256]{3,2,1,0:T(8,128)(2,1)S(1)}, u32[]{:S(2)}, u32[]{:S(2)}) %collective-permute-start.1) | collective-permute-done | bytes 294944 | tf_op jit(solution)/shard_map/ppermute | solution.py:385
  21.4 0.0 collective-permute-done.2.far.far1
  21.4 2.4 %outer.1 = (bf16[4,8,32,256]{3,2,1,0:T(8,128)(2,1)S(1)}, bf16[4,8,32,256]{3,2,1,0:T(8,128)(2,1)S(1)}, bf16[4,9,32,256]{3,2,1,0:T(8,128)(2,1)S(1)}) custom-call(s32[4]{0:T(128)S(1)} %copy-done.2, bf16[2,9,32,256]{3,2,1,0:T(8,128)(2,1)S(1)} %collective-permute-done.1.near.near1, bf16[2,9,32,256]{3,2,1,0:T(8,128)(2,1)S(1)} %collective-permute-done.2.far.far1, ...), custom_call_target="tpu_custom_call" | custom-call | flops 1207959552 | bytes 8388608 | tf_op jit(solution)/shard_map/outer/pallas_call | solution.py:348
  23.7 0.1 collective-permute-start.3
  23.9 0.6 collective-permute-start.4
  24.6 1.3 %collective-permute-done.3.other2.other = bf16[4,9,32,256]{3,2,1,0:T(8,128)(2,1)S(1)} collective-permute-done((bf16[4,9,32,256]{3,2,1,0:T(8,128)(2,1)S(1)}, bf16[4,9,32,256]{3,2,1,0:T(8,128)(2,1)S(1)}, u32[]{:S(2)}, u32[]{:S(2)}) %collective-permute-start.3) | collective-permute-done | bytes 589856 | tf_op jit(solution)/shard_map/ppermute | solution.py:367
  26.0 0.1 broadcast_select_fusion
  26.0 2.6 %collective-permute-start.5 = (bf16[2,9,32,256]{3,2,1,0:T(8,128)(2,1)S(1)}, bf16[2,9,32,256]{3,2,1,0:T(8,128)(2,1)S(1)}, u32[]{:S(2)}, u32[]{:S(2)}) collective-permute-start(bf16[2,9,32,256]{3,2,1,0:T(8,128)(2,1)S(1)} %get-tuple-element.68), channel_id=1, source_target_pairs={{0,2},{2,0},{4,6},{6,4},{8,10},{10,8},{12,14},{14,12},{1,3},{3,1},... | collective-permute-start | bytes 884744 | tf_op jit(solution)/shard_map/ppermute | solution.py:385
  28.6 0.7 collective-permute-start.6
  29.3 0.0 collective-permute-done.4.edges
  29.3 11.4 %weight_terms.1 = (bf16[16,32,896]{2,1,0:T(8,128)(2,1)S(1)}, bf16[16,32,896]{2,1,0:T(8,128)(2,1)S(1)}, bf16[16,32,896]{2,1,0:T(8,128)(2,1)S(1)}, bf16[16,32,896]{2,1,0:T(8,128)(2,1)S(1)}) custom-call(s32[4]{0:T(128)S(1)} %copy-done.2, bf16[4,8,32,256]{3,2,1,0:T(8,128)(2,1)S(1)} %bitcast.76, bf16[4,8,32,256]{3,2,1,0:T(8,128)(2,1)S(1)} %bitcast.81, ...), custom_call_target="tpu_custom_call" | custom-call | flops 7247757312 | bytes 8388608 | tf_op jit(solution)/shard_map/weight_terms/pallas_call | solution.py:348
  40.7 4.6 %collective-permute-start.8 = (bf16[16,32,896]{2,1,0:T(8,128)(2,1)S(1)}, bf16[16,32,896]{2,1,0:T(8,128)(2,1)S(1)}, u32[]{:S(2)}, u32[]{:S(2)}) collective-permute-start(bf16[16,32,896]{2,1,0:T(8,128)(2,1)S(1)} %get-tuple-element.60), channel_id=1, source_target_pairs={{0,12},{2,14},{16,28},{18,30},{32,44},{34,46},{48,60},{50,62},{64,... | collective-permute-start | bytes 2752520 | tf_op jit(solution)/shard_map/ppermute | solution.py:391
  45.3 0.3 collective-permute-start.9
  45.6 0.0 collective-permute-done.5.near
  45.6 0.0 collective-permute-done.6.far
  45.6 1.1 %collective-permute-start.7 = (bf16[16,32,896]{2,1,0:T(8,128)(2,1)S(1)}, bf16[16,32,896]{2,1,0:T(8,128)(2,1)S(1)}, u32[]{:S(2)}, u32[]{:S(2)}) collective-permute-start(bf16[16,32,896]{2,1,0:T(8,128)(2,1)S(1)} %get-tuple-element.59), channel_id=1, source_target_pairs={{0,4},{2,6},{16,20},{18,22},{32,36},{34,38},{48,52},{50,54},{64,68... | collective-permute-start | bytes 2752520 | tf_op jit(solution)/shard_map/ppermute | solution.py:391
  46.7 7.4 %outputs_inner.1 = (bf16[2,8,32,256]{3,2,1,0:T(8,128)(2,1)S(1)}, bf16[2,8,32,256]{3,2,1,0:T(8,128)(2,1)S(1)}, f32[2,256,256]{2,1,0:T(8,128)S(1)}, f32[2,256,256]{2,1,0:T(8,128)S(1)}) custom-call(s32[4]{0:T(128)S(1)} %copy-done.2, bf16[4,8,32,256]{3,2,1,0:T(8,128)(2,1)S(1)} %get-tuple-element.47.hid, bf16[4,8,32,256]{3,2,1,0:T(8,128)(2,1)S(1)} %get-tuple-element.48.pre_grad, ...), custom_call_target="tpu_custom_call" | custom-call | flops 6039797760 | bytes 8388608 | tf_op jit(solution)/shard_map/outputs_inner/pallas_call | solution.py:348
  54.1 3.2 %outputs_outer.1 = (bf16[4,8,32,256]{3,2,1,0:T(8,128)(2,1)}, bf16[4,8,32,256]{3,2,1,0:T(8,128)(2,1)}) custom-call(s32[4]{0:T(128)S(1)} %copy-done.2, bf16[2,9,32,256]{3,2,1,0:T(8,128)(2,1)S(1)} %collective-permute-done.5.near, bf16[2,9,32,256]{3,2,1,0:T(8,128)(2,1)S(1)} %collective-permute-done.6.far, ...), custom_call_target="tpu_custom_call" | custom-call | flops 1207959552 | bytes 8388608 | tf_op jit(solution)/shard_map/outputs_outer/pallas_call | solution.py:348
  57.3 8.7 %collective-permute-done.8 = bf16[16,32,896]{2,1,0:T(8,128)(2,1)S(1)} collective-permute-done((bf16[16,32,896]{2,1,0:T(8,128)(2,1)S(1)}, bf16[16,32,896]{2,1,0:T(8,128)(2,1)S(1)}, u32[]{:S(2)}, u32[]{:S(2)}) %collective-permute-start.8) | collective-permute-done | bytes 917536 | tf_op jit(solution)/shard_map/ppermute | solution.py:391
  66.1 0.0 collective-permute-done.9
  66.1 4.0 %collective-permute-done.7 = bf16[16,32,896]{2,1,0:T(8,128)(2,1)S(1)} collective-permute-done((bf16[16,32,896]{2,1,0:T(8,128)(2,1)S(1)}, bf16[16,32,896]{2,1,0:T(8,128)(2,1)S(1)}, u32[]{:S(2)}, u32[]{:S(2)}) %collective-permute-start.7) | collective-permute-done | bytes 917536 | tf_op jit(solution)/shard_map/ppermute | solution.py:391
  70.0 0.5 fusion.5
  70.5 0.1 fusion.6
  70.6 1.6 %collective-permute-start.10 = (bf16[4,32,896]{2,1,0:T(8,128)(2,1)S(1)}, bf16[4,32,896]{2,1,0:T(8,128)(2,1)S(1)}, u32[]{:S(2)}, u32[]{:S(2)}) collective-permute-start(bf16[4,32,896]{2,1,0:T(8,128)(2,1)S(1)} %get-tuple-element.64), channel_id=1, source_target_pairs={{0,32},{2,34},{16,48},{18,50},{32,64},{34,66},{48,80},{50,82},{64,... | collective-permute-start | bytes 688136 | tf_op jit(solution)/shard_map/ppermute | solution.py:391
  72.2 1.7 %collective-permute-start.11 = (bf16[4,32,896]{2,1,0:T(8,128)(2,1)S(1)}, bf16[4,32,896]{2,1,0:T(8,128)(2,1)S(1)}, u32[]{:S(2)}, u32[]{:S(2)}) collective-permute-start(bf16[4,32,896]{2,1,0:T(8,128)(2,1)S(1)} %get-tuple-element.66), channel_id=1, source_target_pairs={{0,96},{2,98},{16,112},{18,114},{32,0},{34,2},{48,16},{50,18},{64,... | collective-permute-start | bytes 688136 | tf_op jit(solution)/shard_map/ppermute | solution.py:391
  73.9 2.0 %collective-permute-start.12 = (bf16[4,32,896]{2,1,0:T(8,128)(2,1)S(1)}, bf16[4,32,896]{2,1,0:T(8,128)(2,1)S(1)}, u32[]{:S(2)}, u32[]{:S(2)}) collective-permute-start(bf16[4,32,896]{2,1,0:T(8,128)(2,1)S(1)} %get-tuple-element.65), channel_id=1, source_target_pairs={{0,64},{2,66},{16,80},{18,82},{32,96},{34,98},{48,112},{50,114},{6... | collective-permute-start | bytes 688136 | tf_op jit(solution)/shard_map/ppermute | solution.py:391
  75.9 2.0 %collective-permute-done.10 = bf16[4,32,896]{2,1,0:T(8,128)(2,1)S(1)} collective-permute-done((bf16[4,32,896]{2,1,0:T(8,128)(2,1)S(1)}, bf16[4,32,896]{2,1,0:T(8,128)(2,1)S(1)}, u32[]{:S(2)}, u32[]{:S(2)}) %collective-permute-start.10) | collective-permute-done | bytes 229408 | tf_op jit(solution)/shard_map/ppermute | solution.py:391
  77.9 0.4 collective-permute-done.11
  78.3 3.3 %collective-permute-done.12 = bf16[4,32,896]{2,1,0:T(8,128)(2,1)S(1)} collective-permute-done((bf16[4,32,896]{2,1,0:T(8,128)(2,1)S(1)}, bf16[4,32,896]{2,1,0:T(8,128)(2,1)S(1)}, u32[]{:S(2)}, u32[]{:S(2)}) %collective-permute-start.12) | collective-permute-done | bytes 229408 | tf_op jit(solution)/shard_map/ppermute | solution.py:391
  81.6 0.1 fusion.1
  81.7 0.1 collective-permute-start.13
  81.8 3.2 %collective-permute-start.14 = (f32[32,896]{1,0:T(8,128)S(1)}, f32[32,896]{1,0:T(8,128)S(1)}, u32[]{:S(2)}, u32[]{:S(2)}) collective-permute-start(f32[32,896]{1,0:T(8,128)S(1)} %get-tuple-element.85), channel_id=1, source_target_pairs={{0,18},{2,0},{16,2},{18,16},{32,50},{34,32},{48,34},{50,48},{64,82... | collective-permute-start | bytes 344072 | tf_op jit(solution)/shard_map/ppermute | solution.py:391
  85.0 2.5 %collective-permute-start.15 = (f32[32,896]{1,0:T(8,128)S(1)}, f32[32,896]{1,0:T(8,128)S(1)}, u32[]{:S(2)}, u32[]{:S(2)}) collective-permute-start(f32[32,896]{1,0:T(8,128)S(1)} %get-tuple-element.84), channel_id=1, source_target_pairs={{0,16},{2,18},{16,0},{18,2},{32,48},{34,50},{48,32},{50,34},{64,80... | collective-permute-start | bytes 344072 | tf_op jit(solution)/shard_map/ppermute | solution.py:391
  87.5 0.3 collective-permute-done.13
  87.8 0.4 collective-permute-done.14
  88.2 3.1 %collective-permute-done.15 = f32[32,896]{1,0:T(8,128)S(1)} collective-permute-done((f32[32,896]{1,0:T(8,128)S(1)}, f32[32,896]{1,0:T(8,128)S(1)}, u32[]{:S(2)}, u32[]{:S(2)}) %collective-permute-start.15) | collective-permute-done | bytes 114720 | tf_op jit(solution)/shard_map/ppermute | solution.py:391
  91.4 0.1 collective-permute-start.16
  91.5 1.2 %collective-permute-done.16 = f32[16,896]{1,0:T(8,128)S(1)} collective-permute-done((f32[16,896]{1,0:T(8,128)S(1)}, f32[16,896]{1,0:T(8,128)S(1)}, u32[]{:S(2)}, u32[]{:S(2)}) %collective-permute-start.16) | collective-permute-done | bytes 57376 | tf_op jit(solution)/shard_map/ppermute | solution.py:367
  92.7 0.7 select_bitcast_fusion
  (23 shorter events, 0.4 us)
Async XLA Ops:
  0.6 3.4 %copy-start = (bf16[1,4,8,32,256]{4,3,2,1,0:T(8,128)(2,1)S(1)}, bf16[1,4,8,32,256]{4,3,2,1,0:T(8,128)(2,1)}, u32[]{:S(2)}) copy-start(bf16[1,4,8,32,256]{4,3,2,1,0:T(8,128)(2,1)} %param.5) | copy-start | bytes 1572868
  0.6 3.4 %copy-start.1 = (bf16[1,4,8,32,256]{4,3,2,1,0:T(8,128)(2,1)S(1)}, bf16[1,4,8,32,256]{4,3,2,1,0:T(8,128)(2,1)}, u32[]{:S(2)}) copy-start(bf16[1,4,8,32,256]{4,3,2,1,0:T(8,128)(2,1)} %param.4) | copy-start | bytes 1572868
  3.9 2.3 %collective-permute-start = (bf16[4,9,32,256]{3,2,1,0:T(8,128)(2,1)}, bf16[4,9,32,256]{3,2,1,0:T(8,128)(2,1)S(1)}, u32[]{:S(2)}, u32[]{:S(2)}) collective-permute-start(bf16[4,9,32,256]{3,2,1,0:T(8,128)(2,1)} %pack.1), channel_id=1, source_target_pairs={{0,1},{1,0},{2,3},{3,2},{4,5},{5,4},{6,7},{7,6},{8,9},{9,8},{10,11... | collective-permute-start | bytes 1769480 | tf_op jit(solution)/shard_map/ppermute | solution.py:367
  4.0 5.1 %copy-start.2 = (s32[4]{0:T(128)S(1)}, s32[4]{0:T(128)}, u32[]{:S(2)}) copy-start(s32[4]{0:T(128)} %pad_add_fusion.place) | copy-start | bytes 52
  6.4 15.0 %collective-permute-start.1 = (bf16[2,9,32,256]{3,2,1,0:T(8,128)(2,1)S(1)}, bf16[2,9,32,256]{3,2,1,0:T(8,128)(2,1)S(1)}, u32[]{:S(2)}, u32[]{:S(2)}) collective-permute-start(bf16[2,9,32,256]{3,2,1,0:T(8,128)(2,1)S(1)} %get-tuple-element.72), channel_id=1, source_target_pairs={{0,2},{2,0},{4,6},{6,4},{8,10},{10,8},{12,14},{14,12},{1,3},{3,1},... | collective-permute-start | bytes 884744 | tf_op jit(solution)/shard_map/ppermute | solution.py:385
  8.5 12.9 %collective-permute-start.2 = (bf16[2,9,32,256]{3,2,1,0:T(8,128)(2,1)S(1)}, bf16[2,9,32,256]{3,2,1,0:T(8,128)(2,1)S(1)}, u32[]{:S(2)}, u32[]{:S(2)}) collective-permute-start(bf16[2,9,32,256]{3,2,1,0:T(8,128)(2,1)S(1)} %get-tuple-element.71), channel_id=1, source_target_pairs={{2,4},{4,2},{6,8},{8,6},{10,12},{12,10},{3,5},{5,3},{7,9},{9,7},{1... | collective-permute-start | bytes 884744 | tf_op jit(solution)/shard_map/ppermute | solution.py:384
  23.7 2.1 %collective-permute-start.3 = (bf16[4,9,32,256]{3,2,1,0:T(8,128)(2,1)S(1)}, bf16[4,9,32,256]{3,2,1,0:T(8,128)(2,1)S(1)}, u32[]{:S(2)}, u32[]{:S(2)}) collective-permute-start(bf16[4,9,32,256]{3,2,1,0:T(8,128)(2,1)S(1)} %get-tuple-element.41), channel_id=1, source_target_pairs={{0,1},{1,0},{2,3},{3,2},{4,5},{5,4},{6,7},{7,6},{8,9},{9,8},{10,11... | collective-permute-start | bytes 1769480 | tf_op jit(solution)/shard_map/ppermute | solution.py:367
  23.9 5.3 %collective-permute-start.4 = (bf16[2,8,32,256]{3,2,1,0:T(8,128)(2,1)S(1)}, bf16[2,8,32,256]{3,2,1,0:T(8,128)(2,1)S(1)}, u32[]{:S(2)}, u32[]{:S(2)}) collective-permute-start(bf16[2,8,32,256]{3,2,1,0:T(8,128)(2,1)S(1)} %maximum_select_fusion), channel_id=1, source_target_pairs={{0,1},{1,0},{2,3},{3,2},{4,5},{5,4},{6,7},{7,6},{8,9},{9,8},{10,11... | collective-permute-start | bytes 786440 | tf_op jit(solution)/shard_map/ppermute | solution.py:367
  26.0 19.6 %collective-permute-start.5 = (bf16[2,9,32,256]{3,2,1,0:T(8,128)(2,1)S(1)}, bf16[2,9,32,256]{3,2,1,0:T(8,128)(2,1)S(1)}, u32[]{:S(2)}, u32[]{:S(2)}) collective-permute-start(bf16[2,9,32,256]{3,2,1,0:T(8,128)(2,1)S(1)} %get-tuple-element.68), channel_id=1, source_target_pairs={{0,2},{2,0},{4,6},{6,4},{8,10},{10,8},{12,14},{14,12},{1,3},{3,1},... | collective-permute-start | bytes 884744 | tf_op jit(solution)/shard_map/ppermute | solution.py:385
  28.6 17.0 %collective-permute-start.6 = (bf16[2,9,32,256]{3,2,1,0:T(8,128)(2,1)S(1)}, bf16[2,9,32,256]{3,2,1,0:T(8,128)(2,1)S(1)}, u32[]{:S(2)}, u32[]{:S(2)}) collective-permute-start(bf16[2,9,32,256]{3,2,1,0:T(8,128)(2,1)S(1)} %get-tuple-element.67), channel_id=1, source_target_pairs={{2,4},{4,2},{6,8},{8,6},{10,12},{12,10},{3,5},{5,3},{7,9},{9,7},{1... | collective-permute-start | bytes 884744 | tf_op jit(solution)/shard_map/ppermute | solution.py:384
  40.7 25.4 %collective-permute-start.8 = (bf16[16,32,896]{2,1,0:T(8,128)(2,1)S(1)}, bf16[16,32,896]{2,1,0:T(8,128)(2,1)S(1)}, u32[]{:S(2)}, u32[]{:S(2)}) collective-permute-start(bf16[16,32,896]{2,1,0:T(8,128)(2,1)S(1)} %get-tuple-element.60), channel_id=1, source_target_pairs={{0,12},{2,14},{16,28},{18,30},{32,44},{34,46},{48,60},{50,62},{64,... | collective-permute-start | bytes 2752520 | tf_op jit(solution)/shard_map/ppermute | solution.py:391
  45.3 20.7 %collective-permute-start.9 = (bf16[16,32,896]{2,1,0:T(8,128)(2,1)S(1)}, bf16[16,32,896]{2,1,0:T(8,128)(2,1)S(1)}, u32[]{:S(2)}, u32[]{:S(2)}) collective-permute-start(bf16[16,32,896]{2,1,0:T(8,128)(2,1)S(1)} %get-tuple-element.61), channel_id=1, source_target_pairs={{0,8},{2,10},{16,24},{18,26},{32,40},{34,42},{48,56},{50,58},{64,7... | collective-permute-start | bytes 2752520 | tf_op jit(solution)/shard_map/ppermute | solution.py:391
  45.6 24.5 %collective-permute-start.7 = (bf16[16,32,896]{2,1,0:T(8,128)(2,1)S(1)}, bf16[16,32,896]{2,1,0:T(8,128)(2,1)S(1)}, u32[]{:S(2)}, u32[]{:S(2)}) collective-permute-start(bf16[16,32,896]{2,1,0:T(8,128)(2,1)S(1)} %get-tuple-element.59), channel_id=1, source_target_pairs={{0,4},{2,6},{16,20},{18,22},{32,36},{34,38},{48,52},{50,54},{64,68... | collective-permute-start | bytes 2752520 | tf_op jit(solution)/shard_map/ppermute | solution.py:391
  70.6 7.3 %collective-permute-start.10 = (bf16[4,32,896]{2,1,0:T(8,128)(2,1)S(1)}, bf16[4,32,896]{2,1,0:T(8,128)(2,1)S(1)}, u32[]{:S(2)}, u32[]{:S(2)}) collective-permute-start(bf16[4,32,896]{2,1,0:T(8,128)(2,1)S(1)} %get-tuple-element.64), channel_id=1, source_target_pairs={{0,32},{2,34},{16,48},{18,50},{32,64},{34,66},{48,80},{50,82},{64,... | collective-permute-start | bytes 688136 | tf_op jit(solution)/shard_map/ppermute | solution.py:391
  72.2 6.0 %collective-permute-start.11 = (bf16[4,32,896]{2,1,0:T(8,128)(2,1)S(1)}, bf16[4,32,896]{2,1,0:T(8,128)(2,1)S(1)}, u32[]{:S(2)}, u32[]{:S(2)}) collective-permute-start(bf16[4,32,896]{2,1,0:T(8,128)(2,1)S(1)} %get-tuple-element.66), channel_id=1, source_target_pairs={{0,96},{2,98},{16,112},{18,114},{32,0},{34,2},{48,16},{50,18},{64,... | collective-permute-start | bytes 688136 | tf_op jit(solution)/shard_map/ppermute | solution.py:391
  73.9 7.7 %collective-permute-start.12 = (bf16[4,32,896]{2,1,0:T(8,128)(2,1)S(1)}, bf16[4,32,896]{2,1,0:T(8,128)(2,1)S(1)}, u32[]{:S(2)}, u32[]{:S(2)}) collective-permute-start(bf16[4,32,896]{2,1,0:T(8,128)(2,1)S(1)} %get-tuple-element.65), channel_id=1, source_target_pairs={{0,64},{2,66},{16,80},{18,82},{32,96},{34,98},{48,112},{50,114},{6... | collective-permute-start | bytes 688136 | tf_op jit(solution)/shard_map/ppermute | solution.py:391
  81.7 6.1 %collective-permute-start.13 = (f32[32,896]{1,0:T(8,128)S(1)}, f32[32,896]{1,0:T(8,128)S(1)}, u32[]{:S(2)}, u32[]{:S(2)}) collective-permute-start(f32[32,896]{1,0:T(8,128)S(1)} %get-tuple-element.83), channel_id=1, source_target_pairs={{0,2},{2,16},{16,18},{18,0},{32,34},{34,48},{48,50},{50,32},{64,66... | collective-permute-start | bytes 344072 | tf_op jit(solution)/shard_map/ppermute | solution.py:391
  81.8 6.4 %collective-permute-start.14 = (f32[32,896]{1,0:T(8,128)S(1)}, f32[32,896]{1,0:T(8,128)S(1)}, u32[]{:S(2)}, u32[]{:S(2)}) collective-permute-start(f32[32,896]{1,0:T(8,128)S(1)} %get-tuple-element.85), channel_id=1, source_target_pairs={{0,18},{2,0},{16,2},{18,16},{32,50},{34,32},{48,34},{50,48},{64,82... | collective-permute-start | bytes 344072 | tf_op jit(solution)/shard_map/ppermute | solution.py:391
  85.0 6.3 %collective-permute-start.15 = (f32[32,896]{1,0:T(8,128)S(1)}, f32[32,896]{1,0:T(8,128)S(1)}, u32[]{:S(2)}, u32[]{:S(2)}) collective-permute-start(f32[32,896]{1,0:T(8,128)S(1)} %get-tuple-element.84), channel_id=1, source_target_pairs={{0,16},{2,18},{16,0},{18,2},{32,48},{34,50},{48,32},{50,34},{64,80... | collective-permute-start | bytes 344072 | tf_op jit(solution)/shard_map/ppermute | solution.py:391
  91.4 1.3 %collective-permute-start.16 = (f32[16,896]{1,0:T(8,128)S(1)}, f32[16,896]{1,0:T(8,128)S(1)}, u32[]{:S(2)}, u32[]{:S(2)}) collective-permute-start(f32[16,896]{1,0:T(8,128)S(1)} %get-tuple-element.93), channel_id=1, source_target_pairs={{0,1},{1,0},{2,3},{3,2},{4,5},{5,4},{6,7},{7,6},{8,9},{9,8},{10,11... | collective-permute-start | bytes 172040 | tf_op jit(solution)/shard_map/ppermute | solution.py:367

commit v5 on v4

--- a/solution.py
+++ b/solution.py
@@ -9,13 +9,20 @@
 F32 = jnp.float32
 ALL = ("dp", "px", "py")
 X, Y, Z = 0, 1, 2
-ORDER = ((X, Y, Z), (Y, Z, X))
+ORDER = ((X, Z), (Z, X))
 LANES = 896
 
 
 def device(x, y, z, core):
     x, y, z = x % 4, y % 4, z % 4
     return (y * 2 + z // 2) * 16 + (x * 2 + z % 2) * 2 + core
+
+
+LAST_GROUPS = [
+    [device(x, y, z, core) for y in range(4) for core in range(2)]
+    for x in range(4)
+    for z in range(4)
+]
 
 
 def hop_pairs(stage, distance):
@@ -326,16 +333,15 @@
 
     for k in range(8):
         tiles[k] = flat[:, k * 864 : k * 864 + LANES]
-    x, y, z = place[1], place[2], place[3]
+    x, z = place[1], place[3]
     zero = core == 0
     for first, ref in enumerate((own, send1, send2, send3)):
 
         def pick(i, _):
             second, third = i // 4, i % 4
-            to_x = lax.rem(x + jnp.where(zero, first, third), 4)
-            to_y = lax.rem(y + jnp.where(zero, second, first), 4)
-            to_z = lax.rem(z + jnp.where(zero, third, second), 4)
-            to_dp = to_y * 2 + to_z // 2
+            to_x = lax.rem(x + jnp.where(zero, first, second), 4)
+            to_z = lax.rem(z + jnp.where(zero, second, first), 4)
+            to_dp = third * 2 + to_z // 2
             to_px = to_x * 2 + lax.rem(to_z, 2)
             ref[i] = tiles[to_dp, pl.ds(pl.multiple_of(to_px * 32, 32), 32), :]
             return 0
@@ -393,7 +399,7 @@
     ]
 
 
-def reduce_tiles(own, got, core):
+def reduce_tiles(own, got):
     total = own.astype(F32)
     for part in got:
         total = total + part.astype(F32)
@@ -401,14 +407,11 @@
     total = total[0:4]
     for part in got:
         total = total + part.astype(F32)
-    got = hop([total[d] for d in (1, 3, 2)], 2)
-    total = total[0] + got[0] + got[1] + got[2]
-    keep = jnp.where(core == 0, total[:16], total[16:])
-    give = jnp.where(core == 0, total[16:], total[:16])
-    other = swap_cores(give)
-    first = jnp.where(core == 0, keep, other)[:, :864]
-    second = jnp.where(core == 0, other, keep)[:, :864]
-    return first.T, second.T
+    parts = lax.all_to_all(
+        total.reshape(8, 16, LANES), ALL, 0, 0, tiled=True, axis_index_groups=LAST_GROUPS
+    )
+    sums = parts.reshape(4, 2, 16, LANES).sum(axis=0)
+    return sums[0, :, :864].T, sums[1, :, :864].T
 
 
 def body(fields, cotangent, first_weight, second_weight):
@@ -433,10 +436,10 @@
         pack_kernel,
         "pack",
         0,
-        (place, cot, field),
+        (core.astype(jnp.int32).reshape(1), cot, field),
         [shape((4, 9, 32, 256), BF)],
         [pltpu.SemaphoreType.DMA((2,))],
-        56,
+        40,
         (1, 2),
     )
     other1 = swap_cores(sent1)
@@ -454,7 +457,7 @@
         (place, cot, field, other1, *weights),
         [half, half, part, part, shape((6912, 256), BF), shape((6912, 256), BF)],
         own_scratch + [pltpu.SemaphoreType.DMA((2,))],
-        42,
+        38,
         (4, 5),
     )
     inner, weights = inner[:4], inner[4:]
@@ -519,7 +522,7 @@
         24,
     )
     own, output, field_grad = lax.optimization_barrier((own, output, field_grad))
-    first_grad, second_grad = reduce_tiles(own, got, core)
+    first_grad, second_grad = reduce_tiles(own, got)
     return output[None], field_grad[None], first_grad, second_grad
 
 

time: 94.6 us -> 95.5 us (level)
  blocking collectives: 0 us -> 14 us
  waiting for transfers between devices: 29 us -> 22.8 us
  starting transfers between devices: 23.9 us -> 18.5 us
  local copies, waits for them, and re-layouts: 0.24 us -> 3.82 us
  Pallas kernels: 37 us -> 33.8 us
  other arithmetic: 2.25 us -> 1 us
    all_to_all x0 -> x1, blocking collectives: none -> 14 us  [reduce_tiles(): lax.all_to_all(total.reshape(8, 16, LANES), ALL, 0, 0, tiled=True, axis_i...]
    ppermute x9 -> x6, starting transfers between devices: 17.1 us -> 11.8 us  [hop(): lax.ppermute(part, ALL, hop_pairs(stage, distance))]
    ppermute x9 -> x6, waiting for transfers between devices: 22.2 us -> 17.8 us  [hop(): lax.ppermute(part, ALL, hop_pairs(stage, distance))]
    pallas_call x6, Pallas kernels: 37 us -> 33.8 us  [call(): pl.pallas_call(kernel, name=name, out_shape=outs, in_specs=[pl.BlockSpec(...]
    unnamed x6 -> x10, local copies, waits for them, and re-layouts: 0.02 us -> 2.98 us
    ppermute x4 -> x3, waiting for transfers between devices: 4.6 us -> 2.21 us  [swap_cores(): return lax.ppermute(value, 'py', [(0, 1), (1, 0)])]
  transfers between devices with their start and end apart: 17 -> 13, of which waited for: 12 -> 8; matrix products, arithmetic and copies ran while one was open for 0% -> 0% of each run, Pallas kernels for 34% -> 33%
where the time goes in v5:
time: 95.5 us; the launch traced here: 94.8 us
  Pallas kernels  33.8 us (35%)
  waiting for transfers between devices  22.8 us (24%)
  starting transfers between devices  18.5 us (19%)
  blocking collectives  14 us (15%)
  local copies, waits for them, and re-layouts  3.82 us (4%)
  other arithmetic  1 us (1%)
    pallas_call x6, Pallas kernels, call(): pl.pallas_call(kernel, name=name, out_shape=outs, in_specs=[pl.BlockSpec(...  33.8 us
    ppermute x6, waiting for transfers between devices, hop(): lax.ppermute(part, ALL, hop_pairs(stage, distance))  17.8 us
    all_to_all x1, blocking collectives, reduce_tiles(): lax.all_to_all(total.reshape(8, 16, LANES), ALL, 0, 0, tiled=True, axis_i...  14 us
    ppermute x6, starting transfers between devices, hop(): lax.ppermute(part, ALL, hop_pairs(stage, distance))  11.8 us
    ppermute x2, starting transfers between devices, swap_slabs(): got_near = lax.ppermute(jnp.where(low_half, high, low), 'px', near)  4.64 us
    unnamed x10, local copies, waits for them, and re-layouts  2.98 us
    ppermute x2, waiting for transfers between devices, swap_slabs(): got_near = lax.ppermute(jnp.where(low_half, high, low), 'px', near)  2.8 us
    ppermute x3, waiting for transfers between devices, swap_cores(): return lax.ppermute(value, 'py', [(0, 1), (1, 0)])  2.21 us
  transfers between devices with their start and end apart: 13, of which 8 were waited for; matrix products, arithmetic and copies ran while one was open for 0% of the time, Pallas kernels for 33%

profile of v5, /device:TPU:0, one launch (start us, length us, event | category | flops | bytes accessed | tf_op | source)
XLA Modules:
  0.0 94.8 jit_solution(7402019806712067382)
XLA Ops:
  0.6 0.0 copy-start
  0.6 1.0 %copy-done = bf16[1,4,8,32,256]{4,3,2,1,0:T(8,128)(2,1)S(1)} copy-done((bf16[1,4,8,32,256]{4,3,2,1,0:T(8,128)(2,1)S(1)}, bf16[1,4,8,32,256]{4,3,2,1,0:T(8,128)(2,1)}, u32[]{:S(2)}) %copy-start) | copy-done | bytes 524312
  1.7 0.0 copy-start.2
  1.7 1.0 %copy-done.2 = bf16[1,4,8,32,256]{4,3,2,1,0:T(8,128)(2,1)S(1)} copy-done((bf16[1,4,8,32,256]{4,3,2,1,0:T(8,128)(2,1)S(1)}, bf16[1,4,8,32,256]{4,3,2,1,0:T(8,128)(2,1)}, u32[]{:S(2)}) %copy-start.2) | copy-done | bytes 524312
  2.7 0.0 copy-start.1
  2.7 0.0 copy-start.3
  2.7 0.1 pack.1
  2.8 0.1 collective-permute-start
  2.9 0.1 pad_add_fusion.place
  3.0 0.8 copy-done.1
  3.8 0.0 copy-start.4
  3.8 0.1 copy-done.3
  3.9 1.0 %collective-permute-done.other.other1 = bf16[4,9,32,256]{3,2,1,0:T(8,128)(2,1)S(1)} collective-permute-done((bf16[4,9,32,256]{3,2,1,0:T(8,128)(2,1)S(1)}, bf16[4,9,32,256]{3,2,1,0:T(8,128)(2,1)S(1)}, u32[]{:S(2)}, u32[]{:S(2)}) %collective-permute-start) | collective-permute-done | bytes 589856 | tf_op jit(solution)/shard_map/ppermute | solution.py:373
  5.0 0.1 broadcast_select_fusion.2
  5.1 2.1 %collective-permute-start.1 = (bf16[2,9,32,256]{3,2,1,0:T(8,128)(2,1)S(1)}, bf16[2,9,32,256]{3,2,1,0:T(8,128)(2,1)S(1)}, u32[]{:S(2)}, u32[]{:S(2)}) collective-permute-start(bf16[2,9,32,256]{3,2,1,0:T(8,128)(2,1)S(1)} %get-tuple-element.72), channel_id=1, source_target_pairs={{0,2},{2,0},{4,6},{6,4},{8,10},{10,8},{12,14},{14,12},{1,3},{3,1},... | collective-permute-start | bytes 884744 | tf_op jit(solution)/shard_map/ppermute | solution.py:391
  7.2 0.7 collective-permute-start.2
  7.8 0.0 copy-done.4
  7.9 9.4 %inner.1 = (bf16[2,8,32,256]{3,2,1,0:T(8,128)(2,1)S(1)}, bf16[2,8,32,256]{3,2,1,0:T(8,128)(2,1)S(1)}, f32[2,256,256]{2,1,0:T(8,128)S(1)}, f32[2,256,256]{2,1,0:T...) custom-call(s32[4]{0:T(128)S(1)} %pad_add_fusion.place, bf16[4,8,32,256]{3,2,1,0:T(8,128)(2,1)S(1)} %bitcast.67, ...), custom_call_target="tpu_custom_call" | custom-call | flops 6039797760 | bytes 8388608 | tf_op jit(solution)/shard_map/inner/pallas_call | solution.py:354
  17.3 2.8 %collective-permute-done.1.near.near1 = bf16[2,9,32,256]{3,2,1,0:T(8,128)(2,1)S(1)} collective-permute-done((bf16[2,9,32,256]{3,2,1,0:T(8,128)(2,1)S(1)}, bf16[2,9,32,256]{3,2,1,0:T(8,128)(2,1)S(1)}, u32[]{:S(2)}, u32[]{:S(2)}) %collective-permute-start.1) | collective-permute-done | bytes 294944 | tf_op jit(solution)/shard_map/ppermute | solution.py:391
  20.1 0.0 collective-permute-done.2.far.far1
  20.1 2.4 %outer.1 = (bf16[4,8,32,256]{3,2,1,0:T(8,128)(2,1)S(1)}, bf16[4,8,32,256]{3,2,1,0:T(8,128)(2,1)S(1)}, bf16[4,9,32,256]{3,2,1,0:T(8,128)(2,1)S(1)}) custom-call(s32[4]{0:T(128)S(1)} %pad_add_fusion.place, bf16[2,9,32,256]{3,2,1,0:T(8,128)(2,1)S(1)} %collective-permute-done.1.near.near1, bf16[2,9,32,256]{3,2,1,0:T(8,128)(2,1)S(1)} %collective-permute-done.2.far.far1, ...), custom_call_target="tpu_custom_call" | custom-call | flops 1207959552 | bytes 8388608 | tf_op jit(solution)/shard_map/outer/pallas_call | solution.py:354
  22.4 0.1 collective-permute-start.3
  22.6 0.6 collective-permute-start.4
  23.3 1.3 %collective-permute-done.3.other2.other = bf16[4,9,32,256]{3,2,1,0:T(8,128)(2,1)S(1)} collective-permute-done((bf16[4,9,32,256]{3,2,1,0:T(8,128)(2,1)S(1)}, bf16[4,9,32,256]{3,2,1,0:T(8,128)(2,1)S(1)}, u32[]{:S(2)}, u32[]{:S(2)}) %collective-permute-start.3) | collective-permute-done | bytes 589856 | tf_op jit(solution)/shard_map/ppermute | solution.py:373
  24.7 0.1 broadcast_select_fusion
  24.7 2.6 %collective-permute-start.5 = (bf16[2,9,32,256]{3,2,1,0:T(8,128)(2,1)S(1)}, bf16[2,9,32,256]{3,2,1,0:T(8,128)(2,1)S(1)}, u32[]{:S(2)}, u32[]{:S(2)}) collective-permute-start(bf16[2,9,32,256]{3,2,1,0:T(8,128)(2,1)S(1)} %get-tuple-element.68), channel_id=1, source_target_pairs={{0,2},{2,0},{4,6},{6,4},{8,10},{10,8},{12,14},{14,12},{1,3},{3,1},... | collective-permute-start | bytes 884744 | tf_op jit(solution)/shard_map/ppermute | solution.py:391
  27.3 0.7 collective-permute-start.6
  28.0 0.0 collective-permute-done.4.edges
  28.0 11.3 %weight_terms.1 = (bf16[16,32,896]{2,1,0:T(8,128)(2,1)S(1)}, bf16[16,32,896]{2,1,0:T(8,128)(2,1)S(1)}, bf16[16,32,896]{2,1,0:T(8,128)(2,1)S(1)}, bf16[16,32,896]{2,1,0:T(8,128)(2,1)S(1)}) custom-call(s32[4]{0:T(128)S(1)} %pad_add_fusion.place, bf16[4,8,32,256]{3,2,1,0:T(8,128)(2,1)S(1)} %bitcast.68, bf16[4,8,32,256]{3,2,1,0:T(8,128)(2,1)S(1)} %bitcast.73, ...), custom_call_target="tpu_custom_call" | custom-call | flops 7247757312 | bytes 8388608 | tf_op jit(solution)/shard_map/weight_terms/pallas_call | solution.py:354
  39.3 4.6 %collective-permute-start.8 = (bf16[16,32,896]{2,1,0:T(8,128)(2,1)S(1)}, bf16[16,32,896]{2,1,0:T(8,128)(2,1)S(1)}, u32[]{:S(2)}, u32[]{:S(2)}) collective-permute-start(bf16[16,32,896]{2,1,0:T(8,128)(2,1)S(1)} %get-tuple-element.60), channel_id=1, source_target_pairs={{0,12},{2,14},{16,28},{18,30},{32,44},{34,46},{48,60},{50,62},{64,... | collective-permute-start | bytes 2752520 | tf_op jit(solution)/shard_map/ppermute | solution.py:397
  43.9 0.3 collective-permute-start.9
  44.2 0.0 collective-permute-done.5.near
  44.2 0.0 collective-permute-done.6.far
  44.2 1.1 %collective-permute-start.7 = (bf16[16,32,896]{2,1,0:T(8,128)(2,1)S(1)}, bf16[16,32,896]{2,1,0:T(8,128)(2,1)S(1)}, u32[]{:S(2)}, u32[]{:S(2)}) collective-permute-start(bf16[16,32,896]{2,1,0:T(8,128)(2,1)S(1)} %get-tuple-element.59), channel_id=1, source_target_pairs={{0,4},{2,6},{16,20},{18,22},{32,36},{34,38},{48,52},{50,54},{64,68... | collective-permute-start | bytes 2752520 | tf_op jit(solution)/shard_map/ppermute | solution.py:397
  45.3 7.4 %outputs_inner.1 = (bf16[2,8,32,256]{3,2,1,0:T(8,128)(2,1)S(1)}, bf16[2,8,32,256]{3,2,1,0:T(8,128)(2,1)S(1)}, f32[2,256,256]{2,1,0:T(8,128)S(1)}, f32[2,256,256]{2,1,0:T(8,128)S(1)}) custom-call(s32[4]{0:T(128)S(1)} %pad_add_fusion.place, bf16[4,8,32,256]{3,2,1,0:T(8,128)(2,1)S(1)} %get-tuple-element.47.hid, ...), custom_call_target="tpu_custom_call" | custom-call | flops 6039797760 | bytes 8388608 | tf_op jit(solution)/shard_map/outputs_inner/pallas_call | solution.py:354
  52.7 3.2 %outputs_outer.1 = (bf16[4,8,32,256]{3,2,1,0:T(8,128)(2,1)}, bf16[4,8,32,256]{3,2,1,0:T(8,128)(2,1)}) custom-call(s32[4]{0:T(128)S(1)} %pad_add_fusion.place, bf16[2,9,32,256]{3,2,1,0:T(8,128)(2,1)S(1)} %collective-permute-done.5.near, bf16[2,9,32,256]{3,2,1,0:T(8,128)(2,1)S(1)} %collective-permute-done.6.far, ...), custom_call_target="tpu_custom_call" | custom-call | flops 1207959552 | bytes 8388608 | tf_op jit(solution)/shard_map/outputs_outer/pallas_call | solution.py:354
  55.9 8.7 %collective-permute-done.8 = bf16[16,32,896]{2,1,0:T(8,128)(2,1)S(1)} collective-permute-done((bf16[16,32,896]{2,1,0:T(8,128)(2,1)S(1)}, bf16[16,32,896]{2,1,0:T(8,128)(2,1)S(1)}, u32[]{:S(2)}, u32[]{:S(2)}) %collective-permute-start.8) | collective-permute-done | bytes 917536 | tf_op jit(solution)/shard_map/ppermute | solution.py:397
  64.6 0.0 collective-permute-done.9
  64.6 4.0 %collective-permute-done.7 = bf16[16,32,896]{2,1,0:T(8,128)(2,1)S(1)} collective-permute-done((bf16[16,32,896]{2,1,0:T(8,128)(2,1)S(1)}, bf16[16,32,896]{2,1,0:T(8,128)(2,1)S(1)}, u32[]{:S(2)}, u32[]{:S(2)}) %collective-permute-start.7) | collective-permute-done | bytes 917536 | tf_op jit(solution)/shard_map/ppermute | solution.py:397
  68.6 0.5 fusion.2
  69.1 0.1 fusion.3
  69.2 0.1 collective-permute-start.10
  69.3 3.2 %collective-permute-start.11 = (bf16[4,32,896]{2,1,0:T(8,128)(2,1)S(1)}, bf16[4,32,896]{2,1,0:T(8,128)(2,1)S(1)}, u32[]{:S(2)}, u32[]{:S(2)}) collective-permute-start(bf16[4,32,896]{2,1,0:T(8,128)(2,1)S(1)} %get-tuple-element.66), channel_id=1, source_target_pairs={{0,18},{2,0},{16,2},{18,16},{32,50},{34,32},{48,34},{50,48},{64,82... | collective-permute-start | bytes 688136 | tf_op jit(solution)/shard_map/ppermute | solution.py:397
  72.5 2.5 %collective-permute-start.12 = (bf16[4,32,896]{2,1,0:T(8,128)(2,1)S(1)}, bf16[4,32,896]{2,1,0:T(8,128)(2,1)S(1)}, u32[]{:S(2)}, u32[]{:S(2)}) collective-permute-start(bf16[4,32,896]{2,1,0:T(8,128)(2,1)S(1)} %get-tuple-element.65), channel_id=1, source_target_pairs={{0,16},{2,18},{16,0},{18,2},{32,48},{34,50},{48,32},{50,34},{64,80... | collective-permute-start | bytes 688136 | tf_op jit(solution)/shard_map/ppermute | solution.py:397
  75.0 1.5 %collective-permute-done.10 = bf16[4,32,896]{2,1,0:T(8,128)(2,1)S(1)} collective-permute-done((bf16[4,32,896]{2,1,0:T(8,128)(2,1)S(1)}, bf16[4,32,896]{2,1,0:T(8,128)(2,1)S(1)}, u32[]{:S(2)}, u32[]{:S(2)}) %collective-permute-start.10) | collective-permute-done | bytes 229408 | tf_op jit(solution)/shard_map/ppermute | solution.py:397
  76.5 0.4 collective-permute-done.11
  76.9 3.1 %collective-permute-done.12 = bf16[4,32,896]{2,1,0:T(8,128)(2,1)S(1)} collective-permute-done((bf16[4,32,896]{2,1,0:T(8,128)(2,1)S(1)}, bf16[4,32,896]{2,1,0:T(8,128)(2,1)S(1)}, u32[]{:S(2)}, u32[]{:S(2)}) %collective-permute-start.12) | collective-permute-done | bytes 229408 | tf_op jit(solution)/shard_map/ppermute | solution.py:397
  80.0 0.1 fusion.1
  80.1 14.0 %all_to_all.5 = f32[8,16,896]{2,1,0:T(8,128)S(1)} all-to-all(f32[8,16,896]{2,1,0:T(8,128)S(1)} %bitcast.76), channel_id=1, replica_groups={{0,1,32,33,64,65,96,97},{2,3,34,35,66,67,98,99},{16,17,48,49,80,81,112,..., dimensions={0} | all-to-all | bytes 917504 | tf_op jit(solution)/shard_map/all_to_all | solution.py:410
  94.1 0.6 slice_bitcast_fusion.8
  (21 shorter events, 0.4 us)
Async XLA Ops:
  0.6 1.0 %copy-start = (bf16[1,4,8,32,256]{4,3,2,1,0:T(8,128)(2,1)S(1)}, bf16[1,4,8,32,256]{4,3,2,1,0:T(8,128)(2,1)}, u32[]{:S(2)}) copy-start(bf16[1,4,8,32,256]{4,3,2,1,0:T(8,128)(2,1)} %param.5) | copy-start | bytes 1572868
  1.7 1.0 %copy-start.2 = (bf16[1,4,8,32,256]{4,3,2,1,0:T(8,128)(2,1)S(1)}, bf16[1,4,8,32,256]{4,3,2,1,0:T(8,128)(2,1)}, u32[]{:S(2)}) copy-start(bf16[1,4,8,32,256]{4,3,2,1,0:T(8,128)(2,1)} %param.4) | copy-start | bytes 1572868
  2.7 1.0 %copy-start.1 = (bf16[1,4,8,32,256]{4,3,2,1,0:T(8,128)(2,1)S(1)}, bf16[1,4,8,32,256]{4,3,2,1,0:T(8,128)(2,1)}, u32[]{:S(2)}) copy-start(bf16[1,4,8,32,256]{4,3,2,1,0:T(8,128)(2,1)} %param.5) | copy-start | bytes 1572868
  2.7 1.2 %copy-start.3 = (bf16[1,4,8,32,256]{4,3,2,1,0:T(8,128)(2,1)S(1)}, bf16[1,4,8,32,256]{4,3,2,1,0:T(8,128)(2,1)}, u32[]{:S(2)}) copy-start(bf16[1,4,8,32,256]{4,3,2,1,0:T(8,128)(2,1)} %param.4) | copy-start | bytes 1572868
  2.8 2.1 %collective-permute-start = (bf16[4,9,32,256]{3,2,1,0:T(8,128)(2,1)S(1)}, bf16[4,9,32,256]{3,2,1,0:T(8,128)(2,1)S(1)}, u32[]{:S(2)}, u32[]{:S(2)}) collective-permute-start(bf16[4,9,32,256]{3,2,1,0:T(8,128)(2,1)S(1)} %pack.1), channel_id=1, source_target_pairs={{0,1},{1,0},{2,3},{3,2},{4,5},{5,4},{6,7},{7,6},{8,9},{9,8},{10,11... | collective-permute-start | bytes 1769480 | tf_op jit(solution)/shard_map/ppermute | solution.py:373
  3.8 4.1 %copy-start.4 = (bf16[6912,256]{1,0:T(8,128)(2,1)S(1)}, bf16[6912,256]{1,0:T(8,128)(2,1)}, u32[]{:S(2)}) copy-start(bf16[6912,256]{1,0:T(8,128)(2,1)} %first_hbm.1) | copy-start | bytes 10616836
  5.1 15.0 %collective-permute-start.1 = (bf16[2,9,32,256]{3,2,1,0:T(8,128)(2,1)S(1)}, bf16[2,9,32,256]{3,2,1,0:T(8,128)(2,1)S(1)}, u32[]{:S(2)}, u32[]{:S(2)}) collective-permute-start(bf16[2,9,32,256]{3,2,1,0:T(8,128)(2,1)S(1)} %get-tuple-element.72), channel_id=1, source_target_pairs={{0,2},{2,0},{4,6},{6,4},{8,10},{10,8},{12,14},{14,12},{1,3},{3,1},... | collective-permute-start | bytes 884744 | tf_op jit(solution)/shard_map/ppermute | solution.py:391
  7.2 12.9 %collective-permute-start.2 = (bf16[2,9,32,256]{3,2,1,0:T(8,128)(2,1)S(1)}, bf16[2,9,32,256]{3,2,1,0:T(8,128)(2,1)S(1)}, u32[]{:S(2)}, u32[]{:S(2)}) collective-permute-start(bf16[2,9,32,256]{3,2,1,0:T(8,128)(2,1)S(1)} %get-tuple-element.71), channel_id=1, source_target_pairs={{2,4},{4,2},{6,8},{8,6},{10,12},{12,10},{3,5},{5,3},{7,9},{9,7},{1... | collective-permute-start | bytes 884744 | tf_op jit(solution)/shard_map/ppermute | solution.py:390
  22.4 2.1 %collective-permute-start.3 = (bf16[4,9,32,256]{3,2,1,0:T(8,128)(2,1)S(1)}, bf16[4,9,32,256]{3,2,1,0:T(8,128)(2,1)S(1)}, u32[]{:S(2)}, u32[]{:S(2)}) collective-permute-start(bf16[4,9,32,256]{3,2,1,0:T(8,128)(2,1)S(1)} %get-tuple-element.41), channel_id=1, source_target_pairs={{0,1},{1,0},{2,3},{3,2},{4,5},{5,4},{6,7},{7,6},{8,9},{9,8},{10,11... | collective-permute-start | bytes 1769480 | tf_op jit(solution)/shard_map/ppermute | solution.py:373
  22.6 5.3 %collective-permute-start.4 = (bf16[2,8,32,256]{3,2,1,0:T(8,128)(2,1)S(1)}, bf16[2,8,32,256]{3,2,1,0:T(8,128)(2,1)S(1)}, u32[]{:S(2)}, u32[]{:S(2)}) collective-permute-start(bf16[2,8,32,256]{3,2,1,0:T(8,128)(2,1)S(1)} %maximum_select_fusion), channel_id=1, source_target_pairs={{0,1},{1,0},{2,3},{3,2},{4,5},{5,4},{6,7},{7,6},{8,9},{9,8},{10,11... | collective-permute-start | bytes 786440 | tf_op jit(solution)/shard_map/ppermute | solution.py:373
  24.7 19.4 %collective-permute-start.5 = (bf16[2,9,32,256]{3,2,1,0:T(8,128)(2,1)S(1)}, bf16[2,9,32,256]{3,2,1,0:T(8,128)(2,1)S(1)}, u32[]{:S(2)}, u32[]{:S(2)}) collective-permute-start(bf16[2,9,32,256]{3,2,1,0:T(8,128)(2,1)S(1)} %get-tuple-element.68), channel_id=1, source_target_pairs={{0,2},{2,0},{4,6},{6,4},{8,10},{10,8},{12,14},{14,12},{1,3},{3,1},... | collective-permute-start | bytes 884744 | tf_op jit(solution)/shard_map/ppermute | solution.py:391
  27.3 16.9 %collective-permute-start.6 = (bf16[2,9,32,256]{3,2,1,0:T(8,128)(2,1)S(1)}, bf16[2,9,32,256]{3,2,1,0:T(8,128)(2,1)S(1)}, u32[]{:S(2)}, u32[]{:S(2)}) collective-permute-start(bf16[2,9,32,256]{3,2,1,0:T(8,128)(2,1)S(1)} %get-tuple-element.67), channel_id=1, source_target_pairs={{2,4},{4,2},{6,8},{8,6},{10,12},{12,10},{3,5},{5,3},{7,9},{9,7},{1... | collective-permute-start | bytes 884744 | tf_op jit(solution)/shard_map/ppermute | solution.py:390
  39.3 25.4 %collective-permute-start.8 = (bf16[16,32,896]{2,1,0:T(8,128)(2,1)S(1)}, bf16[16,32,896]{2,1,0:T(8,128)(2,1)S(1)}, u32[]{:S(2)}, u32[]{:S(2)}) collective-permute-start(bf16[16,32,896]{2,1,0:T(8,128)(2,1)S(1)} %get-tuple-element.60), channel_id=1, source_target_pairs={{0,12},{2,14},{16,28},{18,30},{32,44},{34,46},{48,60},{50,62},{64,... | collective-permute-start | bytes 2752520 | tf_op jit(solution)/shard_map/ppermute | solution.py:397
  43.9 20.7 %collective-permute-start.9 = (bf16[16,32,896]{2,1,0:T(8,128)(2,1)S(1)}, bf16[16,32,896]{2,1,0:T(8,128)(2,1)S(1)}, u32[]{:S(2)}, u32[]{:S(2)}) collective-permute-start(bf16[16,32,896]{2,1,0:T(8,128)(2,1)S(1)} %get-tuple-element.61), channel_id=1, source_target_pairs={{0,8},{2,10},{16,24},{18,26},{32,40},{34,42},{48,56},{50,58},{64,7... | collective-permute-start | bytes 2752520 | tf_op jit(solution)/shard_map/ppermute | solution.py:397
  44.2 24.5 %collective-permute-start.7 = (bf16[16,32,896]{2,1,0:T(8,128)(2,1)S(1)}, bf16[16,32,896]{2,1,0:T(8,128)(2,1)S(1)}, u32[]{:S(2)}, u32[]{:S(2)}) collective-permute-start(bf16[16,32,896]{2,1,0:T(8,128)(2,1)S(1)} %get-tuple-element.59), channel_id=1, source_target_pairs={{0,4},{2,6},{16,20},{18,22},{32,36},{34,38},{48,52},{50,54},{64,68... | collective-permute-start | bytes 2752520 | tf_op jit(solution)/shard_map/ppermute | solution.py:397
  69.2 7.3 %collective-permute-start.10 = (bf16[4,32,896]{2,1,0:T(8,128)(2,1)S(1)}, bf16[4,32,896]{2,1,0:T(8,128)(2,1)S(1)}, u32[]{:S(2)}, u32[]{:S(2)}) collective-permute-start(bf16[4,32,896]{2,1,0:T(8,128)(2,1)S(1)} %get-tuple-element.64), channel_id=1, source_target_pairs={{0,2},{2,16},{16,18},{18,0},{32,34},{34,48},{48,50},{50,32},{64,66... | collective-permute-start | bytes 688136 | tf_op jit(solution)/shard_map/ppermute | solution.py:397
  69.3 7.6 %collective-permute-start.11 = (bf16[4,32,896]{2,1,0:T(8,128)(2,1)S(1)}, bf16[4,32,896]{2,1,0:T(8,128)(2,1)S(1)}, u32[]{:S(2)}, u32[]{:S(2)}) collective-permute-start(bf16[4,32,896]{2,1,0:T(8,128)(2,1)S(1)} %get-tuple-element.66), channel_id=1, source_target_pairs={{0,18},{2,0},{16,2},{18,16},{32,50},{34,32},{48,34},{50,48},{64,82... | collective-permute-start | bytes 688136 | tf_op jit(solution)/shard_map/ppermute | solution.py:397
  72.5 7.5 %collective-permute-start.12 = (bf16[4,32,896]{2,1,0:T(8,128)(2,1)S(1)}, bf16[4,32,896]{2,1,0:T(8,128)(2,1)S(1)}, u32[]{:S(2)}, u32[]{:S(2)}) collective-permute-start(bf16[4,32,896]{2,1,0:T(8,128)(2,1)S(1)} %get-tuple-element.65), channel_id=1, source_target_pairs={{0,16},{2,18},{16,0},{18,2},{32,48},{34,50},{48,32},{50,34},{64,80... | collective-permute-start | bytes 688136 | tf_op jit(solution)/shard_map/ppermute | solution.py:397

commit v6 on v4

--- a/solution.py
+++ b/solution.py
@@ -261,68 +261,97 @@
         field_grad[1 + i] = inner_grad[i]
 
 
+def chip_kernel(place, cot, field, other, chip):
+    core = place[0]
+
+    def fill(value, half, flip):
+        put_own(chip, 0, 1 + 8 * half, value, flip)
+
+        def step(i, _):
+            put(chip, i, 9 - 8 * half, other[i, 0:8], flip)
+            chip[i, 0:1] = jnp.zeros((1, 32, 768), BF)
+            chip[i, 17:18] = jnp.zeros((1, 32, 768), BF)
+            return 0
+
+        lax.fori_loop(0, 4, step, 0)
+
+    @pl.when(core == 0)
+    def _():
+        fill(field, 0, False)
+
+    @pl.when(core == 1)
+    def _():
+        fill(cot, 1, True)
+
+
 def weight_kernel(
-    place, cot, field, near1, far1, other1, edges, hid, pre_grad, other2,
-    own, send1, send2, send3, stack, turned, local, flat, tiles,
+    place, chip, near1, far1, edges, hid, pre_grad, other2,
+    own, send1, send2, send3, sides, turned, local, flat, tiles,
 ):
     core = place[0]
-
-    def fill(value, which, half, flip):
+    near = near_side(place)
+
+    def fill(which, half, flip):
         mine, others = 1 + 8 * half, 9 - 8 * half
-        near = 5 * near_side(place)
-        put_own(stack, 1, mine, value, flip)
-        put(stack, near, mine, near1[which, 0:8], flip)
-        put(stack, 5 - near, mine, far1[which, 0:8], flip)
-        put(stack, near, others, edges[0], flip)
-        put(stack, 5 - near, others, edges[1], flip)
-
-        def step(i, _):
-            put(stack, i + 1, others, other1[i, 0:8], flip)
-            return 0
-
-        lax.fori_loop(0, 4, step, 0)
-        for i in range(6):
-            stack[i, 0:1] = jnp.zeros((1, 32, 768), BF)
-            stack[i, 17:18] = jnp.zeros((1, 32, 768), BF)
+        put(sides, near, mine, near1[which, 0:8], flip)
+        put(sides, 1 - near, mine, far1[which, 0:8], flip)
+        put(sides, near, others, edges[0], flip)
+        put(sides, 1 - near, others, edges[1], flip)
+        for i in range(2):
+            sides[i, 0:1] = jnp.zeros((1, 32, 768), BF)
+            sides[i, 17:18] = jnp.zeros((1, 32, 768), BF)
+
+    def windows(a, b):
+        rows = slice(b, b + 16)
+        if a == 1:
+            return [(0, chip[0:4, rows].reshape(2048, 768))]
+        if a == 0:
+            return [
+                (0, sides[0, rows].reshape(512, 768)),
+                (512, chip[0:3, rows].reshape(1536, 768)),
+            ]
+        return [
+            (0, chip[1:4, rows].reshape(1536, 768)),
+            (1536, sides[1, rows].reshape(512, 768)),
+        ]
 
     flat[:, 6912:7040] = jnp.zeros((256, 128), BF)
 
     @pl.when(core == 0)
     def _():
-        fill(field, 1, 0, False)
+        fill(1, 0, False)
         for i in range(4):
             turned[:, i * 512 : i * 512 + 256] = pre_grad[i].reshape(256, 256).T
             turned[:, i * 512 + 256 : i * 512 + 512] = other2[i, 0:8].reshape(256, 256).T
-
-        def block(k, _):
-            a, b = k // 3, k % 3
-            rows = stack[pl.ds(a, 4), pl.ds(b, 16)].reshape(2048, 768)
-            term = jnp.dot(turned[...], rows, preferred_element_type=F32)
-            flat[:, pl.ds(pl.multiple_of(k * 768, 768), 768)] = (term * 0.125).astype(BF)
-            return 0
-
-        lax.fori_loop(0, 9, block, 0, unroll=True)
+        for k in range(9):
+            term = None
+            for at, rows in windows(k // 3, k % 3):
+                part = jnp.dot(
+                    turned[:, at : at + rows.shape[0]], rows, preferred_element_type=F32
+                )
+                term = part if term is None else term + part
+            flat[:, k * 768 : (k + 1) * 768] = (term * 0.125).astype(BF)
 
     @pl.when(core == 1)
     def _():
-        fill(cot, 0, 1, True)
+        fill(0, 1, True)
         for i in range(4):
             local[i * 512 : i * 512 + 256] = other2[i, 0:8].reshape(256, 256)
             local[i * 512 + 256 : i * 512 + 512] = hid[i].reshape(256, 256)
-
-        def block(k, _):
-            a, b = 2 - k // 3, 2 - k % 3
-            rows = stack[pl.ds(a, 4), pl.ds(b, 16)].reshape(2048, 768)
-            term = lax.dot_general(
-                rows, local[...], (((0,), (0,)), ((), ())), preferred_element_type=F32
-            )
+        for k in range(9):
+            term = None
+            for at, rows in windows(2 - k // 3, 2 - k % 3):
+                part = lax.dot_general(
+                    rows,
+                    local[at : at + rows.shape[0]],
+                    (((0,), (0,)), ((), ())),
+                    preferred_element_type=F32,
+                )
+                term = part if term is None else term + part
             term = (term * 0.125).astype(BF)
             for c in range(3):
-                lanes = pl.ds(pl.multiple_of((k * 3 + c) * 256, 256), 256)
+                lanes = slice((k * 3 + c) * 256, (k * 3 + c + 1) * 256)
                 flat[:, lanes] = term[c * 256 : (c + 1) * 256]
-            return 0
-
-        lax.fori_loop(0, 9, block, 0, unroll=True)
 
     for k in range(8):
         tiles[k] = flat[:, k * 864 : k * 864 + LANES]
@@ -340,7 +369,7 @@
             ref[i] = tiles[to_dp, pl.ds(pl.multiple_of(to_px * 32, 32), 32), :]
             return 0
 
-        lax.fori_loop(0, 16, pick, 0, unroll=8)
+        lax.fori_loop(0, 16, pick, 0, unroll=True)
 
 
 def call(kernel, name, flops, args, outs, scratch, limit, far=()):
@@ -433,10 +462,10 @@
         pack_kernel,
         "pack",
         0,
-        (place, cot, field),
+        (core.astype(jnp.int32).reshape(1), cot, field),
         [shape((4, 9, 32, 256), BF)],
         [pltpu.SemaphoreType.DMA((2,))],
-        56,
+        40,
         (1, 2),
     )
     other1 = swap_cores(sent1)
@@ -454,10 +483,22 @@
         (place, cot, field, other1, *weights),
         [half, half, part, part, shape((6912, 256), BF), shape((6912, 256), BF)],
         own_scratch + [pltpu.SemaphoreType.DMA((2,))],
-        42,
+        38,
         (4, 5),
     )
     inner, weights = inner[:4], inner[4:]
+    inner_hidden, beside = lax.optimization_barrier((inner[0], other1))
+    (chip,) = call(
+        chip_kernel,
+        "chip",
+        flops // 8,
+        (place, cot, field, beside),
+        [shape((4, 18, 32, 768), BF)],
+        [],
+        12,
+    )
+    inner_hidden, chip = lax.optimization_barrier((inner_hidden, chip))
+    inner = (inner_hidden, *inner[1:])
     hidden, pre_grad, sent2 = call(
         outer_kernel,
         "outer",
@@ -486,10 +527,10 @@
         weight_kernel,
         "weight_terms",
         flops,
-        (place, cot, field, near1, far1, other1, edges, hidden, pre_grad, other2),
+        (place, chip, near1, far1, edges, hidden, pre_grad, other2),
         [shape((16, 32, LANES), BF)] * 4,
         [
-            pltpu.VMEM((6, 18, 32, 768), BF),
+            pltpu.VMEM((2, 18, 32, 768), BF),
             pltpu.VMEM((256, 2048), BF),
             pltpu.VMEM((2048, 256), BF),
             pltpu.VMEM((256, 7040), BF),

time: 94.6 us -> 92 us (0.973)
  Pallas kernels: 37 us -> 33.5 us
  local copies, waits for them, and re-layouts: 0.24 us -> 3.19 us
  waiting for transfers between devices: 29 us -> 27.4 us
    pallas_call x6 -> x7, Pallas kernels: 37 us -> 33.5 us  [call(): pl.pallas_call(kernel, name=name, out_shape=outs, in_specs=[pl.BlockSpec(...]
    unnamed x6 -> x10, local copies, waits for them, and re-layouts: 0.02 us -> 2.98 us
    ppermute x4, waiting for transfers between devices: 4.6 us -> 3.44 us  [swap_cores(): return lax.ppermute(value, 'py', [(0, 1), (1, 0)])]
where the time goes in v6:
time: 92 us; the launch traced here: 90.6 us
  Pallas kernels  33.5 us (36%)
  waiting for transfers between devices  27.4 us (30%)
  starting transfers between devices  23.9 us (26%)
  local copies, waits for them, and re-layouts  3.19 us (3%)
  other arithmetic  1.67 us (2%)
  between operations  0.98 us (1%)
    pallas_call x7, Pallas kernels, call(): pl.pallas_call(kernel, name=name, out_shape=outs, in_specs=[pl.BlockSpec(...  33.5 us
    ppermute x9, waiting for transfers between devices, hop(): lax.ppermute(part, ALL, hop_pairs(stage, distance))  22.2 us
    ppermute x9, starting transfers between devices, hop(): lax.ppermute(part, ALL, hop_pairs(stage, distance))  17 us
    ppermute x2, starting transfers between devices, swap_slabs(): got_near = lax.ppermute(jnp.where(low_half, high, low), 'px', near)  4.68 us
    ppermute x4, waiting for transfers between devices, swap_cores(): return lax.ppermute(value, 'py', [(0, 1), (1, 0)])  3.44 us
    unnamed x10, local copies, waits for them, and re-layouts  2.98 us
  transfers between devices with their start and end apart: 17, of which 12 were waited for; matrix products, arithmetic and copies ran while one was open for 0% of the time, Pallas kernels for 34%

profile of v6, /device:TPU:0, one launch (start us, length us, event | category | flops | bytes accessed | tf_op | source)
XLA Modules:
  0.0 90.6 jit_solution(3789346498355056560)
XLA Ops:
  0.6 0.0 copy-start
  0.6 1.0 %copy-done = bf16[1,4,8,32,256]{4,3,2,1,0:T(8,128)(2,1)S(1)} copy-done((bf16[1,4,8,32,256]{4,3,2,1,0:T(8,128)(2,1)S(1)}, bf16[1,4,8,32,256]{4,3,2,1,0:T(8,128)(2,1)}, u32[]{:S(2)}) %copy-start) | copy-done | bytes 524312
  1.7 0.0 copy-start.2
  1.7 1.0 %copy-done.2 = bf16[1,4,8,32,256]{4,3,2,1,0:T(8,128)(2,1)S(1)} copy-done((bf16[1,4,8,32,256]{4,3,2,1,0:T(8,128)(2,1)S(1)}, bf16[1,4,8,32,256]{4,3,2,1,0:T(8,128)(2,1)}, u32[]{:S(2)}) %copy-start.2) | copy-done | bytes 524312
  2.7 0.0 copy-start.1
  2.7 0.0 copy-start.3
  2.7 0.1 pack.1
  2.8 0.1 collective-permute-start
  2.9 0.1 pad_add_fusion.place
  3.0 0.8 copy-done.1
  3.8 0.0 copy-start.4
  3.8 0.1 copy-done.3
  3.9 1.0 %collective-permute-done.other = bf16[4,9,32,256]{3,2,1,0:T(8,128)(2,1)S(1)} collective-permute-done((bf16[4,9,32,256]{3,2,1,0:T(8,128)(2,1)S(1)}, bf16[4,9,32,256]{3,2,1,0:T(8,128)(2,1)S(1)}, u32[]{:S(2)}, u32[]{:S(2)}) %collective-permute-start) | collective-permute-done | bytes 589856 | tf_op jit(solution)/shard_map/ppermute | solution.py:396
  5.0 0.1 broadcast_select_fusion.2
  5.1 2.1 %collective-permute-start.1 = (bf16[2,9,32,256]{3,2,1,0:T(8,128)(2,1)S(1)}, bf16[2,9,32,256]{3,2,1,0:T(8,128)(2,1)S(1)}, u32[]{:S(2)}, u32[]{:S(2)}) collective-permute-start(bf16[2,9,32,256]{3,2,1,0:T(8,128)(2,1)S(1)} %get-tuple-element.80), channel_id=1, source_target_pairs={{0,2},{2,0},{4,6},{6,4},{8,10},{10,8},{12,14},{14,12},{1,3},{3,1},... | collective-permute-start | bytes 884744 | tf_op jit(solution)/shard_map/ppermute | solution.py:414
  7.2 0.7 collective-permute-start.2
  7.8 0.0 copy-done.4
  7.9 9.4 %inner.1 = (bf16[2,8,32,256]{3,2,1,0:T(8,128)(2,1)S(1)}, bf16[2,8,32,256]{3,2,1,0:T(8,128)(2,1)S(1)}, f32[2,256,256]{2,1,0:T(8,128)S(1)}, f32[2,256,256]{2,1,0:T...) custom-call(s32[4]{0:T(128)S(1)} %pad_add_fusion.place, bf16[4,8,32,256]{3,2,1,0:T(8,128)(2,1)S(1)} %bitcast.75, ...), custom_call_target="tpu_custom_call" | custom-call | flops 6039797760 | bytes 8388608 | tf_op jit(solution)/shard_map/inner/pallas_call | solution.py:377
  17.3 1.1 %chip.1 = bf16[4,18,32,768]{3,2,1,0:T(8,128)(2,1)S(1)} custom-call(s32[4]{0:T(128)S(1)} %pad_add_fusion.place, bf16[4,8,32,256]{3,2,1,0:T(8,128)(2,1)S(1)} %bitcast.76, bf16[4,8,32,256]{3,2,1,0:T(8,128)(2,1)S(1)} %bitcast.81, bf16[4,9,32,256]{3,2,1,0:T(8,128)(2,1)S(1)} %collective-permute-done.other), custom_call_target="tpu_custom_call" | custom-call | flops 905969664 | bytes 8388608 | tf_op jit(solution)/shard_map/chip/pallas_call | solution.py:377
  18.4 1.7 %collective-permute-done.1.near.near1 = bf16[2,9,32,256]{3,2,1,0:T(8,128)(2,1)S(1)} collective-permute-done((bf16[2,9,32,256]{3,2,1,0:T(8,128)(2,1)S(1)}, bf16[2,9,32,256]{3,2,1,0:T(8,128)(2,1)S(1)}, u32[]{:S(2)}, u32[]{:S(2)}) %collective-permute-start.1) | collective-permute-done | bytes 294944 | tf_op jit(solution)/shard_map/ppermute | solution.py:414
  20.1 0.0 collective-permute-done.2.far.far1
  20.1 2.4 %outer.1 = (bf16[4,8,32,256]{3,2,1,0:T(8,128)(2,1)S(1)}, bf16[4,8,32,256]{3,2,1,0:T(8,128)(2,1)S(1)}, bf16[4,9,32,256]{3,2,1,0:T(8,128)(2,1)S(1)}) custom-call(s32[4]{0:T(128)S(1)} %pad_add_fusion.place, bf16[2,9,32,256]{3,2,1,0:T(8,128)(2,1)S(1)} %collective-permute-done.1.near.near1, bf16[2,9,32,256]{3,2,1,0:T(8,128)(2,1)S(1)} %collective-permute-done.2.far.far1, ...), custom_call_target="tpu_custom_call" | custom-call | flops 1207959552 | bytes 8388608 | tf_op jit(solution)/shard_map/outer/pallas_call | solution.py:377
  22.4 0.1 collective-permute-start.3
  22.6 0.6 collective-permute-start.4
  23.3 1.3 %collective-permute-done.3.other2.other = bf16[4,9,32,256]{3,2,1,0:T(8,128)(2,1)S(1)} collective-permute-done((bf16[4,9,32,256]{3,2,1,0:T(8,128)(2,1)S(1)}, bf16[4,9,32,256]{3,2,1,0:T(8,128)(2,1)S(1)}, u32[]{:S(2)}, u32[]{:S(2)}) %collective-permute-start.3) | collective-permute-done | bytes 589856 | tf_op jit(solution)/shard_map/ppermute | solution.py:396
  24.7 0.1 broadcast_select_fusion
  24.7 2.6 %collective-permute-start.5 = (bf16[2,9,32,256]{3,2,1,0:T(8,128)(2,1)S(1)}, bf16[2,9,32,256]{3,2,1,0:T(8,128)(2,1)S(1)}, u32[]{:S(2)}, u32[]{:S(2)}) collective-permute-start(bf16[2,9,32,256]{3,2,1,0:T(8,128)(2,1)S(1)} %get-tuple-element.76), channel_id=1, source_target_pairs={{0,2},{2,0},{4,6},{6,4},{8,10},{10,8},{12,14},{14,12},{1,3},{3,1},... | collective-permute-start | bytes 884744 | tf_op jit(solution)/shard_map/ppermute | solution.py:414
  27.3 0.7 collective-permute-start.6
  28.0 0.0 collective-permute-done.4.edges
  28.0 10.0 %weight_terms.1 = (bf16[16,32,896]{2,1,0:T(8,128)(2,1)S(1)}, bf16[16,32,896]{2,1,0:T(8,128)(2,1)S(1)}, bf16[16,32,896]{2,1,0:T(8,128)(2,1)S(1)}, bf16[16,32,896]{2,1,0:T(8,128)(2,1)S(1)}) custom-call(s32[4]{0:T(128)S(1)} %pad_add_fusion.place, bf16[4,18,32,768]{3,2,1,0:T(8,128)(2,1)S(1)} %chip.1, ...), custom_call_target="tpu_custom_call" | custom-call | flops 7247757312 | bytes 8388608 | tf_op jit(solution)/shard_map/weight_terms/pallas_call | solution.py:377
  38.0 4.6 %collective-permute-start.8 = (bf16[16,32,896]{2,1,0:T(8,128)(2,1)S(1)}, bf16[16,32,896]{2,1,0:T(8,128)(2,1)S(1)}, u32[]{:S(2)}, u32[]{:S(2)}) collective-permute-start(bf16[16,32,896]{2,1,0:T(8,128)(2,1)S(1)} %get-tuple-element.68), channel_id=1, source_target_pairs={{0,12},{2,14},{16,28},{18,30},{32,44},{34,46},{48,60},{50,62},{64,... | collective-permute-start | bytes 2752520 | tf_op jit(solution)/shard_map/ppermute | solution.py:420
  42.6 0.3 collective-permute-start.9
  42.9 0.0 collective-permute-done.5.near
  42.9 0.0 collective-permute-done.6.far
  42.9 1.1 %collective-permute-start.7 = (bf16[16,32,896]{2,1,0:T(8,128)(2,1)S(1)}, bf16[16,32,896]{2,1,0:T(8,128)(2,1)S(1)}, u32[]{:S(2)}, u32[]{:S(2)}) collective-permute-start(bf16[16,32,896]{2,1,0:T(8,128)(2,1)S(1)} %get-tuple-element.67), channel_id=1, source_target_pairs={{0,4},{2,6},{16,20},{18,22},{32,36},{34,38},{48,52},{50,54},{64,68... | collective-permute-start | bytes 2752520 | tf_op jit(solution)/shard_map/ppermute | solution.py:420
  44.0 7.4 %outputs_inner.1 = (bf16[2,8,32,256]{3,2,1,0:T(8,128)(2,1)S(1)}, bf16[2,8,32,256]{3,2,1,0:T(8,128)(2,1)S(1)}, f32[2,256,256]{2,1,0:T(8,128)S(1)}, f32[2,256,256]{2,1,0:T(8,128)S(1)}) custom-call(s32[4]{0:T(128)S(1)} %pad_add_fusion.place, bf16[4,8,32,256]{3,2,1,0:T(8,128)(2,1)S(1)} %get-tuple-element.55.hid, ...), custom_call_target="tpu_custom_call" | custom-call | flops 6039797760 | bytes 8388608 | tf_op jit(solution)/shard_map/outputs_inner/pallas_call | solution.py:377
  51.4 3.2 %outputs_outer.1 = (bf16[4,8,32,256]{3,2,1,0:T(8,128)(2,1)}, bf16[4,8,32,256]{3,2,1,0:T(8,128)(2,1)}) custom-call(s32[4]{0:T(128)S(1)} %pad_add_fusion.place, bf16[2,9,32,256]{3,2,1,0:T(8,128)(2,1)S(1)} %collective-permute-done.5.near, bf16[2,9,32,256]{3,2,1,0:T(8,128)(2,1)S(1)} %collective-permute-done.6.far, ...), custom_call_target="tpu_custom_call" | custom-call | flops 1207959552 | bytes 8388608 | tf_op jit(solution)/shard_map/outputs_outer/pallas_call | solution.py:377
  54.6 8.7 %collective-permute-done.8 = bf16[16,32,896]{2,1,0:T(8,128)(2,1)S(1)} collective-permute-done((bf16[16,32,896]{2,1,0:T(8,128)(2,1)S(1)}, bf16[16,32,896]{2,1,0:T(8,128)(2,1)S(1)}, u32[]{:S(2)}, u32[]{:S(2)}) %collective-permute-start.8) | collective-permute-done | bytes 917536 | tf_op jit(solution)/shard_map/ppermute | solution.py:420
  63.3 0.0 collective-permute-done.9
  63.3 4.0 %collective-permute-done.7 = bf16[16,32,896]{2,1,0:T(8,128)(2,1)S(1)} collective-permute-done((bf16[16,32,896]{2,1,0:T(8,128)(2,1)S(1)}, bf16[16,32,896]{2,1,0:T(8,128)(2,1)S(1)}, u32[]{:S(2)}, u32[]{:S(2)}) %collective-permute-start.7) | collective-permute-done | bytes 917536 | tf_op jit(solution)/shard_map/ppermute | solution.py:420
  67.3 0.5 fusion.5
  67.8 0.1 fusion.6
  67.8 1.6 %collective-permute-start.10 = (bf16[4,32,896]{2,1,0:T(8,128)(2,1)S(1)}, bf16[4,32,896]{2,1,0:T(8,128)(2,1)S(1)}, u32[]{:S(2)}, u32[]{:S(2)}) collective-permute-start(bf16[4,32,896]{2,1,0:T(8,128)(2,1)S(1)} %get-tuple-element.72), channel_id=1, source_target_pairs={{0,32},{2,34},{16,48},{18,50},{32,64},{34,66},{48,80},{50,82},{64,... | collective-permute-start | bytes 688136 | tf_op jit(solution)/shard_map/ppermute | solution.py:420
  69.5 1.7 %collective-permute-start.11 = (bf16[4,32,896]{2,1,0:T(8,128)(2,1)S(1)}, bf16[4,32,896]{2,1,0:T(8,128)(2,1)S(1)}, u32[]{:S(2)}, u32[]{:S(2)}) collective-permute-start(bf16[4,32,896]{2,1,0:T(8,128)(2,1)S(1)} %get-tuple-element.74), channel_id=1, source_target_pairs={{0,96},{2,98},{16,112},{18,114},{32,0},{34,2},{48,16},{50,18},{64,... | collective-permute-start | bytes 688136 | tf_op jit(solution)/shard_map/ppermute | solution.py:420
  71.1 2.0 %collective-permute-start.12 = (bf16[4,32,896]{2,1,0:T(8,128)(2,1)S(1)}, bf16[4,32,896]{2,1,0:T(8,128)(2,1)S(1)}, u32[]{:S(2)}, u32[]{:S(2)}) collective-permute-start(bf16[4,32,896]{2,1,0:T(8,128)(2,1)S(1)} %get-tuple-element.73), channel_id=1, source_target_pairs={{0,64},{2,66},{16,80},{18,82},{32,96},{34,98},{48,112},{50,114},{6... | collective-permute-start | bytes 688136 | tf_op jit(solution)/shard_map/ppermute | solution.py:420
  73.1 2.0 %collective-permute-done.10 = bf16[4,32,896]{2,1,0:T(8,128)(2,1)S(1)} collective-permute-done((bf16[4,32,896]{2,1,0:T(8,128)(2,1)S(1)}, bf16[4,32,896]{2,1,0:T(8,128)(2,1)S(1)}, u32[]{:S(2)}, u32[]{:S(2)}) %collective-permute-start.10) | collective-permute-done | bytes 229408 | tf_op jit(solution)/shard_map/ppermute | solution.py:420
  75.1 0.4 collective-permute-done.11
  75.5 3.3 %collective-permute-done.12 = bf16[4,32,896]{2,1,0:T(8,128)(2,1)S(1)} collective-permute-done((bf16[4,32,896]{2,1,0:T(8,128)(2,1)S(1)}, bf16[4,32,896]{2,1,0:T(8,128)(2,1)S(1)}, u32[]{:S(2)}, u32[]{:S(2)}) %collective-permute-start.12) | collective-permute-done | bytes 229408 | tf_op jit(solution)/shard_map/ppermute | solution.py:420
  78.8 0.1 fusion.1
  79.0 0.1 collective-permute-start.13
  79.1 3.2 %collective-permute-start.14 = (f32[32,896]{1,0:T(8,128)S(1)}, f32[32,896]{1,0:T(8,128)S(1)}, u32[]{:S(2)}, u32[]{:S(2)}) collective-permute-start(f32[32,896]{1,0:T(8,128)S(1)} %get-tuple-element.93), channel_id=1, source_target_pairs={{0,18},{2,0},{16,2},{18,16},{32,50},{34,32},{48,34},{50,48},{64,82... | collective-permute-start | bytes 344072 | tf_op jit(solution)/shard_map/ppermute | solution.py:420
  82.3 2.5 %collective-permute-start.15 = (f32[32,896]{1,0:T(8,128)S(1)}, f32[32,896]{1,0:T(8,128)S(1)}, u32[]{:S(2)}, u32[]{:S(2)}) collective-permute-start(f32[32,896]{1,0:T(8,128)S(1)} %get-tuple-element.92), channel_id=1, source_target_pairs={{0,16},{2,18},{16,0},{18,2},{32,48},{34,50},{48,32},{50,34},{64,80... | collective-permute-start | bytes 344072 | tf_op jit(solution)/shard_map/ppermute | solution.py:420
  84.8 0.3 collective-permute-done.13
  85.1 0.4 collective-permute-done.14
  85.5 3.1 %collective-permute-done.15 = f32[32,896]{1,0:T(8,128)S(1)} collective-permute-done((f32[32,896]{1,0:T(8,128)S(1)}, f32[32,896]{1,0:T(8,128)S(1)}, u32[]{:S(2)}, u32[]{:S(2)}) %collective-permute-start.15) | collective-permute-done | bytes 114720 | tf_op jit(solution)/shard_map/ppermute | solution.py:420
  88.6 0.1 collective-permute-start.16
  88.7 1.2 %collective-permute-done.16 = f32[16,896]{1,0:T(8,128)S(1)} collective-permute-done((f32[16,896]{1,0:T(8,128)S(1)}, f32[16,896]{1,0:T(8,128)S(1)}, u32[]{:S(2)}, u32[]{:S(2)}) %collective-permute-start.16) | collective-permute-done | bytes 57376 | tf_op jit(solution)/shard_map/ppermute | solution.py:396
  90.0 0.7 select_bitcast_fusion
  (23 shorter events, 0.4 us)
Async XLA Ops:
  0.6 1.0 %copy-start = (bf16[1,4,8,32,256]{4,3,2,1,0:T(8,128)(2,1)S(1)}, bf16[1,4,8,32,256]{4,3,2,1,0:T(8,128)(2,1)}, u32[]{:S(2)}) copy-start(bf16[1,4,8,32,256]{4,3,2,1,0:T(8,128)(2,1)} %param.5) | copy-start | bytes 1572868
  1.7 1.0 %copy-start.2 = (bf16[1,4,8,32,256]{4,3,2,1,0:T(8,128)(2,1)S(1)}, bf16[1,4,8,32,256]{4,3,2,1,0:T(8,128)(2,1)}, u32[]{:S(2)}) copy-start(bf16[1,4,8,32,256]{4,3,2,1,0:T(8,128)(2,1)} %param.4) | copy-start | bytes 1572868
  2.7 1.0 %copy-start.1 = (bf16[1,4,8,32,256]{4,3,2,1,0:T(8,128)(2,1)S(1)}, bf16[1,4,8,32,256]{4,3,2,1,0:T(8,128)(2,1)}, u32[]{:S(2)}) copy-start(bf16[1,4,8,32,256]{4,3,2,1,0:T(8,128)(2,1)} %param.5) | copy-start | bytes 1572868
  2.7 1.2 %copy-start.3 = (bf16[1,4,8,32,256]{4,3,2,1,0:T(8,128)(2,1)S(1)}, bf16[1,4,8,32,256]{4,3,2,1,0:T(8,128)(2,1)}, u32[]{:S(2)}) copy-start(bf16[1,4,8,32,256]{4,3,2,1,0:T(8,128)(2,1)} %param.4) | copy-start | bytes 1572868
  2.8 2.1 %collective-permute-start = (bf16[4,9,32,256]{3,2,1,0:T(8,128)(2,1)S(1)}, bf16[4,9,32,256]{3,2,1,0:T(8,128)(2,1)S(1)}, u32[]{:S(2)}, u32[]{:S(2)}) collective-permute-start(bf16[4,9,32,256]{3,2,1,0:T(8,128)(2,1)S(1)} %pack.1), channel_id=1, source_target_pairs={{0,1},{1,0},{2,3},{3,2},{4,5},{5,4},{6,7},{7,6},{8,9},{9,8},{10,11... | collective-permute-start | bytes 1769480 | tf_op jit(solution)/shard_map/ppermute | solution.py:396
  3.8 4.1 %copy-start.4 = (bf16[6912,256]{1,0:T(8,128)(2,1)S(1)}, bf16[6912,256]{1,0:T(8,128)(2,1)}, u32[]{:S(2)}) copy-start(bf16[6912,256]{1,0:T(8,128)(2,1)} %first_hbm.1) | copy-start | bytes 10616836
  5.1 15.0 %collective-permute-start.1 = (bf16[2,9,32,256]{3,2,1,0:T(8,128)(2,1)S(1)}, bf16[2,9,32,256]{3,2,1,0:T(8,128)(2,1)S(1)}, u32[]{:S(2)}, u32[]{:S(2)}) collective-permute-start(bf16[2,9,32,256]{3,2,1,0:T(8,128)(2,1)S(1)} %get-tuple-element.80), channel_id=1, source_target_pairs={{0,2},{2,0},{4,6},{6,4},{8,10},{10,8},{12,14},{14,12},{1,3},{3,1},... | collective-permute-start | bytes 884744 | tf_op jit(solution)/shard_map/ppermute | solution.py:414
  7.2 12.9 %collective-permute-start.2 = (bf16[2,9,32,256]{3,2,1,0:T(8,128)(2,1)S(1)}, bf16[2,9,32,256]{3,2,1,0:T(8,128)(2,1)S(1)}, u32[]{:S(2)}, u32[]{:S(2)}) collective-permute-start(bf16[2,9,32,256]{3,2,1,0:T(8,128)(2,1)S(1)} %get-tuple-element.79), channel_id=1, source_target_pairs={{2,4},{4,2},{6,8},{8,6},{10,12},{12,10},{3,5},{5,3},{7,9},{9,7},{1... | collective-permute-start | bytes 884744 | tf_op jit(solution)/shard_map/ppermute | solution.py:413
  22.4 2.1 %collective-permute-start.3 = (bf16[4,9,32,256]{3,2,1,0:T(8,128)(2,1)S(1)}, bf16[4,9,32,256]{3,2,1,0:T(8,128)(2,1)S(1)}, u32[]{:S(2)}, u32[]{:S(2)}) collective-permute-start(bf16[4,9,32,256]{3,2,1,0:T(8,128)(2,1)S(1)} %get-tuple-element.48), channel_id=1, source_target_pairs={{0,1},{1,0},{2,3},{3,2},{4,5},{5,4},{6,7},{7,6},{8,9},{9,8},{10,11... | collective-permute-start | bytes 1769480 | tf_op jit(solution)/shard_map/ppermute | solution.py:396
  22.6 5.4 %collective-permute-start.4 = (bf16[2,8,32,256]{3,2,1,0:T(8,128)(2,1)S(1)}, bf16[2,8,32,256]{3,2,1,0:T(8,128)(2,1)S(1)}, u32[]{:S(2)}, u32[]{:S(2)}) collective-permute-start(bf16[2,8,32,256]{3,2,1,0:T(8,128)(2,1)S(1)} %maximum_select_fusion), channel_id=1, source_target_pairs={{0,1},{1,0},{2,3},{3,2},{4,5},{5,4},{6,7},{7,6},{8,9},{9,8},{10,11... | collective-permute-start | bytes 786440 | tf_op jit(solution)/shard_map/ppermute | solution.py:396
  24.7 18.2 %collective-permute-start.5 = (bf16[2,9,32,256]{3,2,1,0:T(8,128)(2,1)S(1)}, bf16[2,9,32,256]{3,2,1,0:T(8,128)(2,1)S(1)}, u32[]{:S(2)}, u32[]{:S(2)}) collective-permute-start(bf16[2,9,32,256]{3,2,1,0:T(8,128)(2,1)S(1)} %get-tuple-element.76), channel_id=1, source_target_pairs={{0,2},{2,0},{4,6},{6,4},{8,10},{10,8},{12,14},{14,12},{1,3},{3,1},... | collective-permute-start | bytes 884744 | tf_op jit(solution)/shard_map/ppermute | solution.py:414
  27.3 15.6 %collective-permute-start.6 = (bf16[2,9,32,256]{3,2,1,0:T(8,128)(2,1)S(1)}, bf16[2,9,32,256]{3,2,1,0:T(8,128)(2,1)S(1)}, u32[]{:S(2)}, u32[]{:S(2)}) collective-permute-start(bf16[2,9,32,256]{3,2,1,0:T(8,128)(2,1)S(1)} %get-tuple-element.75), channel_id=1, source_target_pairs={{2,4},{4,2},{6,8},{8,6},{10,12},{12,10},{3,5},{5,3},{7,9},{9,7},{1... | collective-permute-start | bytes 884744 | tf_op jit(solution)/shard_map/ppermute | solution.py:413
  38.0 25.3 %collective-permute-start.8 = (bf16[16,32,896]{2,1,0:T(8,128)(2,1)S(1)}, bf16[16,32,896]{2,1,0:T(8,128)(2,1)S(1)}, u32[]{:S(2)}, u32[]{:S(2)}) collective-permute-start(bf16[16,32,896]{2,1,0:T(8,128)(2,1)S(1)} %get-tuple-element.68), channel_id=1, source_target_pairs={{0,12},{2,14},{16,28},{18,30},{32,44},{34,46},{48,60},{50,62},{64,... | collective-permute-start | bytes 2752520 | tf_op jit(solution)/shard_map/ppermute | solution.py:420
  42.6 20.7 %collective-permute-start.9 = (bf16[16,32,896]{2,1,0:T(8,128)(2,1)S(1)}, bf16[16,32,896]{2,1,0:T(8,128)(2,1)S(1)}, u32[]{:S(2)}, u32[]{:S(2)}) collective-permute-start(bf16[16,32,896]{2,1,0:T(8,128)(2,1)S(1)} %get-tuple-element.69), channel_id=1, source_target_pairs={{0,8},{2,10},{16,24},{18,26},{32,40},{34,42},{48,56},{50,58},{64,7... | collective-permute-start | bytes 2752520 | tf_op jit(solution)/shard_map/ppermute | solution.py:420
  42.9 24.4 %collective-permute-start.7 = (bf16[16,32,896]{2,1,0:T(8,128)(2,1)S(1)}, bf16[16,32,896]{2,1,0:T(8,128)(2,1)S(1)}, u32[]{:S(2)}, u32[]{:S(2)}) collective-permute-start(bf16[16,32,896]{2,1,0:T(8,128)(2,1)S(1)} %get-tuple-element.67), channel_id=1, source_target_pairs={{0,4},{2,6},{16,20},{18,22},{32,36},{34,38},{48,52},{50,54},{64,68... | collective-permute-start | bytes 2752520 | tf_op jit(solution)/shard_map/ppermute | solution.py:420
  67.8 7.3 %collective-permute-start.10 = (bf16[4,32,896]{2,1,0:T(8,128)(2,1)S(1)}, bf16[4,32,896]{2,1,0:T(8,128)(2,1)S(1)}, u32[]{:S(2)}, u32[]{:S(2)}) collective-permute-start(bf16[4,32,896]{2,1,0:T(8,128)(2,1)S(1)} %get-tuple-element.72), channel_id=1, source_target_pairs={{0,32},{2,34},{16,48},{18,50},{32,64},{34,66},{48,80},{50,82},{64,... | collective-permute-start | bytes 688136 | tf_op jit(solution)/shard_map/ppermute | solution.py:420
  69.5 6.0 %collective-permute-start.11 = (bf16[4,32,896]{2,1,0:T(8,128)(2,1)S(1)}, bf16[4,32,896]{2,1,0:T(8,128)(2,1)S(1)}, u32[]{:S(2)}, u32[]{:S(2)}) collective-permute-start(bf16[4,32,896]{2,1,0:T(8,128)(2,1)S(1)} %get-tuple-element.74), channel_id=1, source_target_pairs={{0,96},{2,98},{16,112},{18,114},{32,0},{34,2},{48,16},{50,18},{64,... | collective-permute-start | bytes 688136 | tf_op jit(solution)/shard_map/ppermute | solution.py:420
  71.1 7.7 %collective-permute-start.12 = (bf16[4,32,896]{2,1,0:T(8,128)(2,1)S(1)}, bf16[4,32,896]{2,1,0:T(8,128)(2,1)S(1)}, u32[]{:S(2)}, u32[]{:S(2)}) collective-permute-start(bf16[4,32,896]{2,1,0:T(8,128)(2,1)S(1)} %get-tuple-element.73), channel_id=1, source_target_pairs={{0,64},{2,66},{16,80},{18,82},{32,96},{34,98},{48,112},{50,114},{6... | collective-permute-start | bytes 688136 | tf_op jit(solution)/shard_map/ppermute | solution.py:420
  79.0 6.1 %collective-permute-start.13 = (f32[32,896]{1,0:T(8,128)S(1)}, f32[32,896]{1,0:T(8,128)S(1)}, u32[]{:S(2)}, u32[]{:S(2)}) collective-permute-start(f32[32,896]{1,0:T(8,128)S(1)} %get-tuple-element.91), channel_id=1, source_target_pairs={{0,2},{2,16},{16,18},{18,0},{32,34},{34,48},{48,50},{50,32},{64,66... | collective-permute-start | bytes 344072 | tf_op jit(solution)/shard_map/ppermute | solution.py:420
  79.1 6.4 %collective-permute-start.14 = (f32[32,896]{1,0:T(8,128)S(1)}, f32[32,896]{1,0:T(8,128)S(1)}, u32[]{:S(2)}, u32[]{:S(2)}) collective-permute-start(f32[32,896]{1,0:T(8,128)S(1)} %get-tuple-element.93), channel_id=1, source_target_pairs={{0,18},{2,0},{16,2},{18,16},{32,50},{34,32},{48,34},{50,48},{64,82... | collective-permute-start | bytes 344072 | tf_op jit(solution)/shard_map/ppermute | solution.py:420
  82.3 6.3 %collective-permute-start.15 = (f32[32,896]{1,0:T(8,128)S(1)}, f32[32,896]{1,0:T(8,128)S(1)}, u32[]{:S(2)}, u32[]{:S(2)}) collective-permute-start(f32[32,896]{1,0:T(8,128)S(1)} %get-tuple-element.92), channel_id=1, source_target_pairs={{0,16},{2,18},{16,0},{18,2},{32,48},{34,50},{48,32},{50,34},{64,80... | collective-permute-start | bytes 344072 | tf_op jit(solution)/shard_map/ppermute | solution.py:420
  88.6 1.3 %collective-permute-start.16 = (f32[16,896]{1,0:T(8,128)S(1)}, f32[16,896]{1,0:T(8,128)S(1)}, u32[]{:S(2)}, u32[]{:S(2)}) collective-permute-start(f32[16,896]{1,0:T(8,128)S(1)} %get-tuple-element.101), channel_id=1, source_target_pairs={{0,1},{1,0},{2,3},{3,2},{4,5},{5,4},{6,7},{7,6},{8,9},{9,8},{10,11... | collective-permute-start | bytes 172040 | tf_op jit(solution)/shard_map/ppermute | solution.py:396

commit v7 on v6

--- a/solution.py
+++ b/solution.py
@@ -9,7 +9,7 @@
 F32 = jnp.float32
 ALL = ("dp", "px", "py")
 X, Y, Z = 0, 1, 2
-ORDER = ((X, Y, Z), (Y, Z, X))
+ORDER = ((X, Y, Z), (Z, X, Y))
 LANES = 896
 
 
@@ -284,9 +284,65 @@
         fill(cot, 1, True)
 
 
+def windows(chip, sides, a, b):
+    rows = slice(b, b + 16)
+    if a == 1:
+        return [(0, chip[0:4, rows].reshape(2048, 768))]
+    if a == 0:
+        return [
+            (0, sides[0, rows].reshape(512, 768)),
+            (512, chip[0:3, rows].reshape(1536, 768)),
+        ]
+    return [
+        (0, chip[1:4, rows].reshape(1536, 768)),
+        (1536, sides[1, rows].reshape(512, 768)),
+    ]
+
+
+def terms_of_first(flat, base, steps, chip, sides, turned):
+    for k in steps:
+        term = None
+        for at, rows in windows(chip, sides, k // 3, k % 3):
+            part = jnp.dot(turned[:, at : at + rows.shape[0]], rows, preferred_element_type=F32)
+            term = part if term is None else term + part
+        flat[:, k * 768 - base : (k + 1) * 768 - base] = (term * 0.125).astype(BF)
+
+
+def terms_of_second(flat, base, steps, chip, sides, local):
+    for k in steps:
+        term = None
+        for at, rows in windows(chip, sides, 2 - k // 3, 2 - k % 3):
+            part = lax.dot_general(
+                rows,
+                local[at : at + rows.shape[0]],
+                (((0,), (0,)), ((), ())),
+                preferred_element_type=F32,
+            )
+            term = part if term is None else term + part
+        term = (term * 0.125).astype(BF)
+        for c in range(3):
+            start = (k * 3 + c) * 256 - base
+            flat[:, start : start + 256] = term[c * 256 : (c + 1) * 256]
+
+
+def give_tiles(place, flat, tiles, outs):
+    for k in range(4):
+        tiles[k] = flat[:, k * 864 : k * 864 + LANES]
+    x, z = place[1], place[3]
+    zero = place[0] == 0
+    for first, ref in enumerate(outs):
+        for i in range(8):
+            other, high = i // 2, i % 2
+            to_x = lax.rem(x + jnp.where(zero, first, other), 4)
+            to_z = lax.rem(z + jnp.where(zero, other, first), 4)
+            row = high * 2 + lax.div(to_z, 2)
+            to_px = to_x * 2 + lax.rem(to_z, 2)
+            ref[i] = tiles[row, pl.ds(pl.multiple_of(to_px * 32, 32), 32), :]
+
+
 def weight_kernel(
     place, chip, near1, far1, edges, hid, pre_grad, other2,
-    own, send1, send2, send3, sides, turned, local, flat, tiles,
+    own, send1, send2, send3, sides, turned, local, rest, flat, tiles,
 ):
     core = place[0]
     near = near_side(place)
@@ -301,36 +357,13 @@
             sides[i, 0:1] = jnp.zeros((1, 32, 768), BF)
             sides[i, 17:18] = jnp.zeros((1, 32, 768), BF)
 
-    def windows(a, b):
-        rows = slice(b, b + 16)
-        if a == 1:
-            return [(0, chip[0:4, rows].reshape(2048, 768))]
-        if a == 0:
-            return [
-                (0, sides[0, rows].reshape(512, 768)),
-                (512, chip[0:3, rows].reshape(1536, 768)),
-            ]
-        return [
-            (0, chip[1:4, rows].reshape(1536, 768)),
-            (1536, sides[1, rows].reshape(512, 768)),
-        ]
-
-    flat[:, 6912:7040] = jnp.zeros((256, 128), BF)
-
     @pl.when(core == 0)
     def _():
         fill(1, 0, False)
         for i in range(4):
             turned[:, i * 512 : i * 512 + 256] = pre_grad[i].reshape(256, 256).T
             turned[:, i * 512 + 256 : i * 512 + 512] = other2[i, 0:8].reshape(256, 256).T
-        for k in range(9):
-            term = None
-            for at, rows in windows(k // 3, k % 3):
-                part = jnp.dot(
-                    turned[:, at : at + rows.shape[0]], rows, preferred_element_type=F32
-                )
-                term = part if term is None else term + part
-            flat[:, k * 768 : (k + 1) * 768] = (term * 0.125).astype(BF)
+        terms_of_first(flat, 0, range(5), chip, sides, turned)
 
     @pl.when(core == 1)
     def _():
@@ -338,38 +371,45 @@
         for i in range(4):
             local[i * 512 : i * 512 + 256] = other2[i, 0:8].reshape(256, 256)
             local[i * 512 + 256 : i * 512 + 512] = hid[i].reshape(256, 256)
-        for k in range(9):
-            term = None
-            for at, rows in windows(2 - k // 3, 2 - k % 3):
-                part = lax.dot_general(
-                    rows,
-                    local[at : at + rows.shape[0]],
-                    (((0,), (0,)), ((), ())),
-                    preferred_element_type=F32,
-                )
-                term = part if term is None else term + part
-            term = (term * 0.125).astype(BF)
-            for c in range(3):
-                lanes = slice((k * 3 + c) * 256, (k * 3 + c + 1) * 256)
-                flat[:, lanes] = term[c * 256 : (c + 1) * 256]
-
-    for k in range(8):
-        tiles[k] = flat[:, k * 864 : k * 864 + LANES]
-    x, y, z = place[1], place[2], place[3]
-    zero = core == 0
-    for first, ref in enumerate((own, send1, send2, send3)):
-
-        def pick(i, _):
-            second, third = i // 4, i % 4
-            to_x = lax.rem(x + jnp.where(zero, first, third), 4)
-            to_y = lax.rem(y + jnp.where(zero, second, first), 4)
-            to_z = lax.rem(z + jnp.where(zero, third, second), 4)
-            to_dp = to_y * 2 + to_z // 2
-            to_px = to_x * 2 + lax.rem(to_z, 2)
-            ref[i] = tiles[to_dp, pl.ds(pl.multiple_of(to_px * 32, 32), 32), :]
-            return 0
-
-        lax.fori_loop(0, 16, pick, 0, unroll=True)
+        terms_of_second(flat, 0, range(5), chip, sides, local)
+
+    rest[...] = flat[:, 3456:3840]
+    give_tiles(place, flat, tiles, (own, send1, send2, send3))
+
+
+def weight_rest_kernel(
+    place, chip, sides, turned, local, rest, own, send1, send2, send3, flat, tiles
+):
+    core = place[0]
+    flat[:, 0:384] = rest[...]
+    flat[:, 3456:3584] = jnp.zeros((256, 128), BF)
+
+    @pl.when(core == 0)
+    def _():
+        terms_of_first(flat, 3456, range(5, 9), chip, sides, turned)
+
+    @pl.when(core == 1)
+    def _():
+        terms_of_second(flat, 3456, range(5, 9), chip, sides, local)
+
+    give_tiles(place, flat, tiles, (own, send1, send2, send3))
+
+
+def sum_kernel(place, *refs):
+    ins, (keep, send1, send2, send3, sums) = refs[:8], refs[8:]
+    for half in range(2):
+        for i in range(8):
+            total = ins[4 * half][i].astype(F32)
+            for ref in ins[4 * half + 1 : 4 * half + 4]:
+                total = total + ref[i].astype(F32)
+            sums[half * 8 + i] = total
+    zero, y = place[0] == 0, place[2]
+    for second, ref in enumerate((keep, send1, send2, send3)):
+        for third in range(4):
+            to_y = lax.rem(y + jnp.where(zero, second, third), 4)
+            other = jnp.where(zero, third, second)
+            at = lax.div(to_y, 2) * 8 + other * 2 + lax.rem(to_y, 2)
+            ref[third] = sums[at].astype(ref.dtype)
 
 
 def call(kernel, name, flops, args, outs, scratch, limit, far=()):
@@ -422,13 +462,19 @@
     ]
 
 
-def reduce_tiles(own, got, core):
-    total = own.astype(F32)
-    for part in got:
-        total = total + part.astype(F32)
-    got = hop([total[4 * d : 4 * d + 4].astype(BF) for d in (1, 3, 2)], 1)
-    total = total[0:4]
-    for part in got:
+def reduce_tiles(place, halves, core):
+    shape = jax.ShapeDtypeStruct
+    keep, send1, send2, send3 = call(
+        sum_kernel,
+        "sum",
+        0,
+        (place, *halves),
+        [shape((4, 32, LANES), F32)] + [shape((4, 32, LANES), BF)] * 3,
+        [pltpu.VMEM((16, 32, LANES), F32)],
+        16,
+    )
+    total = keep
+    for part in hop((send1, send3, send2), 1):
         total = total + part.astype(F32)
     got = hop([total[d] for d in (1, 3, 2)], 2)
     total = total[0] + got[0] + got[1] + got[2]
@@ -523,24 +569,37 @@
         jnp.where(zero, other2[:, 0:1], other2[:, 8:9]),
         low_half,
     )
-    own, send1, send2, send3 = call(
+    tiles = [shape((8, 32, LANES), BF)] * 4
+    own1, *sent1, sides, turned, local, rest = call(
         weight_kernel,
         "weight_terms",
-        flops,
+        flops * 5 // 9,
         (place, chip, near1, far1, edges, hidden, pre_grad, other2),
-        [shape((16, 32, LANES), BF)] * 4,
-        [
-            pltpu.VMEM((2, 18, 32, 768), BF),
-            pltpu.VMEM((256, 2048), BF),
-            pltpu.VMEM((2048, 256), BF),
-            pltpu.VMEM((256, 7040), BF),
-            pltpu.VMEM((8, 256, LANES), BF),
+        tiles
+        + [
+            shape((2, 18, 32, 768), BF),
+            shape((256, 2048), BF),
+            shape((2048, 256), BF),
+            shape((256, 384), BF),
         ],
-        34,
-    )
-    send1, near2, far2 = lax.optimization_barrier((send1, near2, far2))
-    got = hop((send1, send3, send2), 0)
-    hidden, pre_grad, other2, own = lax.optimization_barrier((hidden, pre_grad, other2, own))
+        [pltpu.VMEM((256, 3840), BF), pltpu.VMEM((4, 256, LANES), BF)],
+        26,
+    )
+    got1 = hop((sent1[0], sent1[2], sent1[1]), 0)
+    rest, near2, far2 = lax.optimization_barrier((rest, near2, far2))
+    own2, *sent2 = call(
+        weight_rest_kernel,
+        "weight_terms_rest",
+        flops * 4 // 9,
+        (place, chip, sides, turned, local, rest),
+        tiles,
+        [pltpu.VMEM((256, 3584), BF), pltpu.VMEM((4, 256, LANES), BF)],
+        26,
+    )
+    got2 = hop((sent2[0], sent2[2], sent2[1]), 0)
+    hidden, pre_grad, other2, own2, *got1 = lax.optimization_barrier(
+        (hidden, pre_grad, other2, own2, *got1)
+    )
     last = call(
         last_inner_kernel,
         "outputs_inner",
@@ -559,8 +618,8 @@
         edge_scratch,
         24,
     )
-    own, output, field_grad = lax.optimization_barrier((own, output, field_grad))
-    first_grad, second_grad = reduce_tiles(own, got, core)
+    own2, output, field_grad = lax.optimization_barrier((own2, output, field_grad))
+    first_grad, second_grad = reduce_tiles(place, (own1, *got1, own2, *got2), core)
     return output[None], field_grad[None], first_grad, second_grad
 
 

time: 92 us -> 93.3 us (1.014)
  waiting for transfers between devices: 27.4 us -> 16.3 us
  starting transfers between devices: 23.9 us -> 33.8 us
  Pallas kernels: 33.5 us -> 35.3 us
  local copies, waits for them, and re-layouts: 3.19 us -> 4.41 us
    ppermute x9 -> x12, waiting for transfers between devices: 22.2 us -> 9.46 us  [hop(): lax.ppermute(part, ALL, hop_pairs(stage, distance))]
    ppermute x9 -> x12, starting transfers between devices: 17 us -> 22.4 us  [hop(): lax.ppermute(part, ALL, hop_pairs(stage, distance))]
    ppermute x2, starting transfers between devices: 4.68 us -> 9.21 us  [swap_slabs(): got_near = lax.ppermute(jnp.where(low_half, high, low), 'px', near)]
    ppermute x2, waiting for transfers between devices: 1.68 us -> 4.36 us  [swap_slabs(): got_near = lax.ppermute(jnp.where(low_half, high, low), 'px', near)]
    pallas_call x7 -> x9, Pallas kernels: 33.5 us -> 35.3 us  [call(): pl.pallas_call(kernel, name=name, out_shape=outs, in_specs=[pl.BlockSpec(...]
    squeeze x2, local copies, waits for them, and re-layouts: 0.04 us -> 1.16 us  [slab(): second[i]]
    squeeze x2, local copies, waits for them, and re-layouts: 0.04 us -> 1.08 us  [slab(): first[i]]
    ppermute x4, waiting for transfers between devices: 3.44 us -> 2.49 us  [swap_cores(): return lax.ppermute(value, 'py', [(0, 1), (1, 0)])]
  transfers between devices with their start and end apart: 17 -> 20, of which waited for: 12 -> 10; matrix products, arithmetic and copies ran while one was open for 0% -> 3% of each run, Pallas kernels for 34% -> 35%
where the time goes in v7:
time: 93.3 us; the launch traced here: 92 us
  Pallas kernels  35.3 us (38%)
  starting transfers between devices  33.8 us (36%)
  waiting for transfers between devices  16.3 us (17%)
  local copies, waits for them, and re-layouts  4.41 us (5%)
  other arithmetic  1.19 us (1%)
  between operations  0.98 us (1%)
    pallas_call x9, Pallas kernels, call(): pl.pallas_call(kernel, name=name, out_shape=outs, in_specs=[pl.BlockSpec(...  35.3 us
    ppermute x12, starting transfers between devices, hop(): lax.ppermute(part, ALL, hop_pairs(stage, distance))  22.4 us
    ppermute x12, waiting for transfers between devices, hop(): lax.ppermute(part, ALL, hop_pairs(stage, distance))  9.46 us
    ppermute x2, starting transfers between devices, swap_slabs(): got_near = lax.ppermute(jnp.where(low_half, high, low), 'px', near)  9.21 us
    ppermute x2, waiting for transfers between devices, swap_slabs(): got_near = lax.ppermute(jnp.where(low_half, high, low), 'px', near)  4.36 us
    ppermute x4, waiting for transfers between devices, swap_cores(): return lax.ppermute(value, 'py', [(0, 1), (1, 0)])  2.49 us
    unnamed x10, local copies, waits for them, and re-layouts  2.09 us
  transfers between devices with their start and end apart: 20, of which 10 were waited for; matrix products, arithmetic and copies ran while one was open for 3% of the time, Pallas kernels for 35%

profile of v7, /device:TPU:0, one launch (start us, length us, event | category | flops | bytes accessed | tf_op | source)
XLA Modules:
  0.0 92.0 jit_solution(14634232672912238438)
XLA Ops:
  0.6 0.0 copy-start
  0.6 1.0 %copy-done = bf16[1,4,8,32,256]{4,3,2,1,0:T(8,128)(2,1)S(1)} copy-done((bf16[1,4,8,32,256]{4,3,2,1,0:T(8,128)(2,1)S(1)}, bf16[1,4,8,32,256]{4,3,2,1,0:T(8,128)(2,1)}, u32[]{:S(2)}) %copy-start) | copy-done | bytes 524312
  1.7 0.0 copy-start.2
  1.7 1.0 %copy-done.2 = bf16[1,4,8,32,256]{4,3,2,1,0:T(8,128)(2,1)S(1)} copy-done((bf16[1,4,8,32,256]{4,3,2,1,0:T(8,128)(2,1)S(1)}, bf16[1,4,8,32,256]{4,3,2,1,0:T(8,128)(2,1)}, u32[]{:S(2)}) %copy-start.2) | copy-done | bytes 524312
  2.7 0.1 pack.1
  2.8 0.1 collective-permute-start
  2.9 0.0 copy-start.4
  2.9 0.1 pad_add_fusion.place
  3.0 1.1 %slice_bitcast_fusion.6 = (bf16[8,32,256]{2,1,0:T(8,128)(2,1)S(1)}, bf16[8,32,256]{2,1,0:T(8,128)(2,1)S(1)}) fusion(bf16[1,4,8,32,256]{4,3,2,1,0:T(8,128)(2,1)} %param.4), kind=kLoop, calls=%fused_computation.24 | loop fusion | bytes 524288 | tf_op jit(solution)/shard_map/squeeze | solution.py:448
  4.2 1.1 %slice_bitcast_fusion.7 = (bf16[8,32,256]{2,1,0:T(8,128)(2,1)S(1)}, bf16[8,32,256]{2,1,0:T(8,128)(2,1)S(1)}) fusion(bf16[1,4,8,32,256]{4,3,2,1,0:T(8,128)(2,1)} %param.5), kind=kLoop, calls=%fused_computation.25 | loop fusion | bytes 524288 | tf_op jit(solution)/shard_map/squeeze | solution.py:447
  5.2 0.0 collective-permute-done.other
  5.4 0.1 broadcast_select_fusion.2
  5.4 0.7 collective-permute-start.2
  6.1 4.3 %collective-permute-start.1 = (bf16[2,9,32,256]{3,2,1,0:T(8,128)(2,1)S(1)}, bf16[2,9,32,256]{3,2,1,0:T(8,128)(2,1)S(1)}, u32[]{:S(2)}, u32[]{:S(2)}) collective-permute-start(bf16[2,9,32,256]{3,2,1,0:T(8,128)(2,1)S(1)} %get-tuple-element.105), channel_id=1, source_target_pairs={{0,2},{2,0},{4,6},{6,4},{8,10},{10,8},{12,14},{14,12},{1,3},{3,1},... | collective-permute-start | bytes 884744 | tf_op jit(solution)/shard_map/ppermute | solution.py:454
  10.5 0.0 copy-done.1
  10.5 0.0 copy-done.3
  10.5 0.0 copy-done.4
  10.5 9.4 %inner.1 = (bf16[2,8,32,256]{3,2,1,0:T(8,128)(2,1)S(1)}, bf16[2,8,32,256]{3,2,1,0:T(8,128)(2,1)S(1)}, f32[2,256,256]{2,1,0:T(8,128)S(1)}, f32[2,256,256]{2,1,0:T...) custom-call(s32[4]{0:T(128)S(1)} %pad_add_fusion.place, bf16[4,8,32,256]{3,2,1,0:T(8,128)(2,1)S(1)} %bitcast.75, ...), custom_call_target="tpu_custom_call" | custom-call | flops 6039797760 | bytes 8388608 | tf_op jit(solution)/shard_map/inner/pallas_call | solution.py:417
  19.9 1.1 %chip.1 = bf16[4,18,32,768]{3,2,1,0:T(8,128)(2,1)S(1)} custom-call(s32[4]{0:T(128)S(1)} %pad_add_fusion.place, bf16[4,8,32,256]{3,2,1,0:T(8,128)(2,1)S(1)} %bitcast.76, bf16[4,8,32,256]{3,2,1,0:T(8,128)(2,1)S(1)} %bitcast.81, bf16[4,9,32,256]{3,2,1,0:T(8,128)(2,1)S(1)} %collective-permute-done.other), custom_call_target="tpu_custom_call" | custom-call | flops 905969664 | bytes 8388608 | tf_op jit(solution)/shard_map/chip/pallas_call | solution.py:417
  21.0 0.0 collective-permute-done.2.far.far1
  21.0 2.4 %collective-permute-done.1.near.near1 = bf16[2,9,32,256]{3,2,1,0:T(8,128)(2,1)S(1)} collective-permute-done((bf16[2,9,32,256]{3,2,1,0:T(8,128)(2,1)S(1)}, bf16[2,9,32,256]{3,2,1,0:T(8,128)(2,1)S(1)}, u32[]{:S(2)}, u32[]{:S(2)}) %collective-permute-start.1) | collective-permute-done | bytes 294944 | tf_op jit(solution)/shard_map/ppermute | solution.py:454
  23.4 2.3 %outer.1 = (bf16[4,8,32,256]{3,2,1,0:T(8,128)(2,1)S(1)}, bf16[4,8,32,256]{3,2,1,0:T(8,128)(2,1)S(1)}, bf16[4,9,32,256]{3,2,1,0:T(8,128)(2,1)S(1)}) custom-call(s32[4]{0:T(128)S(1)} %pad_add_fusion.place, bf16[2,9,32,256]{3,2,1,0:T(8,128)(2,1)S(1)} %collective-permute-done.1.near.near1, bf16[2,9,32,256]{3,2,1,0:T(8,128)(2,1)S(1)} %collective-permute-done.2.far.far1, ...), custom_call_target="tpu_custom_call" | custom-call | flops 1207959552 | bytes 8388608 | tf_op jit(solution)/shard_map/outer/pallas_call | solution.py:417
  25.7 0.1 collective-permute-start.3
  25.9 0.6 collective-permute-start.4
  26.5 1.3 %collective-permute-done.3.other2.other = bf16[4,9,32,256]{3,2,1,0:T(8,128)(2,1)S(1)} collective-permute-done((bf16[4,9,32,256]{3,2,1,0:T(8,128)(2,1)S(1)}, bf16[4,9,32,256]{3,2,1,0:T(8,128)(2,1)S(1)}, u32[]{:S(2)}, u32[]{:S(2)}) %collective-permute-start.3) | collective-permute-done | bytes 589856 | tf_op jit(solution)/shard_map/ppermute | solution.py:436
  27.9 0.1 broadcast_select_fusion
  28.0 0.7 collective-permute-start.6
  28.7 4.9 %collective-permute-start.5 = (bf16[2,9,32,256]{3,2,1,0:T(8,128)(2,1)S(1)}, bf16[2,9,32,256]{3,2,1,0:T(8,128)(2,1)S(1)}, u32[]{:S(2)}, u32[]{:S(2)}) collective-permute-start(bf16[2,9,32,256]{3,2,1,0:T(8,128)(2,1)S(1)} %get-tuple-element.101), channel_id=1, source_target_pairs={{0,2},{2,0},{4,6},{6,4},{8,10},{10,8},{12,14},{14,12},{1,3},{3,1},... | collective-permute-start | bytes 884744 | tf_op jit(solution)/shard_map/ppermute | solution.py:454
  33.5 0.0 collective-permute-done.4.edges
  33.5 5.9 %weight_terms.1 = (bf16[8,32,896]{2,1,0:T(8,128)(2,1)S(1)}, bf16[8,32,896]{2,1,0:T(8,128)(2,1)S(1)}, bf16[8,32,896]{2,1,0:T(8,128)(2,1)S(1)}, bf16[8,32,896]{2,1...) custom-call(s32[4]{0:T(128)S(1)} %pad_add_fusion.place, ...), custom_call_target="tpu_custom_call" | custom-call | flops 4026531840 | bytes 8388608 | tf_op jit(solution)/shard_map/weight_terms/pallas_call | solution.py:417
  39.4 1.6 %collective-permute-start.7 = (bf16[8,32,896]{2,1,0:T(8,128)(2,1)S(1)}, bf16[8,32,896]{2,1,0:T(8,128)(2,1)S(1)}, u32[]{:S(2)}, u32[]{:S(2)}) collective-permute-start(bf16[8,32,896]{2,1,0:T(8,128)(2,1)S(1)} %get-tuple-element.71), channel_id=1, source_target_pairs={{0,4},{2,6},{16,20},{18,22},{32,36},{34,38},{48,52},{50,54},{64,68... | collective-permute-start | bytes 1376264 | tf_op jit(solution)/shard_map/ppermute | solution.py:460
  41.0 1.7 %collective-permute-start.8 = (bf16[8,32,896]{2,1,0:T(8,128)(2,1)S(1)}, bf16[8,32,896]{2,1,0:T(8,128)(2,1)S(1)}, u32[]{:S(2)}, u32[]{:S(2)}) collective-permute-start(bf16[8,32,896]{2,1,0:T(8,128)(2,1)S(1)} %get-tuple-element.72), channel_id=1, source_target_pairs={{0,12},{2,14},{16,28},{18,30},{32,44},{34,46},{48,60},{50,62},{64,... | collective-permute-start | bytes 1376264 | tf_op jit(solution)/shard_map/ppermute | solution.py:460
  42.7 1.5 %collective-permute-start.9 = (bf16[8,32,896]{2,1,0:T(8,128)(2,1)S(1)}, bf16[8,32,896]{2,1,0:T(8,128)(2,1)S(1)}, u32[]{:S(2)}, u32[]{:S(2)}) collective-permute-start(bf16[8,32,896]{2,1,0:T(8,128)(2,1)S(1)} %get-tuple-element.73), channel_id=1, source_target_pairs={{0,8},{2,10},{16,24},{18,26},{32,40},{34,42},{48,56},{50,58},{64,7... | collective-permute-start | bytes 1376264 | tf_op jit(solution)/shard_map/ppermute | solution.py:460
  44.2 0.0 collective-permute-done.6.far
  44.2 2.0 %collective-permute-done.5.near = bf16[2,9,32,256]{3,2,1,0:T(8,128)(2,1)S(1)} collective-permute-done((bf16[2,9,32,256]{3,2,1,0:T(8,128)(2,1)S(1)}, bf16[2,9,32,256]{3,2,1,0:T(8,128)(2,1)S(1)}, u32[]{:S(2)}, u32[]{:S(2)}) %collective-permute-start.5) | collective-permute-done | bytes 294944 | tf_op jit(solution)/shard_map/ppermute | solution.py:454
  46.2 4.8 %weight_terms_rest.1 = (bf16[8,32,896]{2,1,0:T(8,128)(2,1)S(1)}, bf16[8,32,896]{2,1,0:T(8,128)(2,1)S(1)}, bf16[8,32,896]{2,1,0:T(8,128)(2,1)S(1)}, bf16[8,32,896]{2,1,0:T(8,128)(2,1)S(1)}) custom-call(s32[4]{0:T(128)S(1)} %pad_add_fusion.place, bf16[4,18,32,768]{3,2,1,0:T(8,128)(2,1)S(1)} %chip.1, bf16[2,18,32,768]{3,2,1,0:T(8,128)(2,1)S(1)} %get-tuple-element.65.sides, ...), custom_call_target="tpu_custom_call" | custom-call | flops 3221225472 | bytes 8388608 | tf_op jit(solution)/shard_map/weight_terms_rest/pallas_call | solution.py:417
  51.1 2.2 %collective-permute-start.10 = (bf16[8,32,896]{2,1,0:T(8,128)(2,1)S(1)}, bf16[8,32,896]{2,1,0:T(8,128)(2,1)S(1)}, u32[]{:S(2)}, u32[]{:S(2)}) collective-permute-start(bf16[8,32,896]{2,1,0:T(8,128)(2,1)S(1)} %get-tuple-element.93), channel_id=1, source_target_pairs={{0,4},{2,6},{16,20},{18,22},{32,36},{34,38},{48,52},{50,54},{64,68... | collective-permute-start | bytes 1376264 | tf_op jit(solution)/shard_map/ppermute | solution.py:460
  53.2 1.4 %collective-permute-start.11 = (bf16[8,32,896]{2,1,0:T(8,128)(2,1)S(1)}, bf16[8,32,896]{2,1,0:T(8,128)(2,1)S(1)}, u32[]{:S(2)}, u32[]{:S(2)}) collective-permute-start(bf16[8,32,896]{2,1,0:T(8,128)(2,1)S(1)} %get-tuple-element.94), channel_id=1, source_target_pairs={{0,12},{2,14},{16,28},{18,30},{32,44},{34,46},{48,60},{50,62},{64,... | collective-permute-start | bytes 1376264 | tf_op jit(solution)/shard_map/ppermute | solution.py:460
  54.6 0.0 collective-permute-done.7.refs_1_
  54.6 2.2 %collective-permute-start.12 = (bf16[8,32,896]{2,1,0:T(8,128)(2,1)S(1)}, bf16[8,32,896]{2,1,0:T(8,128)(2,1)S(1)}, u32[]{:S(2)}, u32[]{:S(2)}) collective-permute-start(bf16[8,32,896]{2,1,0:T(8,128)(2,1)S(1)} %get-tuple-element.95), channel_id=1, source_target_pairs={{0,8},{2,10},{16,24},{18,26},{32,40},{34,42},{48,56},{50,58},{64,7... | collective-permute-start | bytes 1376264 | tf_op jit(solution)/shard_map/ppermute | solution.py:460
  56.8 0.0 collective-permute-done.8.refs_2_
  56.8 0.0 collective-permute-done.9.refs_3_
  56.8 7.4 %outputs_inner.1 = (bf16[2,8,32,256]{3,2,1,0:T(8,128)(2,1)S(1)}, bf16[2,8,32,256]{3,2,1,0:T(8,128)(2,1)S(1)}, f32[2,256,256]{2,1,0:T(8,128)S(1)}, f32[2,256,256]{2,1,0:T(8,128)S(1)}) custom-call(s32[4]{0:T(128)S(1)} %pad_add_fusion.place, bf16[4,8,32,256]{3,2,1,0:T(8,128)(2,1)S(1)} %get-tuple-element.77.hid, ...), custom_call_target="tpu_custom_call" | custom-call | flops 6039797760 | bytes 8388608 | tf_op jit(solution)/shard_map/outputs_inner/pallas_call | solution.py:417
  64.2 3.2 %outputs_outer.1 = (bf16[4,8,32,256]{3,2,1,0:T(8,128)(2,1)}, bf16[4,8,32,256]{3,2,1,0:T(8,128)(2,1)}) custom-call(s32[4]{0:T(128)S(1)} %pad_add_fusion.place, bf16[2,9,32,256]{3,2,1,0:T(8,128)(2,1)S(1)} %collective-permute-done.5.near, bf16[2,9,32,256]{3,2,1,0:T(8,128)(2,1)S(1)} %collective-permute-done.6.far, ...), custom_call_target="tpu_custom_call" | custom-call | flops 1207959552 | bytes 8388608 | tf_op jit(solution)/shard_map/outputs_outer/pallas_call | solution.py:417
  67.4 0.0 collective-permute-done.10.refs_5_
  67.4 0.0 collective-permute-done.11.refs_6_
  67.4 0.0 collective-permute-done.12.refs_7_
  67.4 1.1 %sum.1 = (f32[4,32,896]{2,1,0:T(8,128)S(1)}, bf16[4,32,896]{2,1,0:T(8,128)(2,1)S(1)}, bf16[4,32,896]{2,1,0:T(8,128)(2,1)S(1)}, bf16[4,32,896]{2,1,0:T(8,128)(2,1)S(1)}) custom-call(s32[4]{0:T(128)S(1)} %pad_add_fusion.place, bf16[8,32,896]{2,1,0:T(8,128)(2,1)S(1)} %get-tuple-element.88.refs_0_, bf16[8,32,896]{2,1,0:T(8,128)(2,1)S(1)} %collective-permute-done.7.refs_1_, ...), custom_call_target="tpu_custom_call" | custom-call | bytes 8388608 | tf_op jit(solution)/shard_map/sum/pallas_call | solution.py:417
  68.5 1.6 %collective-permute-start.13 = (bf16[4,32,896]{2,1,0:T(8,128)(2,1)S(1)}, bf16[4,32,896]{2,1,0:T(8,128)(2,1)S(1)}, u32[]{:S(2)}, u32[]{:S(2)}) collective-permute-start(bf16[4,32,896]{2,1,0:T(8,128)(2,1)S(1)} %get-tuple-element.97), channel_id=1, source_target_pairs={{0,32},{2,34},{16,48},{18,50},{32,64},{34,66},{48,80},{50,82},{64,... | collective-permute-start | bytes 688136 | tf_op jit(solution)/shard_map/ppermute | solution.py:460
  70.1 1.7 %collective-permute-start.14 = (bf16[4,32,896]{2,1,0:T(8,128)(2,1)S(1)}, bf16[4,32,896]{2,1,0:T(8,128)(2,1)S(1)}, u32[]{:S(2)}, u32[]{:S(2)}) collective-permute-start(bf16[4,32,896]{2,1,0:T(8,128)(2,1)S(1)} %get-tuple-element.98), channel_id=1, source_target_pairs={{0,96},{2,98},{16,112},{18,114},{32,0},{34,2},{48,16},{50,18},{64,... | collective-permute-start | bytes 688136 | tf_op jit(solution)/shard_map/ppermute | solution.py:460
  71.8 2.0 %collective-permute-start.15 = (bf16[4,32,896]{2,1,0:T(8,128)(2,1)S(1)}, bf16[4,32,896]{2,1,0:T(8,128)(2,1)S(1)}, u32[]{:S(2)}, u32[]{:S(2)}) collective-permute-start(bf16[4,32,896]{2,1,0:T(8,128)(2,1)S(1)} %get-tuple-element.99), channel_id=1, source_target_pairs={{0,64},{2,66},{16,80},{18,82},{32,96},{34,98},{48,112},{50,114},{6... | collective-permute-start | bytes 688136 | tf_op jit(solution)/shard_map/ppermute | solution.py:460
  73.8 2.0 %collective-permute-done.13 = bf16[4,32,896]{2,1,0:T(8,128)(2,1)S(1)} collective-permute-done((bf16[4,32,896]{2,1,0:T(8,128)(2,1)S(1)}, bf16[4,32,896]{2,1,0:T(8,128)(2,1)S(1)}, u32[]{:S(2)}, u32[]{:S(2)}) %collective-permute-start.13) | collective-permute-done | bytes 229408 | tf_op jit(solution)/shard_map/ppermute | solution.py:460
  75.8 0.4 collective-permute-done.14
  76.2 3.3 %collective-permute-done.15 = bf16[4,32,896]{2,1,0:T(8,128)(2,1)S(1)} collective-permute-done((bf16[4,32,896]{2,1,0:T(8,128)(2,1)S(1)}, bf16[4,32,896]{2,1,0:T(8,128)(2,1)S(1)}, u32[]{:S(2)}, u32[]{:S(2)}) %collective-permute-start.15) | collective-permute-done | bytes 229408 | tf_op jit(solution)/shard_map/ppermute | solution.py:460
  79.5 0.1 convert_add_fusion
  79.6 1.7 %collective-permute-start.16 = (f32[32,896]{1,0:T(8,128)S(1)}, f32[32,896]{1,0:T(8,128)S(1)}, u32[]{:S(2)}, u32[]{:S(2)}) collective-permute-start(f32[32,896]{1,0:T(8,128)S(1)} %get-tuple-element.116), channel_id=1, source_target_pairs={{0,2},{2,16},{16,18},{18,0},{32,34},{34,48},{48,50},{50,32},{64,66... | collective-permute-start | bytes 344072 | tf_op jit(solution)/shard_map/ppermute | solution.py:460
  81.3 3.9 %collective-permute-start.18 = (f32[32,896]{1,0:T(8,128)S(1)}, f32[32,896]{1,0:T(8,128)S(1)}, u32[]{:S(2)}, u32[]{:S(2)}) collective-permute-start(f32[32,896]{1,0:T(8,128)S(1)} %get-tuple-element.117), channel_id=1, source_target_pairs={{0,16},{2,18},{16,0},{18,2},{32,48},{34,50},{48,32},{50,34},{64,80... | collective-permute-start | bytes 344072 | tf_op jit(solution)/shard_map/ppermute | solution.py:460
  85.1 1.1 %collective-permute-start.17 = (f32[32,896]{1,0:T(8,128)S(1)}, f32[32,896]{1,0:T(8,128)S(1)}, u32[]{:S(2)}, u32[]{:S(2)}) collective-permute-start(f32[32,896]{1,0:T(8,128)S(1)} %get-tuple-element.118), channel_id=1, source_target_pairs={{0,18},{2,0},{16,2},{18,16},{32,50},{34,32},{48,34},{50,48},{64,82... | collective-permute-start | bytes 344072 | tf_op jit(solution)/shard_map/ppermute | solution.py:460
  86.2 0.2 collective-permute-done.16
  86.4 2.7 %collective-permute-done.18 = f32[32,896]{1,0:T(8,128)S(1)} collective-permute-done((f32[32,896]{1,0:T(8,128)S(1)}, f32[32,896]{1,0:T(8,128)S(1)}, u32[]{:S(2)}, u32[]{:S(2)}) %collective-permute-start.18) | collective-permute-done | bytes 114720 | tf_op jit(solution)/shard_map/ppermute | solution.py:460
  89.1 0.8 collective-permute-done.17
  90.0 0.1 collective-permute-start.19
  90.1 1.2 %collective-permute-done.19 = f32[16,896]{1,0:T(8,128)S(1)} collective-permute-done((f32[16,896]{1,0:T(8,128)S(1)}, f32[16,896]{1,0:T(8,128)S(1)}, u32[]{:S(2)}, u32[]{:S(2)}) %collective-permute-start.19) | collective-permute-done | bytes 57376 | tf_op jit(solution)/shard_map/ppermute | solution.py:436
  91.3 0.7 select_bitcast_fusion
  (23 shorter events, 0.4 us)
Async XLA Ops:
  0.6 1.0 %copy-start = (bf16[1,4,8,32,256]{4,3,2,1,0:T(8,128)(2,1)S(1)}, bf16[1,4,8,32,256]{4,3,2,1,0:T(8,128)(2,1)}, u32[]{:S(2)}) copy-start(bf16[1,4,8,32,256]{4,3,2,1,0:T(8,128)(2,1)} %param.5) | copy-start | bytes 1572868
  1.7 1.0 %copy-start.2 = (bf16[1,4,8,32,256]{4,3,2,1,0:T(8,128)(2,1)S(1)}, bf16[1,4,8,32,256]{4,3,2,1,0:T(8,128)(2,1)}, u32[]{:S(2)}) copy-start(bf16[1,4,8,32,256]{4,3,2,1,0:T(8,128)(2,1)} %param.4) | copy-start | bytes 1572868
  2.7 7.7 %copy-start.1 = (bf16[1,4,8,32,256]{4,3,2,1,0:T(8,128)(2,1)S(1)}, bf16[1,4,8,32,256]{4,3,2,1,0:T(8,128)(2,1)}, u32[]{:S(2)}) copy-start(bf16[1,4,8,32,256]{4,3,2,1,0:T(8,128)(2,1)} %param.5) | copy-start | bytes 1572868
  2.7 7.7 %copy-start.3 = (bf16[1,4,8,32,256]{4,3,2,1,0:T(8,128)(2,1)S(1)}, bf16[1,4,8,32,256]{4,3,2,1,0:T(8,128)(2,1)}, u32[]{:S(2)}) copy-start(bf16[1,4,8,32,256]{4,3,2,1,0:T(8,128)(2,1)} %param.4) | copy-start | bytes 1572868
  2.8 2.4 %collective-permute-start = (bf16[4,9,32,256]{3,2,1,0:T(8,128)(2,1)S(1)}, bf16[4,9,32,256]{3,2,1,0:T(8,128)(2,1)S(1)}, u32[]{:S(2)}, u32[]{:S(2)}) collective-permute-start(bf16[4,9,32,256]{3,2,1,0:T(8,128)(2,1)S(1)} %pack.1), channel_id=1, source_target_pairs={{0,1},{1,0},{2,3},{3,2},{4,5},{5,4},{6,7},{7,6},{8,9},{9,8},{10,11... | collective-permute-start | bytes 1769480 | tf_op jit(solution)/shard_map/ppermute | solution.py:436
  2.9 7.5 %copy-start.4 = (bf16[6912,256]{1,0:T(8,128)(2,1)S(1)}, bf16[6912,256]{1,0:T(8,128)(2,1)}, u32[]{:S(2)}) copy-start(bf16[6912,256]{1,0:T(8,128)(2,1)} %first_hbm.1) | copy-start | bytes 10616836
  5.4 15.6 %collective-permute-start.2 = (bf16[2,9,32,256]{3,2,1,0:T(8,128)(2,1)S(1)}, bf16[2,9,32,256]{3,2,1,0:T(8,128)(2,1)S(1)}, u32[]{:S(2)}, u32[]{:S(2)}) collective-permute-start(bf16[2,9,32,256]{3,2,1,0:T(8,128)(2,1)S(1)} %get-tuple-element.104), channel_id=1, source_target_pairs={{2,4},{4,2},{6,8},{8,6},{10,12},{12,10},{3,5},{5,3},{7,9},{9,7},{1... | collective-permute-start | bytes 884744 | tf_op jit(solution)/shard_map/ppermute | solution.py:453
  6.1 17.2 %collective-permute-start.1 = (bf16[2,9,32,256]{3,2,1,0:T(8,128)(2,1)S(1)}, bf16[2,9,32,256]{3,2,1,0:T(8,128)(2,1)S(1)}, u32[]{:S(2)}, u32[]{:S(2)}) collective-permute-start(bf16[2,9,32,256]{3,2,1,0:T(8,128)(2,1)S(1)} %get-tuple-element.105), channel_id=1, source_target_pairs={{0,2},{2,0},{4,6},{6,4},{8,10},{10,8},{12,14},{14,12},{1,3},{3,1},... | collective-permute-start | bytes 884744 | tf_op jit(solution)/shard_map/ppermute | solution.py:454
  25.7 2.1 %collective-permute-start.3 = (bf16[4,9,32,256]{3,2,1,0:T(8,128)(2,1)S(1)}, bf16[4,9,32,256]{3,2,1,0:T(8,128)(2,1)S(1)}, u32[]{:S(2)}, u32[]{:S(2)}) collective-permute-start(bf16[4,9,32,256]{3,2,1,0:T(8,128)(2,1)S(1)} %get-tuple-element.63), channel_id=1, source_target_pairs={{0,1},{1,0},{2,3},{3,2},{4,5},{5,4},{6,7},{7,6},{8,9},{9,8},{10,11... | collective-permute-start | bytes 1769480 | tf_op jit(solution)/shard_map/ppermute | solution.py:436
  25.9 7.6 %collective-permute-start.4 = (bf16[2,8,32,256]{3,2,1,0:T(8,128)(2,1)S(1)}, bf16[2,8,32,256]{3,2,1,0:T(8,128)(2,1)S(1)}, u32[]{:S(2)}, u32[]{:S(2)}) collective-permute-start(bf16[2,8,32,256]{3,2,1,0:T(8,128)(2,1)S(1)} %maximum_select_fusion), channel_id=1, source_target_pairs={{0,1},{1,0},{2,3},{3,2},{4,5},{5,4},{6,7},{7,6},{8,9},{9,8},{10,11... | collective-permute-start | bytes 786440 | tf_op jit(solution)/shard_map/ppermute | solution.py:436
  28.0 16.3 %collective-permute-start.6 = (bf16[2,9,32,256]{3,2,1,0:T(8,128)(2,1)S(1)}, bf16[2,9,32,256]{3,2,1,0:T(8,128)(2,1)S(1)}, u32[]{:S(2)}, u32[]{:S(2)}) collective-permute-start(bf16[2,9,32,256]{3,2,1,0:T(8,128)(2,1)S(1)} %get-tuple-element.100), channel_id=1, source_target_pairs={{2,4},{4,2},{6,8},{8,6},{10,12},{12,10},{3,5},{5,3},{7,9},{9,7},{1... | collective-permute-start | bytes 884744 | tf_op jit(solution)/shard_map/ppermute | solution.py:453
  28.7 17.6 %collective-permute-start.5 = (bf16[2,9,32,256]{3,2,1,0:T(8,128)(2,1)S(1)}, bf16[2,9,32,256]{3,2,1,0:T(8,128)(2,1)S(1)}, u32[]{:S(2)}, u32[]{:S(2)}) collective-permute-start(bf16[2,9,32,256]{3,2,1,0:T(8,128)(2,1)S(1)} %get-tuple-element.101), channel_id=1, source_target_pairs={{0,2},{2,0},{4,6},{6,4},{8,10},{10,8},{12,14},{14,12},{1,3},{3,1},... | collective-permute-start | bytes 884744 | tf_op jit(solution)/shard_map/ppermute | solution.py:454
  39.4 15.2 %collective-permute-start.7 = (bf16[8,32,896]{2,1,0:T(8,128)(2,1)S(1)}, bf16[8,32,896]{2,1,0:T(8,128)(2,1)S(1)}, u32[]{:S(2)}, u32[]{:S(2)}) collective-permute-start(bf16[8,32,896]{2,1,0:T(8,128)(2,1)S(1)} %get-tuple-element.71), channel_id=1, source_target_pairs={{0,4},{2,6},{16,20},{18,22},{32,36},{34,38},{48,52},{50,54},{64,68... | collective-permute-start | bytes 1376264 | tf_op jit(solution)/shard_map/ppermute | solution.py:460
  41.0 15.8 %collective-permute-start.8 = (bf16[8,32,896]{2,1,0:T(8,128)(2,1)S(1)}, bf16[8,32,896]{2,1,0:T(8,128)(2,1)S(1)}, u32[]{:S(2)}, u32[]{:S(2)}) collective-permute-start(bf16[8,32,896]{2,1,0:T(8,128)(2,1)S(1)} %get-tuple-element.72), channel_id=1, source_target_pairs={{0,12},{2,14},{16,28},{18,30},{32,44},{34,46},{48,60},{50,62},{64,... | collective-permute-start | bytes 1376264 | tf_op jit(solution)/shard_map/ppermute | solution.py:460
  42.7 14.1 %collective-permute-start.9 = (bf16[8,32,896]{2,1,0:T(8,128)(2,1)S(1)}, bf16[8,32,896]{2,1,0:T(8,128)(2,1)S(1)}, u32[]{:S(2)}, u32[]{:S(2)}) collective-permute-start(bf16[8,32,896]{2,1,0:T(8,128)(2,1)S(1)} %get-tuple-element.73), channel_id=1, source_target_pairs={{0,8},{2,10},{16,24},{18,26},{32,40},{34,42},{48,56},{50,58},{64,7... | collective-permute-start | bytes 1376264 | tf_op jit(solution)/shard_map/ppermute | solution.py:460
  51.1 16.3 %collective-permute-start.10 = (bf16[8,32,896]{2,1,0:T(8,128)(2,1)S(1)}, bf16[8,32,896]{2,1,0:T(8,128)(2,1)S(1)}, u32[]{:S(2)}, u32[]{:S(2)}) collective-permute-start(bf16[8,32,896]{2,1,0:T(8,128)(2,1)S(1)} %get-tuple-element.93), channel_id=1, source_target_pairs={{0,4},{2,6},{16,20},{18,22},{32,36},{34,38},{48,52},{50,54},{64,68... | collective-permute-start | bytes 1376264 | tf_op jit(solution)/shard_map/ppermute | solution.py:460
  53.2 14.2 %collective-permute-start.11 = (bf16[8,32,896]{2,1,0:T(8,128)(2,1)S(1)}, bf16[8,32,896]{2,1,0:T(8,128)(2,1)S(1)}, u32[]{:S(2)}, u32[]{:S(2)}) collective-permute-start(bf16[8,32,896]{2,1,0:T(8,128)(2,1)S(1)} %get-tuple-element.94), channel_id=1, source_target_pairs={{0,12},{2,14},{16,28},{18,30},{32,44},{34,46},{48,60},{50,62},{64,... | collective-permute-start | bytes 1376264 | tf_op jit(solution)/shard_map/ppermute | solution.py:460
  54.6 12.8 %collective-permute-start.12 = (bf16[8,32,896]{2,1,0:T(8,128)(2,1)S(1)}, bf16[8,32,896]{2,1,0:T(8,128)(2,1)S(1)}, u32[]{:S(2)}, u32[]{:S(2)}) collective-permute-start(bf16[8,32,896]{2,1,0:T(8,128)(2,1)S(1)} %get-tuple-element.95), channel_id=1, source_target_pairs={{0,8},{2,10},{16,24},{18,26},{32,40},{34,42},{48,56},{50,58},{64,7... | collective-permute-start | bytes 1376264 | tf_op jit(solution)/shard_map/ppermute | solution.py:460
  68.5 7.3 %collective-permute-start.13 = (bf16[4,32,896]{2,1,0:T(8,128)(2,1)S(1)}, bf16[4,32,896]{2,1,0:T(8,128)(2,1)S(1)}, u32[]{:S(2)}, u32[]{:S(2)}) collective-permute-start(bf16[4,32,896]{2,1,0:T(8,128)(2,1)S(1)} %get-tuple-element.97), channel_id=1, source_target_pairs={{0,32},{2,34},{16,48},{18,50},{32,64},{34,66},{48,80},{50,82},{64,... | collective-permute-start | bytes 688136 | tf_op jit(solution)/shard_map/ppermute | solution.py:460
  70.1 6.0 %collective-permute-start.14 = (bf16[4,32,896]{2,1,0:T(8,128)(2,1)S(1)}, bf16[4,32,896]{2,1,0:T(8,128)(2,1)S(1)}, u32[]{:S(2)}, u32[]{:S(2)}) collective-permute-start(bf16[4,32,896]{2,1,0:T(8,128)(2,1)S(1)} %get-tuple-element.98), channel_id=1, source_target_pairs={{0,96},{2,98},{16,112},{18,114},{32,0},{34,2},{48,16},{50,18},{64,... | collective-permute-start | bytes 688136 | tf_op jit(solution)/shard_map/ppermute | solution.py:460
  71.8 7.7 %collective-permute-start.15 = (bf16[4,32,896]{2,1,0:T(8,128)(2,1)S(1)}, bf16[4,32,896]{2,1,0:T(8,128)(2,1)S(1)}, u32[]{:S(2)}, u32[]{:S(2)}) collective-permute-start(bf16[4,32,896]{2,1,0:T(8,128)(2,1)S(1)} %get-tuple-element.99), channel_id=1, source_target_pairs={{0,64},{2,66},{16,80},{18,82},{32,96},{34,98},{48,112},{50,114},{6... | collective-permute-start | bytes 688136 | tf_op jit(solution)/shard_map/ppermute | solution.py:460
  79.6 6.8 %collective-permute-start.16 = (f32[32,896]{1,0:T(8,128)S(1)}, f32[32,896]{1,0:T(8,128)S(1)}, u32[]{:S(2)}, u32[]{:S(2)}) collective-permute-start(f32[32,896]{1,0:T(8,128)S(1)} %get-tuple-element.116), channel_id=1, source_target_pairs={{0,2},{2,16},{16,18},{18,0},{32,34},{34,48},{48,50},{50,32},{64,66... | collective-permute-start | bytes 344072 | tf_op jit(solution)/shard_map/ppermute | solution.py:460
  81.3 7.9 %collective-permute-start.18 = (f32[32,896]{1,0:T(8,128)S(1)}, f32[32,896]{1,0:T(8,128)S(1)}, u32[]{:S(2)}, u32[]{:S(2)}) collective-permute-start(f32[32,896]{1,0:T(8,128)S(1)} %get-tuple-element.117), channel_id=1, source_target_pairs={{0,16},{2,18},{16,0},{18,2},{32,48},{34,50},{48,32},{50,34},{64,80... | collective-permute-start | bytes 344072 | tf_op jit(solution)/shard_map/ppermute | solution.py:460
  85.1 4.8 %collective-permute-start.17 = (f32[32,896]{1,0:T(8,128)S(1)}, f32[32,896]{1,0:T(8,128)S(1)}, u32[]{:S(2)}, u32[]{:S(2)}) collective-permute-start(f32[32,896]{1,0:T(8,128)S(1)} %get-tuple-element.118), channel_id=1, source_target_pairs={{0,18},{2,0},{16,2},{18,16},{32,50},{34,32},{48,34},{50,48},{64,82... | collective-permute-start | bytes 344072 | tf_op jit(solution)/shard_map/ppermute | solution.py:460
  90.0 1.3 %collective-permute-start.19 = (f32[16,896]{1,0:T(8,128)S(1)}, f32[16,896]{1,0:T(8,128)S(1)}, u32[]{:S(2)}, u32[]{:S(2)}) collective-permute-start(f32[16,896]{1,0:T(8,128)S(1)} %get-tuple-element.126), channel_id=1, source_target_pairs={{0,1},{1,0},{2,3},{3,2},{4,5},{5,4},{6,7},{7,6},{8,9},{9,8},{10,11... | collective-permute-start | bytes 172040 | tf_op jit(solution)/shard_map/ppermute | solution.py:436

commit v8 on v7

--- a/solution.py
+++ b/solution.py
@@ -9,7 +9,8 @@
 F32 = jnp.float32
 ALL = ("dp", "px", "py")
 X, Y, Z = 0, 1, 2
-ORDER = ((X, Y, Z), (Z, X, Y))
+ORDER = ((X, Y, Z), (Y, Z, X))
+EARLY, LATE = (0, 3, 5, 8), (1, 2, 4, 6, 7)
 LANES = 896
 
 
@@ -299,17 +300,17 @@
     ]
 
 
-def terms_of_first(flat, base, steps, chip, sides, turned):
-    for k in steps:
+def terms_of_first(flat, steps, chip, sides, turned):
+    for j, k in enumerate(steps):
         term = None
         for at, rows in windows(chip, sides, k // 3, k % 3):
             part = jnp.dot(turned[:, at : at + rows.shape[0]], rows, preferred_element_type=F32)
             term = part if term is None else term + part
-        flat[:, k * 768 - base : (k + 1) * 768 - base] = (term * 0.125).astype(BF)
-
-
-def terms_of_second(flat, base, steps, chip, sides, local):
-    for k in steps:
+        flat[:, j * 768 : (j + 1) * 768] = (term * 0.125).astype(BF)
+
+
+def terms_of_second(flat, steps, chip, sides, local):
+    for j, k in enumerate(steps):
         term = None
         for at, rows in windows(chip, sides, 2 - k // 3, 2 - k % 3):
             part = lax.dot_general(
@@ -321,28 +322,26 @@
             term = part if term is None else term + part
         term = (term * 0.125).astype(BF)
         for c in range(3):
-            start = (k * 3 + c) * 256 - base
+            start = (j * 3 + c) * 256
             flat[:, start : start + 256] = term[c * 256 : (c + 1) * 256]
 
 
-def give_tiles(place, flat, tiles, outs):
+def give_tiles(place, flat, tiles, width, outs):
     for k in range(4):
-        tiles[k] = flat[:, k * 864 : k * 864 + LANES]
-    x, z = place[1], place[3]
+        tiles[k] = flat[:, k * width : (k + 1) * width]
+    x, y = place[1], place[2]
     zero = place[0] == 0
     for first, ref in enumerate(outs):
         for i in range(8):
-            other, high = i // 2, i % 2
-            to_x = lax.rem(x + jnp.where(zero, first, other), 4)
-            to_z = lax.rem(z + jnp.where(zero, other, first), 4)
-            row = high * 2 + lax.div(to_z, 2)
-            to_px = to_x * 2 + lax.rem(to_z, 2)
-            ref[i] = tiles[row, pl.ds(pl.multiple_of(to_px * 32, 32), 32), :]
+            to_x = jnp.where(zero, lax.rem(x + first, 4), i // 2)
+            to_y = jnp.where(zero, i // 2, lax.rem(y + first, 4))
+            to_px = to_x * 2 + i % 2
+            ref[i] = tiles[to_y, pl.ds(pl.multiple_of(to_px * 32, 32), 32), :]
 
 
 def weight_kernel(
     place, chip, near1, far1, edges, hid, pre_grad, other2,
-    own, send1, send2, send3, sides, turned, local, rest, flat, tiles,
+    own, send1, send2, send3, sides, turned, local, flat, tiles,
 ):
     core = place[0]
     near = near_side(place)
@@ -363,7 +362,7 @@
         for i in range(4):
             turned[:, i * 512 : i * 512 + 256] = pre_grad[i].reshape(256, 256).T
             turned[:, i * 512 + 256 : i * 512 + 512] = other2[i, 0:8].reshape(256, 256).T
-        terms_of_first(flat, 0, range(5), chip, sides, turned)
+        terms_of_first(flat, EARLY, chip, sides, turned)
 
     @pl.when(core == 1)
     def _():
@@ -371,45 +370,69 @@
         for i in range(4):
             local[i * 512 : i * 512 + 256] = other2[i, 0:8].reshape(256, 256)
             local[i * 512 + 256 : i * 512 + 512] = hid[i].reshape(256, 256)
-        terms_of_second(flat, 0, range(5), chip, sides, local)
-
-    rest[...] = flat[:, 3456:3840]
-    give_tiles(place, flat, tiles, (own, send1, send2, send3))
+        terms_of_second(flat, EARLY, chip, sides, local)
+
+    give_tiles(place, flat, tiles, 768, (own, send1, send2, send3))
 
 
 def weight_rest_kernel(
-    place, chip, sides, turned, local, rest, own, send1, send2, send3, flat, tiles
+    place, chip, sides, turned, local, own, send1, send2, send3, flat, tiles
 ):
     core = place[0]
-    flat[:, 0:384] = rest[...]
-    flat[:, 3456:3584] = jnp.zeros((256, 128), BF)
 
     @pl.when(core == 0)
     def _():
-        terms_of_first(flat, 3456, range(5, 9), chip, sides, turned)
+        terms_of_first(flat, LATE, chip, sides, turned)
 
     @pl.when(core == 1)
     def _():
-        terms_of_second(flat, 3456, range(5, 9), chip, sides, local)
-
-    give_tiles(place, flat, tiles, (own, send1, send2, send3))
+        terms_of_second(flat, LATE, chip, sides, local)
+
+    give_tiles(place, flat, tiles, 960, (own, send1, send2, send3))
 
 
 def sum_kernel(place, *refs):
-    ins, (keep, send1, send2, send3, sums) = refs[:8], refs[8:]
-    for half in range(2):
+    ins, (keep, send1, send2, send3, whole, tiles) = refs[:8], refs[8:]
+    core, x, y, z = place[0], place[1], place[2], place[3]
+    zero = core == 0
+
+    def add(refs, i):
+        total = refs[0][i].astype(F32)
+        for ref in refs[1:]:
+            total = total + ref[i].astype(F32)
+        return total
+
+    def join(i, row):
+        early, late = add(ins[0:4], i), add(ins[4:8], i)
+        before = (0, 576, 384, 960)[row]
+        if before:
+            whole[i, :, 0:before] = late[:, 0:before]
+        whole[i, :, before : before + 768] = early
+        if before < 960:
+            whole[i, :, before + 768 : 1728] = late[:, before:960]
+
+    @pl.when(zero)
+    def _():
         for i in range(8):
-            total = ins[4 * half][i].astype(F32)
-            for ref in ins[4 * half + 1 : 4 * half + 4]:
-                total = total + ref[i].astype(F32)
-            sums[half * 8 + i] = total
-    zero, y = place[0] == 0, place[2]
+            join(i, i // 2)
+
+    for row in range(4):
+
+        @pl.when(jnp.logical_and(core == 1, y == row))
+        def _():
+            for i in range(8):
+                join(i, row)
+
+    for i in range(8):
+        whole[i, :, 1728:1792] = jnp.zeros((32, 64), F32)
+        for high in range(2):
+            tiles[i * 2 + high] = whole[i, :, high * 864 : high * 864 + LANES]
     for second, ref in enumerate((keep, send1, send2, send3)):
         for third in range(4):
-            to_y = lax.rem(y + jnp.where(zero, second, third), 4)
-            other = jnp.where(zero, third, second)
-            at = lax.div(to_y, 2) * 8 + other * 2 + lax.rem(to_y, 2)
-            ref[third] = sums[at].astype(ref.dtype)
+            to_z = lax.rem(z + jnp.where(zero, third, second), 4)
+            other = jnp.where(zero, lax.rem(y + second, 4), lax.rem(x + third, 4))
+            at = (other * 2 + lax.rem(to_z, 2)) * 2 + lax.div(to_z, 2)
+            ref[third] = tiles[at].astype(ref.dtype)
 
 
 def call(kernel, name, flops, args, outs, scratch, limit, far=()):
@@ -470,8 +493,8 @@
         0,
         (place, *halves),
         [shape((4, 32, LANES), F32)] + [shape((4, 32, LANES), BF)] * 3,
-        [pltpu.VMEM((16, 32, LANES), F32)],
-        16,
+        [pltpu.VMEM((8, 32, 1792), F32), pltpu.VMEM((16, 32, LANES), F32)],
+        18,
     )
     total = keep
     for part in hop((send1, send3, send2), 1):
@@ -569,31 +592,25 @@
         jnp.where(zero, other2[:, 0:1], other2[:, 8:9]),
         low_half,
     )
-    tiles = [shape((8, 32, LANES), BF)] * 4
-    own1, *sent1, sides, turned, local, rest = call(
+    own1, *sent1, sides, turned, local = call(
         weight_kernel,
         "weight_terms",
-        flops * 5 // 9,
+        flops * 4 // 9,
         (place, chip, near1, far1, edges, hidden, pre_grad, other2),
-        tiles
-        + [
-            shape((2, 18, 32, 768), BF),
-            shape((256, 2048), BF),
-            shape((2048, 256), BF),
-            shape((256, 384), BF),
-        ],
-        [pltpu.VMEM((256, 3840), BF), pltpu.VMEM((4, 256, LANES), BF)],
+        [shape((8, 32, 768), BF)] * 4
+        + [shape((2, 18, 32, 768), BF), shape((256, 2048), BF), shape((2048, 256), BF)],
+        [pltpu.VMEM((256, 3072), BF), pltpu.VMEM((4, 256, 768), BF)],
         26,
     )
     got1 = hop((sent1[0], sent1[2], sent1[1]), 0)
-    rest, near2, far2 = lax.optimization_barrier((rest, near2, far2))
+    turned, local, near2, far2 = lax.optimization_barrier((turned, local, near2, far2))
     own2, *sent2 = call(
         weight_rest_kernel,
         "weight_terms_rest",
-        flops * 4 // 9,
-        (place, chip, sides, turned, local, rest),
-        tiles,
-        [pltpu.VMEM((256, 3584), BF), pltpu.VMEM((4, 256, LANES), BF)],
+        flops * 5 // 9,
+        (place, chip, sides, turned, local),
+        [shape((8, 32, 960), BF)] * 4,
+        [pltpu.VMEM((256, 3840), BF), pltpu.VMEM((4, 256, 960), BF)],
         26,
     )
     got2 = hop((sent2[0], sent2[2], sent2[1]), 0)

time: 93.3 us -> 94.6 us (1.014)
  waiting for transfers between devices: 16.3 us -> 17.9 us
    ppermute x2, waiting for transfers between devices: 4.36 us -> 5.56 us  [swap_slabs(): got_near = lax.ppermute(jnp.where(low_half, high, low), 'px', near)]
  transfers between devices with their start and end apart: 20 -> 20, of which waited for: 10 -> 10; matrix products, arithmetic and copies ran while one was open for 3% -> 3% of each run, Pallas kernels for 35% -> 33%
where the time goes in v8:
time: 94.6 us; the launch traced here: 93.3 us
  Pallas kernels  35 us (37%)
  starting transfers between devices  33.8 us (36%)
  waiting for transfers between devices  17.9 us (19%)
  local copies, waits for them, and re-layouts  4.41 us (5%)
  other arithmetic  1.19 us (1%)
  between operations  0.98 us (1%)
    pallas_call x9, Pallas kernels, call(): pl.pallas_call(kernel, name=name, out_shape=outs, in_specs=[pl.BlockSpec(...  35 us
    ppermute x12, starting transfers between devices, hop(): lax.ppermute(part, ALL, hop_pairs(stage, distance))  22.4 us
    ppermute x12, waiting for transfers between devices, hop(): lax.ppermute(part, ALL, hop_pairs(stage, distance))  9.87 us
    ppermute x2, starting transfers between devices, swap_slabs(): got_near = lax.ppermute(jnp.where(low_half, high, low), 'px', near)  9.21 us
    ppermute x2, waiting for transfers between devices, swap_slabs(): got_near = lax.ppermute(jnp.where(low_half, high, low), 'px', near)  5.56 us
    ppermute x4, waiting for transfers between devices, swap_cores(): return lax.ppermute(value, 'py', [(0, 1), (1, 0)])  2.49 us
    unnamed x10, local copies, waits for them, and re-layouts  2.09 us
  transfers between devices with their start and end apart: 20, of which 10 were waited for; matrix products, arithmetic and copies ran while one was open for 3% of the time, Pallas kernels for 33%

profile of v8, /device:TPU:0, one launch (start us, length us, event | category | flops | bytes accessed | tf_op | source)
XLA Modules:
  0.0 93.3 jit_solution(2679598659262433029)
XLA Ops:
  0.6 0.0 copy-start
  0.6 1.0 %copy-done = bf16[1,4,8,32,256]{4,3,2,1,0:T(8,128)(2,1)S(1)} copy-done((bf16[1,4,8,32,256]{4,3,2,1,0:T(8,128)(2,1)S(1)}, bf16[1,4,8,32,256]{4,3,2,1,0:T(8,128)(2,1)}, u32[]{:S(2)}) %copy-start) | copy-done | bytes 524312
  1.7 0.0 copy-start.2
  1.7 1.0 %copy-done.2 = bf16[1,4,8,32,256]{4,3,2,1,0:T(8,128)(2,1)S(1)} copy-done((bf16[1,4,8,32,256]{4,3,2,1,0:T(8,128)(2,1)S(1)}, bf16[1,4,8,32,256]{4,3,2,1,0:T(8,128)(2,1)}, u32[]{:S(2)}) %copy-start.2) | copy-done | bytes 524312
  2.7 0.1 pack.1
  2.8 0.1 collective-permute-start
  2.9 0.0 copy-start.4
  2.9 0.1 pad_add_fusion.place
  3.0 1.1 %slice_bitcast_fusion.6 = (bf16[8,32,256]{2,1,0:T(8,128)(2,1)S(1)}, bf16[8,32,256]{2,1,0:T(8,128)(2,1)S(1)}) fusion(bf16[1,4,8,32,256]{4,3,2,1,0:T(8,128)(2,1)} %param.4), kind=kLoop, calls=%fused_computation.24 | loop fusion | bytes 524288 | tf_op jit(solution)/shard_map/squeeze | solution.py:471
  4.2 1.1 %slice_bitcast_fusion.7 = (bf16[8,32,256]{2,1,0:T(8,128)(2,1)S(1)}, bf16[8,32,256]{2,1,0:T(8,128)(2,1)S(1)}) fusion(bf16[1,4,8,32,256]{4,3,2,1,0:T(8,128)(2,1)} %param.5), kind=kLoop, calls=%fused_computation.25 | loop fusion | bytes 524288 | tf_op jit(solution)/shard_map/squeeze | solution.py:470
  5.2 0.0 collective-permute-done.other
  5.4 0.1 broadcast_select_fusion.2
  5.4 0.7 collective-permute-start.2
  6.1 4.3 %collective-permute-start.1 = (bf16[2,9,32,256]{3,2,1,0:T(8,128)(2,1)S(1)}, bf16[2,9,32,256]{3,2,1,0:T(8,128)(2,1)S(1)}, u32[]{:S(2)}, u32[]{:S(2)}) collective-permute-start(bf16[2,9,32,256]{3,2,1,0:T(8,128)(2,1)S(1)} %get-tuple-element.105), channel_id=1, source_target_pairs={{0,2},{2,0},{4,6},{6,4},{8,10},{10,8},{12,14},{14,12},{1,3},{3,1},... | collective-permute-start | bytes 884744 | tf_op jit(solution)/shard_map/ppermute | solution.py:477
  10.5 0.0 copy-done.1
  10.5 0.0 copy-done.3
  10.5 0.0 copy-done.4
  10.5 9.4 %inner.1 = (bf16[2,8,32,256]{3,2,1,0:T(8,128)(2,1)S(1)}, bf16[2,8,32,256]{3,2,1,0:T(8,128)(2,1)S(1)}, f32[2,256,256]{2,1,0:T(8,128)S(1)}, f32[2,256,256]{2,1,0:T...) custom-call(s32[4]{0:T(128)S(1)} %pad_add_fusion.place, bf16[4,8,32,256]{3,2,1,0:T(8,128)(2,1)S(1)} %bitcast.75, ...), custom_call_target="tpu_custom_call" | custom-call | flops 6039797760 | bytes 8388608 | tf_op jit(solution)/shard_map/inner/pallas_call | solution.py:440
  19.9 1.1 %chip.1 = bf16[4,18,32,768]{3,2,1,0:T(8,128)(2,1)S(1)} custom-call(s32[4]{0:T(128)S(1)} %pad_add_fusion.place, bf16[4,8,32,256]{3,2,1,0:T(8,128)(2,1)S(1)} %bitcast.76, bf16[4,8,32,256]{3,2,1,0:T(8,128)(2,1)S(1)} %bitcast.81, bf16[4,9,32,256]{3,2,1,0:T(8,128)(2,1)S(1)} %collective-permute-done.other), custom_call_target="tpu_custom_call" | custom-call | flops 905969664 | bytes 8388608 | tf_op jit(solution)/shard_map/chip/pallas_call | solution.py:440
  21.0 0.0 collective-permute-done.2.far.far1
  21.0 2.4 %collective-permute-done.1.near.near1 = bf16[2,9,32,256]{3,2,1,0:T(8,128)(2,1)S(1)} collective-permute-done((bf16[2,9,32,256]{3,2,1,0:T(8,128)(2,1)S(1)}, bf16[2,9,32,256]{3,2,1,0:T(8,128)(2,1)S(1)}, u32[]{:S(2)}, u32[]{:S(2)}) %collective-permute-start.1) | collective-permute-done | bytes 294944 | tf_op jit(solution)/shard_map/ppermute | solution.py:477
  23.4 2.3 %outer.1 = (bf16[4,8,32,256]{3,2,1,0:T(8,128)(2,1)S(1)}, bf16[4,8,32,256]{3,2,1,0:T(8,128)(2,1)S(1)}, bf16[4,9,32,256]{3,2,1,0:T(8,128)(2,1)S(1)}) custom-call(s32[4]{0:T(128)S(1)} %pad_add_fusion.place, bf16[2,9,32,256]{3,2,1,0:T(8,128)(2,1)S(1)} %collective-permute-done.1.near.near1, bf16[2,9,32,256]{3,2,1,0:T(8,128)(2,1)S(1)} %collective-permute-done.2.far.far1, ...), custom_call_target="tpu_custom_call" | custom-call | flops 1207959552 | bytes 8388608 | tf_op jit(solution)/shard_map/outer/pallas_call | solution.py:440
  25.7 0.1 collective-permute-start.3
  25.9 0.6 collective-permute-start.4
  26.5 1.3 %collective-permute-done.3.other2.other = bf16[4,9,32,256]{3,2,1,0:T(8,128)(2,1)S(1)} collective-permute-done((bf16[4,9,32,256]{3,2,1,0:T(8,128)(2,1)S(1)}, bf16[4,9,32,256]{3,2,1,0:T(8,128)(2,1)S(1)}, u32[]{:S(2)}, u32[]{:S(2)}) %collective-permute-start.3) | collective-permute-done | bytes 589856 | tf_op jit(solution)/shard_map/ppermute | solution.py:459
  27.9 0.1 broadcast_select_fusion
  28.0 0.7 collective-permute-start.6
  28.7 4.9 %collective-permute-start.5 = (bf16[2,9,32,256]{3,2,1,0:T(8,128)(2,1)S(1)}, bf16[2,9,32,256]{3,2,1,0:T(8,128)(2,1)S(1)}, u32[]{:S(2)}, u32[]{:S(2)}) collective-permute-start(bf16[2,9,32,256]{3,2,1,0:T(8,128)(2,1)S(1)} %get-tuple-element.101), channel_id=1, source_target_pairs={{0,2},{2,0},{4,6},{6,4},{8,10},{10,8},{12,14},{14,12},{1,3},{3,1},... | collective-permute-start | bytes 884744 | tf_op jit(solution)/shard_map/ppermute | solution.py:477
  33.5 0.0 collective-permute-done.4.edges
  33.5 4.6 %weight_terms.1 = (bf16[8,32,768]{2,1,0:T(8,128)(2,1)S(1)}, bf16[8,32,768]{2,1,0:T(8,128)(2,1)S(1)}, bf16[8,32,768]{2,1,0:T(8,128)(2,1)S(1)}, bf16[8,32,768]{2,1...) custom-call(s32[4]{0:T(128)S(1)} %pad_add_fusion.place, ...), custom_call_target="tpu_custom_call" | custom-call | flops 3221225472 | bytes 8388608 | tf_op jit(solution)/shard_map/weight_terms/pallas_call | solution.py:440
  38.1 1.6 %collective-permute-start.7 = (bf16[8,32,768]{2,1,0:T(8,128)(2,1)S(1)}, bf16[8,32,768]{2,1,0:T(8,128)(2,1)S(1)}, u32[]{:S(2)}, u32[]{:S(2)}) collective-permute-start(bf16[8,32,768]{2,1,0:T(8,128)(2,1)S(1)} %get-tuple-element.71), channel_id=1, source_target_pairs={{0,4},{2,6},{16,20},{18,22},{32,36},{34,38},{48,52},{50,54},{64,68... | collective-permute-start | bytes 1179656 | tf_op jit(solution)/shard_map/ppermute | solution.py:483
  39.7 1.7 %collective-permute-start.8 = (bf16[8,32,768]{2,1,0:T(8,128)(2,1)S(1)}, bf16[8,32,768]{2,1,0:T(8,128)(2,1)S(1)}, u32[]{:S(2)}, u32[]{:S(2)}) collective-permute-start(bf16[8,32,768]{2,1,0:T(8,128)(2,1)S(1)} %get-tuple-element.72), channel_id=1, source_target_pairs={{0,12},{2,14},{16,28},{18,30},{32,44},{34,46},{48,60},{50,62},{64,... | collective-permute-start | bytes 1179656 | tf_op jit(solution)/shard_map/ppermute | solution.py:483
  41.4 1.5 %collective-permute-start.9 = (bf16[8,32,768]{2,1,0:T(8,128)(2,1)S(1)}, bf16[8,32,768]{2,1,0:T(8,128)(2,1)S(1)}, u32[]{:S(2)}, u32[]{:S(2)}) collective-permute-start(bf16[8,32,768]{2,1,0:T(8,128)(2,1)S(1)} %get-tuple-element.73), channel_id=1, source_target_pairs={{0,8},{2,10},{16,24},{18,26},{32,40},{34,42},{48,56},{50,58},{64,7... | collective-permute-start | bytes 1179656 | tf_op jit(solution)/shard_map/ppermute | solution.py:483
  42.9 0.0 collective-permute-done.6.far
  42.9 3.2 %collective-permute-done.5.near = bf16[2,9,32,256]{3,2,1,0:T(8,128)(2,1)S(1)} collective-permute-done((bf16[2,9,32,256]{3,2,1,0:T(8,128)(2,1)S(1)}, bf16[2,9,32,256]{3,2,1,0:T(8,128)(2,1)S(1)}, u32[]{:S(2)}, u32[]{:S(2)}) %collective-permute-start.5) | collective-permute-done | bytes 294944 | tf_op jit(solution)/shard_map/ppermute | solution.py:477
  46.1 5.5 %weight_terms_rest.1 = (bf16[8,32,960]{2,1,0:T(8,128)(2,1)S(1)}, bf16[8,32,960]{2,1,0:T(8,128)(2,1)S(1)}, bf16[8,32,960]{2,1,0:T(8,128)(2,1)S(1)}, bf16[8,32,960]{2,1,0:T(8,128)(2,1)S(1)}) custom-call(s32[4]{0:T(128)S(1)} %pad_add_fusion.place, bf16[4,18,32,768]{3,2,1,0:T(8,128)(2,1)S(1)} %chip.1, bf16[2,18,32,768]{3,2,1,0:T(8,128)(2,1)S(1)} %get-tuple-element.65.sides, ...), custom_call_target="tpu_custom_call" | custom-call | flops 4026531840 | bytes 8388608 | tf_op jit(solution)/shard_map/weight_terms_rest/pallas_call | solution.py:440
  51.6 2.2 %collective-permute-start.10 = (bf16[8,32,960]{2,1,0:T(8,128)(2,1)S(1)}, bf16[8,32,960]{2,1,0:T(8,128)(2,1)S(1)}, u32[]{:S(2)}, u32[]{:S(2)}) collective-permute-start(bf16[8,32,960]{2,1,0:T(8,128)(2,1)S(1)} %get-tuple-element.93), channel_id=1, source_target_pairs={{0,4},{2,6},{16,20},{18,22},{32,36},{34,38},{48,52},{50,54},{64,68... | collective-permute-start | bytes 1474568 | tf_op jit(solution)/shard_map/ppermute | solution.py:483
  53.8 1.4 %collective-permute-start.11 = (bf16[8,32,960]{2,1,0:T(8,128)(2,1)S(1)}, bf16[8,32,960]{2,1,0:T(8,128)(2,1)S(1)}, u32[]{:S(2)}, u32[]{:S(2)}) collective-permute-start(bf16[8,32,960]{2,1,0:T(8,128)(2,1)S(1)} %get-tuple-element.94), channel_id=1, source_target_pairs={{0,12},{2,14},{16,28},{18,30},{32,44},{34,46},{48,60},{50,62},{64,... | collective-permute-start | bytes 1474568 | tf_op jit(solution)/shard_map/ppermute | solution.py:483
  55.1 0.0 collective-permute-done.7.refs_1_
  55.1 2.2 %collective-permute-start.12 = (bf16[8,32,960]{2,1,0:T(8,128)(2,1)S(1)}, bf16[8,32,960]{2,1,0:T(8,128)(2,1)S(1)}, u32[]{:S(2)}, u32[]{:S(2)}) collective-permute-start(bf16[8,32,960]{2,1,0:T(8,128)(2,1)S(1)} %get-tuple-element.95), channel_id=1, source_target_pairs={{0,8},{2,10},{16,24},{18,26},{32,40},{34,42},{48,56},{50,58},{64,7... | collective-permute-start | bytes 1474568 | tf_op jit(solution)/shard_map/ppermute | solution.py:483
  57.4 0.0 collective-permute-done.8.refs_2_
  57.4 0.0 collective-permute-done.9.refs_3_
  57.4 7.4 %outputs_inner.1 = (bf16[2,8,32,256]{3,2,1,0:T(8,128)(2,1)S(1)}, bf16[2,8,32,256]{3,2,1,0:T(8,128)(2,1)S(1)}, f32[2,256,256]{2,1,0:T(8,128)S(1)}, f32[2,256,256]{2,1,0:T(8,128)S(1)}) custom-call(s32[4]{0:T(128)S(1)} %pad_add_fusion.place, bf16[4,8,32,256]{3,2,1,0:T(8,128)(2,1)S(1)} %get-tuple-element.77.hid, ...), custom_call_target="tpu_custom_call" | custom-call | flops 6039797760 | bytes 8388608 | tf_op jit(solution)/shard_map/outputs_inner/pallas_call | solution.py:440
  64.8 3.2 %outputs_outer.1 = (bf16[4,8,32,256]{3,2,1,0:T(8,128)(2,1)}, bf16[4,8,32,256]{3,2,1,0:T(8,128)(2,1)}) custom-call(s32[4]{0:T(128)S(1)} %pad_add_fusion.place, bf16[2,9,32,256]{3,2,1,0:T(8,128)(2,1)S(1)} %collective-permute-done.5.near, bf16[2,9,32,256]{3,2,1,0:T(8,128)(2,1)S(1)} %collective-permute-done.6.far, ...), custom_call_target="tpu_custom_call" | custom-call | flops 1207959552 | bytes 8388608 | tf_op jit(solution)/shard_map/outputs_outer/pallas_call | solution.py:440
  67.9 0.0 collective-permute-done.10.refs_5_
  67.9 0.0 collective-permute-done.11.refs_6_
  67.9 1.3 %collective-permute-done.12.refs_7_ = bf16[8,32,960]{2,1,0:T(8,128)(2,1)S(1)} collective-permute-done((bf16[8,32,960]{2,1,0:T(8,128)(2,1)S(1)}, bf16[8,32,960]{2,1,0:T(8,128)(2,1)S(1)}, u32[]{:S(2)}, u32[]{:S(2)}) %collective-permute-start.12) | collective-permute-done | bytes 491552 | tf_op jit(solution)/shard_map/ppermute | solution.py:483
  69.3 1.5 %sum.1 = (f32[4,32,896]{2,1,0:T(8,128)S(1)}, bf16[4,32,896]{2,1,0:T(8,128)(2,1)S(1)}, bf16[4,32,896]{2,1,0:T(8,128)(2,1)S(1)}, bf16[4,32,896]{2,1,0:T(8,128)(2,1)S(1)}) custom-call(s32[4]{0:T(128)S(1)} %pad_add_fusion.place, bf16[8,32,768]{2,1,0:T(8,128)(2,1)S(1)} %get-tuple-element.88.refs_0_, bf16[8,32,768]{2,1,0:T(8,128)(2,1)S(1)} %collective-permute-done.7.refs_1_, ...), custom_call_target="tpu_custom_call" | custom-call | bytes 8388608 | tf_op jit(solution)/shard_map/sum/pallas_call | solution.py:440
  70.8 1.6 %collective-permute-start.13 = (bf16[4,32,896]{2,1,0:T(8,128)(2,1)S(1)}, bf16[4,32,896]{2,1,0:T(8,128)(2,1)S(1)}, u32[]{:S(2)}, u32[]{:S(2)}) collective-permute-start(bf16[4,32,896]{2,1,0:T(8,128)(2,1)S(1)} %get-tuple-element.97), channel_id=1, source_target_pairs={{0,32},{2,34},{16,48},{18,50},{32,64},{34,66},{48,80},{50,82},{64,... | collective-permute-start | bytes 688136 | tf_op jit(solution)/shard_map/ppermute | solution.py:483
  72.4 1.7 %collective-permute-start.14 = (bf16[4,32,896]{2,1,0:T(8,128)(2,1)S(1)}, bf16[4,32,896]{2,1,0:T(8,128)(2,1)S(1)}, u32[]{:S(2)}, u32[]{:S(2)}) collective-permute-start(bf16[4,32,896]{2,1,0:T(8,128)(2,1)S(1)} %get-tuple-element.98), channel_id=1, source_target_pairs={{0,96},{2,98},{16,112},{18,114},{32,0},{34,2},{48,16},{50,18},{64,... | collective-permute-start | bytes 688136 | tf_op jit(solution)/shard_map/ppermute | solution.py:483
  74.1 2.0 %collective-permute-start.15 = (bf16[4,32,896]{2,1,0:T(8,128)(2,1)S(1)}, bf16[4,32,896]{2,1,0:T(8,128)(2,1)S(1)}, u32[]{:S(2)}, u32[]{:S(2)}) collective-permute-start(bf16[4,32,896]{2,1,0:T(8,128)(2,1)S(1)} %get-tuple-element.99), channel_id=1, source_target_pairs={{0,64},{2,66},{16,80},{18,82},{32,96},{34,98},{48,112},{50,114},{6... | collective-permute-start | bytes 688136 | tf_op jit(solution)/shard_map/ppermute | solution.py:483
  76.0 2.0 %collective-permute-done.13 = bf16[4,32,896]{2,1,0:T(8,128)(2,1)S(1)} collective-permute-done((bf16[4,32,896]{2,1,0:T(8,128)(2,1)S(1)}, bf16[4,32,896]{2,1,0:T(8,128)(2,1)S(1)}, u32[]{:S(2)}, u32[]{:S(2)}) %collective-permute-start.13) | collective-permute-done | bytes 229408 | tf_op jit(solution)/shard_map/ppermute | solution.py:483
  78.1 0.4 collective-permute-done.14
  78.4 3.3 %collective-permute-done.15 = bf16[4,32,896]{2,1,0:T(8,128)(2,1)S(1)} collective-permute-done((bf16[4,32,896]{2,1,0:T(8,128)(2,1)S(1)}, bf16[4,32,896]{2,1,0:T(8,128)(2,1)S(1)}, u32[]{:S(2)}, u32[]{:S(2)}) %collective-permute-start.15) | collective-permute-done | bytes 229408 | tf_op jit(solution)/shard_map/ppermute | solution.py:483
  81.8 0.1 convert_add_fusion
  81.9 1.0 %collective-permute-start.16 = (f32[32,896]{1,0:T(8,128)S(1)}, f32[32,896]{1,0:T(8,128)S(1)}, u32[]{:S(2)}, u32[]{:S(2)}) collective-permute-start(f32[32,896]{1,0:T(8,128)S(1)} %get-tuple-element.116), channel_id=1, source_target_pairs={{0,2},{2,16},{16,18},{18,0},{32,34},{34,48},{48,50},{50,32},{64,66... | collective-permute-start | bytes 344072 | tf_op jit(solution)/shard_map/ppermute | solution.py:483
  82.9 3.6 %collective-permute-start.18 = (f32[32,896]{1,0:T(8,128)S(1)}, f32[32,896]{1,0:T(8,128)S(1)}, u32[]{:S(2)}, u32[]{:S(2)}) collective-permute-start(f32[32,896]{1,0:T(8,128)S(1)} %get-tuple-element.117), channel_id=1, source_target_pairs={{0,16},{2,18},{16,0},{18,2},{32,48},{34,50},{48,32},{50,34},{64,80... | collective-permute-start | bytes 344072 | tf_op jit(solution)/shard_map/ppermute | solution.py:483
  86.5 2.0 %collective-permute-start.17 = (f32[32,896]{1,0:T(8,128)S(1)}, f32[32,896]{1,0:T(8,128)S(1)}, u32[]{:S(2)}, u32[]{:S(2)}) collective-permute-start(f32[32,896]{1,0:T(8,128)S(1)} %get-tuple-element.118), channel_id=1, source_target_pairs={{0,18},{2,0},{16,2},{18,16},{32,50},{34,32},{48,34},{50,48},{64,82... | collective-permute-start | bytes 344072 | tf_op jit(solution)/shard_map/ppermute | solution.py:483
  88.5 0.0 collective-permute-done.16
  88.5 2.0 %collective-permute-done.18 = f32[32,896]{1,0:T(8,128)S(1)} collective-permute-done((f32[32,896]{1,0:T(8,128)S(1)}, f32[32,896]{1,0:T(8,128)S(1)}, u32[]{:S(2)}, u32[]{:S(2)}) %collective-permute-start.18) | collective-permute-done | bytes 114720 | tf_op jit(solution)/shard_map/ppermute | solution.py:483
  90.5 0.8 collective-permute-done.17
  91.3 0.1 collective-permute-start.19
  91.4 1.2 %collective-permute-done.19 = f32[16,896]{1,0:T(8,128)S(1)} collective-permute-done((f32[16,896]{1,0:T(8,128)S(1)}, f32[16,896]{1,0:T(8,128)S(1)}, u32[]{:S(2)}, u32[]{:S(2)}) %collective-permute-start.19) | collective-permute-done | bytes 57376 | tf_op jit(solution)/shard_map/ppermute | solution.py:459
  92.6 0.7 select_bitcast_fusion
  (23 shorter events, 0.4 us)
Async XLA Ops:
  0.6 1.0 %copy-start = (bf16[1,4,8,32,256]{4,3,2,1,0:T(8,128)(2,1)S(1)}, bf16[1,4,8,32,256]{4,3,2,1,0:T(8,128)(2,1)}, u32[]{:S(2)}) copy-start(bf16[1,4,8,32,256]{4,3,2,1,0:T(8,128)(2,1)} %param.5) | copy-start | bytes 1572868
  1.7 1.0 %copy-start.2 = (bf16[1,4,8,32,256]{4,3,2,1,0:T(8,128)(2,1)S(1)}, bf16[1,4,8,32,256]{4,3,2,1,0:T(8,128)(2,1)}, u32[]{:S(2)}) copy-start(bf16[1,4,8,32,256]{4,3,2,1,0:T(8,128)(2,1)} %param.4) | copy-start | bytes 1572868
  2.7 7.7 %copy-start.1 = (bf16[1,4,8,32,256]{4,3,2,1,0:T(8,128)(2,1)S(1)}, bf16[1,4,8,32,256]{4,3,2,1,0:T(8,128)(2,1)}, u32[]{:S(2)}) copy-start(bf16[1,4,8,32,256]{4,3,2,1,0:T(8,128)(2,1)} %param.5) | copy-start | bytes 1572868
  2.7 7.7 %copy-start.3 = (bf16[1,4,8,32,256]{4,3,2,1,0:T(8,128)(2,1)S(1)}, bf16[1,4,8,32,256]{4,3,2,1,0:T(8,128)(2,1)}, u32[]{:S(2)}) copy-start(bf16[1,4,8,32,256]{4,3,2,1,0:T(8,128)(2,1)} %param.4) | copy-start | bytes 1572868
  2.8 2.4 %collective-permute-start = (bf16[4,9,32,256]{3,2,1,0:T(8,128)(2,1)S(1)}, bf16[4,9,32,256]{3,2,1,0:T(8,128)(2,1)S(1)}, u32[]{:S(2)}, u32[]{:S(2)}) collective-permute-start(bf16[4,9,32,256]{3,2,1,0:T(8,128)(2,1)S(1)} %pack.1), channel_id=1, source_target_pairs={{0,1},{1,0},{2,3},{3,2},{4,5},{5,4},{6,7},{7,6},{8,9},{9,8},{10,11... | collective-permute-start | bytes 1769480 | tf_op jit(solution)/shard_map/ppermute | solution.py:459
  2.9 7.5 %copy-start.4 = (bf16[6912,256]{1,0:T(8,128)(2,1)S(1)}, bf16[6912,256]{1,0:T(8,128)(2,1)}, u32[]{:S(2)}) copy-start(bf16[6912,256]{1,0:T(8,128)(2,1)} %first_hbm.1) | copy-start | bytes 10616836
  5.4 15.6 %collective-permute-start.2 = (bf16[2,9,32,256]{3,2,1,0:T(8,128)(2,1)S(1)}, bf16[2,9,32,256]{3,2,1,0:T(8,128)(2,1)S(1)}, u32[]{:S(2)}, u32[]{:S(2)}) collective-permute-start(bf16[2,9,32,256]{3,2,1,0:T(8,128)(2,1)S(1)} %get-tuple-element.104), channel_id=1, source_target_pairs={{2,4},{4,2},{6,8},{8,6},{10,12},{12,10},{3,5},{5,3},{7,9},{9,7},{1... | collective-permute-start | bytes 884744 | tf_op jit(solution)/shard_map/ppermute | solution.py:476
  6.1 17.2 %collective-permute-start.1 = (bf16[2,9,32,256]{3,2,1,0:T(8,128)(2,1)S(1)}, bf16[2,9,32,256]{3,2,1,0:T(8,128)(2,1)S(1)}, u32[]{:S(2)}, u32[]{:S(2)}) collective-permute-start(bf16[2,9,32,256]{3,2,1,0:T(8,128)(2,1)S(1)} %get-tuple-element.105), channel_id=1, source_target_pairs={{0,2},{2,0},{4,6},{6,4},{8,10},{10,8},{12,14},{14,12},{1,3},{3,1},... | collective-permute-start | bytes 884744 | tf_op jit(solution)/shard_map/ppermute | solution.py:477
  25.7 2.1 %collective-permute-start.3 = (bf16[4,9,32,256]{3,2,1,0:T(8,128)(2,1)S(1)}, bf16[4,9,32,256]{3,2,1,0:T(8,128)(2,1)S(1)}, u32[]{:S(2)}, u32[]{:S(2)}) collective-permute-start(bf16[4,9,32,256]{3,2,1,0:T(8,128)(2,1)S(1)} %get-tuple-element.63), channel_id=1, source_target_pairs={{0,1},{1,0},{2,3},{3,2},{4,5},{5,4},{6,7},{7,6},{8,9},{9,8},{10,11... | collective-permute-start | bytes 1769480 | tf_op jit(solution)/shard_map/ppermute | solution.py:459
  25.9 7.6 %collective-permute-start.4 = (bf16[2,8,32,256]{3,2,1,0:T(8,128)(2,1)S(1)}, bf16[2,8,32,256]{3,2,1,0:T(8,128)(2,1)S(1)}, u32[]{:S(2)}, u32[]{:S(2)}) collective-permute-start(bf16[2,8,32,256]{3,2,1,0:T(8,128)(2,1)S(1)} %maximum_select_fusion), channel_id=1, source_target_pairs={{0,1},{1,0},{2,3},{3,2},{4,5},{5,4},{6,7},{7,6},{8,9},{9,8},{10,11... | collective-permute-start | bytes 786440 | tf_op jit(solution)/shard_map/ppermute | solution.py:459
  28.0 15.0 %collective-permute-start.6 = (bf16[2,9,32,256]{3,2,1,0:T(8,128)(2,1)S(1)}, bf16[2,9,32,256]{3,2,1,0:T(8,128)(2,1)S(1)}, u32[]{:S(2)}, u32[]{:S(2)}) collective-permute-start(bf16[2,9,32,256]{3,2,1,0:T(8,128)(2,1)S(1)} %get-tuple-element.100), channel_id=1, source_target_pairs={{2,4},{4,2},{6,8},{8,6},{10,12},{12,10},{3,5},{5,3},{7,9},{9,7},{1... | collective-permute-start | bytes 884744 | tf_op jit(solution)/shard_map/ppermute | solution.py:476
  28.7 17.5 %collective-permute-start.5 = (bf16[2,9,32,256]{3,2,1,0:T(8,128)(2,1)S(1)}, bf16[2,9,32,256]{3,2,1,0:T(8,128)(2,1)S(1)}, u32[]{:S(2)}, u32[]{:S(2)}) collective-permute-start(bf16[2,9,32,256]{3,2,1,0:T(8,128)(2,1)S(1)} %get-tuple-element.101), channel_id=1, source_target_pairs={{0,2},{2,0},{4,6},{6,4},{8,10},{10,8},{12,14},{14,12},{1,3},{3,1},... | collective-permute-start | bytes 884744 | tf_op jit(solution)/shard_map/ppermute | solution.py:477
  38.1 17.0 %collective-permute-start.7 = (bf16[8,32,768]{2,1,0:T(8,128)(2,1)S(1)}, bf16[8,32,768]{2,1,0:T(8,128)(2,1)S(1)}, u32[]{:S(2)}, u32[]{:S(2)}) collective-permute-start(bf16[8,32,768]{2,1,0:T(8,128)(2,1)S(1)} %get-tuple-element.71), channel_id=1, source_target_pairs={{0,4},{2,6},{16,20},{18,22},{32,36},{34,38},{48,52},{50,54},{64,68... | collective-permute-start | bytes 1179656 | tf_op jit(solution)/shard_map/ppermute | solution.py:483
  39.7 17.7 %collective-permute-start.8 = (bf16[8,32,768]{2,1,0:T(8,128)(2,1)S(1)}, bf16[8,32,768]{2,1,0:T(8,128)(2,1)S(1)}, u32[]{:S(2)}, u32[]{:S(2)}) collective-permute-start(bf16[8,32,768]{2,1,0:T(8,128)(2,1)S(1)} %get-tuple-element.72), channel_id=1, source_target_pairs={{0,12},{2,14},{16,28},{18,30},{32,44},{34,46},{48,60},{50,62},{64,... | collective-permute-start | bytes 1179656 | tf_op jit(solution)/shard_map/ppermute | solution.py:483
  41.4 15.9 %collective-permute-start.9 = (bf16[8,32,768]{2,1,0:T(8,128)(2,1)S(1)}, bf16[8,32,768]{2,1,0:T(8,128)(2,1)S(1)}, u32[]{:S(2)}, u32[]{:S(2)}) collective-permute-start(bf16[8,32,768]{2,1,0:T(8,128)(2,1)S(1)} %get-tuple-element.73), channel_id=1, source_target_pairs={{0,8},{2,10},{16,24},{18,26},{32,40},{34,42},{48,56},{50,58},{64,7... | collective-permute-start | bytes 1179656 | tf_op jit(solution)/shard_map/ppermute | solution.py:483
  51.6 16.3 %collective-permute-start.10 = (bf16[8,32,960]{2,1,0:T(8,128)(2,1)S(1)}, bf16[8,32,960]{2,1,0:T(8,128)(2,1)S(1)}, u32[]{:S(2)}, u32[]{:S(2)}) collective-permute-start(bf16[8,32,960]{2,1,0:T(8,128)(2,1)S(1)} %get-tuple-element.93), channel_id=1, source_target_pairs={{0,4},{2,6},{16,20},{18,22},{32,36},{34,38},{48,52},{50,54},{64,68... | collective-permute-start | bytes 1474568 | tf_op jit(solution)/shard_map/ppermute | solution.py:483
  53.8 14.2 %collective-permute-start.11 = (bf16[8,32,960]{2,1,0:T(8,128)(2,1)S(1)}, bf16[8,32,960]{2,1,0:T(8,128)(2,1)S(1)}, u32[]{:S(2)}, u32[]{:S(2)}) collective-permute-start(bf16[8,32,960]{2,1,0:T(8,128)(2,1)S(1)} %get-tuple-element.94), channel_id=1, source_target_pairs={{0,12},{2,14},{16,28},{18,30},{32,44},{34,46},{48,60},{50,62},{64,... | collective-permute-start | bytes 1474568 | tf_op jit(solution)/shard_map/ppermute | solution.py:483
  55.1 14.1 %collective-permute-start.12 = (bf16[8,32,960]{2,1,0:T(8,128)(2,1)S(1)}, bf16[8,32,960]{2,1,0:T(8,128)(2,1)S(1)}, u32[]{:S(2)}, u32[]{:S(2)}) collective-permute-start(bf16[8,32,960]{2,1,0:T(8,128)(2,1)S(1)} %get-tuple-element.95), channel_id=1, source_target_pairs={{0,8},{2,10},{16,24},{18,26},{32,40},{34,42},{48,56},{50,58},{64,7... | collective-permute-start | bytes 1474568 | tf_op jit(solution)/shard_map/ppermute | solution.py:483
  70.8 7.3 %collective-permute-start.13 = (bf16[4,32,896]{2,1,0:T(8,128)(2,1)S(1)}, bf16[4,32,896]{2,1,0:T(8,128)(2,1)S(1)}, u32[]{:S(2)}, u32[]{:S(2)}) collective-permute-start(bf16[4,32,896]{2,1,0:T(8,128)(2,1)S(1)} %get-tuple-element.97), channel_id=1, source_target_pairs={{0,32},{2,34},{16,48},{18,50},{32,64},{34,66},{48,80},{50,82},{64,... | collective-permute-start | bytes 688136 | tf_op jit(solution)/shard_map/ppermute | solution.py:483
  72.4 6.0 %collective-permute-start.14 = (bf16[4,32,896]{2,1,0:T(8,128)(2,1)S(1)}, bf16[4,32,896]{2,1,0:T(8,128)(2,1)S(1)}, u32[]{:S(2)}, u32[]{:S(2)}) collective-permute-start(bf16[4,32,896]{2,1,0:T(8,128)(2,1)S(1)} %get-tuple-element.98), channel_id=1, source_target_pairs={{0,96},{2,98},{16,112},{18,114},{32,0},{34,2},{48,16},{50,18},{64,... | collective-permute-start | bytes 688136 | tf_op jit(solution)/shard_map/ppermute | solution.py:483
  74.1 7.7 %collective-permute-start.15 = (bf16[4,32,896]{2,1,0:T(8,128)(2,1)S(1)}, bf16[4,32,896]{2,1,0:T(8,128)(2,1)S(1)}, u32[]{:S(2)}, u32[]{:S(2)}) collective-permute-start(bf16[4,32,896]{2,1,0:T(8,128)(2,1)S(1)} %get-tuple-element.99), channel_id=1, source_target_pairs={{0,64},{2,66},{16,80},{18,82},{32,96},{34,98},{48,112},{50,114},{6... | collective-permute-start | bytes 688136 | tf_op jit(solution)/shard_map/ppermute | solution.py:483
  81.9 6.6 %collective-permute-start.16 = (f32[32,896]{1,0:T(8,128)S(1)}, f32[32,896]{1,0:T(8,128)S(1)}, u32[]{:S(2)}, u32[]{:S(2)}) collective-permute-start(f32[32,896]{1,0:T(8,128)S(1)} %get-tuple-element.116), channel_id=1, source_target_pairs={{0,2},{2,16},{16,18},{18,0},{32,34},{34,48},{48,50},{50,32},{64,66... | collective-permute-start | bytes 344072 | tf_op jit(solution)/shard_map/ppermute | solution.py:483
  82.9 7.6 %collective-permute-start.18 = (f32[32,896]{1,0:T(8,128)S(1)}, f32[32,896]{1,0:T(8,128)S(1)}, u32[]{:S(2)}, u32[]{:S(2)}) collective-permute-start(f32[32,896]{1,0:T(8,128)S(1)} %get-tuple-element.117), channel_id=1, source_target_pairs={{0,16},{2,18},{16,0},{18,2},{32,48},{34,50},{48,32},{50,34},{64,80... | collective-permute-start | bytes 344072 | tf_op jit(solution)/shard_map/ppermute | solution.py:483
  86.5 4.8 %collective-permute-start.17 = (f32[32,896]{1,0:T(8,128)S(1)}, f32[32,896]{1,0:T(8,128)S(1)}, u32[]{:S(2)}, u32[]{:S(2)}) collective-permute-start(f32[32,896]{1,0:T(8,128)S(1)} %get-tuple-element.118), channel_id=1, source_target_pairs={{0,18},{2,0},{16,2},{18,16},{32,50},{34,32},{48,34},{50,48},{64,82... | collective-permute-start | bytes 344072 | tf_op jit(solution)/shard_map/ppermute | solution.py:483
  91.3 1.3 %collective-permute-start.19 = (f32[16,896]{1,0:T(8,128)S(1)}, f32[16,896]{1,0:T(8,128)S(1)}, u32[]{:S(2)}, u32[]{:S(2)}) collective-permute-start(f32[16,896]{1,0:T(8,128)S(1)} %get-tuple-element.126), channel_id=1, source_target_pairs={{0,1},{1,0},{2,3},{3,2},{4,5},{5,4},{6,7},{7,6},{8,9},{9,8},{10,11... | collective-permute-start | bytes 172040 | tf_op jit(solution)/shard_map/ppermute | solution.py:459

commit v9 on v8

--- a/solution.py
+++ b/solution.py
@@ -603,7 +603,6 @@
         26,
     )
     got1 = hop((sent1[0], sent1[2], sent1[1]), 0)
-    turned, local, near2, far2 = lax.optimization_barrier((turned, local, near2, far2))
     own2, *sent2 = call(
         weight_rest_kernel,
         "weight_terms_rest",

time: 94.6 us -> 88 us (0.930)
  starting transfers between devices: 33.8 us -> 28.6 us
  waiting for transfers between devices: 17.9 us -> 16.2 us
    ppermute x2, starting transfers between devices: 9.21 us -> 3.91 us  [swap_slabs(): got_near = lax.ppermute(jnp.where(low_half, high, low), 'px', near)]
    ppermute x2, waiting for transfers between devices: 5.56 us -> 1.96 us  [swap_slabs(): got_near = lax.ppermute(jnp.where(low_half, high, low), 'px', near)]
    ppermute x12, waiting for transfers between devices: 9.87 us -> 11.4 us  [hop(): lax.ppermute(part, ALL, hop_pairs(stage, distance))]
  transfers between devices with their start and end apart: 20 -> 20, of which waited for: 10 -> 9; matrix products, arithmetic and copies ran while one was open for 3% -> 3% of each run, Pallas kernels for 33% -> 31%
where the time goes in v9:
time: 88 us; the launch traced here: 86.6 us
  Pallas kernels  35.3 us (40%)
  starting transfers between devices  28.6 us (32%)
  waiting for transfers between devices  16.2 us (18%)
  local copies, waits for them, and re-layouts  4.41 us (5%)
  other arithmetic  1.19 us (1%)
  between operations  1.02 us (1%)
    pallas_call x9, Pallas kernels, call(): pl.pallas_call(kernel, name=name, out_shape=outs, in_specs=[pl.BlockSpec(...  35.3 us
    ppermute x12, starting transfers between devices, hop(): lax.ppermute(part, ALL, hop_pairs(stage, distance))  22.5 us
    ppermute x12, waiting for transfers between devices, hop(): lax.ppermute(part, ALL, hop_pairs(stage, distance))  11.4 us
    ppermute x2, starting transfers between devices, swap_slabs(): got_near = lax.ppermute(jnp.where(low_half, high, low), 'px', near)  3.91 us
    ppermute x4, waiting for transfers between devices, swap_cores(): return lax.ppermute(value, 'py', [(0, 1), (1, 0)])  2.87 us
    unnamed x10, local copies, waits for them, and re-layouts  2.09 us
    ppermute x2, waiting for transfers between devices, swap_slabs(): got_near = lax.ppermute(jnp.where(low_half, high, low), 'px', near)  1.96 us
  transfers between devices with their start and end apart: 20, of which 9 were waited for; matrix products, arithmetic and copies ran while one was open for 3% of the time, Pallas kernels for 31%

profile of v9, /device:TPU:0, one launch (start us, length us, event | category | flops | bytes accessed | tf_op | source)
XLA Modules:
  0.0 86.6 jit_solution(14174437788799517940)
XLA Ops:
  0.6 0.0 copy-start
  0.6 1.0 %copy-done = bf16[1,4,8,32,256]{4,3,2,1,0:T(8,128)(2,1)S(1)} copy-done((bf16[1,4,8,32,256]{4,3,2,1,0:T(8,128)(2,1)S(1)}, bf16[1,4,8,32,256]{4,3,2,1,0:T(8,128)(2,1)}, u32[]{:S(2)}) %copy-start) | copy-done | bytes 524312
  1.7 0.0 copy-start.2
  1.7 1.0 %copy-done.2 = bf16[1,4,8,32,256]{4,3,2,1,0:T(8,128)(2,1)S(1)} copy-done((bf16[1,4,8,32,256]{4,3,2,1,0:T(8,128)(2,1)S(1)}, bf16[1,4,8,32,256]{4,3,2,1,0:T(8,128)(2,1)}, u32[]{:S(2)}) %copy-start.2) | copy-done | bytes 524312
  2.7 0.1 pack.1
  2.8 0.1 collective-permute-start
  2.9 0.0 copy-start.4
  2.9 0.1 pad_add_fusion.place
  3.0 1.1 %slice_bitcast_fusion.7 = (bf16[8,32,256]{2,1,0:T(8,128)(2,1)S(1)}, bf16[8,32,256]{2,1,0:T(8,128)(2,1)S(1)}) fusion(bf16[1,4,8,32,256]{4,3,2,1,0:T(8,128)(2,1)} %param.5), kind=kLoop, calls=%fused_computation.25 | loop fusion | bytes 524288 | tf_op jit(solution)/shard_map/squeeze | solution.py:470
  4.2 1.1 %slice_bitcast_fusion.6 = (bf16[8,32,256]{2,1,0:T(8,128)(2,1)S(1)}, bf16[8,32,256]{2,1,0:T(8,128)(2,1)S(1)}) fusion(bf16[1,4,8,32,256]{4,3,2,1,0:T(8,128)(2,1)} %param.4), kind=kLoop, calls=%fused_computation.24 | loop fusion | bytes 524288 | tf_op jit(solution)/shard_map/squeeze | solution.py:471
  5.2 0.0 collective-permute-done.other
  5.4 0.1 broadcast_select_fusion.2
  5.4 2.1 %collective-permute-start.1 = (bf16[2,9,32,256]{3,2,1,0:T(8,128)(2,1)S(1)}, bf16[2,9,32,256]{3,2,1,0:T(8,128)(2,1)S(1)}, u32[]{:S(2)}, u32[]{:S(2)}) collective-permute-start(bf16[2,9,32,256]{3,2,1,0:T(8,128)(2,1)S(1)} %get-tuple-element.97), channel_id=1, source_target_pairs={{0,2},{2,0},{4,6},{6,4},{8,10},{10,8},{12,14},{14,12},{1,3},{3,1},... | collective-permute-start | bytes 884744 | tf_op jit(solution)/shard_map/ppermute | solution.py:477
  7.5 0.7 collective-permute-start.2
  8.2 0.0 copy-done.1
  8.2 0.0 copy-done.3
  8.2 0.0 copy-done.4
  8.2 9.4 %inner.1 = (bf16[2,8,32,256]{3,2,1,0:T(8,128)(2,1)S(1)}, bf16[2,8,32,256]{3,2,1,0:T(8,128)(2,1)S(1)}, f32[2,256,256]{2,1,0:T(8,128)S(1)}, f32[2,256,256]{2,1,0:T...) custom-call(s32[4]{0:T(128)S(1)} %pad_add_fusion.place, bf16[4,8,32,256]{3,2,1,0:T(8,128)(2,1)S(1)} %bitcast.75, ...), custom_call_target="tpu_custom_call" | custom-call | flops 6039797760 | bytes 8388608 | tf_op jit(solution)/shard_map/inner/pallas_call | solution.py:440
  17.6 1.1 %chip.1 = bf16[4,18,32,768]{3,2,1,0:T(8,128)(2,1)S(1)} custom-call(s32[4]{0:T(128)S(1)} %pad_add_fusion.place, bf16[4,8,32,256]{3,2,1,0:T(8,128)(2,1)S(1)} %bitcast.76, bf16[4,8,32,256]{3,2,1,0:T(8,128)(2,1)S(1)} %bitcast.81, bf16[4,9,32,256]{3,2,1,0:T(8,128)(2,1)S(1)} %collective-permute-done.other), custom_call_target="tpu_custom_call" | custom-call | flops 905969664 | bytes 8388608 | tf_op jit(solution)/shard_map/chip/pallas_call | solution.py:440
  18.7 2.0 %collective-permute-done.1.near.near1 = bf16[2,9,32,256]{3,2,1,0:T(8,128)(2,1)S(1)} collective-permute-done((bf16[2,9,32,256]{3,2,1,0:T(8,128)(2,1)S(1)}, bf16[2,9,32,256]{3,2,1,0:T(8,128)(2,1)S(1)}, u32[]{:S(2)}, u32[]{:S(2)}) %collective-permute-start.1) | collective-permute-done | bytes 294944 | tf_op jit(solution)/shard_map/ppermute | solution.py:477
  20.7 0.0 collective-permute-done.2.far.far1
  20.7 2.3 %outer.1 = (bf16[4,8,32,256]{3,2,1,0:T(8,128)(2,1)S(1)}, bf16[4,8,32,256]{3,2,1,0:T(8,128)(2,1)S(1)}, bf16[4,9,32,256]{3,2,1,0:T(8,128)(2,1)S(1)}) custom-call(s32[4]{0:T(128)S(1)} %pad_add_fusion.place, bf16[2,9,32,256]{3,2,1,0:T(8,128)(2,1)S(1)} %collective-permute-done.1.near.near1, bf16[2,9,32,256]{3,2,1,0:T(8,128)(2,1)S(1)} %collective-permute-done.2.far.far1, ...), custom_call_target="tpu_custom_call" | custom-call | flops 1207959552 | bytes 8388608 | tf_op jit(solution)/shard_map/outer/pallas_call | solution.py:440
  23.0 0.1 collective-permute-start.3
  23.2 0.6 collective-permute-start.4
  23.9 1.6 %collective-permute-done.4.edges = bf16[2,8,32,256]{3,2,1,0:T(8,128)(2,1)S(1)} collective-permute-done((bf16[2,8,32,256]{3,2,1,0:T(8,128)(2,1)S(1)}, bf16[2,8,32,256]{3,2,1,0:T(8,128)(2,1)S(1)}, u32[]{:S(2)}, u32[]{:S(2)}) %collective-permute-start.4) | collective-permute-done | bytes 262176 | tf_op jit(solution)/shard_map/ppermute | solution.py:459
  25.5 0.0 collective-permute-done.3.other2.other
  25.5 4.6 %weight_terms.1 = (bf16[8,32,768]{2,1,0:T(8,128)(2,1)S(1)}, bf16[8,32,768]{2,1,0:T(8,128)(2,1)S(1)}, bf16[8,32,768]{2,1,0:T(8,128)(2,1)S(1)}, bf16[8,32,768]{2,1...) custom-call(s32[4]{0:T(128)S(1)} %pad_add_fusion.place, ...), custom_call_target="tpu_custom_call" | custom-call | flops 3221225472 | bytes 8388608 | tf_op jit(solution)/shard_map/weight_terms/pallas_call | solution.py:440
  30.1 2.3 %collective-permute-start.5 = (bf16[8,32,768]{2,1,0:T(8,128)(2,1)S(1)}, bf16[8,32,768]{2,1,0:T(8,128)(2,1)S(1)}, u32[]{:S(2)}, u32[]{:S(2)}) collective-permute-start(bf16[8,32,768]{2,1,0:T(8,128)(2,1)S(1)} %get-tuple-element.65), channel_id=1, source_target_pairs={{0,4},{2,6},{16,20},{18,22},{32,36},{34,38},{48,52},{50,54},{64,68... | collective-permute-start | bytes 1179656 | tf_op jit(solution)/shard_map/ppermute | solution.py:483
  32.3 1.4 %collective-permute-start.6 = (bf16[8,32,768]{2,1,0:T(8,128)(2,1)S(1)}, bf16[8,32,768]{2,1,0:T(8,128)(2,1)S(1)}, u32[]{:S(2)}, u32[]{:S(2)}) collective-permute-start(bf16[8,32,768]{2,1,0:T(8,128)(2,1)S(1)} %get-tuple-element.66), channel_id=1, source_target_pairs={{0,12},{2,14},{16,28},{18,30},{32,44},{34,46},{48,60},{50,62},{64,... | collective-permute-start | bytes 1179656 | tf_op jit(solution)/shard_map/ppermute | solution.py:483
  33.7 2.2 %collective-permute-start.7 = (bf16[8,32,768]{2,1,0:T(8,128)(2,1)S(1)}, bf16[8,32,768]{2,1,0:T(8,128)(2,1)S(1)}, u32[]{:S(2)}, u32[]{:S(2)}) collective-permute-start(bf16[8,32,768]{2,1,0:T(8,128)(2,1)S(1)} %get-tuple-element.67), channel_id=1, source_target_pairs={{0,8},{2,10},{16,24},{18,26},{32,40},{34,42},{48,56},{50,58},{64,7... | collective-permute-start | bytes 1179656 | tf_op jit(solution)/shard_map/ppermute | solution.py:483
  36.0 0.1 broadcast_select_fusion
  36.1 1.8 %collective-permute-start.8 = (bf16[2,9,32,256]{3,2,1,0:T(8,128)(2,1)S(1)}, bf16[2,9,32,256]{3,2,1,0:T(8,128)(2,1)S(1)}, u32[]{:S(2)}, u32[]{:S(2)}) collective-permute-start(bf16[2,9,32,256]{3,2,1,0:T(8,128)(2,1)S(1)} %get-tuple-element.93), channel_id=1, source_target_pairs={{0,2},{2,0},{4,6},{6,4},{8,10},{10,8},{12,14},{14,12},{1,3},{3,1},... | collective-permute-start | bytes 884744 | tf_op jit(solution)/shard_map/ppermute | solution.py:477
  37.9 0.7 collective-permute-start.9
  38.6 5.5 %weight_terms_rest.1 = (bf16[8,32,960]{2,1,0:T(8,128)(2,1)S(1)}, bf16[8,32,960]{2,1,0:T(8,128)(2,1)S(1)}, bf16[8,32,960]{2,1,0:T(8,128)(2,1)S(1)}, bf16[8,32,960]{2,1,0:T(8,128)(2,1)S(1)}) custom-call(s32[4]{0:T(128)S(1)} %pad_add_fusion.place, bf16[4,18,32,768]{3,2,1,0:T(8,128)(2,1)S(1)} %chip.1, bf16[2,18,32,768]{3,2,1,0:T(8,128)(2,1)S(1)} %get-tuple-element.61.sides, ...), custom_call_target="tpu_custom_call" | custom-call | flops 4026531840 | bytes 8388608 | tf_op jit(solution)/shard_map/weight_terms_rest/pallas_call | solution.py:440
  44.1 0.0 collective-permute-done.5.refs_1_
  44.1 3.0 %collective-permute-start.10 = (bf16[8,32,960]{2,1,0:T(8,128)(2,1)S(1)}, bf16[8,32,960]{2,1,0:T(8,128)(2,1)S(1)}, u32[]{:S(2)}, u32[]{:S(2)}) collective-permute-start(bf16[8,32,960]{2,1,0:T(8,128)(2,1)S(1)} %get-tuple-element.85), channel_id=1, source_target_pairs={{0,4},{2,6},{16,20},{18,22},{32,36},{34,38},{48,52},{50,54},{64,68... | collective-permute-start | bytes 1474568 | tf_op jit(solution)/shard_map/ppermute | solution.py:483
  47.1 0.0 collective-permute-done.6.refs_2_
  47.1 0.3 collective-permute-start.11
  47.4 0.0 collective-permute-done.7.refs_3_
  47.4 2.4 %collective-permute-start.12 = (bf16[8,32,960]{2,1,0:T(8,128)(2,1)S(1)}, bf16[8,32,960]{2,1,0:T(8,128)(2,1)S(1)}, u32[]{:S(2)}, u32[]{:S(2)}) collective-permute-start(bf16[8,32,960]{2,1,0:T(8,128)(2,1)S(1)} %get-tuple-element.87), channel_id=1, source_target_pairs={{0,8},{2,10},{16,24},{18,26},{32,40},{34,42},{48,56},{50,58},{64,7... | collective-permute-start | bytes 1474568 | tf_op jit(solution)/shard_map/ppermute | solution.py:483
  49.8 7.4 %outputs_inner.1 = (bf16[2,8,32,256]{3,2,1,0:T(8,128)(2,1)S(1)}, bf16[2,8,32,256]{3,2,1,0:T(8,128)(2,1)S(1)}, f32[2,256,256]{2,1,0:T(8,128)S(1)}, f32[2,256,256]{2,1,0:T(8,128)S(1)}) custom-call(s32[4]{0:T(128)S(1)} %pad_add_fusion.place, bf16[4,8,32,256]{3,2,1,0:T(8,128)(2,1)S(1)} %get-tuple-element.69.hid, ...), custom_call_target="tpu_custom_call" | custom-call | flops 6039797760 | bytes 8388608 | tf_op jit(solution)/shard_map/outputs_inner/pallas_call | solution.py:440
  57.2 0.0 collective-permute-done.8.near
  57.3 0.0 collective-permute-done.9.far
  57.3 3.2 %outputs_outer.1 = (bf16[4,8,32,256]{3,2,1,0:T(8,128)(2,1)}, bf16[4,8,32,256]{3,2,1,0:T(8,128)(2,1)}) custom-call(s32[4]{0:T(128)S(1)} %pad_add_fusion.place, bf16[2,9,32,256]{3,2,1,0:T(8,128)(2,1)S(1)} %collective-permute-done.8.near, bf16[2,9,32,256]{3,2,1,0:T(8,128)(2,1)S(1)} %collective-permute-done.9.far, ...), custom_call_target="tpu_custom_call" | custom-call | flops 1207959552 | bytes 8388608 | tf_op jit(solution)/shard_map/outputs_outer/pallas_call | solution.py:440
  60.4 0.0 collective-permute-done.10.refs_5_
  60.4 0.0 collective-permute-done.11.refs_6_
  60.4 1.0 %collective-permute-done.12.refs_7_ = bf16[8,32,960]{2,1,0:T(8,128)(2,1)S(1)} collective-permute-done((bf16[8,32,960]{2,1,0:T(8,128)(2,1)S(1)}, bf16[8,32,960]{2,1,0:T(8,128)(2,1)S(1)}, u32[]{:S(2)}, u32[]{:S(2)}) %collective-permute-start.12) | collective-permute-done | bytes 491552 | tf_op jit(solution)/shard_map/ppermute | solution.py:483
  61.4 1.7 %sum.1 = (f32[4,32,896]{2,1,0:T(8,128)S(1)}, bf16[4,32,896]{2,1,0:T(8,128)(2,1)S(1)}, bf16[4,32,896]{2,1,0:T(8,128)(2,1)S(1)}, bf16[4,32,896]{2,1,0:T(8,128)(2,1)S(1)}) custom-call(s32[4]{0:T(128)S(1)} %pad_add_fusion.place, bf16[8,32,768]{2,1,0:T(8,128)(2,1)S(1)} %get-tuple-element.80.refs_0_, bf16[8,32,768]{2,1,0:T(8,128)(2,1)S(1)} %collective-permute-done.5.refs_1_, ...), custom_call_target="tpu_custom_call" | custom-call | bytes 8388608 | tf_op jit(solution)/shard_map/sum/pallas_call | solution.py:440
  63.1 1.6 %collective-permute-start.13 = (bf16[4,32,896]{2,1,0:T(8,128)(2,1)S(1)}, bf16[4,32,896]{2,1,0:T(8,128)(2,1)S(1)}, u32[]{:S(2)}, u32[]{:S(2)}) collective-permute-start(bf16[4,32,896]{2,1,0:T(8,128)(2,1)S(1)} %get-tuple-element.89), channel_id=1, source_target_pairs={{0,32},{2,34},{16,48},{18,50},{32,64},{34,66},{48,80},{50,82},{64,... | collective-permute-start | bytes 688136 | tf_op jit(solution)/shard_map/ppermute | solution.py:483
  64.8 1.7 %collective-permute-start.14 = (bf16[4,32,896]{2,1,0:T(8,128)(2,1)S(1)}, bf16[4,32,896]{2,1,0:T(8,128)(2,1)S(1)}, u32[]{:S(2)}, u32[]{:S(2)}) collective-permute-start(bf16[4,32,896]{2,1,0:T(8,128)(2,1)S(1)} %get-tuple-element.90), channel_id=1, source_target_pairs={{0,96},{2,98},{16,112},{18,114},{32,0},{34,2},{48,16},{50,18},{64,... | collective-permute-start | bytes 688136 | tf_op jit(solution)/shard_map/ppermute | solution.py:483
  66.4 2.0 %collective-permute-start.15 = (bf16[4,32,896]{2,1,0:T(8,128)(2,1)S(1)}, bf16[4,32,896]{2,1,0:T(8,128)(2,1)S(1)}, u32[]{:S(2)}, u32[]{:S(2)}) collective-permute-start(bf16[4,32,896]{2,1,0:T(8,128)(2,1)S(1)} %get-tuple-element.91), channel_id=1, source_target_pairs={{0,64},{2,66},{16,80},{18,82},{32,96},{34,98},{48,112},{50,114},{6... | collective-permute-start | bytes 688136 | tf_op jit(solution)/shard_map/ppermute | solution.py:483
  68.4 2.0 %collective-permute-done.13 = bf16[4,32,896]{2,1,0:T(8,128)(2,1)S(1)} collective-permute-done((bf16[4,32,896]{2,1,0:T(8,128)(2,1)S(1)}, bf16[4,32,896]{2,1,0:T(8,128)(2,1)S(1)}, u32[]{:S(2)}, u32[]{:S(2)}) %collective-permute-start.13) | collective-permute-done | bytes 229408 | tf_op jit(solution)/shard_map/ppermute | solution.py:483
  70.4 0.4 collective-permute-done.14
  70.8 3.3 %collective-permute-done.15 = bf16[4,32,896]{2,1,0:T(8,128)(2,1)S(1)} collective-permute-done((bf16[4,32,896]{2,1,0:T(8,128)(2,1)S(1)}, bf16[4,32,896]{2,1,0:T(8,128)(2,1)S(1)}, u32[]{:S(2)}, u32[]{:S(2)}) %collective-permute-start.15) | collective-permute-done | bytes 229408 | tf_op jit(solution)/shard_map/ppermute | solution.py:483
  74.1 0.1 convert_add_fusion
  74.3 1.8 %collective-permute-start.16 = (f32[32,896]{1,0:T(8,128)S(1)}, f32[32,896]{1,0:T(8,128)S(1)}, u32[]{:S(2)}, u32[]{:S(2)}) collective-permute-start(f32[32,896]{1,0:T(8,128)S(1)} %get-tuple-element.108), channel_id=1, source_target_pairs={{0,2},{2,16},{16,18},{18,0},{32,34},{34,48},{48,50},{50,32},{64,66... | collective-permute-start | bytes 344072 | tf_op jit(solution)/shard_map/ppermute | solution.py:483
  76.1 2.2 %collective-permute-start.17 = (f32[32,896]{1,0:T(8,128)S(1)}, f32[32,896]{1,0:T(8,128)S(1)}, u32[]{:S(2)}, u32[]{:S(2)}) collective-permute-start(f32[32,896]{1,0:T(8,128)S(1)} %get-tuple-element.110), channel_id=1, source_target_pairs={{0,18},{2,0},{16,2},{18,16},{32,50},{34,32},{48,34},{50,48},{64,82... | collective-permute-start | bytes 344072 | tf_op jit(solution)/shard_map/ppermute | solution.py:483
  78.3 1.6 %collective-permute-start.18 = (f32[32,896]{1,0:T(8,128)S(1)}, f32[32,896]{1,0:T(8,128)S(1)}, u32[]{:S(2)}, u32[]{:S(2)}) collective-permute-start(f32[32,896]{1,0:T(8,128)S(1)} %get-tuple-element.109), channel_id=1, source_target_pairs={{0,16},{2,18},{16,0},{18,2},{32,48},{34,50},{48,32},{50,34},{64,80... | collective-permute-start | bytes 344072 | tf_op jit(solution)/shard_map/ppermute | solution.py:483
  79.9 1.1 %collective-permute-done.16 = f32[32,896]{1,0:T(8,128)S(1)} collective-permute-done((f32[32,896]{1,0:T(8,128)S(1)}, f32[32,896]{1,0:T(8,128)S(1)}, u32[]{:S(2)}, u32[]{:S(2)}) %collective-permute-start.16) | collective-permute-done | bytes 114720 | tf_op jit(solution)/shard_map/ppermute | solution.py:483
  81.0 0.0 collective-permute-done.17
  81.0 3.6 %collective-permute-done.18 = f32[32,896]{1,0:T(8,128)S(1)} collective-permute-done((f32[32,896]{1,0:T(8,128)S(1)}, f32[32,896]{1,0:T(8,128)S(1)}, u32[]{:S(2)}, u32[]{:S(2)}) %collective-permute-start.18) | collective-permute-done | bytes 114720 | tf_op jit(solution)/shard_map/ppermute | solution.py:483
  84.7 0.1 collective-permute-start.19
  84.7 1.2 %collective-permute-done.19 = f32[16,896]{1,0:T(8,128)S(1)} collective-permute-done((f32[16,896]{1,0:T(8,128)S(1)}, f32[16,896]{1,0:T(8,128)S(1)}, u32[]{:S(2)}, u32[]{:S(2)}) %collective-permute-start.19) | collective-permute-done | bytes 57376 | tf_op jit(solution)/shard_map/ppermute | solution.py:459
  86.0 0.7 select_bitcast_fusion
  (23 shorter events, 0.4 us)
Async XLA Ops:
  0.6 1.0 %copy-start = (bf16[1,4,8,32,256]{4,3,2,1,0:T(8,128)(2,1)S(1)}, bf16[1,4,8,32,256]{4,3,2,1,0:T(8,128)(2,1)}, u32[]{:S(2)}) copy-start(bf16[1,4,8,32,256]{4,3,2,1,0:T(8,128)(2,1)} %param.5) | copy-start | bytes 1572868
  1.7 1.0 %copy-start.2 = (bf16[1,4,8,32,256]{4,3,2,1,0:T(8,128)(2,1)S(1)}, bf16[1,4,8,32,256]{4,3,2,1,0:T(8,128)(2,1)}, u32[]{:S(2)}) copy-start(bf16[1,4,8,32,256]{4,3,2,1,0:T(8,128)(2,1)} %param.4) | copy-start | bytes 1572868
  2.7 5.5 %copy-start.1 = (bf16[1,4,8,32,256]{4,3,2,1,0:T(8,128)(2,1)S(1)}, bf16[1,4,8,32,256]{4,3,2,1,0:T(8,128)(2,1)}, u32[]{:S(2)}) copy-start(bf16[1,4,8,32,256]{4,3,2,1,0:T(8,128)(2,1)} %param.5) | copy-start | bytes 1572868
  2.7 5.5 %copy-start.3 = (bf16[1,4,8,32,256]{4,3,2,1,0:T(8,128)(2,1)S(1)}, bf16[1,4,8,32,256]{4,3,2,1,0:T(8,128)(2,1)}, u32[]{:S(2)}) copy-start(bf16[1,4,8,32,256]{4,3,2,1,0:T(8,128)(2,1)} %param.4) | copy-start | bytes 1572868
  2.8 2.4 %collective-permute-start = (bf16[4,9,32,256]{3,2,1,0:T(8,128)(2,1)S(1)}, bf16[4,9,32,256]{3,2,1,0:T(8,128)(2,1)S(1)}, u32[]{:S(2)}, u32[]{:S(2)}) collective-permute-start(bf16[4,9,32,256]{3,2,1,0:T(8,128)(2,1)S(1)} %pack.1), channel_id=1, source_target_pairs={{0,1},{1,0},{2,3},{3,2},{4,5},{5,4},{6,7},{7,6},{8,9},{9,8},{10,11... | collective-permute-start | bytes 1769480 | tf_op jit(solution)/shard_map/ppermute | solution.py:459
  2.9 5.3 %copy-start.4 = (bf16[6912,256]{1,0:T(8,128)(2,1)S(1)}, bf16[6912,256]{1,0:T(8,128)(2,1)}, u32[]{:S(2)}) copy-start(bf16[6912,256]{1,0:T(8,128)(2,1)} %first_hbm.1) | copy-start | bytes 10616836
  5.4 15.3 %collective-permute-start.1 = (bf16[2,9,32,256]{3,2,1,0:T(8,128)(2,1)S(1)}, bf16[2,9,32,256]{3,2,1,0:T(8,128)(2,1)S(1)}, u32[]{:S(2)}, u32[]{:S(2)}) collective-permute-start(bf16[2,9,32,256]{3,2,1,0:T(8,128)(2,1)S(1)} %get-tuple-element.97), channel_id=1, source_target_pairs={{0,2},{2,0},{4,6},{6,4},{8,10},{10,8},{12,14},{14,12},{1,3},{3,1},... | collective-permute-start | bytes 884744 | tf_op jit(solution)/shard_map/ppermute | solution.py:477
  7.5 13.2 %collective-permute-start.2 = (bf16[2,9,32,256]{3,2,1,0:T(8,128)(2,1)S(1)}, bf16[2,9,32,256]{3,2,1,0:T(8,128)(2,1)S(1)}, u32[]{:S(2)}, u32[]{:S(2)}) collective-permute-start(bf16[2,9,32,256]{3,2,1,0:T(8,128)(2,1)S(1)} %get-tuple-element.96), channel_id=1, source_target_pairs={{2,4},{4,2},{6,8},{8,6},{10,12},{12,10},{3,5},{5,3},{7,9},{9,7},{1... | collective-permute-start | bytes 884744 | tf_op jit(solution)/shard_map/ppermute | solution.py:476
  23.0 2.5 %collective-permute-start.3 = (bf16[4,9,32,256]{3,2,1,0:T(8,128)(2,1)S(1)}, bf16[4,9,32,256]{3,2,1,0:T(8,128)(2,1)S(1)}, u32[]{:S(2)}, u32[]{:S(2)}) collective-permute-start(bf16[4,9,32,256]{3,2,1,0:T(8,128)(2,1)S(1)} %get-tuple-element.59), channel_id=1, source_target_pairs={{0,1},{1,0},{2,3},{3,2},{4,5},{5,4},{6,7},{7,6},{8,9},{9,8},{10,11... | collective-permute-start | bytes 1769480 | tf_op jit(solution)/shard_map/ppermute | solution.py:459
  23.2 2.3 %collective-permute-start.4 = (bf16[2,8,32,256]{3,2,1,0:T(8,128)(2,1)S(1)}, bf16[2,8,32,256]{3,2,1,0:T(8,128)(2,1)S(1)}, u32[]{:S(2)}, u32[]{:S(2)}) collective-permute-start(bf16[2,8,32,256]{3,2,1,0:T(8,128)(2,1)S(1)} %maximum_select_fusion), channel_id=1, source_target_pairs={{0,1},{1,0},{2,3},{3,2},{4,5},{5,4},{6,7},{7,6},{8,9},{9,8},{10,11... | collective-permute-start | bytes 786440 | tf_op jit(solution)/shard_map/ppermute | solution.py:459
  30.1 14.0 %collective-permute-start.5 = (bf16[8,32,768]{2,1,0:T(8,128)(2,1)S(1)}, bf16[8,32,768]{2,1,0:T(8,128)(2,1)S(1)}, u32[]{:S(2)}, u32[]{:S(2)}) collective-permute-start(bf16[8,32,768]{2,1,0:T(8,128)(2,1)S(1)} %get-tuple-element.65), channel_id=1, source_target_pairs={{0,4},{2,6},{16,20},{18,22},{32,36},{34,38},{48,52},{50,54},{64,68... | collective-permute-start | bytes 1179656 | tf_op jit(solution)/shard_map/ppermute | solution.py:483
  32.3 14.8 %collective-permute-start.6 = (bf16[8,32,768]{2,1,0:T(8,128)(2,1)S(1)}, bf16[8,32,768]{2,1,0:T(8,128)(2,1)S(1)}, u32[]{:S(2)}, u32[]{:S(2)}) collective-permute-start(bf16[8,32,768]{2,1,0:T(8,128)(2,1)S(1)} %get-tuple-element.66), channel_id=1, source_target_pairs={{0,12},{2,14},{16,28},{18,30},{32,44},{34,46},{48,60},{50,62},{64,... | collective-permute-start | bytes 1179656 | tf_op jit(solution)/shard_map/ppermute | solution.py:483
  33.7 13.7 %collective-permute-start.7 = (bf16[8,32,768]{2,1,0:T(8,128)(2,1)S(1)}, bf16[8,32,768]{2,1,0:T(8,128)(2,1)S(1)}, u32[]{:S(2)}, u32[]{:S(2)}) collective-permute-start(bf16[8,32,768]{2,1,0:T(8,128)(2,1)S(1)} %get-tuple-element.67), channel_id=1, source_target_pairs={{0,8},{2,10},{16,24},{18,26},{32,40},{34,42},{48,56},{50,58},{64,7... | collective-permute-start | bytes 1179656 | tf_op jit(solution)/shard_map/ppermute | solution.py:483
  36.1 21.1 %collective-permute-start.8 = (bf16[2,9,32,256]{3,2,1,0:T(8,128)(2,1)S(1)}, bf16[2,9,32,256]{3,2,1,0:T(8,128)(2,1)S(1)}, u32[]{:S(2)}, u32[]{:S(2)}) collective-permute-start(bf16[2,9,32,256]{3,2,1,0:T(8,128)(2,1)S(1)} %get-tuple-element.93), channel_id=1, source_target_pairs={{0,2},{2,0},{4,6},{6,4},{8,10},{10,8},{12,14},{14,12},{1,3},{3,1},... | collective-permute-start | bytes 884744 | tf_op jit(solution)/shard_map/ppermute | solution.py:477
  37.9 19.3 %collective-permute-start.9 = (bf16[2,9,32,256]{3,2,1,0:T(8,128)(2,1)S(1)}, bf16[2,9,32,256]{3,2,1,0:T(8,128)(2,1)S(1)}, u32[]{:S(2)}, u32[]{:S(2)}) collective-permute-start(bf16[2,9,32,256]{3,2,1,0:T(8,128)(2,1)S(1)} %get-tuple-element.92), channel_id=1, source_target_pairs={{2,4},{4,2},{6,8},{8,6},{10,12},{12,10},{3,5},{5,3},{7,9},{9,7},{1... | collective-permute-start | bytes 884744 | tf_op jit(solution)/shard_map/ppermute | solution.py:476
  44.1 16.3 %collective-permute-start.10 = (bf16[8,32,960]{2,1,0:T(8,128)(2,1)S(1)}, bf16[8,32,960]{2,1,0:T(8,128)(2,1)S(1)}, u32[]{:S(2)}, u32[]{:S(2)}) collective-permute-start(bf16[8,32,960]{2,1,0:T(8,128)(2,1)S(1)} %get-tuple-element.85), channel_id=1, source_target_pairs={{0,4},{2,6},{16,20},{18,22},{32,36},{34,38},{48,52},{50,54},{64,68... | collective-permute-start | bytes 1474568 | tf_op jit(solution)/shard_map/ppermute | solution.py:483
  47.1 13.3 %collective-permute-start.11 = (bf16[8,32,960]{2,1,0:T(8,128)(2,1)S(1)}, bf16[8,32,960]{2,1,0:T(8,128)(2,1)S(1)}, u32[]{:S(2)}, u32[]{:S(2)}) collective-permute-start(bf16[8,32,960]{2,1,0:T(8,128)(2,1)S(1)} %get-tuple-element.86), channel_id=1, source_target_pairs={{0,12},{2,14},{16,28},{18,30},{32,44},{34,46},{48,60},{50,62},{64,... | collective-permute-start | bytes 1474568 | tf_op jit(solution)/shard_map/ppermute | solution.py:483
  47.4 14.0 %collective-permute-start.12 = (bf16[8,32,960]{2,1,0:T(8,128)(2,1)S(1)}, bf16[8,32,960]{2,1,0:T(8,128)(2,1)S(1)}, u32[]{:S(2)}, u32[]{:S(2)}) collective-permute-start(bf16[8,32,960]{2,1,0:T(8,128)(2,1)S(1)} %get-tuple-element.87), channel_id=1, source_target_pairs={{0,8},{2,10},{16,24},{18,26},{32,40},{34,42},{48,56},{50,58},{64,7... | collective-permute-start | bytes 1474568 | tf_op jit(solution)/shard_map/ppermute | solution.py:483
  63.1 7.3 %collective-permute-start.13 = (bf16[4,32,896]{2,1,0:T(8,128)(2,1)S(1)}, bf16[4,32,896]{2,1,0:T(8,128)(2,1)S(1)}, u32[]{:S(2)}, u32[]{:S(2)}) collective-permute-start(bf16[4,32,896]{2,1,0:T(8,128)(2,1)S(1)} %get-tuple-element.89), channel_id=1, source_target_pairs={{0,32},{2,34},{16,48},{18,50},{32,64},{34,66},{48,80},{50,82},{64,... | collective-permute-start | bytes 688136 | tf_op jit(solution)/shard_map/ppermute | solution.py:483
  64.8 6.0 %collective-permute-start.14 = (bf16[4,32,896]{2,1,0:T(8,128)(2,1)S(1)}, bf16[4,32,896]{2,1,0:T(8,128)(2,1)S(1)}, u32[]{:S(2)}, u32[]{:S(2)}) collective-permute-start(bf16[4,32,896]{2,1,0:T(8,128)(2,1)S(1)} %get-tuple-element.90), channel_id=1, source_target_pairs={{0,96},{2,98},{16,112},{18,114},{32,0},{34,2},{48,16},{50,18},{64,... | collective-permute-start | bytes 688136 | tf_op jit(solution)/shard_map/ppermute | solution.py:483
  66.4 7.7 %collective-permute-start.15 = (bf16[4,32,896]{2,1,0:T(8,128)(2,1)S(1)}, bf16[4,32,896]{2,1,0:T(8,128)(2,1)S(1)}, u32[]{:S(2)}, u32[]{:S(2)}) collective-permute-start(bf16[4,32,896]{2,1,0:T(8,128)(2,1)S(1)} %get-tuple-element.91), channel_id=1, source_target_pairs={{0,64},{2,66},{16,80},{18,82},{32,96},{34,98},{48,112},{50,114},{6... | collective-permute-start | bytes 688136 | tf_op jit(solution)/shard_map/ppermute | solution.py:483
  74.3 6.7 %collective-permute-start.16 = (f32[32,896]{1,0:T(8,128)S(1)}, f32[32,896]{1,0:T(8,128)S(1)}, u32[]{:S(2)}, u32[]{:S(2)}) collective-permute-start(f32[32,896]{1,0:T(8,128)S(1)} %get-tuple-element.108), channel_id=1, source_target_pairs={{0,2},{2,16},{16,18},{18,0},{32,34},{34,48},{48,50},{50,32},{64,66... | collective-permute-start | bytes 344072 | tf_op jit(solution)/shard_map/ppermute | solution.py:483
  76.1 4.9 %collective-permute-start.17 = (f32[32,896]{1,0:T(8,128)S(1)}, f32[32,896]{1,0:T(8,128)S(1)}, u32[]{:S(2)}, u32[]{:S(2)}) collective-permute-start(f32[32,896]{1,0:T(8,128)S(1)} %get-tuple-element.110), channel_id=1, source_target_pairs={{0,18},{2,0},{16,2},{18,16},{32,50},{34,32},{48,34},{50,48},{64,82... | collective-permute-start | bytes 344072 | tf_op jit(solution)/shard_map/ppermute | solution.py:483
  78.3 6.3 %collective-permute-start.18 = (f32[32,896]{1,0:T(8,128)S(1)}, f32[32,896]{1,0:T(8,128)S(1)}, u32[]{:S(2)}, u32[]{:S(2)}) collective-permute-start(f32[32,896]{1,0:T(8,128)S(1)} %get-tuple-element.109), channel_id=1, source_target_pairs={{0,16},{2,18},{16,0},{18,2},{32,48},{34,50},{48,32},{50,34},{64,80... | collective-permute-start | bytes 344072 | tf_op jit(solution)/shard_map/ppermute | solution.py:483
  84.7 1.3 %collective-permute-start.19 = (f32[16,896]{1,0:T(8,128)S(1)}, f32[16,896]{1,0:T(8,128)S(1)}, u32[]{:S(2)}, u32[]{:S(2)}) collective-permute-start(f32[16,896]{1,0:T(8,128)S(1)} %get-tuple-element.118), channel_id=1, source_target_pairs={{0,1},{1,0},{2,3},{3,2},{4,5},{5,4},{6,7},{7,6},{8,9},{9,8},{10,11... | collective-permute-start | bytes 172040 | tf_op jit(solution)/shard_map/ppermute | solution.py:459

commit v10 on v9

--- a/solution.py
+++ b/solution.py
@@ -138,8 +138,15 @@
     return 1 - lax.rem(place[3], 2)
 
 
-def pack_kernel(place, cot, field, send, arrived):
-    core = place[0]
+def pack_kernel(place, cot, field, send, edges, arrived):
+    core = place[0]
+    slabs = [
+        pltpu.make_async_copy(whole.at[3 * i], edges.at[i, j], arrived.at[2 + 2 * i + j])
+        for i in range(2)
+        for j, whole in enumerate((cot, field))
+    ]
+    for copy in slabs:
+        copy.start()
 
     def pack(whole, row):
         copies = [
@@ -158,6 +165,9 @@
     @pl.when(core == 1)
     def _():
         pack(field, cot.at[:, 0:1])
+
+    for copy in slabs:
+        copy.wait()
 
 
 def inner_kernel(
@@ -527,20 +537,20 @@
     edge_scratch = [pltpu.VMEM((2, 10, 32, 768), BF)] * 2
     weights = (first_weight, second_weight)
     flops = 2 * 2 * 1024 * 6912 * 256
-    (sent1,) = call(
+    sent1, slabs = call(
         pack_kernel,
         "pack",
         0,
         (core.astype(jnp.int32).reshape(1), cot, field),
-        [shape((4, 9, 32, 256), BF)],
-        [pltpu.SemaphoreType.DMA((2,))],
+        [shape((4, 9, 32, 256), BF), shape((2, 2, 8, 32, 256), BF)],
+        [pltpu.SemaphoreType.DMA((6,))],
         40,
         (1, 2),
     )
     other1 = swap_cores(sent1)
     near1, far1 = swap_slabs(
-        cot,
-        field,
+        {0: slabs[0, 0], 3: slabs[1, 0]},
+        {0: slabs[0, 1], 3: slabs[1, 1]},
         jnp.where(zero, other1[:, 8:9], other1[:, 7:8]),
         jnp.where(zero, other1[:, 0:1], other1[:, 8:9]),
         low_half,

time: 88 us -> 88.1 us (level)
  local copies, waits for them, and re-layouts: 4.41 us -> 2.24 us
  waiting for transfers between devices: 16.2 us -> 17.7 us
    ppermute x4, waiting for transfers between devices: 2.87 us -> 4.71 us  [swap_cores(): return lax.ppermute(value, 'py', [(0, 1), (1, 0)])]
    squeeze x2 -> x1, local copies, waits for them, and re-layouts: 1.15 us -> 0.02 us  [slab(): first[i]]
    squeeze x2 -> x1, local copies, waits for them, and re-layouts: 1.08 us -> 0.02 us  [slab(): second[i]]
  transfers between devices with their start and end apart: 20 -> 20, of which waited for: 9 -> 10; matrix products, arithmetic and copies ran while one was open for 3% -> 0% of each run, Pallas kernels for 31% -> 31%
where the time goes in v10:
time: 88.1 us; the launch traced here: 86.8 us
  Pallas kernels  36.1 us (41%)
  starting transfers between devices  28.6 us (32%)
  waiting for transfers between devices  17.7 us (20%)
  local copies, waits for them, and re-layouts  2.24 us (3%)
  other arithmetic  1.19 us (1%)
  between operations  1.01 us (1%)
    pallas_call x9, Pallas kernels, call(): pl.pallas_call(kernel, name=name, out_shape=outs, in_specs=[pl.BlockSpec(...  36.1 us
    ppermute x12, starting transfers between devices, hop(): lax.ppermute(part, ALL, hop_pairs(stage, distance))  22.5 us
    ppermute x12, waiting for transfers between devices, hop(): lax.ppermute(part, ALL, hop_pairs(stage, distance))  11.3 us
    ppermute x4, waiting for transfers between devices, swap_cores(): return lax.ppermute(value, 'py', [(0, 1), (1, 0)])  4.71 us
    ppermute x2, starting transfers between devices, swap_slabs(): got_near = lax.ppermute(jnp.where(low_half, high, low), 'px', near)  3.9 us
    unnamed x10, local copies, waits for them, and re-layouts  2.09 us
  transfers between devices with their start and end apart: 20, of which 10 were waited for; matrix products, arithmetic and copies ran while one was open for 0% of the time, Pallas kernels for 31%

profile of v10, /device:TPU:0, one launch (start us, length us, event | category | flops | bytes accessed | tf_op | source)
XLA Modules:
  0.0 86.8 jit_solution(16388513880172663198)
XLA Ops:
  0.6 0.0 copy-start
  0.6 1.0 %copy-done = bf16[1,4,8,32,256]{4,3,2,1,0:T(8,128)(2,1)S(1)} copy-done((bf16[1,4,8,32,256]{4,3,2,1,0:T(8,128)(2,1)S(1)}, bf16[1,4,8,32,256]{4,3,2,1,0:T(8,128)(2,1)}, u32[]{:S(2)}) %copy-start) | copy-done | bytes 524312
  1.7 0.0 copy-start.2
  1.7 1.0 %copy-done.2 = bf16[1,4,8,32,256]{4,3,2,1,0:T(8,128)(2,1)S(1)} copy-done((bf16[1,4,8,32,256]{4,3,2,1,0:T(8,128)(2,1)S(1)}, bf16[1,4,8,32,256]{4,3,2,1,0:T(8,128)(2,1)}, u32[]{:S(2)}) %copy-start.2) | copy-done | bytes 524312
  2.7 0.0 copy-start.1
  2.7 0.0 copy-start.3
  2.7 0.8 pack.1
  3.5 0.1 collective-permute-start
  3.6 0.0 copy-start.4
  3.6 0.1 pad_add_fusion.place
  3.8 1.8 %collective-permute-done.other = bf16[4,9,32,256]{3,2,1,0:T(8,128)(2,1)S(1)} collective-permute-done((bf16[4,9,32,256]{3,2,1,0:T(8,128)(2,1)S(1)}, bf16[4,9,32,256]{3,2,1,0:T(8,128)(2,1)S(1)}, u32[]{:S(2)}, u32[]{:S(2)}) %collective-permute-start) | collective-permute-done | bytes 589856 | tf_op jit(solution)/shard_map/ppermute | solution.py:469
  5.7 0.1 broadcast_select_fusion.2
  5.8 2.1 %collective-permute-start.1 = (bf16[2,9,32,256]{3,2,1,0:T(8,128)(2,1)S(1)}, bf16[2,9,32,256]{3,2,1,0:T(8,128)(2,1)S(1)}, u32[]{:S(2)}, u32[]{:S(2)}) collective-permute-start(bf16[2,9,32,256]{3,2,1,0:T(8,128)(2,1)S(1)} %get-tuple-element.101), channel_id=1, source_target_pairs={{0,2},{2,0},{4,6},{6,4},{8,10},{10,8},{12,14},{14,12},{1,3},{3,1},... | collective-permute-start | bytes 884744 | tf_op jit(solution)/shard_map/ppermute | solution.py:487
  7.9 0.7 collective-permute-start.2
  8.6 0.0 copy-done.1
  8.6 0.0 copy-done.3
  8.6 0.0 copy-done.4
  8.6 9.4 %inner.1 = (bf16[2,8,32,256]{3,2,1,0:T(8,128)(2,1)S(1)}, bf16[2,8,32,256]{3,2,1,0:T(8,128)(2,1)S(1)}, f32[2,256,256]{2,1,0:T(8,128)S(1)}, f32[2,256,256]{2,1,0:T...) custom-call(s32[4]{0:T(128)S(1)} %pad_add_fusion.place, bf16[4,8,32,256]{3,2,1,0:T(8,128)(2,1)S(1)} %bitcast.75, ...), custom_call_target="tpu_custom_call" | custom-call | flops 6039797760 | bytes 8388608 | tf_op jit(solution)/shard_map/inner/pallas_call | solution.py:450
  18.0 1.1 %chip.1 = bf16[4,18,32,768]{3,2,1,0:T(8,128)(2,1)S(1)} custom-call(s32[4]{0:T(128)S(1)} %pad_add_fusion.place, bf16[4,8,32,256]{3,2,1,0:T(8,128)(2,1)S(1)} %bitcast.76, bf16[4,8,32,256]{3,2,1,0:T(8,128)(2,1)S(1)} %bitcast.81, bf16[4,9,32,256]{3,2,1,0:T(8,128)(2,1)S(1)} %collective-permute-done.other), custom_call_target="tpu_custom_call" | custom-call | flops 905969664 | bytes 8388608 | tf_op jit(solution)/shard_map/chip/pallas_call | solution.py:450
  19.1 1.7 %collective-permute-done.1.near.near1 = bf16[2,9,32,256]{3,2,1,0:T(8,128)(2,1)S(1)} collective-permute-done((bf16[2,9,32,256]{3,2,1,0:T(8,128)(2,1)S(1)}, bf16[2,9,32,256]{3,2,1,0:T(8,128)(2,1)S(1)}, u32[]{:S(2)}, u32[]{:S(2)}) %collective-permute-start.1) | collective-permute-done | bytes 294944 | tf_op jit(solution)/shard_map/ppermute | solution.py:487
  20.8 0.0 collective-permute-done.2.far.far1
  20.8 2.4 %outer.1 = (bf16[4,8,32,256]{3,2,1,0:T(8,128)(2,1)S(1)}, bf16[4,8,32,256]{3,2,1,0:T(8,128)(2,1)S(1)}, bf16[4,9,32,256]{3,2,1,0:T(8,128)(2,1)S(1)}) custom-call(s32[4]{0:T(128)S(1)} %pad_add_fusion.place, bf16[2,9,32,256]{3,2,1,0:T(8,128)(2,1)S(1)} %collective-permute-done.1.near.near1, bf16[2,9,32,256]{3,2,1,0:T(8,128)(2,1)S(1)} %collective-permute-done.2.far.far1, ...), custom_call_target="tpu_custom_call" | custom-call | flops 1207959552 | bytes 8388608 | tf_op jit(solution)/shard_map/outer/pallas_call | solution.py:450
  23.1 0.1 collective-permute-start.3
  23.3 0.6 collective-permute-start.4
  24.0 1.6 %collective-permute-done.4.edges = bf16[2,8,32,256]{3,2,1,0:T(8,128)(2,1)S(1)} collective-permute-done((bf16[2,8,32,256]{3,2,1,0:T(8,128)(2,1)S(1)}, bf16[2,8,32,256]{3,2,1,0:T(8,128)(2,1)S(1)}, u32[]{:S(2)}, u32[]{:S(2)}) %collective-permute-start.4) | collective-permute-done | bytes 262176 | tf_op jit(solution)/shard_map/ppermute | solution.py:469
  25.6 0.0 collective-permute-done.3.other2.other
  25.6 4.6 %weight_terms.1 = (bf16[8,32,768]{2,1,0:T(8,128)(2,1)S(1)}, bf16[8,32,768]{2,1,0:T(8,128)(2,1)S(1)}, bf16[8,32,768]{2,1,0:T(8,128)(2,1)S(1)}, bf16[8,32,768]{2,1...) custom-call(s32[4]{0:T(128)S(1)} %pad_add_fusion.place, ...), custom_call_target="tpu_custom_call" | custom-call | flops 3221225472 | bytes 8388608 | tf_op jit(solution)/shard_map/weight_terms/pallas_call | solution.py:450
  30.2 2.3 %collective-permute-start.5 = (bf16[8,32,768]{2,1,0:T(8,128)(2,1)S(1)}, bf16[8,32,768]{2,1,0:T(8,128)(2,1)S(1)}, u32[]{:S(2)}, u32[]{:S(2)}) collective-permute-start(bf16[8,32,768]{2,1,0:T(8,128)(2,1)S(1)} %get-tuple-element.69), channel_id=1, source_target_pairs={{0,4},{2,6},{16,20},{18,22},{32,36},{34,38},{48,52},{50,54},{64,68... | collective-permute-start | bytes 1179656 | tf_op jit(solution)/shard_map/ppermute | solution.py:493
  32.5 1.3 %collective-permute-start.6 = (bf16[8,32,768]{2,1,0:T(8,128)(2,1)S(1)}, bf16[8,32,768]{2,1,0:T(8,128)(2,1)S(1)}, u32[]{:S(2)}, u32[]{:S(2)}) collective-permute-start(bf16[8,32,768]{2,1,0:T(8,128)(2,1)S(1)} %get-tuple-element.70), channel_id=1, source_target_pairs={{0,12},{2,14},{16,28},{18,30},{32,44},{34,46},{48,60},{50,62},{64,... | collective-permute-start | bytes 1179656 | tf_op jit(solution)/shard_map/ppermute | solution.py:493
  33.9 2.2 %collective-permute-start.7 = (bf16[8,32,768]{2,1,0:T(8,128)(2,1)S(1)}, bf16[8,32,768]{2,1,0:T(8,128)(2,1)S(1)}, u32[]{:S(2)}, u32[]{:S(2)}) collective-permute-start(bf16[8,32,768]{2,1,0:T(8,128)(2,1)S(1)} %get-tuple-element.71), channel_id=1, source_target_pairs={{0,8},{2,10},{16,24},{18,26},{32,40},{34,42},{48,56},{50,58},{64,7... | collective-permute-start | bytes 1179656 | tf_op jit(solution)/shard_map/ppermute | solution.py:493
  36.2 0.1 broadcast_select_fusion
  36.3 1.8 %collective-permute-start.8 = (bf16[2,9,32,256]{3,2,1,0:T(8,128)(2,1)S(1)}, bf16[2,9,32,256]{3,2,1,0:T(8,128)(2,1)S(1)}, u32[]{:S(2)}, u32[]{:S(2)}) collective-permute-start(bf16[2,9,32,256]{3,2,1,0:T(8,128)(2,1)S(1)} %get-tuple-element.97), channel_id=1, source_target_pairs={{0,2},{2,0},{4,6},{6,4},{8,10},{10,8},{12,14},{14,12},{1,3},{3,1},... | collective-permute-start | bytes 884744 | tf_op jit(solution)/shard_map/ppermute | solution.py:487
  38.1 0.7 collective-permute-start.9
  38.8 5.5 %weight_terms_rest.1 = (bf16[8,32,960]{2,1,0:T(8,128)(2,1)S(1)}, bf16[8,32,960]{2,1,0:T(8,128)(2,1)S(1)}, bf16[8,32,960]{2,1,0:T(8,128)(2,1)S(1)}, bf16[8,32,960]{2,1,0:T(8,128)(2,1)S(1)}) custom-call(s32[4]{0:T(128)S(1)} %pad_add_fusion.place, bf16[4,18,32,768]{3,2,1,0:T(8,128)(2,1)S(1)} %chip.1, bf16[2,18,32,768]{3,2,1,0:T(8,128)(2,1)S(1)} %get-tuple-element.65.sides, ...), custom_call_target="tpu_custom_call" | custom-call | flops 4026531840 | bytes 8388608 | tf_op jit(solution)/shard_map/weight_terms_rest/pallas_call | solution.py:450
  44.3 0.0 collective-permute-done.5.refs_1_
  44.3 3.0 %collective-permute-start.10 = (bf16[8,32,960]{2,1,0:T(8,128)(2,1)S(1)}, bf16[8,32,960]{2,1,0:T(8,128)(2,1)S(1)}, u32[]{:S(2)}, u32[]{:S(2)}) collective-permute-start(bf16[8,32,960]{2,1,0:T(8,128)(2,1)S(1)} %get-tuple-element.89), channel_id=1, source_target_pairs={{0,4},{2,6},{16,20},{18,22},{32,36},{34,38},{48,52},{50,54},{64,68... | collective-permute-start | bytes 1474568 | tf_op jit(solution)/shard_map/ppermute | solution.py:493
  47.4 0.0 collective-permute-done.6.refs_2_
  47.4 0.3 collective-permute-start.11
  47.6 0.0 collective-permute-done.7.refs_3_
  47.6 2.4 %collective-permute-start.12 = (bf16[8,32,960]{2,1,0:T(8,128)(2,1)S(1)}, bf16[8,32,960]{2,1,0:T(8,128)(2,1)S(1)}, u32[]{:S(2)}, u32[]{:S(2)}) collective-permute-start(bf16[8,32,960]{2,1,0:T(8,128)(2,1)S(1)} %get-tuple-element.91), channel_id=1, source_target_pairs={{0,8},{2,10},{16,24},{18,26},{32,40},{34,42},{48,56},{50,58},{64,7... | collective-permute-start | bytes 1474568 | tf_op jit(solution)/shard_map/ppermute | solution.py:493
  50.0 7.4 %outputs_inner.1 = (bf16[2,8,32,256]{3,2,1,0:T(8,128)(2,1)S(1)}, bf16[2,8,32,256]{3,2,1,0:T(8,128)(2,1)S(1)}, f32[2,256,256]{2,1,0:T(8,128)S(1)}, f32[2,256,256]{2,1,0:T(8,128)S(1)}) custom-call(s32[4]{0:T(128)S(1)} %pad_add_fusion.place, bf16[4,8,32,256]{3,2,1,0:T(8,128)(2,1)S(1)} %get-tuple-element.73.hid, ...), custom_call_target="tpu_custom_call" | custom-call | flops 6039797760 | bytes 8388608 | tf_op jit(solution)/shard_map/outputs_inner/pallas_call | solution.py:450
  57.5 0.0 collective-permute-done.8.near
  57.5 0.0 collective-permute-done.9.far
  57.5 3.2 %outputs_outer.1 = (bf16[4,8,32,256]{3,2,1,0:T(8,128)(2,1)}, bf16[4,8,32,256]{3,2,1,0:T(8,128)(2,1)}) custom-call(s32[4]{0:T(128)S(1)} %pad_add_fusion.place, bf16[2,9,32,256]{3,2,1,0:T(8,128)(2,1)S(1)} %collective-permute-done.8.near, bf16[2,9,32,256]{3,2,1,0:T(8,128)(2,1)S(1)} %collective-permute-done.9.far, ...), custom_call_target="tpu_custom_call" | custom-call | flops 1207959552 | bytes 8388608 | tf_op jit(solution)/shard_map/outputs_outer/pallas_call | solution.py:450
  60.7 0.0 collective-permute-done.10.refs_5_
  60.7 0.0 collective-permute-done.11.refs_6_
  60.7 1.0 %collective-permute-done.12.refs_7_ = bf16[8,32,960]{2,1,0:T(8,128)(2,1)S(1)} collective-permute-done((bf16[8,32,960]{2,1,0:T(8,128)(2,1)S(1)}, bf16[8,32,960]{2,1,0:T(8,128)(2,1)S(1)}, u32[]{:S(2)}, u32[]{:S(2)}) %collective-permute-start.12) | collective-permute-done | bytes 491552 | tf_op jit(solution)/shard_map/ppermute | solution.py:493
  61.7 1.7 %sum.1 = (f32[4,32,896]{2,1,0:T(8,128)S(1)}, bf16[4,32,896]{2,1,0:T(8,128)(2,1)S(1)}, bf16[4,32,896]{2,1,0:T(8,128)(2,1)S(1)}, bf16[4,32,896]{2,1,0:T(8,128)(2,1)S(1)}) custom-call(s32[4]{0:T(128)S(1)} %pad_add_fusion.place, bf16[8,32,768]{2,1,0:T(8,128)(2,1)S(1)} %get-tuple-element.84.refs_0_, bf16[8,32,768]{2,1,0:T(8,128)(2,1)S(1)} %collective-permute-done.5.refs_1_, ...), custom_call_target="tpu_custom_call" | custom-call | bytes 8388608 | tf_op jit(solution)/shard_map/sum/pallas_call | solution.py:450
  63.4 1.6 %collective-permute-start.13 = (bf16[4,32,896]{2,1,0:T(8,128)(2,1)S(1)}, bf16[4,32,896]{2,1,0:T(8,128)(2,1)S(1)}, u32[]{:S(2)}, u32[]{:S(2)}) collective-permute-start(bf16[4,32,896]{2,1,0:T(8,128)(2,1)S(1)} %get-tuple-element.93), channel_id=1, source_target_pairs={{0,32},{2,34},{16,48},{18,50},{32,64},{34,66},{48,80},{50,82},{64,... | collective-permute-start | bytes 688136 | tf_op jit(solution)/shard_map/ppermute | solution.py:493
  65.0 1.7 %collective-permute-start.14 = (bf16[4,32,896]{2,1,0:T(8,128)(2,1)S(1)}, bf16[4,32,896]{2,1,0:T(8,128)(2,1)S(1)}, u32[]{:S(2)}, u32[]{:S(2)}) collective-permute-start(bf16[4,32,896]{2,1,0:T(8,128)(2,1)S(1)} %get-tuple-element.94), channel_id=1, source_target_pairs={{0,96},{2,98},{16,112},{18,114},{32,0},{34,2},{48,16},{50,18},{64,... | collective-permute-start | bytes 688136 | tf_op jit(solution)/shard_map/ppermute | solution.py:493
  66.7 2.0 %collective-permute-start.15 = (bf16[4,32,896]{2,1,0:T(8,128)(2,1)S(1)}, bf16[4,32,896]{2,1,0:T(8,128)(2,1)S(1)}, u32[]{:S(2)}, u32[]{:S(2)}) collective-permute-start(bf16[4,32,896]{2,1,0:T(8,128)(2,1)S(1)} %get-tuple-element.95), channel_id=1, source_target_pairs={{0,64},{2,66},{16,80},{18,82},{32,96},{34,98},{48,112},{50,114},{6... | collective-permute-start | bytes 688136 | tf_op jit(solution)/shard_map/ppermute | solution.py:493
  68.7 2.0 %collective-permute-done.13 = bf16[4,32,896]{2,1,0:T(8,128)(2,1)S(1)} collective-permute-done((bf16[4,32,896]{2,1,0:T(8,128)(2,1)S(1)}, bf16[4,32,896]{2,1,0:T(8,128)(2,1)S(1)}, u32[]{:S(2)}, u32[]{:S(2)}) %collective-permute-start.13) | collective-permute-done | bytes 229408 | tf_op jit(solution)/shard_map/ppermute | solution.py:493
  70.7 0.4 collective-permute-done.14
  71.0 3.3 %collective-permute-done.15 = bf16[4,32,896]{2,1,0:T(8,128)(2,1)S(1)} collective-permute-done((bf16[4,32,896]{2,1,0:T(8,128)(2,1)S(1)}, bf16[4,32,896]{2,1,0:T(8,128)(2,1)S(1)}, u32[]{:S(2)}, u32[]{:S(2)}) %collective-permute-start.15) | collective-permute-done | bytes 229408 | tf_op jit(solution)/shard_map/ppermute | solution.py:493
  74.4 0.1 convert_add_fusion
  74.5 1.7 %collective-permute-start.16 = (f32[32,896]{1,0:T(8,128)S(1)}, f32[32,896]{1,0:T(8,128)S(1)}, u32[]{:S(2)}, u32[]{:S(2)}) collective-permute-start(f32[32,896]{1,0:T(8,128)S(1)} %get-tuple-element.112), channel_id=1, source_target_pairs={{0,2},{2,16},{16,18},{18,0},{32,34},{34,48},{48,50},{50,32},{64,66... | collective-permute-start | bytes 344072 | tf_op jit(solution)/shard_map/ppermute | solution.py:493
  76.2 2.2 %collective-permute-start.17 = (f32[32,896]{1,0:T(8,128)S(1)}, f32[32,896]{1,0:T(8,128)S(1)}, u32[]{:S(2)}, u32[]{:S(2)}) collective-permute-start(f32[32,896]{1,0:T(8,128)S(1)} %get-tuple-element.114), channel_id=1, source_target_pairs={{0,18},{2,0},{16,2},{18,16},{32,50},{34,32},{48,34},{50,48},{64,82... | collective-permute-start | bytes 344072 | tf_op jit(solution)/shard_map/ppermute | solution.py:493
  78.5 1.7 %collective-permute-start.18 = (f32[32,896]{1,0:T(8,128)S(1)}, f32[32,896]{1,0:T(8,128)S(1)}, u32[]{:S(2)}, u32[]{:S(2)}) collective-permute-start(f32[32,896]{1,0:T(8,128)S(1)} %get-tuple-element.113), channel_id=1, source_target_pairs={{0,16},{2,18},{16,0},{18,2},{32,48},{34,50},{48,32},{50,34},{64,80... | collective-permute-start | bytes 344072 | tf_op jit(solution)/shard_map/ppermute | solution.py:493
  80.2 1.0 %collective-permute-done.16 = f32[32,896]{1,0:T(8,128)S(1)} collective-permute-done((f32[32,896]{1,0:T(8,128)S(1)}, f32[32,896]{1,0:T(8,128)S(1)}, u32[]{:S(2)}, u32[]{:S(2)}) %collective-permute-start.16) | collective-permute-done | bytes 114720 | tf_op jit(solution)/shard_map/ppermute | solution.py:493
  81.1 0.0 collective-permute-done.17
  81.1 3.6 %collective-permute-done.18 = f32[32,896]{1,0:T(8,128)S(1)} collective-permute-done((f32[32,896]{1,0:T(8,128)S(1)}, f32[32,896]{1,0:T(8,128)S(1)}, u32[]{:S(2)}, u32[]{:S(2)}) %collective-permute-start.18) | collective-permute-done | bytes 114720 | tf_op jit(solution)/shard_map/ppermute | solution.py:493
  84.8 0.1 collective-permute-start.19
  84.9 1.2 %collective-permute-done.19 = f32[16,896]{1,0:T(8,128)S(1)} collective-permute-done((f32[16,896]{1,0:T(8,128)S(1)}, f32[16,896]{1,0:T(8,128)S(1)}, u32[]{:S(2)}, u32[]{:S(2)}) %collective-permute-start.19) | collective-permute-done | bytes 57376 | tf_op jit(solution)/shard_map/ppermute | solution.py:469
  86.1 0.7 select_bitcast_fusion
  (22 shorter events, 0.4 us)
Async XLA Ops:
  0.6 1.0 %copy-start = (bf16[1,4,8,32,256]{4,3,2,1,0:T(8,128)(2,1)S(1)}, bf16[1,4,8,32,256]{4,3,2,1,0:T(8,128)(2,1)}, u32[]{:S(2)}) copy-start(bf16[1,4,8,32,256]{4,3,2,1,0:T(8,128)(2,1)} %param.5) | copy-start | bytes 1572868
  1.7 1.0 %copy-start.2 = (bf16[1,4,8,32,256]{4,3,2,1,0:T(8,128)(2,1)S(1)}, bf16[1,4,8,32,256]{4,3,2,1,0:T(8,128)(2,1)}, u32[]{:S(2)}) copy-start(bf16[1,4,8,32,256]{4,3,2,1,0:T(8,128)(2,1)} %param.4) | copy-start | bytes 1572868
  2.7 5.8 %copy-start.1 = (bf16[1,4,8,32,256]{4,3,2,1,0:T(8,128)(2,1)S(1)}, bf16[1,4,8,32,256]{4,3,2,1,0:T(8,128)(2,1)}, u32[]{:S(2)}) copy-start(bf16[1,4,8,32,256]{4,3,2,1,0:T(8,128)(2,1)} %param.5) | copy-start | bytes 1572868
  2.7 5.8 %copy-start.3 = (bf16[1,4,8,32,256]{4,3,2,1,0:T(8,128)(2,1)S(1)}, bf16[1,4,8,32,256]{4,3,2,1,0:T(8,128)(2,1)}, u32[]{:S(2)}) copy-start(bf16[1,4,8,32,256]{4,3,2,1,0:T(8,128)(2,1)} %param.4) | copy-start | bytes 1572868
  3.5 2.1 %collective-permute-start = (bf16[4,9,32,256]{3,2,1,0:T(8,128)(2,1)S(1)}, bf16[4,9,32,256]{3,2,1,0:T(8,128)(2,1)S(1)}, u32[]{:S(2)}, u32[]{:S(2)}) collective-permute-start(bf16[4,9,32,256]{3,2,1,0:T(8,128)(2,1)S(1)} %get-tuple-element.51), channel_id=1, source_target_pairs={{0,1},{1,0},{2,3},{3,2},{4,5},{5,4},{6,7},{7,6},{8,9},{9,8},{10,11... | collective-permute-start | bytes 1769480 | tf_op jit(solution)/shard_map/ppermute | solution.py:469
  3.6 4.9 %copy-start.4 = (bf16[6912,256]{1,0:T(8,128)(2,1)S(1)}, bf16[6912,256]{1,0:T(8,128)(2,1)}, u32[]{:S(2)}) copy-start(bf16[6912,256]{1,0:T(8,128)(2,1)} %first_hbm.1) | copy-start | bytes 10616836
  5.8 15.0 %collective-permute-start.1 = (bf16[2,9,32,256]{3,2,1,0:T(8,128)(2,1)S(1)}, bf16[2,9,32,256]{3,2,1,0:T(8,128)(2,1)S(1)}, u32[]{:S(2)}, u32[]{:S(2)}) collective-permute-start(bf16[2,9,32,256]{3,2,1,0:T(8,128)(2,1)S(1)} %get-tuple-element.101), channel_id=1, source_target_pairs={{0,2},{2,0},{4,6},{6,4},{8,10},{10,8},{12,14},{14,12},{1,3},{3,1},... | collective-permute-start | bytes 884744 | tf_op jit(solution)/shard_map/ppermute | solution.py:487
  7.9 12.9 %collective-permute-start.2 = (bf16[2,9,32,256]{3,2,1,0:T(8,128)(2,1)S(1)}, bf16[2,9,32,256]{3,2,1,0:T(8,128)(2,1)S(1)}, u32[]{:S(2)}, u32[]{:S(2)}) collective-permute-start(bf16[2,9,32,256]{3,2,1,0:T(8,128)(2,1)S(1)} %get-tuple-element.100), channel_id=1, source_target_pairs={{2,4},{4,2},{6,8},{8,6},{10,12},{12,10},{3,5},{5,3},{7,9},{9,7},{1... | collective-permute-start | bytes 884744 | tf_op jit(solution)/shard_map/ppermute | solution.py:486
  23.1 2.5 %collective-permute-start.3 = (bf16[4,9,32,256]{3,2,1,0:T(8,128)(2,1)S(1)}, bf16[4,9,32,256]{3,2,1,0:T(8,128)(2,1)S(1)}, u32[]{:S(2)}, u32[]{:S(2)}) collective-permute-start(bf16[4,9,32,256]{3,2,1,0:T(8,128)(2,1)S(1)} %get-tuple-element.63), channel_id=1, source_target_pairs={{0,1},{1,0},{2,3},{3,2},{4,5},{5,4},{6,7},{7,6},{8,9},{9,8},{10,11... | collective-permute-start | bytes 1769480 | tf_op jit(solution)/shard_map/ppermute | solution.py:469
  23.3 2.3 %collective-permute-start.4 = (bf16[2,8,32,256]{3,2,1,0:T(8,128)(2,1)S(1)}, bf16[2,8,32,256]{3,2,1,0:T(8,128)(2,1)S(1)}, u32[]{:S(2)}, u32[]{:S(2)}) collective-permute-start(bf16[2,8,32,256]{3,2,1,0:T(8,128)(2,1)S(1)} %maximum_select_fusion), channel_id=1, source_target_pairs={{0,1},{1,0},{2,3},{3,2},{4,5},{5,4},{6,7},{7,6},{8,9},{9,8},{10,11... | collective-permute-start | bytes 786440 | tf_op jit(solution)/shard_map/ppermute | solution.py:469
  30.2 14.1 %collective-permute-start.5 = (bf16[8,32,768]{2,1,0:T(8,128)(2,1)S(1)}, bf16[8,32,768]{2,1,0:T(8,128)(2,1)S(1)}, u32[]{:S(2)}, u32[]{:S(2)}) collective-permute-start(bf16[8,32,768]{2,1,0:T(8,128)(2,1)S(1)} %get-tuple-element.69), channel_id=1, source_target_pairs={{0,4},{2,6},{16,20},{18,22},{32,36},{34,38},{48,52},{50,54},{64,68... | collective-permute-start | bytes 1179656 | tf_op jit(solution)/shard_map/ppermute | solution.py:493
  32.5 14.8 %collective-permute-start.6 = (bf16[8,32,768]{2,1,0:T(8,128)(2,1)S(1)}, bf16[8,32,768]{2,1,0:T(8,128)(2,1)S(1)}, u32[]{:S(2)}, u32[]{:S(2)}) collective-permute-start(bf16[8,32,768]{2,1,0:T(8,128)(2,1)S(1)} %get-tuple-element.70), channel_id=1, source_target_pairs={{0,12},{2,14},{16,28},{18,30},{32,44},{34,46},{48,60},{50,62},{64,... | collective-permute-start | bytes 1179656 | tf_op jit(solution)/shard_map/ppermute | solution.py:493
  33.9 13.7 %collective-permute-start.7 = (bf16[8,32,768]{2,1,0:T(8,128)(2,1)S(1)}, bf16[8,32,768]{2,1,0:T(8,128)(2,1)S(1)}, u32[]{:S(2)}, u32[]{:S(2)}) collective-permute-start(bf16[8,32,768]{2,1,0:T(8,128)(2,1)S(1)} %get-tuple-element.71), channel_id=1, source_target_pairs={{0,8},{2,10},{16,24},{18,26},{32,40},{34,42},{48,56},{50,58},{64,7... | collective-permute-start | bytes 1179656 | tf_op jit(solution)/shard_map/ppermute | solution.py:493
  36.3 21.2 %collective-permute-start.8 = (bf16[2,9,32,256]{3,2,1,0:T(8,128)(2,1)S(1)}, bf16[2,9,32,256]{3,2,1,0:T(8,128)(2,1)S(1)}, u32[]{:S(2)}, u32[]{:S(2)}) collective-permute-start(bf16[2,9,32,256]{3,2,1,0:T(8,128)(2,1)S(1)} %get-tuple-element.97), channel_id=1, source_target_pairs={{0,2},{2,0},{4,6},{6,4},{8,10},{10,8},{12,14},{14,12},{1,3},{3,1},... | collective-permute-start | bytes 884744 | tf_op jit(solution)/shard_map/ppermute | solution.py:487
  38.1 19.4 %collective-permute-start.9 = (bf16[2,9,32,256]{3,2,1,0:T(8,128)(2,1)S(1)}, bf16[2,9,32,256]{3,2,1,0:T(8,128)(2,1)S(1)}, u32[]{:S(2)}, u32[]{:S(2)}) collective-permute-start(bf16[2,9,32,256]{3,2,1,0:T(8,128)(2,1)S(1)} %get-tuple-element.96), channel_id=1, source_target_pairs={{2,4},{4,2},{6,8},{8,6},{10,12},{12,10},{3,5},{5,3},{7,9},{9,7},{1... | collective-permute-start | bytes 884744 | tf_op jit(solution)/shard_map/ppermute | solution.py:486
  44.3 16.3 %collective-permute-start.10 = (bf16[8,32,960]{2,1,0:T(8,128)(2,1)S(1)}, bf16[8,32,960]{2,1,0:T(8,128)(2,1)S(1)}, u32[]{:S(2)}, u32[]{:S(2)}) collective-permute-start(bf16[8,32,960]{2,1,0:T(8,128)(2,1)S(1)} %get-tuple-element.89), channel_id=1, source_target_pairs={{0,4},{2,6},{16,20},{18,22},{32,36},{34,38},{48,52},{50,54},{64,68... | collective-permute-start | bytes 1474568 | tf_op jit(solution)/shard_map/ppermute | solution.py:493
  47.4 13.3 %collective-permute-start.11 = (bf16[8,32,960]{2,1,0:T(8,128)(2,1)S(1)}, bf16[8,32,960]{2,1,0:T(8,128)(2,1)S(1)}, u32[]{:S(2)}, u32[]{:S(2)}) collective-permute-start(bf16[8,32,960]{2,1,0:T(8,128)(2,1)S(1)} %get-tuple-element.90), channel_id=1, source_target_pairs={{0,12},{2,14},{16,28},{18,30},{32,44},{34,46},{48,60},{50,62},{64,... | collective-permute-start | bytes 1474568 | tf_op jit(solution)/shard_map/ppermute | solution.py:493
  47.6 14.0 %collective-permute-start.12 = (bf16[8,32,960]{2,1,0:T(8,128)(2,1)S(1)}, bf16[8,32,960]{2,1,0:T(8,128)(2,1)S(1)}, u32[]{:S(2)}, u32[]{:S(2)}) collective-permute-start(bf16[8,32,960]{2,1,0:T(8,128)(2,1)S(1)} %get-tuple-element.91), channel_id=1, source_target_pairs={{0,8},{2,10},{16,24},{18,26},{32,40},{34,42},{48,56},{50,58},{64,7... | collective-permute-start | bytes 1474568 | tf_op jit(solution)/shard_map/ppermute | solution.py:493
  63.4 7.3 %collective-permute-start.13 = (bf16[4,32,896]{2,1,0:T(8,128)(2,1)S(1)}, bf16[4,32,896]{2,1,0:T(8,128)(2,1)S(1)}, u32[]{:S(2)}, u32[]{:S(2)}) collective-permute-start(bf16[4,32,896]{2,1,0:T(8,128)(2,1)S(1)} %get-tuple-element.93), channel_id=1, source_target_pairs={{0,32},{2,34},{16,48},{18,50},{32,64},{34,66},{48,80},{50,82},{64,... | collective-permute-start | bytes 688136 | tf_op jit(solution)/shard_map/ppermute | solution.py:493
  65.0 6.0 %collective-permute-start.14 = (bf16[4,32,896]{2,1,0:T(8,128)(2,1)S(1)}, bf16[4,32,896]{2,1,0:T(8,128)(2,1)S(1)}, u32[]{:S(2)}, u32[]{:S(2)}) collective-permute-start(bf16[4,32,896]{2,1,0:T(8,128)(2,1)S(1)} %get-tuple-element.94), channel_id=1, source_target_pairs={{0,96},{2,98},{16,112},{18,114},{32,0},{34,2},{48,16},{50,18},{64,... | collective-permute-start | bytes 688136 | tf_op jit(solution)/shard_map/ppermute | solution.py:493
  66.7 7.7 %collective-permute-start.15 = (bf16[4,32,896]{2,1,0:T(8,128)(2,1)S(1)}, bf16[4,32,896]{2,1,0:T(8,128)(2,1)S(1)}, u32[]{:S(2)}, u32[]{:S(2)}) collective-permute-start(bf16[4,32,896]{2,1,0:T(8,128)(2,1)S(1)} %get-tuple-element.95), channel_id=1, source_target_pairs={{0,64},{2,66},{16,80},{18,82},{32,96},{34,98},{48,112},{50,114},{6... | collective-permute-start | bytes 688136 | tf_op jit(solution)/shard_map/ppermute | solution.py:493
  74.5 6.6 %collective-permute-start.16 = (f32[32,896]{1,0:T(8,128)S(1)}, f32[32,896]{1,0:T(8,128)S(1)}, u32[]{:S(2)}, u32[]{:S(2)}) collective-permute-start(f32[32,896]{1,0:T(8,128)S(1)} %get-tuple-element.112), channel_id=1, source_target_pairs={{0,2},{2,16},{16,18},{18,0},{32,34},{34,48},{48,50},{50,32},{64,66... | collective-permute-start | bytes 344072 | tf_op jit(solution)/shard_map/ppermute | solution.py:493
  76.2 4.9 %collective-permute-start.17 = (f32[32,896]{1,0:T(8,128)S(1)}, f32[32,896]{1,0:T(8,128)S(1)}, u32[]{:S(2)}, u32[]{:S(2)}) collective-permute-start(f32[32,896]{1,0:T(8,128)S(1)} %get-tuple-element.114), channel_id=1, source_target_pairs={{0,18},{2,0},{16,2},{18,16},{32,50},{34,32},{48,34},{50,48},{64,82... | collective-permute-start | bytes 344072 | tf_op jit(solution)/shard_map/ppermute | solution.py:493
  78.5 6.3 %collective-permute-start.18 = (f32[32,896]{1,0:T(8,128)S(1)}, f32[32,896]{1,0:T(8,128)S(1)}, u32[]{:S(2)}, u32[]{:S(2)}) collective-permute-start(f32[32,896]{1,0:T(8,128)S(1)} %get-tuple-element.113), channel_id=1, source_target_pairs={{0,16},{2,18},{16,0},{18,2},{32,48},{34,50},{48,32},{50,34},{64,80... | collective-permute-start | bytes 344072 | tf_op jit(solution)/shard_map/ppermute | solution.py:493
  84.8 1.3 %collective-permute-start.19 = (f32[16,896]{1,0:T(8,128)S(1)}, f32[16,896]{1,0:T(8,128)S(1)}, u32[]{:S(2)}, u32[]{:S(2)}) collective-permute-start(f32[16,896]{1,0:T(8,128)S(1)} %get-tuple-element.122), channel_id=1, source_target_pairs={{0,1},{1,0},{2,3},{3,2},{4,5},{5,4},{6,7},{7,6},{8,9},{9,8},{10,11... | collective-permute-start | bytes 172040 | tf_op jit(solution)/shard_map/ppermute | solution.py:469
